TPU v7x, 256 devices: a whole 4x4x8 slice. The times are simulated.
256 devices in a mesh: ctx: 16 (over y_lo, x, core), tp: 16 (over z, y_hi).
Axes of the slice: x: 4, y: 4 (y_hi: 2, y_lo: 2; y = y_hi * 2 + y_lo), z: 8, core: 2. Of those that a mesh axis runs over, the one named last changes fastest.
Arguments:
- hidden: bfloat16 [16384, 8192], P('ctx', 'tp'), may hold values from -20 to 20
- norm_gain: bfloat16 [8192], P('tp'), may hold values from 0.5 to 1.5
- router_weight: bfloat16 [8192], P('tp'), may hold values from -0.0625 to 0.0625
- query_weight: bfloat16 [8192, 4096], P('tp'), may hold values from -29 to 29
- key_value_weight: bfloat16 [2, 8192, 512], P(None, 'tp'), may hold values from -1 to 1
- out_weight: bfloat16 [4096, 8192], P(None, 'tp'), may hold values from -0.5 to 0.5
- kept_rows: int32 [16, 512], replicated, may hold values from 0 to 1024, as said below
Outputs:
- block_update: bfloat16 [16384, 8192], P('ctx', 'tp')
Inputs may be any that keep to these rules, and one draw needn't show every extreme that they name: `kept_rows`: row c lists, in rising order, the distinct local indices of the kept rows of context shard c, then 1024 in every unused slot. The counts of kept rows over all shards sum to 4096; every shard keeps at least one row and some shard keeps exactly 512.
All inputs are finite; a program needn't handle non-finite values.
Results may differ from a plain program's by a relative error of at most 0.025.
Values may be sent and summed in bfloat16 or wider, within the bound.
No kernel may reach another device: no remote copies, remote signals or barrier semaphores. Data moves between devices by JAX's collectives and lax.ppermute only.
A program may use at most 128 MiB of HBM per device.

v0:
```python
import jax
import jax.numpy as jnp
from jax import lax
from jax.sharding import PartitionSpec as P

D = 8192
H = 32
KVH = 4
HD = 128


EPSILON = 1e-05
MASKED_SCORE = -1e30


def shards(hidden, norm_gain, router_weight, query_weight, key_value_weight, out_weight, kept_rows):
    shard_index = lax.axis_index("ctx")
    tp_index = lax.axis_index("tp")
    ctx_count = lax.axis_size("ctx")
    tp_count = lax.axis_size("tp")
    token_count, width_local = hidden.shape
    capacity = kept_rows.shape[1]
    heads_local = H // tp_count
    own_rows = lax.dynamic_index_in_dim(kept_rows, shard_index, 0, keepdims=False)
    is_valid = own_rows < token_count
    safe_rows = jnp.minimum(own_rows, token_count - 1)
    kept_states = hidden[safe_rows]
    widened = kept_states.astype(jnp.float32)
    square_part = jnp.sum(widened * widened, axis=1)
    router_part = jnp.dot(kept_states, router_weight, preferred_element_type=jnp.float32)
    normed = (widened * norm_gain.astype(jnp.float32)).astype(jnp.bfloat16)
    square_sum, router_logit = lax.psum((square_part, router_part), "tp")
    inverse_rms = lax.rsqrt(square_sum / D + EPSILON)
    key_terms = lax.dot_general(
        key_value_weight, normed, (((1,), (1,)), ((), ())), preferred_element_type=jnp.float32
    )
    key_group = tp_index * heads_local // (H // KVH)
    query_sum = lax.psum_scatter(
        lax.dot_general(
            query_weight, normed, (((0,), (1,)), ((), ())), preferred_element_type=jnp.float32
        ).astype(jnp.bfloat16),
        "tp",
        scatter_dimension=0,
        tiled=True,
    ).astype(jnp.float32)
    key_sum = lax.psum(key_terms, "tp").reshape(2, KVH, HD, capacity)
    group_keys = lax.dynamic_index_in_dim(key_sum, key_group, 1, keepdims=False)
    query_heads = (
        (query_sum * inverse_rms[None, :]).astype(jnp.bfloat16).reshape(heads_local, HD, capacity)
    )
    key_values = (group_keys * inverse_rms[None, None, :]).astype(jnp.bfloat16)
    shard_ids = jnp.arange(ctx_count, dtype=jnp.int32)[:, None]
    key_positions = jnp.where(
        kept_rows < token_count, shard_ids * token_count + kept_rows, ctx_count * token_count
    ).reshape(-1)
    query_positions = jnp.where(is_valid, shard_index * token_count + own_rows, -1)
    score_scale = HD ** (-0.5)

    def advance(state, kv_block, block_positions):
        running_peak, running_total, running_acc = state
        scores = (
            jnp.einsum("hdq,dk->hqk", query_heads, kv_block[0], preferred_element_type=jnp.float32)
            * score_scale
        )
        allowed = block_positions[None, None, :] <= query_positions[None, :, None]
        scores = jnp.where(allowed, scores, MASKED_SCORE)
        new_peak = jnp.maximum(running_peak, jnp.max(scores, axis=2))
        exp_weights = jnp.where(allowed, jnp.exp(scores - new_peak[..., None]), 0.0)
        rescale = jnp.exp(running_peak - new_peak)
        new_total = running_total * rescale + jnp.sum(exp_weights, axis=2)
        mixed = jnp.einsum(
            "hqk,dk->hqd",
            exp_weights.astype(jnp.bfloat16),
            kv_block[1],
            preferred_element_type=jnp.float32,
        )
        return (new_peak, new_total, running_acc * rescale[..., None] + mixed)

    initial = (
        jnp.full((heads_local, capacity), MASKED_SCORE, jnp.float32),
        jnp.zeros((heads_local, capacity), jnp.float32),
        jnp.zeros((heads_local, capacity, HD), jnp.float32),
    )
    kv_piece = lax.all_gather(key_values, "ctx", axis=2, tiled=True)
    kv_count = kv_piece.shape[2]
    block_count = kv_count // capacity
    kv_blocks = jnp.transpose(kv_piece.reshape(2, HD, block_count, capacity), (2, 0, 1, 3))
    position_blocks = key_positions.reshape(block_count, capacity)

    def one_block(inner_state, element):
        kv_block, block_positions = element
        inner_state = advance(inner_state, kv_block, block_positions)
        return (inner_state, None)

    final_state, _ = lax.scan(one_block, initial, (kv_blocks, position_blocks))
    final_peak, final_total, final_acc = final_state
    safe_total = jnp.where(is_valid[None, :], final_total, 1.0)
    head_output = (final_acc / safe_total[..., None]).astype(jnp.bfloat16)
    heads_piece = lax.all_gather(head_output, "tp", axis=0, tiled=True)
    head_count = heads_piece.shape[0]
    out_rows = out_weight.reshape(head_count, HD, width_local)
    projected = jnp.einsum("hqd,hde->qe", heads_piece, out_rows, preferred_element_type=jnp.float32)
    row_update = (jax.nn.sigmoid(router_logit)[:, None] * projected).astype(jnp.bfloat16)
    target_rows = jnp.where(is_valid, own_rows, token_count)
    return jnp.zeros_like(hidden).at[target_rows].set(row_update, mode="drop")


def solution(mesh):
    return jax.shard_map(
        shards,
        mesh=mesh,
        in_specs=(
            P("ctx", "tp"),
            P("tp"),
            P("tp"),
            P("tp", None),
            P(None, "tp", None),
            P(None, "tp"),
            P(),
        ),
        out_specs=P("ctx", "tp"),
        check_vma=False,
    )
```

profile of v0, /device:TPU:14, one launch (start us, length us, event | category | flops | bytes accessed | tf_op | source)
XLA Modules:
  0.0 655.3 jit_solution(7662420278019016044)
XLA Ops:
  8.1 3.3 gather_fusion
  11.4 2.1 fusion.20
  13.6 6.5 fusion.14
  21.1 44.4 %all-reduce = (f32[512]{0:T(512)S(1)}, f32[512]{0:T(512)S(1)}) all-reduce(f32[512]{0:T(512)S(1)} %fusion.18, f32[512]{0:T(512)S(1)} %bitcast.86), channel_id=1, replica_groups=mesh['ctx'=16,'tp'=16] {'tp'}, use_global_device_ids=true, to_apply=%region_3.4 | all-reduce | flops 1024 | bytes 8192 | tf_op jit(solution)/shard_map/psum | solution.py:32
  65.5 117.3 %all-reduce.3.cloned.1.call-done = f32[2,4,128,512]{3,2,1,0:T(8,128)} async-done(((f32[2,4,128,512]{3,2,1,0:T(8,128)}), f32[2,4,128,512]{3,2,1,0:T(8,128)}) %all-reduce.3.cloned.1.call-update) | async-done | bytes 2097168 | tf_op jit(solution)/shard_map/psum | solution.py:46
  182.8 1.1 constant_dynamic-slice_fusion.1
  185.2 211.0 %reduce-scatter.2.cloned.1.call-done = bf16[256,512]{0,1:T(8,128)(2,1)} async-done(((bf16[4096,512]{0,1:T(8,128)(2,1)}), bf16[256,512]{0,1:T(8,128)(2,1)}) %reduce-scatter.2.cloned.1.call-update) | async-done | bytes 262160 | tf_op jit(solution)/shard_map/reduce_scatter | solution.py:38
  396.2 1.1 multiply_convert_fusion
  398.1 37.3 %all-gather.3.cloned.1.call-done = bf16[2,128,8192]{1,2,0:T(8,128)(2,1)} async-done(((bf16[2,128,512]{1,2,0:T(8,128)(2,1)}), bf16[2,128,8192]{1,2,0:T(8,128)(2,1)}) %all-gather.3.cloned.1.call-update) | async-done | bytes 4194320 | tf_op jit(solution)/shard_map/all_gather | solution.py:84
  435.4 101.2 %while.15 = (s32[]{:T(128)}, f32[2,512]{1,0:T(2,128)S(1)}, f32[2,512]{1,0:T(2,128)S(1)}, f32[2,512,128]{2,1,0:T(8,128)}, s32[16,512]{1,0:T(8,128)S(1)}, /*index=...) while((s32[]{:T(128)}, f32[2,512]{1,0:T(2,128)S(1)}, ...), condition=%wide.region_8.9_spmd.clone, body=%wide.region_5.8_spmd.clone.sunk | while | flops 275911680 | bytes 15802601 | solution.py:95
  435.6 1.0 dynamic-slice_bitcast_fusion.2
  437.3 1.5 fusion.42
  439.9 1.0 convolution_add_fusion.2
  442.0 1.0 dynamic-slice_bitcast_fusion.2
  443.6 1.5 fusion.42
  448.3 1.0 dynamic-slice_bitcast_fusion.2
  450.0 1.5 fusion.42
  454.6 1.0 dynamic-slice_bitcast_fusion.2
  456.3 1.5 fusion.42
  460.9 1.0 dynamic-slice_bitcast_fusion.2
  462.6 1.5 fusion.42
  467.2 1.0 dynamic-slice_bitcast_fusion.2
  468.9 1.5 fusion.42
  473.6 1.0 dynamic-slice_bitcast_fusion.2
  475.3 1.5 fusion.42
  479.9 1.0 dynamic-slice_bitcast_fusion.2
  481.6 1.5 fusion.42
  486.2 1.0 dynamic-slice_bitcast_fusion.2
  487.9 1.5 fusion.42
  490.5 1.0 convolution_add_fusion.2
  492.5 1.0 dynamic-slice_bitcast_fusion.2
  494.2 1.5 fusion.42
  498.9 1.0 dynamic-slice_bitcast_fusion.2
  500.6 1.5 fusion.42
  505.2 1.0 dynamic-slice_bitcast_fusion.2
  506.9 1.5 fusion.42
  511.5 1.0 dynamic-slice_bitcast_fusion.2
  513.2 1.5 fusion.42
  517.8 1.0 dynamic-slice_bitcast_fusion.2
  519.5 1.5 fusion.42
  524.2 1.0 dynamic-slice_bitcast_fusion.2
  525.9 1.5 fusion.42
  530.5 1.0 dynamic-slice_bitcast_fusion.2
  532.2 1.5 fusion.42
  536.6 1.9 divide_convert_fusion
  538.6 100.9 %all-gather.5.cloned.1.call-done = bf16[32,512,128]{2,1,0:T(8,128)(2,1)} async-done(((bf16[2,512,128]{2,1,0:T(8,128)(2,1)}), bf16[32,512,128]{2,1,0:T(8,128)(2,1)}) %all-gather.5.cloned.1.call-update) | async-done | bytes 4194320 | tf_op jit(solution)/shard_map/all_gather | solution.py:99
  639.5 5.8 fusion.16
  645.3 3.5 scatter_custom_fusion
  (271 shorter events, 63.2 us)
Async XLA Ops:
  6.5 4.9 copy-start
  6.5 176.3 %all-reduce.3.cloned.1.call-start = ((), (), s32[]{:S(2)}) async-start(), calls=%async_computation.1 | async-start | bytes 4194304 | tf_op jit(solution)/shard_map/psum | solution.py:46
  13.5 382.7 %reduce-scatter.2.cloned.1.call-start = ((), (), s32[]{:S(2)}) async-start(), calls=%async_computation.3 | async-start | bytes 4456448 | tf_op jit(solution)/shard_map/reduce_scatter | solution.py:38
  20.1 415.3 %all-gather.3.cloned.1.call-start = ((), (), s32[]{:S(2)}) async-start(), calls=%async_computation.2 | async-start | bytes 4456448 | tf_op jit(solution)/shard_map/all_gather | solution.py:84
  20.7 164.3 %copy-start.5 = (s32[16,512]{1,0:T(8,128)S(1)}, s32[16,512]{1,0:T(8,128)}, u32[]{:S(2)}) copy-start(s32[16,512]{1,0:T(8,128)} %param.15) | copy-start | bytes 98308
  184.9 454.6 %all-gather.5.cloned.1.call-start = ((), (), s32[]{:S(2)}) async-start(), calls=%async_computation.4 | async-start | bytes 4456448 | tf_op jit(solution)/shard_map/all_gather | solution.py:99
  438.8 1.0 copy-start.2
  438.8 1.1 copy-start.3
  440.9 0.8 copy-start.4
  445.1 1.0 copy-start.2
  445.2 1.1 copy-start.3
  447.2 0.8 copy-start.4
  451.5 1.0 copy-start.2
  451.5 1.1 copy-start.3
  453.6 0.8 copy-start.4
  457.8 1.0 copy-start.2
  457.8 1.1 copy-start.3
  459.9 0.8 copy-start.4
  464.1 1.0 copy-start.2
  464.1 1.1 copy-start.3
  466.2 0.8 copy-start.4
  470.4 1.0 copy-start.2
  470.4 1.1 copy-start.3
  472.5 0.8 copy-start.4
  476.8 1.0 copy-start.2
  476.8 1.1 copy-start.3
  478.9 0.8 copy-start.4
  483.1 1.0 copy-start.2
  483.1 1.1 copy-start.3
  485.2 0.8 copy-start.4
  489.4 1.0 copy-start.2
  489.4 1.1 copy-start.3
  491.5 0.8 copy-start.4
  495.7 1.0 copy-start.2
  495.7 1.1 copy-start.3
  497.8 0.8 copy-start.4
  502.1 1.0 copy-start.2
  502.1 1.1 copy-start.3
  508.4 1.0 copy-start.2
  508.4 1.1 copy-start.3
  514.7 1.0 copy-start.2
  514.7 1.1 copy-start.3
  521.0 1.0 copy-start.2
  521.0 1.1 copy-start.3
  527.4 1.0 copy-start.2
  527.4 1.1 copy-start.3
  533.7 1.0 copy-start.2
  533.7 1.1 copy-start.3
  (23 other events, 16.7 us)
Sparse Core Ops, SparseCore 0:
  13.6 169.1 all-reduce.2
  186.8 209.2 reduce-scatter.1
  398.1 37.2 all-gather.2
  538.7 100.7 all-gather.4
where the time goes:
time: 658 us; the launch traced here: 655 us
  waiting for transfers between devices  467 us (71%)
  local copies, waits for them, and re-layouts  57.2 us (9%)
  matrix products  54 us (8%)
  blocking collectives  44.4 us (7%)
  other arithmetic  18.6 us (3%)
  between operations  13.3 us (2%)
    reduce_scatter x1, waiting for transfers between devices, shards(): lax.psum_scatter(lax.dot_general(query_weight, normed, (((0,), (1,)), (()...  211 us
    psum x1, waiting for transfers between devices, shards(): key_sum = lax.psum(key_terms, 'tp').reshape(2, KVH, HD, capacity)  117 us
    all_gather x1, waiting for transfers between devices, shards(): heads_piece = lax.all_gather(head_output, 'tp', axis=0, tiled=True)  101 us
    psum x1, blocking collectives, shards(): square_sum, router_logit = lax.psum((square_part, router_part), 'tp')  44.4 us
    all_gather x1, waiting for transfers between devices, shards(): kv_piece = lax.all_gather(key_values, 'ctx', axis=2, tiled=True)  37.3 us
    while x144, local copies, waits for them, and re-layouts  31.9 us
    dot_general x16, matrix products, advance(): jnp.einsum('hdq,dk->hqk', query_heads, kv_block[0], preferred_element_typ...  23.9 us
    dynamic_slice x32, local copies, waits for them, and re-layouts, shards(): final_state, _ = lax.scan(one_block, initial, (kv_blocks, position_blocks))  15.8 us
  transfers between devices with their start and end apart: 4, of which 4 were waited for; matrix products, arithmetic and copies ran while one was open for 2% of the time, Pallas kernels for 0%

commit v1 on v0

v1 whole, which is shorter than its diff:
```python
import functools

import jax
import jax.numpy as jnp
from jax import lax
from jax.experimental import pallas as pl
from jax.experimental.pallas import tpu as pltpu
from jax.sharding import PartitionSpec as P

D = 8192
H = 32
KVH = 4
HD = 128
ZN = 8
EPSILON = 1e-05
MASKED_SCORE = -1e30
EXP_SCALE = HD ** (-0.5) * 1.4426950408889634
KEY_BLOCK = 256


def z_shift(dz):
    return [(z * 2 + y, ((z + dz) % ZN) * 2 + y) for z in range(ZN) for y in range(2)]


def y_swap():
    return [(t, t ^ 1) for t in range(2 * ZN)]


def core_swap(count):
    return [(c, c ^ 1) for c in range(count)]


def quad_shift(k):
    def target(z):
        return (z // 4) * 4 + (z % 4 + k) % 4

    return [(z * 2 + y, target(z) * 2 + y) for z in range(ZN) for y in range(2)]


def attention_kernel(info_ref, q_ref, kv_ref, o_ref, qt_ref, peak_ref, total_ref, acc_ref):
    shard = pl.program_id(0)
    rows = q_ref.shape[0]
    own = info_ref[pl.num_programs(0)]
    count = info_ref[shard]

    @pl.when(shard == 0)
    def _():
        for head in range(2):
            qt_ref[:, head * rows : (head + 1) * rows] = (
                q_ref[:, head * HD : (head + 1) * HD].astype(jnp.float32).T.astype(jnp.bfloat16)
            )
        peak_ref[...] = jnp.full_like(peak_ref, MASKED_SCORE)
        total_ref[...] = jnp.zeros_like(total_ref)
        acc_ref[...] = jnp.zeros_like(acc_ref)

    for sub in range(rows // KEY_BLOCK):
        start = sub * KEY_BLOCK

        @pl.when((shard <= own) & (start < count))
        def _():
            keys = kv_ref[0, :HD, start : start + KEY_BLOCK]
            values = kv_ref[0, HD:, start : start + KEY_BLOCK]
            scores = lax.dot_general(
                keys, qt_ref[...], (((0,), (0,)), ((), ())), preferred_element_type=jnp.float32
            )
            slot = lax.broadcasted_iota(jnp.int32, (1, 2 * rows), 1) % rows
            limit = jnp.where(shard < own, count, jnp.minimum(count, slot + 1)) - start
            key_slot = lax.broadcasted_iota(jnp.int32, scores.shape, 0)
            scores = jnp.where(key_slot < limit, scores, MASKED_SCORE)
            peak = peak_ref[...]
            new_peak = jnp.maximum(peak, jnp.max(scores, axis=0, keepdims=True))
            weights = jnp.exp2((scores - new_peak) * EXP_SCALE)
            rescale = jnp.exp2((peak - new_peak) * EXP_SCALE)
            total_ref[...] = total_ref[...] * rescale + jnp.sum(weights, axis=0, keepdims=True)
            acc_ref[...] = acc_ref[...] * rescale + jnp.dot(
                values, weights.astype(jnp.bfloat16), preferred_element_type=jnp.float32
            )
            peak_ref[...] = new_peak

    @pl.when(shard == pl.num_programs(0) - 1)
    def _():
        mixed = acc_ref[...] / total_ref[...]
        for head in range(2):
            o_ref[:, head * HD : (head + 1) * HD] = mixed[:, head * rows : (head + 1) * rows].T.astype(
                jnp.bfloat16
            )


def attention(info, queries, kv):
    shards_n, _, rows = kv.shape
    return pl.pallas_call(
        attention_kernel,
        out_shape=jax.ShapeDtypeStruct(queries.shape, jnp.bfloat16),
        grid_spec=pltpu.PrefetchScalarGridSpec(
            num_scalar_prefetch=1,
            grid=(shards_n,),
            in_specs=[
                pl.BlockSpec(queries.shape, lambda s, info: (0, 0)),
                pl.BlockSpec((1, 2 * HD, rows), lambda s, info: (jnp.minimum(s, info[shards_n]), 0, 0)),
            ],
            out_specs=pl.BlockSpec(queries.shape, lambda s, info: (0, 0)),
            scratch_shapes=[
                pltpu.VMEM((HD, 2 * rows), jnp.bfloat16),
                pltpu.VMEM((1, 2 * rows), jnp.float32),
                pltpu.VMEM((1, 2 * rows), jnp.float32),
                pltpu.VMEM((HD, 2 * rows), jnp.float32),
            ],
        ),
        compiler_params=pltpu.CompilerParams(vmem_limit_bytes=32 * 1024 * 1024),
        cost_estimate=pl.CostEstimate(
            flops=4 * 2 * rows * HD * shards_n * rows, bytes_accessed=kv.size * 2, transcendentals=rows * rows * shards_n
        ),
    )(info, queries, kv)


def dot(a, b):
    return jnp.dot(a, b, preferred_element_type=jnp.float32)


def shards(hidden, norm_gain, router_weight, query_weight, key_value_weight, out_weight, kept_rows):
    bf16 = jnp.bfloat16
    shard = lax.axis_index("ctx")
    tp = lax.axis_index("tp")
    shard_n = lax.axis_size("ctx")
    z, y, core = tp // 2, tp % 2, shard % 2
    tokens, width = hidden.shape
    rows = kept_rows.shape[1]
    half_cols = query_weight.shape[1] // 2
    chunk = half_cols // ZN

    def fetch(block, axis):
        got = lax.ppermute(block, "tp", y_swap())
        other = lax.ppermute(got, "ctx", core_swap(shard_n))
        low = jnp.where(core == 0, got, other)
        high = jnp.where(core == 0, other, got)
        return jnp.concatenate([low, high], axis=axis)

    wq_in = fetch(
        lax.dynamic_slice(query_weight, (core * (width // 2), (1 - y) * half_cols), (width // 2, half_cols)), 0
    )
    wo_rows = out_weight.shape[0] // 2
    wo_in = fetch(
        lax.dynamic_slice(out_weight, ((1 - y) * wo_rows + core * (wo_rows // 2), 0), (wo_rows // 2, width)), 0
    )

    own_rows = lax.dynamic_index_in_dim(kept_rows, shard, 0, keepdims=False)
    select = (own_rows[:, None] == jnp.arange(tokens, dtype=jnp.int32)[None, :]).astype(bf16)
    kept = dot(select, hidden)
    square_part = jnp.sum(kept * kept, axis=1)
    router_part = jnp.sum(kept * router_weight.astype(jnp.float32)[None, :], axis=1)
    x_own = (kept * norm_gain.astype(jnp.float32)[None, :]).astype(bf16)
    x_in = lax.ppermute(x_own, "tp", y_swap())

    kv_part = lax.dot_general(
        key_value_weight, x_own, (((1,), (1,)), ((), ())), preferred_element_type=jnp.float32
    ).astype(bf16)
    kv_part = (
        kv_part.reshape(2, 2, 2, 2, HD // 2, rows).transpose(2, 0, 3, 1, 4, 5).reshape(2 * ZN, HD // 2, rows)
    )
    stats = jnp.stack([square_part, router_part])
    stats_high = lax.reduce_precision(stats, 8, 7)
    stats_low = stats - stats_high
    stats_rows = jnp.concatenate([stats_high, stats_low, jnp.zeros((4, rows), jnp.float32)]).astype(bf16)
    sent = jnp.concatenate([kv_part, jnp.broadcast_to(stats_rows[None], (2 * ZN, 8, rows))], axis=1)
    summed = jnp.sum(lax.all_to_all(sent, "tp", 0, 0, tiled=True).astype(jnp.float32), axis=0)
    square_sum = summed[HD // 2] + summed[HD // 2 + 2]
    router_logit = summed[HD // 2 + 1] + summed[HD // 2 + 3]
    inverse_rms = lax.rsqrt(square_sum / D + EPSILON)
    piece = (summed[: HD // 2] * inverse_rms[None, :]).astype(bf16)
    pieces = [lax.ppermute(piece, "tp", quad_shift(k)) for k in (3, 2, 1)] + [piece]
    ordered = jnp.stack(pieces + pieces[:3])
    kv_own = lax.dynamic_slice_in_dim(ordered, (3 - z % 4) % 4, 4, 0).reshape(2 * HD, rows)
    kv_all = lax.all_gather(kv_own, "ctx", axis=0, tiled=False)

    def query_part(offset):
        d = (z + offset) % ZN
        own_w = lax.dynamic_slice(query_weight, (0, y * half_cols + d * chunk), (width, chunk))
        in_w = lax.dynamic_slice(wq_in, (0, d * chunk), (width, chunk))
        return dot(x_own, own_w) + dot(x_in, in_w)

    def right(a):
        return lax.ppermute(a.astype(bf16), "tp", z_shift(1))

    def left(a):
        return lax.ppermute(a.astype(bf16), "tp", z_shift(-1))

    cut = chunk // 2
    far = query_part(4)
    going_right, going_left = right(far[:, :cut]), left(far[:, cut:])
    part = query_part(3)
    going_right = right(jnp.concatenate([part[:, :cut] + going_right, part[:, cut:]], axis=1))
    part = query_part(-3)
    going_left = left(jnp.concatenate([part[:, :cut], part[:, cut:] + going_left], axis=1))
    for step in (2, 1):
        going_right = right(query_part(step) + going_right)
        going_left = left(query_part(-step) + going_left)
    queries = (query_part(0) + going_right + going_left) * inverse_rms[:, None]

    counts = jnp.sum((kept_rows < tokens).astype(jnp.int32), axis=1)
    info = jnp.concatenate([counts, shard[None].astype(jnp.int32)])
    mixed = attention(info, queries.astype(bf16), kv_all)

    def project(piece, offset, low, high):
        start = ((z + offset) % ZN) * chunk + low
        own_w = lax.dynamic_slice(out_weight, (y * wo_rows + start, 0), (high - low, width))
        in_w = lax.dynamic_slice(wo_in, (start, 0), (high - low, width))
        return dot(piece, own_w), dot(piece, in_w)

    terms = [project(mixed, 0, 0, chunk)]
    from_left, from_right = mixed, mixed
    for step in (1, 2, 3):
        from_left, from_right = right(from_left), left(from_right)
        terms.append(project(from_left, -step, 0, chunk))
        terms.append(project(from_right, step, 0, chunk))
    terms.append(project(right(from_left[:, :cut]), 4, 0, cut))
    terms.append(project(left(from_right[:, cut:]), 4, cut, chunk))
    for_partner = functools.reduce(jnp.add, [t[1] for t in terms])
    received = lax.ppermute(for_partner.astype(bf16), "tp", y_swap())
    projected = functools.reduce(jnp.add, [t[0] for t in terms]) + received
    row_update = (jax.nn.sigmoid(router_logit)[:, None] * projected).astype(bf16)
    return lax.dot_general(select, row_update, (((0,), (0,)), ((), ())), preferred_element_type=jnp.float32).astype(
        bf16
    )


def solution(mesh):
    return jax.shard_map(
        shards,
        mesh=mesh,
        in_specs=(
            P("ctx", "tp"),
            P("tp"),
            P("tp"),
            P("tp", None),
            P(None, "tp", None),
            P(None, "tp"),
            P(),
        ),
        out_specs=P("ctx", "tp"),
        check_vma=False,
    )
```

time: 658 us -> 274 us (0.42)
  waiting for transfers between devices: 467 us -> 96.2 us
  local copies, waits for them, and re-layouts: 57.2 us -> 8.38 us
  starting transfers between devices: 0.13 us -> 35.6 us
  Pallas kernels: 0 us -> 20.8 us
  other arithmetic: 18.6 us -> 5.53 us
    reduce_scatter x1 -> x0, waiting for transfers between devices: 211 us -> none  [shards(): lax.psum_scatter(lax.dot_general(query_weight, normed, (((0,), (1,)), (()...]
    all_gather x2 -> x1, waiting for transfers between devices: 138 us -> 0.02 us  [shards(): kv_all = lax.all_gather(kv_own, 'ctx', axis=0, tiled=False)]
    psum x1 -> x0, waiting for transfers between devices: 117 us -> none  [shards(): key_sum = lax.psum(key_terms, 'tp').reshape(2, KVH, HD, capacity)]
    ppermute x0 -> x25, waiting for transfers between devices: none -> 96.1 us  [the longest x2 59.7 us: fetch(): got = lax.ppermute(block, 'tp', y_swap())]
    psum x1 -> x0, blocking collectives: 44.4 us -> none  [shards(): square_sum, router_logit = lax.psum((square_part, router_part), 'tp')]
    all_to_all x0 -> x1, blocking collectives: none -> 43.7 us  [shards(): lax.all_to_all(sent, 'tp', 0, 0, tiled=True).astype(jnp.float32)]
    ppermute x0 -> x25, starting transfers between devices: none -> 35.6 us  [the longest x8 25.6 us: left(): return lax.ppermute(a.astype(bf16), 'tp', z_shift(-1))]
    while x144 -> x0, local copies, waits for them, and re-layouts: 31.9 us -> none
  transfers between devices with their start and end apart: 4 -> 26, of which waited for: 4 -> 17; matrix products, arithmetic and copies ran while one was open for 2% -> 17% of each run, Pallas kernels for 0% -> 8%
where the time goes in v1:
time: 274 us; the launch traced here: 275 us
  waiting for transfers between devices  96.2 us (35%)
  matrix products  51 us (19%)
  blocking collectives  43.7 us (16%)
  starting transfers between devices  35.6 us (13%)
  Pallas kernels  20.8 us (8%)
  between operations  14 us (5%)
  local copies, waits for them, and re-layouts  8.38 us (3%)
  other arithmetic  5.53 us (2%)
    ppermute x2, waiting for transfers between devices, fetch(): got = lax.ppermute(block, 'tp', y_swap())  59.7 us
    dot_general x34, matrix products, dot(): return jnp.dot(a, b, preferred_element_type=jnp.float32)  45.4 us
    all_to_all x1, blocking collectives, shards(): lax.all_to_all(sent, 'tp', 0, 0, tiled=True).astype(jnp.float32)  43.7 us
    ppermute x8, starting transfers between devices, left(): return lax.ppermute(a.astype(bf16), 'tp', z_shift(-1))  25.6 us
    pallas_call x1, Pallas kernels, attention(): pl.pallas_call(attention_kernel, out_shape=jax.ShapeDtypeStruct(queries.s...  20.8 us
    ppermute x8, waiting for transfers between devices, right(): return lax.ppermute(a.astype(bf16), 'tp', z_shift(1))  19.5 us
    ppermute x8, waiting for transfers between devices, left(): return lax.ppermute(a.astype(bf16), 'tp', z_shift(-1))  6.05 us
    ppermute x1, waiting for transfers between devices, shards(): received = lax.ppermute(for_partner.astype(bf16), 'tp', y_swap())  5.64 us
  transfers between devices with their start and end apart: 26, of which 17 were waited for; matrix products, arithmetic and copies ran while one was open for 17% of the time, Pallas kernels for 8%

profile of v1, /device:TPU:14, one launch (start us, length us, event | category | flops | bytes accessed | tf_op | source)
XLA Modules:
  0.0 275.2 jit_solution(17239458979684779919)
XLA Ops:
  8.7 3.0 %multiply_reduce_fusion.1 = (f32[512]{0:T(512)S(1)}, f32[512]{0:T(512)S(1)}, bf16[512,512]{0,1:T(8,128)(2,1)}) fusion(f32[512]{0:T(512)S(1)} %convert_element_type.89, f32[512]{0:T(512)S(1)} %convert_element_type.85, bf16[1024,512]{1,0:T(8,128)(2,1)} %param.7, s32[512]{0:T(512)S(1)} %bitcast.69), kind=kOutput, calls=%fused_computation.84 | convolution fusion | flops 538967040 | bytes 1583104 | tf_op jit(solution)/shard_map/dot_general | solution.py:117
  11.7 1.8 convolution_convert_fusion
  13.9 43.7 %all_to_all.5 = bf16[16,72,512]{2,1,0:T(8,128)(2,1)S(1)} all-to-all(bf16[16,72,512]{2,1,0:T(8,128)(2,1)S(1)} %pad_maximum_fusion), channel_id=1, replica_groups=mesh['ctx'=16,'tp'=16] {'tp'}, dimensions={0} | all-to-all | bytes 2359296 | tf_op jit(solution)/shard_map/all_to_all | solution.py:165
  60.6 1.9 collective-permute-done.11
  62.5 2.6 collective-permute-done.12
  66.7 2.3 dynamic_slice.117
  69.7 2.8 %collective-permute-start = (bf16[512,512]{0,1:T(8,128)(2,1)}, bf16[512,512]{0,1:T(8,128)(2,1)}, u32[]{:S(2)}, u32[]{:S(2)}) collective-permute-start(bf16[512,512]{0,1:T(8,128)(2,1)} %get-tuple-element.11), channel_id=1, source_target_pairs={{0,1},{1,0},{2,3},{3,2},{4,5},{5,4},{6,7},{7,6},{8,9},{9,8},{10,11... | collective-permute-start | bytes 1572872 | tf_op jit(solution)/shard_map/ppermute | solution.py:152
  74.7 2.3 fusion.89
  77.0 2.2 fusion.87
  79.2 2.2 fusion.91
  81.5 34.8 %collective-permute-done.1 = bf16[256,2048]{1,0:T(8,128)(2,1)S(1)} collective-permute-done((bf16[256,2048]{1,0:T(8,128)(2,1)}, bf16[256,2048]{1,0:T(8,128)(2,1)S(1)}, u32[]{:S(2)}, u32[]{:S(2)}) %collective-permute-start.1) | collective-permute-done | bytes 1048608 | tf_op jit(solution)/shard_map/ppermute | solution.py:132
  116.6 1.6 fusion.93
  118.1 1.4 fusion.81
  119.6 1.4 fusion.83
  121.0 1.4 fusion.85
  122.5 24.8 %collective-permute-done.22 = bf16[1024,512]{1,0:T(8,128)(2,1)} collective-permute-done((bf16[1024,512]{1,0:T(8,128)(2,1)S(1)}, bf16[1024,512]{1,0:T(8,128)(2,1)}, u32[]{:S(2)}, u32[]{:S(2)}) %collective-permute-start.22) | collective-permute-done | bytes 1048608 | tf_op jit(solution)/shard_map/ppermute | solution.py:132
  147.4 1.7 broadcast_select_fusion.2
  149.1 1.4 fusion.27
  150.6 1.6 collective-permute-start.3
  152.1 1.4 convolution_add_fusion.11
  153.6 2.0 collective-permute-start.7
  155.5 1.4 convolution_add_fusion.7
  158.2 2.0 collective-permute-done.7
  160.3 2.3 collective-permute-start.8
  162.5 4.5 %collective-permute-done.4 = bf16[512,256]{1,0:T(8,128)(2,1)S(1)} collective-permute-done((bf16[512,256]{1,0:T(8,128)(2,1)S(1)}, bf16[512,256]{1,0:T(8,128)(2,1)S(1)}, u32[]{:S(2)}, u32[]{:S(2)}) %collective-permute-start.4) | collective-permute-done | bytes 262176 | tf_op jit(solution)/shard_map/ppermute | solution.py:182
  167.0 1.4 fusion.24
  168.5 1.4 fusion.26
  169.9 3.3 %collective-permute-start.9 = (bf16[512,256]{1,0:T(8,128)(2,1)S(1)}, bf16[512,256]{1,0:T(8,128)(2,1)S(1)}, u32[]{:S(2)}, u32[]{:S(2)}) collective-permute-start(bf16[512,256]{1,0:T(8,128)(2,1)S(1)} %fusion.26), channel_id=1, source_target_pairs={{0,14},{1,15},{2,0},{3,1},{4,2},{5,3},{6,4},{7,5},{8,6},{9,7},{10,... | collective-permute-start | bytes 786440 | tf_op jit(solution)/shard_map/ppermute | solution.py:185
  173.2 3.5 %collective-permute-done.5 = bf16[512,256]{1,0:T(8,128)(2,1)S(1)} collective-permute-done((bf16[512,256]{1,0:T(8,128)(2,1)S(1)}, bf16[512,256]{1,0:T(8,128)(2,1)S(1)}, u32[]{:S(2)}, u32[]{:S(2)}) %collective-permute-start.5) | collective-permute-done | bytes 262176 | tf_op jit(solution)/shard_map/ppermute | solution.py:182
  176.8 1.4 fusion.23
  178.3 2.1 fusion.25
  180.4 3.2 %collective-permute-start.10 = (bf16[512,256]{1,0:T(8,128)(2,1)}, bf16[512,256]{1,0:T(8,128)(2,1)}, u32[]{:S(2)}, u32[]{:S(2)}) collective-permute-start(bf16[512,256]{1,0:T(8,128)(2,1)} %fusion.25), channel_id=1, source_target_pairs={{0,14},{1,15},{2,0},{3,1},{4,2},{5,3},{6,4},{7,5},{8,6},{9,7},{10,... | collective-permute-start | bytes 786440 | tf_op jit(solution)/shard_map/ppermute | solution.py:185
  183.7 1.4 fusion.95
  185.9 1.9 collective-permute-done.10
  187.8 1.5 fusion.28.q_ref
  189.4 2.2 copy-done.1
  191.6 20.8 %shard_map.73 = bf16[512,256]{1,0:T(8,128)(2,1)S(1)} custom-call(s32[17]{0:T(128)S(1)} %pad_add_fusion.info_ref, bf16[512,256]{1,0:T(8,128)(2,1)S(1)} %fusion.28.q_ref, bf16[16,256,512]{2,1,0:T(8,128)(2,1)S(1)} %copy-done.1), custom_call_target="tpu_custom_call" | custom-call | flops 4294967296 | bytes 4194304 | tf_op jit(solution)/shard_map/pallas_call | solution.py:91
  212.5 1.7 broadcast_select_fusion
  214.2 4.0 %collective-permute-start.15 = (bf16[512,256]{1,0:T(8,128)(2,1)S(1)}, bf16[512,256]{1,0:T(8,128)(2,1)S(1)}, u32[]{:S(2)}, u32[]{:S(2)}) collective-permute-start(bf16[512,256]{1,0:T(8,128)(2,1)S(1)} %shard_map.73), channel_id=1, source_target_pairs={{0,14},{1,15},{2,0},{3,1},{4,2},{5,3},{6,4},{7,5},{8,6},{9,7},{10,... | collective-permute-start | bytes 786440 | tf_op jit(solution)/shard_map/ppermute | solution.py:185
  223.1 3.8 %collective-permute-start.17 = (bf16[512,256]{1,0:T(8,128)(2,1)S(1)}, bf16[512,256]{1,0:T(8,128)(2,1)S(1)}, u32[]{:S(2)}, u32[]{:S(2)}) collective-permute-start(bf16[512,256]{1,0:T(8,128)(2,1)S(1)} %collective-permute-done.15), channel_id=1, source_target_pairs={{0,14},{1,15},{2,0},{3,1},{4,2},{5,3},{6,4},{7,5},{8,6},{9,7},{10,... | collective-permute-start | bytes 786440 | tf_op jit(solution)/shard_map/ppermute | solution.py:185
  231.2 3.8 %collective-permute-start.19 = (bf16[512,256]{1,0:T(8,128)(2,1)S(1)}, bf16[512,256]{1,0:T(8,128)(2,1)S(1)}, u32[]{:S(2)}, u32[]{:S(2)}) collective-permute-start(bf16[512,256]{1,0:T(8,128)(2,1)S(1)} %collective-permute-done.17), channel_id=1, source_target_pairs={{0,14},{1,15},{2,0},{3,1},{4,2},{5,3},{6,4},{7,5},{8,6},{9,7},{10,... | collective-permute-start | bytes 786440 | tf_op jit(solution)/shard_map/ppermute | solution.py:185
  236.8 2.3 fusion.7
  239.1 6.2 %collective-permute-done.18 = bf16[512,256]{1,0:T(8,128)(2,1)S(1)} collective-permute-done((bf16[512,256]{1,0:T(8,128)(2,1)S(1)}, bf16[512,256]{1,0:T(8,128)(2,1)S(1)}, u32[]{:S(2)}, u32[]{:S(2)}) %collective-permute-start.18) | collective-permute-done | bytes 262176 | tf_op jit(solution)/shard_map/ppermute | solution.py:182
  245.4 3.3 %collective-permute-start.21 = (bf16[512,128]{1,0:T(8,128)(2,1)S(1)}, bf16[512,128]{1,0:T(8,128)(2,1)S(1)}, u32[]{:S(2)}, u32[]{:S(2)}) collective-permute-start(bf16[512,128]{1,0:T(8,128)(2,1)S(1)} %slice.68), channel_id=1, source_target_pairs={{0,14},{1,15},{2,0},{3,1},{4,2},{5,3},{6,4},{7,5},{8,6},{9,7},{10,... | collective-permute-start | bytes 393224 | tf_op jit(solution)/shard_map/ppermute | solution.py:185
  249.2 2.4 collective-permute-done.20
  255.9 2.2 fusion.104
  258.1 5.6 %collective-permute-done.24 = bf16[512,512]{1,0:T(8,128)(2,1)S(1)} collective-permute-done((bf16[512,512]{1,0:T(8,128)(2,1)S(1)}, bf16[512,512]{1,0:T(8,128)(2,1)S(1)}, u32[]{:S(2)}, u32[]{:S(2)}) %collective-permute-start.24) | collective-permute-done | bytes 524320 | tf_op jit(solution)/shard_map/ppermute | solution.py:218
  264.5 3.8 %fusion.2 = bf16[1024,512]{1,0:T(8,128)(2,1)} fusion(f32[512,512]{1,0:T(8,128)} %fusion.104, f32[512,512]{1,0:T(8,128)S(1)} %fusion.106, f32[512,512]{1,0:T(8,128)S(1)} %fusion.70, f32[512,512]{1,0:T(8,128)} %fusion.7, bf16[512,256]{1,0:T(8,128)(2,1)S(1)} %collective-permute-done.18, bf16[512,512]{1,0:T(8,128)(2,1)} %copy-done.6, s32[512]{0:T(512)S(1)} %bitcast.70, ...), kind=kOutput, calls=%fused_computation.38 | convolution fusion | flops 674234368 | bytes 6295556 | tf_op jit(solution)/shard_map/dot_general | solution.py:221
  (95 shorter events, 29.4 us)
Async XLA Ops:
  6.5 5.2 %copy-start = (bf16[2,512,512]{2,1,0:T(8,128)(2,1)S(1)}, bf16[2,512,512]{2,1,0:T(8,128)(2,1)}, u32[]{:S(2)}) copy-start(bf16[2,512,512]{2,1,0:T(8,128)(2,1)} %param.11) | copy-start | bytes 3145732
  6.5 182.8 %all-gather.2.cloned.1.call-start = ((), (), s32[]{:S(2)}) async-start(), calls=%async_computation.1 | async-start | bytes 4456448 | tf_op jit(solution)/shard_map/all_gather | solution.py:173
  57.8 4.6 %collective-permute-start.11 = (bf16[64,512]{1,0:T(8,128)(2,1)S(1)}, bf16[64,512]{1,0:T(8,128)(2,1)S(1)}, u32[]{:S(2)}, u32[]{:S(2)}) collective-permute-start(bf16[64,512]{1,0:T(8,128)(2,1)S(1)} %fusion.103), channel_id=1, source_target_pairs={{0,6},{1,7},{2,0},{3,1},{4,2},{5,3},{6,4},{7,5},{8,14},{9,15},{10,... | collective-permute-start | bytes 196616 | tf_op jit(solution)/shard_map/ppermute | solution.py:170
  58.7 6.4 %collective-permute-start.12 = (bf16[64,512]{1,0:T(8,128)(2,1)S(1)}, bf16[64,512]{1,0:T(8,128)(2,1)S(1)}, u32[]{:S(2)}, u32[]{:S(2)}) collective-permute-start(bf16[64,512]{1,0:T(8,128)(2,1)S(1)} %fusion.103), channel_id=1, source_target_pairs={{0,4},{1,5},{2,6},{3,7},{4,0},{5,1},{6,2},{7,3},{8,12},{9,13},{10,... | collective-permute-start | bytes 196616 | tf_op jit(solution)/shard_map/ppermute | solution.py:170
  59.8 6.1 %collective-permute-start.13 = (bf16[64,512]{1,0:T(8,128)(2,1)S(1)}, bf16[64,512]{1,0:T(8,128)(2,1)S(1)}, u32[]{:S(2)}, u32[]{:S(2)}) collective-permute-start(bf16[64,512]{1,0:T(8,128)(2,1)S(1)} %fusion.103), channel_id=1, source_target_pairs={{0,2},{1,3},{2,4},{3,5},{4,6},{5,7},{6,0},{7,1},{8,10},{9,11},{10,... | collective-permute-start | bytes 196616 | tf_op jit(solution)/shard_map/ppermute | solution.py:170
  69.0 47.3 %collective-permute-start.1 = (bf16[256,2048]{1,0:T(8,128)(2,1)}, bf16[256,2048]{1,0:T(8,128)(2,1)S(1)}, u32[]{:S(2)}, u32[]{:S(2)}) collective-permute-start(bf16[256,2048]{1,0:T(8,128)(2,1)} %dynamic_slice.117), channel_id=1, source_target_pairs={{0,1},{1,0},{2,3},{3,2},{4,5},{5,4},{6,7},{7,6},{8,9},{9,8},{10,11... | collective-permute-start | bytes 3145736 | tf_op jit(solution)/shard_map/ppermute | solution.py:132
  69.7 79.3 %collective-permute-start = (bf16[512,512]{0,1:T(8,128)(2,1)}, bf16[512,512]{0,1:T(8,128)(2,1)}, u32[]{:S(2)}, u32[]{:S(2)}) collective-permute-start(bf16[512,512]{0,1:T(8,128)(2,1)} %get-tuple-element.11), channel_id=1, source_target_pairs={{0,1},{1,0},{2,3},{3,2},{4,5},{5,4},{6,7},{7,6},{8,9},{9,8},{10,11... | collective-permute-start | bytes 1572872 | tf_op jit(solution)/shard_map/ppermute | solution.py:152
  73.8 42.5 %copy-start.7 = (s32[16,512]{1,0:T(8,128)S(1)}, s32[16,512]{1,0:T(8,128)}, u32[]{:S(2)}) copy-start(s32[16,512]{1,0:T(8,128)} %param.13) | copy-start | bytes 98308
  73.8 73.5 %collective-permute-start.22 = (bf16[1024,512]{1,0:T(8,128)(2,1)S(1)}, bf16[1024,512]{1,0:T(8,128)(2,1)}, u32[]{:S(2)}, u32[]{:S(2)}) collective-permute-start(bf16[1024,512]{1,0:T(8,128)(2,1)S(1)} %constant_dynamic-slice_fusion), channel_id=1, source_target_pairs={{0,1},{1,0},{2,3},{3,2},{4,5},{5,4},{6,7},{7,6},{8,9},{9,8},{10,11... | collective-permute-start | bytes 3145736 | tf_op jit(solution)/shard_map/ppermute | solution.py:132
  116.3 6.2 %copy-start.5 = (bf16[256,2048]{1,0:T(8,128)(2,1)}, bf16[256,2048]{1,0:T(8,128)(2,1)S(1)}, u32[]{:S(2)}) copy-start(bf16[256,2048]{1,0:T(8,128)(2,1)S(1)} %collective-permute-done.1) | copy-start | bytes 3145732
  116.3 31.1 %collective-permute-start.2 = (bf16[256,2048]{1,0:T(8,128)(2,1)S(1)}, bf16[256,2048]{1,0:T(8,128)(2,1)}, u32[]{:S(2)}, u32[]{:S(2)}) collective-permute-start(bf16[256,2048]{1,0:T(8,128)(2,1)S(1)} %collective-permute-done.1), channel_id=1, source_target_pairs={{0,16},{16,0},{32,48},{48,32},{64,80},{80,64},{96,112},{112,96},{1... | collective-permute-start | bytes 3145736 | tf_op jit(solution)/shard_map/ppermute | solution.py:133
  122.5 26.6 %copy-start.4 = (f32[512,256]{1,0:T(8,128)S(1)}, f32[512,256]{1,0:T(8,128)}, u32[]{:S(2)}) copy-start(f32[512,256]{1,0:T(8,128)} %fusion.87) | copy-start | bytes 1572868
  147.3 65.1 %collective-permute-start.23 = (bf16[1024,512]{1,0:T(8,128)(2,1)}, bf16[1024,512]{1,0:T(8,128)(2,1)}, u32[]{:S(2)}, u32[]{:S(2)}) collective-permute-start(bf16[1024,512]{1,0:T(8,128)(2,1)} %collective-permute-done.22), channel_id=1, source_target_pairs={{0,16},{16,0},{32,48},{48,32},{64,80},{80,64},{96,112},{112,96},{1... | collective-permute-start | bytes 3145736 | tf_op jit(solution)/shard_map/ppermute | solution.py:133
  149.0 3.1 %copy-start.3 = (f32[512,256]{1,0:T(8,128)S(1)}, f32[512,256]{1,0:T(8,128)}, u32[]{:S(2)}) copy-start(f32[512,256]{1,0:T(8,128)} %fusion.89) | copy-start | bytes 1572868
  150.6 7.2 %collective-permute-start.3 = (bf16[512,128]{1,0:T(8,128)(2,1)S(1)}, bf16[512,128]{1,0:T(8,128)(2,1)S(1)}, u32[]{:S(2)}, u32[]{:S(2)}) collective-permute-start(bf16[512,128]{1,0:T(8,128)(2,1)S(1)} %get-tuple-element.12), channel_id=1, source_target_pairs={{0,2},{1,3},{2,4},{3,5},{4,6},{5,7},{6,8},{7,9},{8,10},{9,11},{10,... | collective-permute-start | bytes 393224 | tf_op jit(solution)/shard_map/ppermute | solution.py:182
  153.6 6.6 %collective-permute-start.7 = (bf16[512,128]{1,0:T(8,128)(2,1)S(1)}, bf16[512,128]{1,0:T(8,128)(2,1)S(1)}, u32[]{:S(2)}, u32[]{:S(2)}) collective-permute-start(bf16[512,128]{1,0:T(8,128)(2,1)S(1)} %get-tuple-element.13), channel_id=1, source_target_pairs={{0,14},{1,15},{2,0},{3,1},{4,2},{5,3},{6,4},{7,5},{8,6},{9,7},{10,... | collective-permute-start | bytes 393224 | tf_op jit(solution)/shard_map/ppermute | solution.py:185
  156.9 10.1 %copy-start.2 = (f32[512,256]{1,0:T(8,128)S(1)}, f32[512,256]{1,0:T(8,128)}, u32[]{:S(2)}) copy-start(f32[512,256]{1,0:T(8,128)} %fusion.91) | copy-start | bytes 1572868
  157.8 9.2 %collective-permute-start.4 = (bf16[512,256]{1,0:T(8,128)(2,1)S(1)}, bf16[512,256]{1,0:T(8,128)(2,1)S(1)}, u32[]{:S(2)}, u32[]{:S(2)}) collective-permute-start(bf16[512,256]{1,0:T(8,128)(2,1)S(1)} %pad_maximum_fusion.1), channel_id=1, source_target_pairs={{0,2},{1,3},{2,4},{3,5},{4,6},{5,7},{6,8},{7,9},{8,10},{9,11},{10,... | collective-permute-start | bytes 786440 | tf_op jit(solution)/shard_map/ppermute | solution.py:182
  160.3 8.3 %collective-permute-start.8 = (bf16[512,256]{1,0:T(8,128)(2,1)S(1)}, bf16[512,256]{1,0:T(8,128)(2,1)S(1)}, u32[]{:S(2)}, u32[]{:S(2)}) collective-permute-start(bf16[512,256]{1,0:T(8,128)(2,1)S(1)} %pad_maximum_fusion.2), channel_id=1, source_target_pairs={{0,14},{1,15},{2,0},{3,1},{4,2},{5,3},{6,4},{7,5},{8,6},{9,7},{10,... | collective-permute-start | bytes 786440 | tf_op jit(solution)/shard_map/ppermute | solution.py:185
  168.4 8.3 %collective-permute-start.5 = (bf16[512,256]{1,0:T(8,128)(2,1)S(1)}, bf16[512,256]{1,0:T(8,128)(2,1)S(1)}, u32[]{:S(2)}, u32[]{:S(2)}) collective-permute-start(bf16[512,256]{1,0:T(8,128)(2,1)S(1)} %fusion.24), channel_id=1, source_target_pairs={{0,2},{1,3},{2,4},{3,5},{4,6},{5,7},{6,8},{7,9},{8,10},{9,11},{10,... | collective-permute-start | bytes 786440 | tf_op jit(solution)/shard_map/ppermute | solution.py:182
  169.9 8.3 %collective-permute-start.9 = (bf16[512,256]{1,0:T(8,128)(2,1)S(1)}, bf16[512,256]{1,0:T(8,128)(2,1)S(1)}, u32[]{:S(2)}, u32[]{:S(2)}) collective-permute-start(bf16[512,256]{1,0:T(8,128)(2,1)S(1)} %fusion.26), channel_id=1, source_target_pairs={{0,14},{1,15},{2,0},{3,1},{4,2},{5,3},{6,4},{7,5},{8,6},{9,7},{10,... | collective-permute-start | bytes 786440 | tf_op jit(solution)/shard_map/ppermute | solution.py:185
  178.2 7.8 %collective-permute-start.6 = (bf16[512,256]{1,0:T(8,128)(2,1)S(1)}, bf16[512,256]{1,0:T(8,128)(2,1)}, u32[]{:S(2)}, u32[]{:S(2)}) collective-permute-start(bf16[512,256]{1,0:T(8,128)(2,1)S(1)} %fusion.23), channel_id=1, source_target_pairs={{0,2},{1,3},{2,4},{3,5},{4,6},{5,7},{6,8},{7,9},{8,10},{9,11},{10,... | collective-permute-start | bytes 786440 | tf_op jit(solution)/shard_map/ppermute | solution.py:182
  180.4 7.4 %collective-permute-start.10 = (bf16[512,256]{1,0:T(8,128)(2,1)}, bf16[512,256]{1,0:T(8,128)(2,1)}, u32[]{:S(2)}, u32[]{:S(2)}) collective-permute-start(bf16[512,256]{1,0:T(8,128)(2,1)} %fusion.25), channel_id=1, source_target_pairs={{0,14},{1,15},{2,0},{3,1},{4,2},{5,3},{6,4},{7,5},{8,6},{9,7},{10,... | collective-permute-start | bytes 786440 | tf_op jit(solution)/shard_map/ppermute | solution.py:185
  189.4 2.2 copy-start.1
  212.4 8.4 %collective-permute-start.14 = (bf16[512,256]{1,0:T(8,128)(2,1)S(1)}, bf16[512,256]{1,0:T(8,128)(2,1)S(1)}, u32[]{:S(2)}, u32[]{:S(2)}) collective-permute-start(bf16[512,256]{1,0:T(8,128)(2,1)S(1)} %shard_map.73), channel_id=1, source_target_pairs={{0,2},{1,3},{2,4},{3,5},{4,6},{5,7},{6,8},{7,9},{8,10},{9,11},{10,... | collective-permute-start | bytes 786440 | tf_op jit(solution)/shard_map/ppermute | solution.py:182
  214.2 7.9 %collective-permute-start.15 = (bf16[512,256]{1,0:T(8,128)(2,1)S(1)}, bf16[512,256]{1,0:T(8,128)(2,1)S(1)}, u32[]{:S(2)}, u32[]{:S(2)}) collective-permute-start(bf16[512,256]{1,0:T(8,128)(2,1)S(1)} %shard_map.73), channel_id=1, source_target_pairs={{0,14},{1,15},{2,0},{3,1},{4,2},{5,3},{6,4},{7,5},{8,6},{9,7},{10,... | collective-permute-start | bytes 786440 | tf_op jit(solution)/shard_map/ppermute | solution.py:185
  223.1 7.7 %collective-permute-start.17 = (bf16[512,256]{1,0:T(8,128)(2,1)S(1)}, bf16[512,256]{1,0:T(8,128)(2,1)S(1)}, u32[]{:S(2)}, u32[]{:S(2)}) collective-permute-start(bf16[512,256]{1,0:T(8,128)(2,1)S(1)} %collective-permute-done.15), channel_id=1, source_target_pairs={{0,14},{1,15},{2,0},{3,1},{4,2},{5,3},{6,4},{7,5},{8,6},{9,7},{10,... | collective-permute-start | bytes 786440 | tf_op jit(solution)/shard_map/ppermute | solution.py:185
  226.8 9.4 %collective-permute-start.16 = (bf16[512,256]{1,0:T(8,128)(2,1)S(1)}, bf16[512,256]{1,0:T(8,128)(2,1)S(1)}, u32[]{:S(2)}, u32[]{:S(2)}) collective-permute-start(bf16[512,256]{1,0:T(8,128)(2,1)S(1)} %collective-permute-done.14), channel_id=1, source_target_pairs={{0,2},{1,3},{2,4},{3,5},{4,6},{5,7},{6,8},{7,9},{8,10},{9,11},{10,... | collective-permute-start | bytes 786440 | tf_op jit(solution)/shard_map/ppermute | solution.py:182
  231.2 14.2 %collective-permute-start.19 = (bf16[512,256]{1,0:T(8,128)(2,1)S(1)}, bf16[512,256]{1,0:T(8,128)(2,1)S(1)}, u32[]{:S(2)}, u32[]{:S(2)}) collective-permute-start(bf16[512,256]{1,0:T(8,128)(2,1)S(1)} %collective-permute-done.17), channel_id=1, source_target_pairs={{0,14},{1,15},{2,0},{3,1},{4,2},{5,3},{6,4},{7,5},{8,6},{9,7},{10,... | collective-permute-start | bytes 786440 | tf_op jit(solution)/shard_map/ppermute | solution.py:185
  236.2 9.1 %collective-permute-start.18 = (bf16[512,256]{1,0:T(8,128)(2,1)S(1)}, bf16[512,256]{1,0:T(8,128)(2,1)S(1)}, u32[]{:S(2)}, u32[]{:S(2)}) collective-permute-start(bf16[512,256]{1,0:T(8,128)(2,1)S(1)} %collective-permute-done.16), channel_id=1, source_target_pairs={{0,2},{1,3},{2,4},{3,5},{4,6},{5,7},{6,8},{7,9},{8,10},{9,11},{10,... | collective-permute-start | bytes 786440 | tf_op jit(solution)/shard_map/ppermute | solution.py:182
  245.3 6.3 %collective-permute-start.20 = (bf16[512,128]{1,0:T(8,128)(2,1)S(1)}, bf16[512,128]{1,0:T(8,128)(2,1)S(1)}, u32[]{:S(2)}, u32[]{:S(2)}) collective-permute-start(bf16[512,128]{1,0:T(8,128)(2,1)S(1)} %slice.67), channel_id=1, source_target_pairs={{0,2},{1,3},{2,4},{3,5},{4,6},{5,7},{6,8},{7,9},{8,10},{9,11},{10,... | collective-permute-start | bytes 393224 | tf_op jit(solution)/shard_map/ppermute | solution.py:182
  245.4 6.5 %collective-permute-start.21 = (bf16[512,128]{1,0:T(8,128)(2,1)S(1)}, bf16[512,128]{1,0:T(8,128)(2,1)S(1)}, u32[]{:S(2)}, u32[]{:S(2)}) collective-permute-start(bf16[512,128]{1,0:T(8,128)(2,1)S(1)} %slice.68), channel_id=1, source_target_pairs={{0,14},{1,15},{2,0},{3,1},{4,2},{5,3},{6,4},{7,5},{8,6},{9,7},{10,... | collective-permute-start | bytes 393224 | tf_op jit(solution)/shard_map/ppermute | solution.py:185
  253.0 10.8 %collective-permute-start.24 = (bf16[512,512]{1,0:T(8,128)(2,1)S(1)}, bf16[512,512]{1,0:T(8,128)(2,1)S(1)}, u32[]{:S(2)}, u32[]{:S(2)}) collective-permute-start(bf16[512,512]{1,0:T(8,128)(2,1)S(1)} %fusion.14), channel_id=1, source_target_pairs={{0,1},{1,0},{2,3},{3,2},{4,5},{5,4},{6,7},{7,6},{8,9},{9,8},{10,11... | collective-permute-start | bytes 1572872 | tf_op jit(solution)/shard_map/ppermute | solution.py:218
  263.7 0.8 copy-start.6
Sparse Core Ops, SparseCore 0:
  66.8 49.8 all-gather.1

commit v2 on v1

--- a/solution.py
+++ b/solution.py
@@ -16,6 +16,8 @@
 MASKED_SCORE = -1e30
 EXP_SCALE = HD ** (-0.5) * 1.4426950408889634
 KEY_BLOCK = 256
+ROW_TILE = 128
+TILES_AT_ONCE = 2
 
 
 def z_shift(dz):
@@ -42,52 +44,75 @@
     rows = q_ref.shape[0]
     own = info_ref[pl.num_programs(0)]
     count = info_ref[shard]
+    own_count = info_ref[own]
+    tiles = rows // ROW_TILE
+    lanes = 2 * ROW_TILE
 
     @pl.when(shard == 0)
     def _():
-        for head in range(2):
-            qt_ref[:, head * rows : (head + 1) * rows] = (
-                q_ref[:, head * HD : (head + 1) * HD].astype(jnp.float32).T.astype(jnp.bfloat16)
-            )
+        for tile in range(tiles):
+            for head in range(2):
+                block = q_ref[tile * ROW_TILE : (tile + 1) * ROW_TILE, head * HD : (head + 1) * HD]
+                qt_ref[tile, :, head * ROW_TILE : (head + 1) * ROW_TILE] = (
+                    block.astype(jnp.float32).T.astype(jnp.bfloat16)
+                )
         peak_ref[...] = jnp.full_like(peak_ref, MASKED_SCORE)
         total_ref[...] = jnp.zeros_like(total_ref)
         acc_ref[...] = jnp.zeros_like(acc_ref)
 
-    for sub in range(rows // KEY_BLOCK):
-        start = sub * KEY_BLOCK
-
-        @pl.when((shard <= own) & (start < count))
-        def _():
-            keys = kv_ref[0, :HD, start : start + KEY_BLOCK]
-            values = kv_ref[0, HD:, start : start + KEY_BLOCK]
-            scores = lax.dot_general(
-                keys, qt_ref[...], (((0,), (0,)), ((), ())), preferred_element_type=jnp.float32
-            )
-            slot = lax.broadcasted_iota(jnp.int32, (1, 2 * rows), 1) % rows
+    def update(tile, start, masked):
+        keys = kv_ref[0, :HD, start : start + KEY_BLOCK]
+        values = kv_ref[0, HD:, start : start + KEY_BLOCK]
+        scores = lax.dot_general(
+            keys, qt_ref[tile], (((0,), (0,)), ((), ())), preferred_element_type=jnp.float32
+        )
+        if masked:
+            slot = tile * ROW_TILE + lax.broadcasted_iota(jnp.int32, (1, lanes), 1) % ROW_TILE
             limit = jnp.where(shard < own, count, jnp.minimum(count, slot + 1)) - start
             key_slot = lax.broadcasted_iota(jnp.int32, scores.shape, 0)
             scores = jnp.where(key_slot < limit, scores, MASKED_SCORE)
-            peak = peak_ref[...]
-            new_peak = jnp.maximum(peak, jnp.max(scores, axis=0, keepdims=True))
-            weights = jnp.exp2((scores - new_peak) * EXP_SCALE)
-            rescale = jnp.exp2((peak - new_peak) * EXP_SCALE)
-            total_ref[...] = total_ref[...] * rescale + jnp.sum(weights, axis=0, keepdims=True)
-            acc_ref[...] = acc_ref[...] * rescale + jnp.dot(
-                values, weights.astype(jnp.bfloat16), preferred_element_type=jnp.float32
-            )
-            peak_ref[...] = new_peak
+        peak = peak_ref[tile]
+        new_peak = jnp.maximum(peak, jnp.max(scores, axis=0, keepdims=True))
+        weights = jnp.exp2(scores - new_peak)
+        rescale = jnp.exp2(peak - new_peak)
+        total_ref[tile] = total_ref[tile] * rescale + jnp.sum(weights, axis=0, keepdims=True)
+        acc_ref[tile] = acc_ref[tile] * rescale + jnp.dot(
+            values, weights.astype(jnp.bfloat16), preferred_element_type=jnp.float32
+        )
+        peak_ref[tile] = new_peak
+
+    for start in range(0, rows, KEY_BLOCK):
+        whole = (shard < own) & (start + KEY_BLOCK <= count)
+        some = (shard <= own) & (start < count) & jnp.logical_not(whole)
+        for pair in range(tiles // TILES_AT_ONCE):
+            first = pair * TILES_AT_ONCE
+            used = first * ROW_TILE < own_count
+            reached = (shard < own) | ((first + TILES_AT_ONCE) * ROW_TILE > start)
+
+            @pl.when(whole & used)
+            def _():
+                for tile in range(first, first + TILES_AT_ONCE):
+                    update(tile, start, False)
+
+            @pl.when(some & used & reached)
+            def _():
+                for tile in range(first, first + TILES_AT_ONCE):
+                    update(tile, start, True)
 
     @pl.when(shard == pl.num_programs(0) - 1)
     def _():
-        mixed = acc_ref[...] / total_ref[...]
-        for head in range(2):
-            o_ref[:, head * HD : (head + 1) * HD] = mixed[:, head * rows : (head + 1) * rows].T.astype(
-                jnp.bfloat16
-            )
+        for tile in range(tiles):
+            total = total_ref[tile]
+            mixed = acc_ref[tile] / jnp.where(total > 0.0, total, 1.0)
+            for head in range(2):
+                o_ref[tile * ROW_TILE : (tile + 1) * ROW_TILE, head * HD : (head + 1) * HD] = mixed[
+                    :, head * ROW_TILE : (head + 1) * ROW_TILE
+                ].T.astype(jnp.bfloat16)
 
 
 def attention(info, queries, kv):
     shards_n, _, rows = kv.shape
+    tiles, lanes = rows // ROW_TILE, 2 * ROW_TILE
     return pl.pallas_call(
         attention_kernel,
         out_shape=jax.ShapeDtypeStruct(queries.shape, jnp.bfloat16),
@@ -100,10 +125,10 @@
             ],
             out_specs=pl.BlockSpec(queries.shape, lambda s, info: (0, 0)),
             scratch_shapes=[
-                pltpu.VMEM((HD, 2 * rows), jnp.bfloat16),
-                pltpu.VMEM((1, 2 * rows), jnp.float32),
-                pltpu.VMEM((1, 2 * rows), jnp.float32),
-                pltpu.VMEM((HD, 2 * rows), jnp.float32),
+                pltpu.VMEM((tiles, HD, lanes), jnp.bfloat16),
+                pltpu.VMEM((tiles, 1, lanes), jnp.float32),
+                pltpu.VMEM((tiles, 1, lanes), jnp.float32),
+                pltpu.VMEM((tiles, HD, lanes), jnp.float32),
             ],
         ),
         compiler_params=pltpu.CompilerParams(vmem_limit_bytes=32 * 1024 * 1024),
@@ -128,19 +153,16 @@
     half_cols = query_weight.shape[1] // 2
     chunk = half_cols // ZN
 
-    def fetch(block, axis):
-        got = lax.ppermute(block, "tp", y_swap())
+    def merge(got, axis):
         other = lax.ppermute(got, "ctx", core_swap(shard_n))
         low = jnp.where(core == 0, got, other)
         high = jnp.where(core == 0, other, got)
         return jnp.concatenate([low, high], axis=axis)
 
-    wq_in = fetch(
-        lax.dynamic_slice(query_weight, (core * (width // 2), (1 - y) * half_cols), (width // 2, half_cols)), 0
-    )
-    wo_rows = out_weight.shape[0] // 2
-    wo_in = fetch(
-        lax.dynamic_slice(out_weight, ((1 - y) * wo_rows + core * (wo_rows // 2), 0), (wo_rows // 2, width)), 0
+    wq_got = lax.ppermute(
+        lax.dynamic_slice(query_weight, (core * (width // 2), (1 - y) * half_cols), (width // 2, half_cols)),
+        "tp",
+        y_swap(),
     )
 
     own_rows = lax.dynamic_index_in_dim(kept_rows, shard, 0, keepdims=False)
@@ -167,6 +189,8 @@
     router_logit = summed[HD // 2 + 1] + summed[HD // 2 + 3]
     inverse_rms = lax.rsqrt(square_sum / D + EPSILON)
     piece = (summed[: HD // 2] * inverse_rms[None, :]).astype(bf16)
+    piece, wq_got, x_in = lax.optimization_barrier((piece, wq_got, x_in))
+    wq_in = merge(wq_got, 0)
     pieces = [lax.ppermute(piece, "tp", quad_shift(k)) for k in (3, 2, 1)] + [piece]
     ordered = jnp.stack(pieces + pieces[:3])
     kv_own = lax.dynamic_slice_in_dim(ordered, (3 - z % 4) % 4, 4, 0).reshape(2 * HD, rows)
@@ -194,11 +218,19 @@
     for step in (2, 1):
         going_right = right(query_part(step) + going_right)
         going_left = left(query_part(-step) + going_left)
-    queries = (query_part(0) + going_right + going_left) * inverse_rms[:, None]
+    wo_rows = out_weight.shape[0] // 2
+    wo_start = (1 - y) * wo_rows + core * (wo_rows // 2)
+    going_right, wo_start = lax.optimization_barrier((going_right, wo_start))
+    wo_got = lax.ppermute(
+        lax.dynamic_slice(out_weight, (wo_start, 0), (wo_rows // 2, width)), "tp", y_swap()
+    )
+    queries = (query_part(0) + going_right + going_left) * (inverse_rms * EXP_SCALE)[:, None]
 
     counts = jnp.sum((kept_rows < tokens).astype(jnp.int32), axis=1)
     info = jnp.concatenate([counts, shard[None].astype(jnp.int32)])
     mixed = attention(info, queries.astype(bf16), kv_all)
+    mixed, wo_got = lax.optimization_barrier((mixed, wo_got))
+    wo_in = merge(wo_got, 0)
 
     def project(piece, offset, low, high):
         start = ((z + offset) % ZN) * chunk + low

time: 274 us -> 246 us (0.90)
  blocking collectives: 43.7 us -> 0 us
  Pallas kernels: 20.8 us -> 35.7 us
  matrix products: 51 us -> 43.2 us
  starting transfers between devices: 35.6 us -> 40.6 us
    ppermute x4, waiting for transfers between devices: 59.7 us -> 0.01 us  [the longest x2 0.01 us: merge(): other = lax.ppermute(got, 'ctx', core_swap(shard_n))]
    all_to_all x1 -> x0, blocking collectives: 43.7 us -> none  [shards(): lax.all_to_all(sent, 'tp', 0, 0, tiled=True).astype(jnp.float32)]
    all_to_all x0 -> x1, waiting for transfers between devices: none -> 27 us  [shards(): lax.all_to_all(sent, 'tp', 0, 0, tiled=True).astype(jnp.float32)]
    ppermute x1, waiting for transfers between devices: 0.01 us -> 17.9 us  [shards(): x_in = lax.ppermute(x_own, 'tp', y_swap())]
    pallas_call x1, Pallas kernels: 20.8 us -> 35.7 us  [attention(): pl.pallas_call(attention_kernel, out_shape=jax.ShapeDtypeStruct(queries.s...]
    all_to_all x0 -> x1, starting transfers between devices: none -> 10.3 us  [shards(): lax.all_to_all(sent, 'tp', 0, 0, tiled=True).astype(jnp.float32)]
    ppermute x8, starting transfers between devices: 25.6 us -> 16.3 us  [left(): return lax.ppermute(a.astype(bf16), 'tp', z_shift(-1))]
    ppermute x8, waiting for transfers between devices: 6.05 us -> 14.8 us  [left(): return lax.ppermute(a.astype(bf16), 'tp', z_shift(-1))]
  transfers between devices with their start and end apart: 26 -> 27, of which waited for: 17 -> 15; matrix products, arithmetic and copies ran while one was open for 17% -> 18% of each run, Pallas kernels for 8% -> 14%
where the time goes in v2:
time: 246 us; the launch traced here: 247 us
  waiting for transfers between devices  96.7 us (39%)
  matrix products  43.2 us (18%)
  starting transfers between devices  40.6 us (17%)
  Pallas kernels  35.7 us (15%)
  between operations  14 us (6%)
  local copies, waits for them, and re-layouts  10.2 us (4%)
  other arithmetic  6.31 us (3%)
    dot_general x34, matrix products, dot(): return jnp.dot(a, b, preferred_element_type=jnp.float32)  38.6 us
    pallas_call x1, Pallas kernels, attention(): pl.pallas_call(attention_kernel, out_shape=jax.ShapeDtypeStruct(queries.s...  35.7 us
    all_to_all x1, waiting for transfers between devices, shards(): lax.all_to_all(sent, 'tp', 0, 0, tiled=True).astype(jnp.float32)  27 us
    ppermute x8, waiting for transfers between devices, right(): return lax.ppermute(a.astype(bf16), 'tp', z_shift(1))  26.4 us
    ppermute x1, waiting for transfers between devices, shards(): x_in = lax.ppermute(x_own, 'tp', y_swap())  17.9 us
    ppermute x8, starting transfers between devices, left(): return lax.ppermute(a.astype(bf16), 'tp', z_shift(-1))  16.3 us
    ppermute x8, waiting for transfers between devices, left(): return lax.ppermute(a.astype(bf16), 'tp', z_shift(-1))  14.8 us
    all_to_all x1, starting transfers between devices, shards(): lax.all_to_all(sent, 'tp', 0, 0, tiled=True).astype(jnp.float32)  10.3 us
  transfers between devices with their start and end apart: 27, of which 15 were waited for; matrix products, arithmetic and copies ran while one was open for 18% of the time, Pallas kernels for 14%

profile of v2, /device:TPU:14, one launch (start us, length us, event | category | flops | bytes accessed | tf_op | source)
XLA Modules:
  0.0 246.6 jit_solution(17714307659453128059)
XLA Ops:
  8.7 2.2 multiply_reduce_fusion.1
  13.1 10.3 %all-to-all-start = ((bf16[16,72,512]{2,1,0:T(8,128)(2,1)}), bf16[16,72,512]{2,1,0:T(8,128)(2,1)S(1)}, u32[]{:S(2)}, u32[]{:S(2)}) async-start(bf16[16,72,512]{2,1,0:T(8,128)(2,1)} %pad_maximum_fusion), calls=%async_computation | async-start | bytes 2359296 | tf_op jit(solution)/shard_map/all_to_all | solution.py:187
  23.5 2.3 dynamic_slice.117
  25.8 3.4 %collective-permute-start = (bf16[256,2048]{1,0:T(8,128)(2,1)}, bf16[256,2048]{1,0:T(8,128)(2,1)}, u32[]{:S(2)}, u32[]{:S(2)}) collective-permute-start(bf16[256,2048]{1,0:T(8,128)(2,1)} %dynamic_slice.117), channel_id=1, source_target_pairs={{0,1},{1,0},{2,3},{3,2},{4,5},{5,4},{6,7},{7,6},{8,9},{9,8},{10,11... | collective-permute-start | bytes 3145736 | tf_op jit(solution)/shard_map/ppermute | solution.py:162
  29.3 27.0 %all-to-all-done = bf16[16,72,512]{2,1,0:T(8,128)(2,1)S(1)} async-done(((bf16[16,72,512]{2,1,0:T(8,128)(2,1)}), bf16[16,72,512]{2,1,0:T(8,128)(2,1)S(1)}, u32[]{:S(2)}, u32[]{:S(2)}) %all-to-all-start) | async-done | bytes 1179680 | tf_op jit(solution)/shard_map/all_to_all | solution.py:187
  56.5 17.9 %collective-permute-done.1 = bf16[512,512]{0,1:T(8,128)(2,1)S(1)} collective-permute-done((bf16[512,512]{0,1:T(8,128)(2,1)S(1)}, bf16[512,512]{0,1:T(8,128)(2,1)S(1)}, u32[]{:S(2)}, u32[]{:S(2)}) %collective-permute-start.1) | collective-permute-done | bytes 524320 | tf_op jit(solution)/shard_map/ppermute | solution.py:174
  74.4 3.4 %collective-permute-start.11 = (bf16[64,512]{1,0:T(8,128)(2,1)S(1)}, bf16[64,512]{1,0:T(8,128)(2,1)S(1)}, u32[]{:S(2)}, u32[]{:S(2)}) collective-permute-start(bf16[64,512]{1,0:T(8,128)(2,1)S(1)} %fusion.105), channel_id=1, source_target_pairs={{0,6},{1,7},{2,0},{3,1},{4,2},{5,3},{6,4},{7,5},{8,14},{9,15},{10,... | collective-permute-start | bytes 196616 | tf_op jit(solution)/shard_map/ppermute | solution.py:194
  79.8 3.3 %collective-permute-done.12 = bf16[64,512]{1,0:T(8,128)(2,1)S(1)} collective-permute-done((bf16[64,512]{1,0:T(8,128)(2,1)S(1)}, bf16[64,512]{1,0:T(8,128)(2,1)S(1)}, u32[]{:S(2)}, u32[]{:S(2)}) %collective-permute-start.12) | collective-permute-done | bytes 65568 | tf_op jit(solution)/shard_map/ppermute | solution.py:194
  84.8 2.1 fusion.91
  87.0 2.1 fusion.89
  89.0 2.1 fusion.93
  91.2 1.3 fusion.95
  92.4 1.3 fusion.83
  93.7 1.3 fusion.85
  95.1 2.1 fusion.87
  97.2 1.8 broadcast_select_fusion.2
  100.4 2.8 %collective-permute-start.7 = (bf16[512,128]{1,0:T(8,128)(2,1)S(1)}, bf16[512,128]{1,0:T(8,128)(2,1)S(1)}, u32[]{:S(2)}, u32[]{:S(2)}) collective-permute-start(bf16[512,128]{1,0:T(8,128)(2,1)S(1)} %get-tuple-element.27), channel_id=1, source_target_pairs={{0,14},{1,15},{2,0},{3,1},{4,2},{5,3},{6,4},{7,5},{8,6},{9,7},{10,... | collective-permute-start | bytes 393224 | tf_op jit(solution)/shard_map/ppermute | solution.py:209
  103.6 3.1 %collective-permute-done.3 = bf16[512,128]{1,0:T(8,128)(2,1)S(1)} collective-permute-done((bf16[512,128]{1,0:T(8,128)(2,1)S(1)}, bf16[512,128]{1,0:T(8,128)(2,1)S(1)}, u32[]{:S(2)}, u32[]{:S(2)}) %collective-permute-start.3) | collective-permute-done | bytes 131104 | tf_op jit(solution)/shard_map/ppermute | solution.py:206
  107.1 3.3 %collective-permute-start.8 = (bf16[512,256]{1,0:T(8,128)(2,1)S(1)}, bf16[512,256]{1,0:T(8,128)(2,1)S(1)}, u32[]{:S(2)}, u32[]{:S(2)}) collective-permute-start(bf16[512,256]{1,0:T(8,128)(2,1)S(1)} %pad_maximum_fusion.2), channel_id=1, source_target_pairs={{0,14},{1,15},{2,0},{3,1},{4,2},{5,3},{6,4},{7,5},{8,6},{9,7},{10,... | collective-permute-start | bytes 786440 | tf_op jit(solution)/shard_map/ppermute | solution.py:209
  110.4 5.8 %collective-permute-done.4 = bf16[512,256]{1,0:T(8,128)(2,1)S(1)} collective-permute-done((bf16[512,256]{1,0:T(8,128)(2,1)S(1)}, bf16[512,256]{1,0:T(8,128)(2,1)S(1)}, u32[]{:S(2)}, u32[]{:S(2)}) %collective-permute-start.4) | collective-permute-done | bytes 262176 | tf_op jit(solution)/shard_map/ppermute | solution.py:206
  117.0 3.3 %collective-permute-start.9 = (bf16[512,256]{1,0:T(8,128)(2,1)S(1)}, bf16[512,256]{1,0:T(8,128)(2,1)}, u32[]{:S(2)}, u32[]{:S(2)}) collective-permute-start(bf16[512,256]{1,0:T(8,128)(2,1)S(1)} %fusion.27), channel_id=1, source_target_pairs={{0,14},{1,15},{2,0},{3,1},{4,2},{5,3},{6,4},{7,5},{8,6},{9,7},{10,... | collective-permute-start | bytes 786440 | tf_op jit(solution)/shard_map/ppermute | solution.py:209
  120.3 4.6 %collective-permute-done.5 = bf16[512,256]{1,0:T(8,128)(2,1)S(1)} collective-permute-done((bf16[512,256]{1,0:T(8,128)(2,1)S(1)}, bf16[512,256]{1,0:T(8,128)(2,1)S(1)}, u32[]{:S(2)}, u32[]{:S(2)}) %collective-permute-start.5) | collective-permute-done | bytes 262176 | tf_op jit(solution)/shard_map/ppermute | solution.py:206
  125.9 2.1 fusion.97
  128.1 5.7 %collective-permute-done.6 = bf16[512,256]{1,0:T(8,128)(2,1)} collective-permute-done((bf16[512,256]{1,0:T(8,128)(2,1)}, bf16[512,256]{1,0:T(8,128)(2,1)}, u32[]{:S(2)}, u32[]{:S(2)}) %collective-permute-start.6) | collective-permute-done | bytes 262176 | tf_op jit(solution)/shard_map/ppermute | solution.py:206
  133.8 2.5 %constant_dynamic-slice_fusion = bf16[1024,512]{1,0:T(8,128)(2,1)} fusion(bf16[4096,512]{1,0:T(8,128)(2,1)} %param.12, s32[]{:T(128)S(6)} %select_n.219), kind=kLoop, calls=%fused_computation.184 | loop fusion | bytes 2097156 | tf_op jit(solution)/shard_map/dynamic_slice | solution.py:225
  136.4 3.0 %collective-permute-start.14 = (bf16[1024,512]{1,0:T(8,128)(2,1)}, bf16[1024,512]{1,0:T(8,128)(2,1)}, u32[]{:S(2)}, u32[]{:S(2)}) collective-permute-start(bf16[1024,512]{1,0:T(8,128)(2,1)} %constant_dynamic-slice_fusion), channel_id=1, source_target_pairs={{0,1},{1,0},{2,3},{3,2},{4,5},{5,4},{6,7},{7,6},{8,9},{9,8},{10,11... | collective-permute-start | bytes 3145736 | tf_op jit(solution)/shard_map/ppermute | solution.py:224
  139.4 1.3 fusion.26
  140.9 6.4 %collective-permute-done.10 = bf16[512,256]{1,0:T(8,128)(2,1)} collective-permute-done((bf16[512,256]{1,0:T(8,128)(2,1)S(1)}, bf16[512,256]{1,0:T(8,128)(2,1)}, u32[]{:S(2)}, u32[]{:S(2)}) %collective-permute-start.10) | collective-permute-done | bytes 262176 | tf_op jit(solution)/shard_map/ppermute | solution.py:209
  147.3 1.7 fusion.29.q_ref
  149.0 2.2 copy-done.1
  151.2 35.7 %shard_map.73 = bf16[512,256]{1,0:T(8,128)(2,1)S(1)} custom-call(s32[17]{0:T(128)S(1)} %pad_add_fusion.info_ref, bf16[512,256]{1,0:T(8,128)(2,1)S(1)} %fusion.29.q_ref, bf16[16,256,512]{2,1,0:T(8,128)(2,1)S(1)} %copy-done.1), custom_call_target="tpu_custom_call" | custom-call | flops 4294967296 | bytes 4194304 | tf_op jit(solution)/shard_map/pallas_call | solution.py:116
  186.9 1.3 collective-permute-start.16
  189.0 5.5 %collective-permute-done.16 = bf16[512,256]{1,0:T(8,128)(2,1)S(1)} collective-permute-done((bf16[512,256]{1,0:T(8,128)(2,1)S(1)}, bf16[512,256]{1,0:T(8,128)(2,1)S(1)}, u32[]{:S(2)}, u32[]{:S(2)}) %collective-permute-start.16) | collective-permute-done | bytes 262176 | tf_op jit(solution)/shard_map/ppermute | solution.py:209
  194.5 1.3 collective-permute-start.18
  195.8 1.2 fusion.78
  197.9 1.2 fusion.80
  199.1 1.3 fusion.8
  200.4 2.9 %collective-permute-done.18 = bf16[512,256]{1,0:T(8,128)(2,1)S(1)} collective-permute-done((bf16[512,256]{1,0:T(8,128)(2,1)S(1)}, bf16[512,256]{1,0:T(8,128)(2,1)S(1)}, u32[]{:S(2)}, u32[]{:S(2)}) %collective-permute-start.18) | collective-permute-done | bytes 262176 | tf_op jit(solution)/shard_map/ppermute | solution.py:209
  204.3 1.8 collective-permute-done.17
  206.2 1.2 fusion.75
  207.4 2.2 fusion.7
  209.6 5.4 %collective-permute-done.19 = bf16[512,256]{1,0:T(8,128)(2,1)S(1)} collective-permute-done((bf16[512,256]{1,0:T(8,128)(2,1)S(1)}, bf16[512,256]{1,0:T(8,128)(2,1)S(1)}, u32[]{:S(2)}, u32[]{:S(2)}) %collective-permute-start.19) | collective-permute-done | bytes 262176 | tf_op jit(solution)/shard_map/ppermute | solution.py:206
  215.2 3.3 %collective-permute-start.22 = (bf16[512,128]{1,0:T(8,128)(2,1)S(1)}, bf16[512,128]{1,0:T(8,128)(2,1)S(1)}, u32[]{:S(2)}, u32[]{:S(2)}) collective-permute-start(bf16[512,128]{1,0:T(8,128)(2,1)S(1)} %slice.68), channel_id=1, source_target_pairs={{0,14},{1,15},{2,0},{3,1},{4,2},{5,3},{6,4},{7,5},{8,6},{9,7},{10,... | collective-permute-start | bytes 393224 | tf_op jit(solution)/shard_map/ppermute | solution.py:209
  218.5 1.4 broadcast_select_fusion
  224.9 1.2 fusion.71
  227.4 2.2 fusion.106
  229.5 5.6 %collective-permute-done.24 = bf16[512,512]{1,0:T(8,128)(2,1)S(1)} collective-permute-done((bf16[512,512]{1,0:T(8,128)(2,1)S(1)}, bf16[512,512]{1,0:T(8,128)(2,1)S(1)}, u32[]{:S(2)}, u32[]{:S(2)}) %collective-permute-start.24) | collective-permute-done | bytes 524320 | tf_op jit(solution)/shard_map/ppermute | solution.py:250
  235.9 3.8 %fusion.2 = bf16[1024,512]{1,0:T(8,128)(2,1)} fusion(f32[512,512]{1,0:T(8,128)} %fusion.106, f32[512,512]{1,0:T(8,128)S(1)} %fusion.108, f32[512,512]{1,0:T(8,128)S(1)} %fusion.71, f32[512,512]{1,0:T(8,128)} %fusion.7, bf16[512,256]{1,0:T(8,128)(2,1)S(1)} %collective-permute-done.19, bf16[512,512]{1,0:T(8,128)(2,1)} %copy-done.11, s32[512]{0:T(512)S(1)} %bitcast.69, ...), kind=kOutput, calls=%fused_computation.38 | convolution fusion | flops 674234368 | bytes 6295556 | tf_op jit(solution)/shard_map/dot_general | solution.py:253
  (107 shorter events, 22.4 us)
Async XLA Ops:
  6.5 4.4 %copy-start = (bf16[2,512,512]{2,1,0:T(8,128)(2,1)S(1)}, bf16[2,512,512]{2,1,0:T(8,128)(2,1)}, u32[]{:S(2)}) copy-start(bf16[2,512,512]{2,1,0:T(8,128)(2,1)} %param.11) | copy-start | bytes 3145732
  10.9 84.1 %copy-start.2 = (bf16[512,512]{0,1:T(8,128)(2,1)}, bf16[512,512]{0,1:T(8,128)(2,1)S(1)}, u32[]{:S(2)}) copy-start(bf16[512,512]{0,1:T(8,128)(2,1)S(1)} %get-tuple-element.25) | copy-start | bytes 1572868
  13.1 43.2 %all-to-all-start = ((bf16[16,72,512]{2,1,0:T(8,128)(2,1)}), bf16[16,72,512]{2,1,0:T(8,128)(2,1)S(1)}, u32[]{:S(2)}, u32[]{:S(2)}) async-start(bf16[16,72,512]{2,1,0:T(8,128)(2,1)} %pad_maximum_fusion), calls=%async_computation | async-start | bytes 2359296 | tf_op jit(solution)/shard_map/all_to_all | solution.py:187
  23.4 125.6 %all-gather.2.cloned.1.call-start = ((), (), s32[]{:S(2)}) async-start(), calls=%async_computation.1 | async-start | bytes 4456448 | tf_op jit(solution)/shard_map/all_gather | solution.py:197
  25.8 48.6 %collective-permute-start = (bf16[256,2048]{1,0:T(8,128)(2,1)}, bf16[256,2048]{1,0:T(8,128)(2,1)}, u32[]{:S(2)}, u32[]{:S(2)}) collective-permute-start(bf16[256,2048]{1,0:T(8,128)(2,1)} %dynamic_slice.117), channel_id=1, source_target_pairs={{0,1},{1,0},{2,3},{3,2},{4,5},{5,4},{6,7},{7,6},{8,9},{9,8},{10,11... | collective-permute-start | bytes 3145736 | tf_op jit(solution)/shard_map/ppermute | solution.py:162
  29.2 45.2 %collective-permute-start.1 = (bf16[512,512]{0,1:T(8,128)(2,1)S(1)}, bf16[512,512]{0,1:T(8,128)(2,1)S(1)}, u32[]{:S(2)}, u32[]{:S(2)}) collective-permute-start(bf16[512,512]{0,1:T(8,128)(2,1)S(1)} %get-tuple-element.25), channel_id=1, source_target_pairs={{0,1},{1,0},{2,3},{3,2},{4,5},{5,4},{6,7},{7,6},{8,9},{9,8},{10,11... | collective-permute-start | bytes 1572872 | tf_op jit(solution)/shard_map/ppermute | solution.py:174
  74.4 22.8 %copy-start.4 = (bf16[512,512]{0,1:T(8,128)(2,1)}, bf16[512,512]{0,1:T(8,128)(2,1)S(1)}, u32[]{:S(2)}) copy-start(bf16[512,512]{0,1:T(8,128)(2,1)S(1)} %collective-permute-done.1) | copy-start | bytes 1572868
  74.4 5.3 %collective-permute-start.11 = (bf16[64,512]{1,0:T(8,128)(2,1)S(1)}, bf16[64,512]{1,0:T(8,128)(2,1)S(1)}, u32[]{:S(2)}, u32[]{:S(2)}) collective-permute-start(bf16[64,512]{1,0:T(8,128)(2,1)S(1)} %fusion.105), channel_id=1, source_target_pairs={{0,6},{1,7},{2,0},{3,1},{4,2},{5,3},{6,4},{7,5},{8,14},{9,15},{10,... | collective-permute-start | bytes 196616 | tf_op jit(solution)/shard_map/ppermute | solution.py:194
  77.9 5.2 %collective-permute-start.12 = (bf16[64,512]{1,0:T(8,128)(2,1)S(1)}, bf16[64,512]{1,0:T(8,128)(2,1)S(1)}, u32[]{:S(2)}, u32[]{:S(2)}) collective-permute-start(bf16[64,512]{1,0:T(8,128)(2,1)S(1)} %fusion.105), channel_id=1, source_target_pairs={{0,4},{1,5},{2,6},{3,7},{4,0},{5,1},{6,2},{7,3},{8,12},{9,13},{10,... | collective-permute-start | bytes 196616 | tf_op jit(solution)/shard_map/ppermute | solution.py:194
  77.9 6.1 %collective-permute-start.13 = (bf16[64,512]{1,0:T(8,128)(2,1)S(1)}, bf16[64,512]{1,0:T(8,128)(2,1)S(1)}, u32[]{:S(2)}, u32[]{:S(2)}) collective-permute-start(bf16[64,512]{1,0:T(8,128)(2,1)S(1)} %fusion.105), channel_id=1, source_target_pairs={{0,2},{1,3},{2,4},{3,5},{4,6},{5,7},{6,0},{7,1},{8,10},{9,11},{10,... | collective-permute-start | bytes 196616 | tf_op jit(solution)/shard_map/ppermute | solution.py:194
  89.0 8.2 %collective-permute-start.2 = (bf16[256,2048]{1,0:T(8,128)(2,1)}, bf16[256,2048]{1,0:T(8,128)(2,1)}, u32[]{:S(2)}, u32[]{:S(2)}) collective-permute-start(bf16[256,2048]{1,0:T(8,128)(2,1)} %collective-permute-done), channel_id=1, source_target_pairs={{0,16},{16,0},{32,48},{48,32},{64,80},{80,64},{96,112},{112,96},{1... | collective-permute-start | bytes 3145736 | tf_op jit(solution)/shard_map/ppermute | solution.py:157
  97.2 1.8 copy-start.9
  97.2 1.8 copy-start.5
  99.0 1.1 copy-start.8
  99.4 7.2 %collective-permute-start.3 = (bf16[512,128]{1,0:T(8,128)(2,1)S(1)}, bf16[512,128]{1,0:T(8,128)(2,1)S(1)}, u32[]{:S(2)}, u32[]{:S(2)}) collective-permute-start(bf16[512,128]{1,0:T(8,128)(2,1)S(1)} %get-tuple-element.26), channel_id=1, source_target_pairs={{0,2},{1,3},{2,4},{3,5},{4,6},{5,7},{6,8},{7,9},{8,10},{9,11},{10,... | collective-permute-start | bytes 393224 | tf_op jit(solution)/shard_map/ppermute | solution.py:206
  100.4 6.6 %collective-permute-start.7 = (bf16[512,128]{1,0:T(8,128)(2,1)S(1)}, bf16[512,128]{1,0:T(8,128)(2,1)S(1)}, u32[]{:S(2)}, u32[]{:S(2)}) collective-permute-start(bf16[512,128]{1,0:T(8,128)(2,1)S(1)} %get-tuple-element.27), channel_id=1, source_target_pairs={{0,14},{1,15},{2,0},{3,1},{4,2},{5,3},{6,4},{7,5},{8,6},{9,7},{10,... | collective-permute-start | bytes 393224 | tf_op jit(solution)/shard_map/ppermute | solution.py:209
  103.5 12.6 %copy-start.7 = (f32[512,256]{1,0:T(8,128)S(1)}, f32[512,256]{1,0:T(8,128)}, u32[]{:S(2)}) copy-start(f32[512,256]{1,0:T(8,128)} %fusion.93) | copy-start | bytes 1572868
  106.7 9.4 %collective-permute-start.4 = (bf16[512,256]{1,0:T(8,128)(2,1)S(1)}, bf16[512,256]{1,0:T(8,128)(2,1)S(1)}, u32[]{:S(2)}, u32[]{:S(2)}) collective-permute-start(bf16[512,256]{1,0:T(8,128)(2,1)S(1)} %pad_maximum_fusion.1), channel_id=1, source_target_pairs={{0,2},{1,3},{2,4},{3,5},{4,6},{5,7},{6,8},{7,9},{8,10},{9,11},{10,... | collective-permute-start | bytes 786440 | tf_op jit(solution)/shard_map/ppermute | solution.py:206
  107.1 9.5 %collective-permute-start.8 = (bf16[512,256]{1,0:T(8,128)(2,1)S(1)}, bf16[512,256]{1,0:T(8,128)(2,1)S(1)}, u32[]{:S(2)}, u32[]{:S(2)}) collective-permute-start(bf16[512,256]{1,0:T(8,128)(2,1)S(1)} %pad_maximum_fusion.2), channel_id=1, source_target_pairs={{0,14},{1,15},{2,0},{3,1},{4,2},{5,3},{6,4},{7,5},{8,6},{9,7},{10,... | collective-permute-start | bytes 786440 | tf_op jit(solution)/shard_map/ppermute | solution.py:209
  116.5 8.4 %collective-permute-start.5 = (bf16[512,256]{1,0:T(8,128)(2,1)S(1)}, bf16[512,256]{1,0:T(8,128)(2,1)S(1)}, u32[]{:S(2)}, u32[]{:S(2)}) collective-permute-start(bf16[512,256]{1,0:T(8,128)(2,1)S(1)} %fusion.25), channel_id=1, source_target_pairs={{0,2},{1,3},{2,4},{3,5},{4,6},{5,7},{6,8},{7,9},{8,10},{9,11},{10,... | collective-permute-start | bytes 786440 | tf_op jit(solution)/shard_map/ppermute | solution.py:206
  117.0 9.0 %copy-start.3 = (bf16[512,512]{0,1:T(8,128)(2,1)S(1)}, bf16[512,512]{0,1:T(8,128)(2,1)}, u32[]{:S(2)}) copy-start(bf16[512,512]{0,1:T(8,128)(2,1)} %copy-done.2) | copy-start | bytes 1572868
  117.0 11.0 %copy-start.12 = (s32[16,512]{1,0:T(8,128)S(1)}, s32[16,512]{1,0:T(8,128)}, u32[]{:S(2)}) copy-start(s32[16,512]{1,0:T(8,128)} %param.13) | copy-start | bytes 98308
  117.0 22.4 %collective-permute-start.9 = (bf16[512,256]{1,0:T(8,128)(2,1)S(1)}, bf16[512,256]{1,0:T(8,128)(2,1)}, u32[]{:S(2)}, u32[]{:S(2)}) collective-permute-start(bf16[512,256]{1,0:T(8,128)(2,1)S(1)} %fusion.27), channel_id=1, source_target_pairs={{0,14},{1,15},{2,0},{3,1},{4,2},{5,3},{6,4},{7,5},{8,6},{9,7},{10,... | collective-permute-start | bytes 786440 | tf_op jit(solution)/shard_map/ppermute | solution.py:209
  125.9 7.9 %collective-permute-start.6 = (bf16[512,256]{1,0:T(8,128)(2,1)}, bf16[512,256]{1,0:T(8,128)(2,1)}, u32[]{:S(2)}, u32[]{:S(2)}) collective-permute-start(bf16[512,256]{1,0:T(8,128)(2,1)} %fusion.24), channel_id=1, source_target_pairs={{0,2},{1,3},{2,4},{3,5},{4,6},{5,7},{6,8},{7,9},{8,10},{9,11},{10,... | collective-permute-start | bytes 786440 | tf_op jit(solution)/shard_map/ppermute | solution.py:206
  133.8 5.6 %copy-start.6 = (bf16[512,512]{0,1:T(8,128)(2,1)S(1)}, bf16[512,512]{0,1:T(8,128)(2,1)}, u32[]{:S(2)}) copy-start(bf16[512,512]{0,1:T(8,128)(2,1)} %copy-done.4) | copy-start | bytes 1572868
  133.8 5.6 %copy-start.10 = (f32[512,256]{1,0:T(8,128)S(1)}, f32[512,256]{1,0:T(8,128)}, u32[]{:S(2)}) copy-start(f32[512,256]{1,0:T(8,128)} %fusion.87) | copy-start | bytes 1572868
  136.4 50.5 %collective-permute-start.14 = (bf16[1024,512]{1,0:T(8,128)(2,1)}, bf16[1024,512]{1,0:T(8,128)(2,1)}, u32[]{:S(2)}, u32[]{:S(2)}) collective-permute-start(bf16[1024,512]{1,0:T(8,128)(2,1)} %constant_dynamic-slice_fusion), channel_id=1, source_target_pairs={{0,1},{1,0},{2,3},{3,2},{4,5},{5,4},{6,7},{7,6},{8,9},{9,8},{10,11... | collective-permute-start | bytes 3145736 | tf_op jit(solution)/shard_map/ppermute | solution.py:224
  140.7 6.6 %collective-permute-start.10 = (bf16[512,256]{1,0:T(8,128)(2,1)S(1)}, bf16[512,256]{1,0:T(8,128)(2,1)}, u32[]{:S(2)}, u32[]{:S(2)}) collective-permute-start(bf16[512,256]{1,0:T(8,128)(2,1)S(1)} %fusion.26), channel_id=1, source_target_pairs={{0,14},{1,15},{2,0},{3,1},{4,2},{5,3},{6,4},{7,5},{8,6},{9,7},{10,... | collective-permute-start | bytes 786440 | tf_op jit(solution)/shard_map/ppermute | solution.py:209
  149.0 2.2 copy-start.1
  186.9 7.6 %collective-permute-start.16 = (bf16[512,256]{1,0:T(8,128)(2,1)S(1)}, bf16[512,256]{1,0:T(8,128)(2,1)S(1)}, u32[]{:S(2)}, u32[]{:S(2)}) collective-permute-start(bf16[512,256]{1,0:T(8,128)(2,1)S(1)} %shard_map.73), channel_id=1, source_target_pairs={{0,14},{1,15},{2,0},{3,1},{4,2},{5,3},{6,4},{7,5},{8,6},{9,7},{10,... | collective-permute-start | bytes 786440 | tf_op jit(solution)/shard_map/ppermute | solution.py:209
  188.2 8.8 %collective-permute-start.15 = (bf16[512,256]{1,0:T(8,128)(2,1)S(1)}, bf16[512,256]{1,0:T(8,128)(2,1)S(1)}, u32[]{:S(2)}, u32[]{:S(2)}) collective-permute-start(bf16[512,256]{1,0:T(8,128)(2,1)S(1)} %shard_map.73), channel_id=1, source_target_pairs={{0,2},{1,3},{2,4},{3,5},{4,6},{5,7},{6,8},{7,9},{8,10},{9,11},{10,... | collective-permute-start | bytes 786440 | tf_op jit(solution)/shard_map/ppermute | solution.py:206
  189.0 29.5 %collective-permute-start.23 = (bf16[1024,512]{1,0:T(8,128)(2,1)}, bf16[1024,512]{1,0:T(8,128)(2,1)S(1)}, u32[]{:S(2)}, u32[]{:S(2)}) collective-permute-start(bf16[1024,512]{1,0:T(8,128)(2,1)} %collective-permute-done.14), channel_id=1, source_target_pairs={{0,16},{16,0},{32,48},{48,32},{64,80},{80,64},{96,112},{112,96},{1... | collective-permute-start | bytes 3145736 | tf_op jit(solution)/shard_map/ppermute | solution.py:157
  194.5 8.8 %collective-permute-start.18 = (bf16[512,256]{1,0:T(8,128)(2,1)S(1)}, bf16[512,256]{1,0:T(8,128)(2,1)S(1)}, u32[]{:S(2)}, u32[]{:S(2)}) collective-permute-start(bf16[512,256]{1,0:T(8,128)(2,1)S(1)} %collective-permute-done.16), channel_id=1, source_target_pairs={{0,14},{1,15},{2,0},{3,1},{4,2},{5,3},{6,4},{7,5},{8,6},{9,7},{10,... | collective-permute-start | bytes 786440 | tf_op jit(solution)/shard_map/ppermute | solution.py:209
  197.0 9.1 %collective-permute-start.17 = (bf16[512,256]{1,0:T(8,128)(2,1)S(1)}, bf16[512,256]{1,0:T(8,128)(2,1)S(1)}, u32[]{:S(2)}, u32[]{:S(2)}) collective-permute-start(bf16[512,256]{1,0:T(8,128)(2,1)S(1)} %collective-permute-done.15), channel_id=1, source_target_pairs={{0,2},{1,3},{2,4},{3,5},{4,6},{5,7},{6,8},{7,9},{8,10},{9,11},{10,... | collective-permute-start | bytes 786440 | tf_op jit(solution)/shard_map/ppermute | solution.py:206
  203.3 11.9 %collective-permute-start.20 = (bf16[512,256]{1,0:T(8,128)(2,1)S(1)}, bf16[512,256]{1,0:T(8,128)(2,1)S(1)}, u32[]{:S(2)}, u32[]{:S(2)}) collective-permute-start(bf16[512,256]{1,0:T(8,128)(2,1)S(1)} %collective-permute-done.18), channel_id=1, source_target_pairs={{0,14},{1,15},{2,0},{3,1},{4,2},{5,3},{6,4},{7,5},{8,6},{9,7},{10,... | collective-permute-start | bytes 786440 | tf_op jit(solution)/shard_map/ppermute | solution.py:209
  206.1 9.0 %collective-permute-start.19 = (bf16[512,256]{1,0:T(8,128)(2,1)S(1)}, bf16[512,256]{1,0:T(8,128)(2,1)S(1)}, u32[]{:S(2)}, u32[]{:S(2)}) collective-permute-start(bf16[512,256]{1,0:T(8,128)(2,1)S(1)} %collective-permute-done.17), channel_id=1, source_target_pairs={{0,2},{1,3},{2,4},{3,5},{4,6},{5,7},{6,8},{7,9},{8,10},{9,11},{10,... | collective-permute-start | bytes 786440 | tf_op jit(solution)/shard_map/ppermute | solution.py:206
  215.1 7.8 %collective-permute-start.21 = (bf16[512,128]{1,0:T(8,128)(2,1)S(1)}, bf16[512,128]{1,0:T(8,128)(2,1)S(1)}, u32[]{:S(2)}, u32[]{:S(2)}) collective-permute-start(bf16[512,128]{1,0:T(8,128)(2,1)S(1)} %slice.67), channel_id=1, source_target_pairs={{0,2},{1,3},{2,4},{3,5},{4,6},{5,7},{6,8},{7,9},{8,10},{9,11},{10,... | collective-permute-start | bytes 393224 | tf_op jit(solution)/shard_map/ppermute | solution.py:206
  215.2 8.1 %collective-permute-start.22 = (bf16[512,128]{1,0:T(8,128)(2,1)S(1)}, bf16[512,128]{1,0:T(8,128)(2,1)S(1)}, u32[]{:S(2)}, u32[]{:S(2)}) collective-permute-start(bf16[512,128]{1,0:T(8,128)(2,1)S(1)} %slice.68), channel_id=1, source_target_pairs={{0,14},{1,15},{2,0},{3,1},{4,2},{5,3},{6,4},{7,5},{8,6},{9,7},{10,... | collective-permute-start | bytes 393224 | tf_op jit(solution)/shard_map/ppermute | solution.py:209
  224.4 10.8 %collective-permute-start.24 = (bf16[512,512]{1,0:T(8,128)(2,1)S(1)}, bf16[512,512]{1,0:T(8,128)(2,1)S(1)}, u32[]{:S(2)}, u32[]{:S(2)}) collective-permute-start(bf16[512,512]{1,0:T(8,128)(2,1)S(1)} %fusion.15), channel_id=1, source_target_pairs={{0,1},{1,0},{2,3},{3,2},{4,5},{5,4},{6,7},{7,6},{8,9},{9,8},{10,11... | collective-permute-start | bytes 1572872 | tf_op jit(solution)/shard_map/ppermute | solution.py:250
  235.1 0.8 copy-start.11
Sparse Core Ops, SparseCore 0:
  84.9 38.6 all-gather.1

commit v3 on v2

--- a/solution.py
+++ b/solution.py
@@ -16,8 +16,8 @@
 MASKED_SCORE = -1e30
 EXP_SCALE = HD ** (-0.5) * 1.4426950408889634
 KEY_BLOCK = 256
-ROW_TILE = 128
-TILES_AT_ONCE = 2
+ROW_TILE = 512
+TILES_AT_ONCE = 1
 
 
 def z_shift(dz):
@@ -26,10 +26,6 @@
 
 def y_swap():
     return [(t, t ^ 1) for t in range(2 * ZN)]
-
-
-def core_swap(count):
-    return [(c, c ^ 1) for c in range(count)]
 
 
 def quad_shift(k):
@@ -147,23 +143,21 @@
     shard = lax.axis_index("ctx")
     tp = lax.axis_index("tp")
     shard_n = lax.axis_size("ctx")
-    z, y, core = tp // 2, tp % 2, shard % 2
+    z, y = tp // 2, tp % 2
     tokens, width = hidden.shape
     rows = kept_rows.shape[1]
     half_cols = query_weight.shape[1] // 2
     chunk = half_cols // ZN
 
-    def merge(got, axis):
-        other = lax.ppermute(got, "ctx", core_swap(shard_n))
-        low = jnp.where(core == 0, got, other)
-        high = jnp.where(core == 0, other, got)
-        return jnp.concatenate([low, high], axis=axis)
-
-    wq_got = lax.ppermute(
-        lax.dynamic_slice(query_weight, (core * (width // 2), (1 - y) * half_cols), (width // 2, half_cols)),
-        "tp",
-        y_swap(),
-    )
+    group = 2 * ZN // 2
+    groups = [list(range(g, g + group)) for g in range(0, shard_n, group)]
+    mine = shard % group
+
+    def share(got):
+        return lax.all_gather(got, "ctx", axis=0, tiled=False, axis_index_groups=groups)
+
+    wq_sent = lax.dynamic_slice(query_weight, (0, (1 - y) * half_cols + mine * chunk), (width, chunk))
+    wq_got = lax.ppermute(wq_sent, "tp", y_swap())
 
     own_rows = lax.dynamic_index_in_dim(kept_rows, shard, 0, keepdims=False)
     select = (own_rows[:, None] == jnp.arange(tokens, dtype=jnp.int32)[None, :]).astype(bf16)
@@ -184,13 +178,16 @@
     stats_low = stats - stats_high
     stats_rows = jnp.concatenate([stats_high, stats_low, jnp.zeros((4, rows), jnp.float32)]).astype(bf16)
     sent = jnp.concatenate([kv_part, jnp.broadcast_to(stats_rows[None], (2 * ZN, 8, rows))], axis=1)
+    sent, wq_got = lax.optimization_barrier((sent, wq_got))
+    wq_in = share(wq_got)
+    own_weights = lax.dynamic_slice(query_weight, (0, y * half_cols), (width, half_cols))
+    query_own = dot(x_own, own_weights)
     summed = jnp.sum(lax.all_to_all(sent, "tp", 0, 0, tiled=True).astype(jnp.float32), axis=0)
     square_sum = summed[HD // 2] + summed[HD // 2 + 2]
     router_logit = summed[HD // 2 + 1] + summed[HD // 2 + 3]
     inverse_rms = lax.rsqrt(square_sum / D + EPSILON)
     piece = (summed[: HD // 2] * inverse_rms[None, :]).astype(bf16)
-    piece, wq_got, x_in = lax.optimization_barrier((piece, wq_got, x_in))
-    wq_in = merge(wq_got, 0)
+    piece, wq_in, x_in, query_own = lax.optimization_barrier((piece, wq_in, x_in, query_own))
     pieces = [lax.ppermute(piece, "tp", quad_shift(k)) for k in (3, 2, 1)] + [piece]
     ordered = jnp.stack(pieces + pieces[:3])
     kv_own = lax.dynamic_slice_in_dim(ordered, (3 - z % 4) % 4, 4, 0).reshape(2 * HD, rows)
@@ -198,9 +195,8 @@
 
     def query_part(offset):
         d = (z + offset) % ZN
-        own_w = lax.dynamic_slice(query_weight, (0, y * half_cols + d * chunk), (width, chunk))
-        in_w = lax.dynamic_slice(wq_in, (0, d * chunk), (width, chunk))
-        return dot(x_own, own_w) + dot(x_in, in_w)
+        own = lax.dynamic_slice(query_own, (0, d * chunk), (rows, chunk))
+        return own + dot(x_in, lax.dynamic_index_in_dim(wq_in, d, 0, keepdims=False))
 
     def right(a):
         return lax.ppermute(a.astype(bf16), "tp", z_shift(1))
@@ -208,29 +204,33 @@
     def left(a):
         return lax.ppermute(a.astype(bf16), "tp", z_shift(-1))
 
+    def both(going_right, going_left):
+        return lax.optimization_barrier((right(going_right), left(going_left)))
+
     cut = chunk // 2
     far = query_part(4)
-    going_right, going_left = right(far[:, :cut]), left(far[:, cut:])
-    part = query_part(3)
-    going_right = right(jnp.concatenate([part[:, :cut] + going_right, part[:, cut:]], axis=1))
-    part = query_part(-3)
-    going_left = left(jnp.concatenate([part[:, :cut], part[:, cut:] + going_left], axis=1))
-    for step in (2, 1):
-        going_right = right(query_part(step) + going_right)
-        going_left = left(query_part(-step) + going_left)
+    going_right, going_left = both(far[:, :cut], far[:, cut:])
+    part_right, part_left = query_part(3), query_part(-3)
+    going_right, going_left = both(
+        jnp.concatenate([part_right[:, :cut] + going_right, part_right[:, cut:]], axis=1),
+        jnp.concatenate([part_left[:, :cut], part_left[:, cut:] + going_left], axis=1),
+    )
     wo_rows = out_weight.shape[0] // 2
-    wo_start = (1 - y) * wo_rows + core * (wo_rows // 2)
+    wo_start = (1 - y) * wo_rows + mine * chunk
     going_right, wo_start = lax.optimization_barrier((going_right, wo_start))
     wo_got = lax.ppermute(
-        lax.dynamic_slice(out_weight, (wo_start, 0), (wo_rows // 2, width)), "tp", y_swap()
-    )
+        lax.dynamic_slice(out_weight, (wo_start, 0), (chunk, width)), "tp", y_swap()
+    )
+    for step in (2, 1):
+        going_right, going_left = both(query_part(step) + going_right, query_part(-step) + going_left)
     queries = (query_part(0) + going_right + going_left) * (inverse_rms * EXP_SCALE)[:, None]
+
+    queries, wo_got = lax.optimization_barrier((queries.astype(bf16), wo_got))
+    wo_in = share(wo_got).reshape(wo_rows, width)
 
     counts = jnp.sum((kept_rows < tokens).astype(jnp.int32), axis=1)
     info = jnp.concatenate([counts, shard[None].astype(jnp.int32)])
-    mixed = attention(info, queries.astype(bf16), kv_all)
-    mixed, wo_got = lax.optimization_barrier((mixed, wo_got))
-    wo_in = merge(wo_got, 0)
+    mixed = attention(info, queries, kv_all)
 
     def project(piece, offset, low, high):
         start = ((z + offset) % ZN) * chunk + low
@@ -241,7 +241,7 @@
     terms = [project(mixed, 0, 0, chunk)]
     from_left, from_right = mixed, mixed
     for step in (1, 2, 3):
-        from_left, from_right = right(from_left), left(from_right)
+        from_left, from_right = both(from_left, from_right)
         terms.append(project(from_left, -step, 0, chunk))
         terms.append(project(from_right, step, 0, chunk))
     terms.append(project(right(from_left[:, :cut]), 4, 0, cut))

time: 246 us -> 193 us (0.78)
  waiting for transfers between devices: 96.7 us -> 58.3 us
  Pallas kernels: 35.7 us -> 17 us
  starting transfers between devices: 40.6 us -> 46.2 us
  local copies, waits for them, and re-layouts: 10.2 us -> 7.46 us
    pallas_call x1, Pallas kernels: 35.7 us -> 17 us  [attention(): pl.pallas_call(attention_kernel, out_shape=jax.ShapeDtypeStruct(queries.s...]
    ppermute x1, waiting for transfers between devices: 17.9 us -> 0.01 us  [shards(): x_in = lax.ppermute(x_own, 'tp', y_swap())]
    ppermute x8, waiting for transfers between devices: 26.4 us -> 15.7 us  [right(): return lax.ppermute(a.astype(bf16), 'tp', z_shift(1))]
    ppermute x8, waiting for transfers between devices: 14.8 us -> 6.34 us  [left(): return lax.ppermute(a.astype(bf16), 'tp', z_shift(-1))]
    convert_element_type x0 -> x3, other arithmetic: none -> 4.41 us  [the longest x2 3.24 us: left(): return lax.ppermute(a.astype(bf16), 'tp', z_shift(-1))]
    ppermute x8, starting transfers between devices: 16.3 us -> 20.4 us  [left(): return lax.ppermute(a.astype(bf16), 'tp', z_shift(-1))]
    all_to_all x1, waiting for transfers between devices: 27 us -> 23.2 us  [shards(): lax.all_to_all(sent, 'tp', 0, 0, tiled=True).astype(jnp.float32)]
    ppermute x4 -> x2, waiting for transfers between devices: 0.01 us -> 3.68 us  [the longest x1 2.88 us: shards(): lax.ppermute(lax.dynamic_slice(out_weight, (wo_start, 0), (chunk, width))...]
  transfers between devices with their start and end apart: 27 -> 27, of which waited for: 15 -> 15; matrix products, arithmetic and copies ran while one was open for 18% -> 24% of each run, Pallas kernels for 14% -> 9%
where the time goes in v3:
time: 193 us; the launch traced here: 192 us
  waiting for transfers between devices  58.3 us (30%)
  starting transfers between devices  46.2 us (24%)
  matrix products  41.7 us (22%)
  Pallas kernels  17 us (9%)
  between operations  13.8 us (7%)
  other arithmetic  7.5 us (4%)
  local copies, waits for them, and re-layouts  7.46 us (4%)
    dot_general x27, matrix products, dot(): return jnp.dot(a, b, preferred_element_type=jnp.float32)  35.9 us
    all_to_all x1, waiting for transfers between devices, shards(): lax.all_to_all(sent, 'tp', 0, 0, tiled=True).astype(jnp.float32)  23.2 us
    ppermute x8, starting transfers between devices, left(): return lax.ppermute(a.astype(bf16), 'tp', z_shift(-1))  20.4 us
    pallas_call x1, Pallas kernels, attention(): pl.pallas_call(attention_kernel, out_shape=jax.ShapeDtypeStruct(queries.s...  17 us
    ppermute x8, waiting for transfers between devices, right(): return lax.ppermute(a.astype(bf16), 'tp', z_shift(1))  15.7 us
    all_to_all x1, starting transfers between devices, shards(): lax.all_to_all(sent, 'tp', 0, 0, tiled=True).astype(jnp.float32)  10.3 us
    ppermute x8, waiting for transfers between devices, left(): return lax.ppermute(a.astype(bf16), 'tp', z_shift(-1))  6.34 us
    ppermute x3, waiting for transfers between devices, shards(): lax.ppermute(piece, 'tp', quad_shift(k))  5.71 us
  transfers between devices with their start and end apart: 27, of which 15 were waited for; matrix products, arithmetic and copies ran while one was open for 24% of the time, Pallas kernels for 9%

profile of v3, /device:TPU:14, one launch (start us, length us, event | category | flops | bytes accessed | tf_op | source)
XLA Modules:
  0.0 191.9 jit_solution(7108397655136314570)
XLA Ops:
  7.6 2.4 %collective-permute-start = (bf16[512,256]{1,0:T(8,128)(2,1)S(1)}, bf16[512,256]{1,0:T(8,128)(2,1)S(1)}, u32[]{:S(2)}, u32[]{:S(2)}) collective-permute-start(bf16[512,256]{1,0:T(8,128)(2,1)S(1)} %constant_dynamic-slice_fusion.2), channel_id=1, source_target_pairs={{0,1},{1,0},{2,3},{3,2},{4,5},{5,4},{6,7},{7,6},{8,9},{9,8},{10,11... | collective-permute-start | bytes 786440 | tf_op jit(solution)/shard_map/ppermute | solution.py:160
  12.1 2.2 %multiply_reduce_fusion.1 = (f32[512]{0:T(512)S(1)}, f32[512]{0:T(512)S(1)}, bf16[512,512]{0,1:T(8,128)(2,1)S(1)}) fusion(f32[512]{0:T(512)S(1)} %convert_element_type.89, f32[512]{0:T(512)S(1)} %convert_element_type.85, bf16[1024,512]{1,0:T(8,128)(2,1)} %param.7, s32[512]{0:T(512)S(1)} %bitcast.102), kind=kOutput, calls=%fused_computation.30 | convolution fusion | flops 538967040 | bytes 1583104 | tf_op jit(solution)/shard_map/dot_general | solution.py:138
  18.0 10.3 %all-to-all-start = ((bf16[16,72,512]{2,1,0:T(8,128)(2,1)}), bf16[16,72,512]{2,1,0:T(8,128)(2,1)S(1)}, u32[]{:S(2)}, u32[]{:S(2)}) async-start(bf16[16,72,512]{2,1,0:T(8,128)(2,1)} %pad_maximum_fusion), calls=%async_computation | async-start | bytes 2359296 | tf_op jit(solution)/shard_map/all_to_all | solution.py:185
  28.3 3.5 %collective-permute-start.1 = (bf16[512,512]{0,1:T(8,128)(2,1)S(1)}, bf16[512,512]{0,1:T(8,128)(2,1)S(1)}, u32[]{:S(2)}, u32[]{:S(2)}) collective-permute-start(bf16[512,512]{0,1:T(8,128)(2,1)S(1)} %get-tuple-element.57), channel_id=1, source_target_pairs={{0,1},{1,0},{2,3},{3,2},{4,5},{5,4},{6,7},{7,6},{8,9},{9,8},{10,11... | collective-permute-start | bytes 1572872 | tf_op jit(solution)/shard_map/ppermute | solution.py:168
  31.8 5.0 %fusion = f32[512,2048]{1,0:T(8,128)} fusion(bf16[512,512]{0,1:T(8,128)(2,1)S(1)} %get-tuple-element.57, bf16[512,4096]{1,0:T(8,128)(2,1)} %param.10, s32[]{:T(128)S(6)} %select_n.180), kind=kOutput, calls=%fused_computation.1 | convolution fusion | flops 1073741824 | bytes 6815748 | tf_op jit(solution)/shard_map/dot_general | solution.py:138
  36.8 23.2 %all-to-all-done = bf16[16,72,512]{2,1,0:T(8,128)(2,1)S(1)} async-done(((bf16[16,72,512]{2,1,0:T(8,128)(2,1)}), bf16[16,72,512]{2,1,0:T(8,128)(2,1)S(1)}, u32[]{:S(2)}, u32[]{:S(2)}) %all-to-all-start) | async-done | bytes 1179680 | tf_op jit(solution)/shard_map/all_to_all | solution.py:185
  60.2 1.9 %collective-permute-start.11 = (bf16[64,512]{1,0:T(8,128)(2,1)S(1)}, bf16[64,512]{1,0:T(8,128)(2,1)S(1)}, u32[]{:S(2)}, u32[]{:S(2)}) collective-permute-start(bf16[64,512]{1,0:T(8,128)(2,1)S(1)} %fusion.84), channel_id=1, source_target_pairs={{0,6},{1,7},{2,0},{3,1},{4,2},{5,3},{6,4},{7,5},{8,14},{9,15},{10,... | collective-permute-start | bytes 196616 | tf_op jit(solution)/shard_map/ppermute | solution.py:191
  62.2 1.2 collective-permute-start.13
  63.3 1.3 collective-permute-done.11
  64.6 4.4 %collective-permute-done.12 = bf16[64,512]{1,0:T(8,128)(2,1)S(1)} collective-permute-done((bf16[64,512]{1,0:T(8,128)(2,1)S(1)}, bf16[64,512]{1,0:T(8,128)(2,1)S(1)}, u32[]{:S(2)}, u32[]{:S(2)}) %collective-permute-start.12) | collective-permute-done | bytes 65568 | tf_op jit(solution)/shard_map/ppermute | solution.py:191
  70.2 1.6 add_convert_fusion.4
  71.9 3.2 %collective-permute-start.3 = (bf16[512,128]{1,0:T(8,128)(2,1)S(1)}, bf16[512,128]{1,0:T(8,128)(2,1)S(1)}, u32[]{:S(2)}, u32[]{:S(2)}) collective-permute-start(bf16[512,128]{1,0:T(8,128)(2,1)S(1)} %get-tuple-element.58), channel_id=1, source_target_pairs={{0,14},{1,15},{2,0},{3,1},{4,2},{5,3},{6,4},{7,5},{8,6},{9,7},{10,... | collective-permute-start | bytes 393224 | tf_op jit(solution)/shard_map/ppermute | solution.py:205
  75.1 1.4 dynamic-slice_add_fusion
  76.6 1.4 dynamic-slice_add_fusion.1
  78.2 3.3 %collective-permute-start.5 = (bf16[512,256]{1,0:T(8,128)(2,1)S(1)}, bf16[512,256]{1,0:T(8,128)(2,1)S(1)}, u32[]{:S(2)}, u32[]{:S(2)}) collective-permute-start(bf16[512,256]{1,0:T(8,128)(2,1)S(1)} %pad_maximum_fusion.2), channel_id=1, source_target_pairs={{0,14},{1,15},{2,0},{3,1},{4,2},{5,3},{6,4},{7,5},{8,6},{9,7},{10,... | collective-permute-start | bytes 786440 | tf_op jit(solution)/shard_map/ppermute | solution.py:205
  82.0 3.4 %collective-permute-done.5 = bf16[512,256]{1,0:T(8,128)(2,1)S(1)} collective-permute-done((bf16[512,256]{1,0:T(8,128)(2,1)S(1)}, bf16[512,256]{1,0:T(8,128)(2,1)S(1)}, u32[]{:S(2)}, u32[]{:S(2)}) %collective-permute-start.5) | collective-permute-done | bytes 262176 | tf_op jit(solution)/shard_map/ppermute | solution.py:205
  85.4 3.8 %collective-permute-done.4 = bf16[512,256]{1,0:T(8,128)(2,1)S(1)} collective-permute-done((bf16[512,256]{1,0:T(8,128)(2,1)S(1)}, bf16[512,256]{1,0:T(8,128)(2,1)S(1)}, u32[]{:S(2)}, u32[]{:S(2)}) %collective-permute-start.4) | collective-permute-done | bytes 262176 | tf_op jit(solution)/shard_map/ppermute | solution.py:202
  89.2 1.8 add_convert_fusion.2
  91.0 1.4 add_convert_fusion.3
  92.5 2.1 %collective-permute-start.6 = (bf16[512,256]{1,0:T(8,128)(2,1)S(1)}, bf16[512,256]{1,0:T(8,128)(2,1)S(1)}, u32[]{:S(2)}, u32[]{:S(2)}) collective-permute-start(bf16[512,256]{1,0:T(8,128)(2,1)S(1)} %add_convert_fusion.3), channel_id=1, source_target_pairs={{0,2},{1,3},{2,4},{3,5},{4,6},{5,7},{6,8},{7,9},{8,10},{9,11},{10,... | collective-permute-start | bytes 786440 | tf_op jit(solution)/shard_map/ppermute | solution.py:202
  95.2 2.4 %collective-permute-done.7 = bf16[512,256]{1,0:T(8,128)(2,1)S(1)} collective-permute-done((bf16[512,256]{1,0:T(8,128)(2,1)}, bf16[512,256]{1,0:T(8,128)(2,1)S(1)}, u32[]{:S(2)}, u32[]{:S(2)}) %collective-permute-start.7) | collective-permute-done | bytes 262176 | tf_op jit(solution)/shard_map/ppermute | solution.py:205
  97.6 2.5 %collective-permute-done.6 = bf16[512,256]{1,0:T(8,128)(2,1)S(1)} collective-permute-done((bf16[512,256]{1,0:T(8,128)(2,1)S(1)}, bf16[512,256]{1,0:T(8,128)(2,1)S(1)}, u32[]{:S(2)}, u32[]{:S(2)}) %collective-permute-start.6) | collective-permute-done | bytes 262176 | tf_op jit(solution)/shard_map/ppermute | solution.py:202
  100.1 1.4 add_convert_fusion
  101.6 1.9 collective-permute-start.8
  103.4 1.5 collective-permute-start.9
  106.9 1.3 fusion.49
  109.8 1.2 multiply_convert_fusion.1.q_ref
  111.0 2.9 %collective-permute-done.10 = bf16[256,512]{1,0:T(8,128)(2,1)S(1)} collective-permute-done((bf16[256,512]{1,0:T(8,128)(2,1)S(1)}, bf16[256,512]{1,0:T(8,128)(2,1)S(1)}, u32[]{:S(2)}, u32[]{:S(2)}) %collective-permute-start.10) | collective-permute-done | bytes 262176 | tf_op jit(solution)/shard_map/ppermute | solution.py:221
  114.8 2.2 %copy-done.1 = bf16[16,256,512]{2,1,0:T(8,128)(2,1)S(1)} copy-done((bf16[16,256,512]{2,1,0:T(8,128)(2,1)S(1)}, bf16[16,256,512]{2,1,0:T(8,128)(2,1)}, u32[]{:S(2)}) %copy-start.1) | copy-done | bytes 4194328
  117.0 17.0 %shard_map.73 = bf16[512,256]{1,0:T(8,128)(2,1)S(1)} custom-call(s32[17]{0:T(128)S(1)} %pad_add_fusion.info_ref, bf16[512,256]{1,0:T(8,128)(2,1)S(1)} %multiply_convert_fusion.1.q_ref, bf16[16,256,512]{2,1,0:T(8,128)(2,1)S(1)} %copy-done.1), custom_call_target="tpu_custom_call" | custom-call | flops 4294967296 | bytes 4194304 | tf_op jit(solution)/shard_map/pallas_call | solution.py:112
  134.7 2.7 %collective-permute-start.15 = (bf16[512,256]{1,0:T(8,128)(2,1)S(1)}, bf16[512,256]{1,0:T(8,128)(2,1)S(1)}, u32[]{:S(2)}, u32[]{:S(2)}) collective-permute-start(bf16[512,256]{1,0:T(8,128)(2,1)S(1)} %shard_map.73), channel_id=1, source_target_pairs={{0,14},{1,15},{2,0},{3,1},{4,2},{5,3},{6,4},{7,5},{8,6},{9,7},{10,... | collective-permute-start | bytes 786440 | tf_op jit(solution)/shard_map/ppermute | solution.py:205
  137.3 7.1 %collective-permute-done.14 = bf16[512,256]{1,0:T(8,128)(2,1)S(1)} collective-permute-done((bf16[512,256]{1,0:T(8,128)(2,1)S(1)}, bf16[512,256]{1,0:T(8,128)(2,1)S(1)}, u32[]{:S(2)}, u32[]{:S(2)}) %collective-permute-start.14) | collective-permute-done | bytes 262176 | tf_op jit(solution)/shard_map/ppermute | solution.py:202
  144.4 3.2 %collective-permute-start.17 = (bf16[512,256]{1,0:T(8,128)(2,1)S(1)}, bf16[512,256]{1,0:T(8,128)(2,1)S(1)}, u32[]{:S(2)}, u32[]{:S(2)}) collective-permute-start(bf16[512,256]{1,0:T(8,128)(2,1)S(1)} %collective-permute-done.15), channel_id=1, source_target_pairs={{0,14},{1,15},{2,0},{3,1},{4,2},{5,3},{6,4},{7,5},{8,6},{9,7},{10,... | collective-permute-start | bytes 786440 | tf_op jit(solution)/shard_map/ppermute | solution.py:205
  147.6 1.2 fusion.73
  148.9 1.3 convolution_add_fusion.3
  150.2 1.2 fusion.61
  151.4 1.3 convolution_add_fusion.1
  152.7 1.1 collective-permute-done.16
  153.8 3.2 %collective-permute-start.19 = (bf16[512,256]{1,0:T(8,128)(2,1)S(1)}, bf16[512,256]{1,0:T(8,128)(2,1)S(1)}, u32[]{:S(2)}, u32[]{:S(2)}) collective-permute-start(bf16[512,256]{1,0:T(8,128)(2,1)S(1)} %collective-permute-done.17), channel_id=1, source_target_pairs={{0,14},{1,15},{2,0},{3,1},{4,2},{5,3},{6,4},{7,5},{8,6},{9,7},{10,... | collective-permute-start | bytes 786440 | tf_op jit(solution)/shard_map/ppermute | solution.py:205
  157.1 2.2 %fusion.67 = f32[512,512]{1,0:T(8,128)} fusion(bf16[512,256]{1,0:T(8,128)(2,1)S(1)} %collective-permute-done.17, bf16[4096,512]{1,0:T(8,128)(2,1)} %param.12, s32[]{:T(128)S(6)} %select_n.214), kind=kOutput, calls=%fused_computation.84 | convolution fusion | flops 134217728 | bytes 1572868 | tf_op jit(solution)/shard_map/dot_general | solution.py:138
  159.3 2.2 %fusion.69 = f32[512,512]{1,0:T(8,128)} fusion(bf16[512,256]{1,0:T(8,128)(2,1)S(1)} %collective-permute-done.16, bf16[4096,512]{1,0:T(8,128)(2,1)} %param.12, s32[]{:T(128)S(6)} %select_n.213), kind=kOutput, calls=%fused_computation.86 | convolution fusion | flops 134217728 | bytes 1572868 | tf_op jit(solution)/shard_map/dot_general | solution.py:138
  162.3 3.3 %collective-permute-start.21 = (bf16[512,128]{1,0:T(8,128)(2,1)S(1)}, bf16[512,128]{1,0:T(8,128)(2,1)S(1)}, u32[]{:S(2)}, u32[]{:S(2)}) collective-permute-start(bf16[512,128]{1,0:T(8,128)(2,1)S(1)} %slice.55), channel_id=1, source_target_pairs={{0,14},{1,15},{2,0},{3,1},{4,2},{5,3},{6,4},{7,5},{8,6},{9,7},{10,... | collective-permute-start | bytes 393224 | tf_op jit(solution)/shard_map/ppermute | solution.py:205
  165.6 2.2 %fusion.65 = f32[512,512]{1,0:T(8,128)} fusion(bf16[512,256]{1,0:T(8,128)(2,1)S(1)} %collective-permute-done.18, bf16[4096,512]{1,0:T(8,128)(2,1)} %param.12, s32[]{:T(128)S(6)} %select_n.215), kind=kOutput, calls=%fused_computation.82 | convolution fusion | flops 134217728 | bytes 1572868 | tf_op jit(solution)/shard_map/dot_general | solution.py:138
  170.1 2.3 %fusion.63 = f32[512,512]{1,0:T(8,128)} fusion(bf16[512,256]{1,0:T(8,128)(2,1)S(1)} %collective-permute-done.19, bf16[4096,512]{1,0:T(8,128)(2,1)} %param.12, s32[]{:T(128)S(6)} %select_n.216), kind=kOutput, calls=%fused_computation.80 | convolution fusion | flops 134217728 | bytes 1572868 | tf_op jit(solution)/shard_map/dot_general | solution.py:138
  172.4 2.2 %fusion.91 = f32[512,512]{1,0:T(8,128)} fusion(bf16[512,128]{1,0:T(8,128)(2,1)S(1)} %collective-permute-done.20, bf16[4096,512]{1,0:T(8,128)(2,1)} %param.12, s32[]{:T(128)S(6)} %select_n.217), kind=kOutput, calls=%fused_computation.108 | convolution fusion | flops 67108864 | bytes 1310724 | tf_op jit(solution)/shard_map/dot_general | solution.py:138
  174.6 2.2 %fusion.89 = f32[512,512]{1,0:T(8,128)} fusion(bf16[512,128]{1,0:T(8,128)(2,1)S(1)} %collective-permute-done.21, bf16[4096,512]{1,0:T(8,128)(2,1)} %param.12, s32[]{:T(128)S(6)} %select_n.218), kind=kOutput, calls=%fused_computation.106 | convolution fusion | flops 67108864 | bytes 1310724 | tf_op jit(solution)/shard_map/dot_general | solution.py:138
  176.7 3.6 %collective-permute-done.22 = bf16[512,512]{1,0:T(8,128)(2,1)S(1)} collective-permute-done((bf16[512,512]{1,0:T(8,128)(2,1)S(1)}, bf16[512,512]{1,0:T(8,128)(2,1)S(1)}, u32[]{:S(2)}, u32[]{:S(2)}) %collective-permute-start.22) | collective-permute-done | bytes 524320 | tf_op jit(solution)/shard_map/ppermute | solution.py:250
  180.3 5.0 %fusion.4 = bf16[1024,512]{1,0:T(8,128)(2,1)} fusion(s32[512]{0:T(512)S(1)} %bitcast.103, f32[512,512]{1,0:T(8,128)} %fusion.89, f32[512,512]{1,0:T(8,128)} %fusion.91, f32[512,512]{1,0:T(8,128)} %fusion.63, f32[512,512]{1,0:T(8,128)} %fusion.65, f32[512,512]{1,0:T(8,128)} %fusion.67, f32[512,512]{1,0:T(8,128)} %fusion.69, ...), kind=kOutput, calls=%fused_computation.6 | convolution fusion | flops 675020800 | bytes 9441284 | tf_op jit(solution)/shard_map/dot_general | solution.py:253
  (91 shorter events, 17.6 us)
Async XLA Ops:
  6.5 7.7 %copy-start = (bf16[2,512,512]{2,1,0:T(8,128)(2,1)S(1)}, bf16[2,512,512]{2,1,0:T(8,128)(2,1)}, u32[]{:S(2)}) copy-start(bf16[2,512,512]{2,1,0:T(8,128)(2,1)} %param.11) | copy-start | bytes 3145732
  6.5 53.7 %all-gather.8.cloned.1.call-start = ((), (), s32[]{:S(2)}) async-start(), calls=%async_computation.2 | async-start | bytes 2359296 | tf_op jit(solution)/shard_map/all_gather | solution.py:157
  7.6 9.6 %collective-permute-start = (bf16[512,256]{1,0:T(8,128)(2,1)S(1)}, bf16[512,256]{1,0:T(8,128)(2,1)S(1)}, u32[]{:S(2)}, u32[]{:S(2)}) collective-permute-start(bf16[512,256]{1,0:T(8,128)(2,1)S(1)} %constant_dynamic-slice_fusion.2), channel_id=1, source_target_pairs={{0,1},{1,0},{2,3},{3,2},{4,5},{5,4},{6,7},{7,6},{8,9},{9,8},{10,11... | collective-permute-start | bytes 786440 | tf_op jit(solution)/shard_map/ppermute | solution.py:160
  17.2 0.7 copy-start.5
  18.0 42.0 %all-to-all-start = ((bf16[16,72,512]{2,1,0:T(8,128)(2,1)}), bf16[16,72,512]{2,1,0:T(8,128)(2,1)S(1)}, u32[]{:S(2)}, u32[]{:S(2)}) async-start(bf16[16,72,512]{2,1,0:T(8,128)(2,1)} %pad_maximum_fusion), calls=%async_computation | async-start | bytes 2359296 | tf_op jit(solution)/shard_map/all_to_all | solution.py:185
  28.3 86.5 %all-gather.6.cloned.1.call-start = ((), (), s32[]{:S(2)}) async-start(), calls=%async_computation.1 | async-start | bytes 4456448 | tf_op jit(solution)/shard_map/all_gather | solution.py:194
  28.3 31.9 %collective-permute-start.1 = (bf16[512,512]{0,1:T(8,128)(2,1)S(1)}, bf16[512,512]{0,1:T(8,128)(2,1)S(1)}, u32[]{:S(2)}, u32[]{:S(2)}) collective-permute-start(bf16[512,512]{0,1:T(8,128)(2,1)S(1)} %get-tuple-element.57), channel_id=1, source_target_pairs={{0,1},{1,0},{2,3},{3,2},{4,5},{5,4},{6,7},{7,6},{8,9},{9,8},{10,11... | collective-permute-start | bytes 1572872 | tf_op jit(solution)/shard_map/ppermute | solution.py:168
  60.2 4.4 %collective-permute-start.11 = (bf16[64,512]{1,0:T(8,128)(2,1)S(1)}, bf16[64,512]{1,0:T(8,128)(2,1)S(1)}, u32[]{:S(2)}, u32[]{:S(2)}) collective-permute-start(bf16[64,512]{1,0:T(8,128)(2,1)S(1)} %fusion.84), channel_id=1, source_target_pairs={{0,6},{1,7},{2,0},{3,1},{4,2},{5,3},{6,4},{7,5},{8,14},{9,15},{10,... | collective-permute-start | bytes 196616 | tf_op jit(solution)/shard_map/ppermute | solution.py:191
  62.2 6.9 %collective-permute-start.12 = (bf16[64,512]{1,0:T(8,128)(2,1)S(1)}, bf16[64,512]{1,0:T(8,128)(2,1)S(1)}, u32[]{:S(2)}, u32[]{:S(2)}) collective-permute-start(bf16[64,512]{1,0:T(8,128)(2,1)S(1)} %fusion.84), channel_id=1, source_target_pairs={{0,4},{1,5},{2,6},{3,7},{4,0},{5,1},{6,2},{7,3},{8,12},{9,13},{10,... | collective-permute-start | bytes 196616 | tf_op jit(solution)/shard_map/ppermute | solution.py:191
  62.2 6.9 %collective-permute-start.13 = (bf16[64,512]{1,0:T(8,128)(2,1)S(1)}, bf16[64,512]{1,0:T(8,128)(2,1)S(1)}, u32[]{:S(2)}, u32[]{:S(2)}) collective-permute-start(bf16[64,512]{1,0:T(8,128)(2,1)S(1)} %fusion.84), channel_id=1, source_target_pairs={{0,2},{1,3},{2,4},{3,5},{4,6},{5,7},{6,0},{7,1},{8,10},{9,11},{10,... | collective-permute-start | bytes 196616 | tf_op jit(solution)/shard_map/ppermute | solution.py:191
  69.9 80.3 %all-gather.10.cloned.1.call-start = ((), (), s32[]{:S(2)}) async-start(), calls=%async_computation.3 | async-start | bytes 2359296 | tf_op jit(solution)/shard_map/all_gather | solution.py:157
  70.2 5.0 %copy-start.2 = (bf16[4096,256]{1,0:T(8,128)(2,1)S(1)}, bf16[4096,256]{1,0:T(8,128)(2,1)}, u32[]{:S(2)}) copy-start(bf16[4096,256]{1,0:T(8,128)(2,1)} %all-gather.8.cloned.1.call-done) | copy-start | bytes 6291460
  71.8 6.3 %collective-permute-start.2 = (bf16[512,128]{1,0:T(8,128)(2,1)S(1)}, bf16[512,128]{1,0:T(8,128)(2,1)S(1)}, u32[]{:S(2)}, u32[]{:S(2)}) collective-permute-start(bf16[512,128]{1,0:T(8,128)(2,1)S(1)} %get-tuple-element.59), channel_id=1, source_target_pairs={{0,2},{1,3},{2,4},{3,5},{4,6},{5,7},{6,8},{7,9},{8,10},{9,11},{10,... | collective-permute-start | bytes 393224 | tf_op jit(solution)/shard_map/ppermute | solution.py:202
  71.9 6.2 %collective-permute-start.3 = (bf16[512,128]{1,0:T(8,128)(2,1)S(1)}, bf16[512,128]{1,0:T(8,128)(2,1)S(1)}, u32[]{:S(2)}, u32[]{:S(2)}) collective-permute-start(bf16[512,128]{1,0:T(8,128)(2,1)S(1)} %get-tuple-element.58), channel_id=1, source_target_pairs={{0,14},{1,15},{2,0},{3,1},{4,2},{5,3},{6,4},{7,5},{8,6},{9,7},{10,... | collective-permute-start | bytes 393224 | tf_op jit(solution)/shard_map/ppermute | solution.py:205
  78.2 7.2 %collective-permute-start.5 = (bf16[512,256]{1,0:T(8,128)(2,1)S(1)}, bf16[512,256]{1,0:T(8,128)(2,1)S(1)}, u32[]{:S(2)}, u32[]{:S(2)}) collective-permute-start(bf16[512,256]{1,0:T(8,128)(2,1)S(1)} %pad_maximum_fusion.2), channel_id=1, source_target_pairs={{0,14},{1,15},{2,0},{3,1},{4,2},{5,3},{6,4},{7,5},{8,6},{9,7},{10,... | collective-permute-start | bytes 786440 | tf_op jit(solution)/shard_map/ppermute | solution.py:205
  81.5 7.7 %collective-permute-start.4 = (bf16[512,256]{1,0:T(8,128)(2,1)S(1)}, bf16[512,256]{1,0:T(8,128)(2,1)S(1)}, u32[]{:S(2)}, u32[]{:S(2)}) collective-permute-start(bf16[512,256]{1,0:T(8,128)(2,1)S(1)} %pad_maximum_fusion.1), channel_id=1, source_target_pairs={{0,2},{1,3},{2,4},{3,5},{4,6},{5,7},{6,8},{7,9},{8,10},{9,11},{10,... | collective-permute-start | bytes 786440 | tf_op jit(solution)/shard_map/ppermute | solution.py:202
  91.0 6.6 %collective-permute-start.7 = (bf16[512,256]{1,0:T(8,128)(2,1)}, bf16[512,256]{1,0:T(8,128)(2,1)S(1)}, u32[]{:S(2)}, u32[]{:S(2)}) collective-permute-start(bf16[512,256]{1,0:T(8,128)(2,1)} %add_convert_fusion.2), channel_id=1, source_target_pairs={{0,14},{1,15},{2,0},{3,1},{4,2},{5,3},{6,4},{7,5},{8,6},{9,7},{10,... | collective-permute-start | bytes 786440 | tf_op jit(solution)/shard_map/ppermute | solution.py:205
  92.5 7.7 %collective-permute-start.6 = (bf16[512,256]{1,0:T(8,128)(2,1)S(1)}, bf16[512,256]{1,0:T(8,128)(2,1)S(1)}, u32[]{:S(2)}, u32[]{:S(2)}) collective-permute-start(bf16[512,256]{1,0:T(8,128)(2,1)S(1)} %add_convert_fusion.3), channel_id=1, source_target_pairs={{0,2},{1,3},{2,4},{3,5},{4,6},{5,7},{6,8},{7,9},{8,10},{9,11},{10,... | collective-permute-start | bytes 786440 | tf_op jit(solution)/shard_map/ppermute | solution.py:202
  101.5 13.0 %copy-start.6 = (s32[16,512]{1,0:T(8,128)S(1)}, s32[16,512]{1,0:T(8,128)}, u32[]{:S(2)}) copy-start(s32[16,512]{1,0:T(8,128)} %param.13) | copy-start | bytes 98308
  101.6 7.7 %collective-permute-start.8 = (bf16[512,256]{1,0:T(8,128)(2,1)S(1)}, bf16[512,256]{1,0:T(8,128)(2,1)S(1)}, u32[]{:S(2)}, u32[]{:S(2)}) collective-permute-start(bf16[512,256]{1,0:T(8,128)(2,1)S(1)} %get-tuple-element.56), channel_id=1, source_target_pairs={{0,2},{1,3},{2,4},{3,5},{4,6},{5,7},{6,8},{7,9},{8,10},{9,11},{10,... | collective-permute-start | bytes 786440 | tf_op jit(solution)/shard_map/ppermute | solution.py:202
  103.4 6.4 %collective-permute-start.9 = (bf16[512,256]{1,0:T(8,128)(2,1)S(1)}, bf16[512,256]{1,0:T(8,128)(2,1)S(1)}, u32[]{:S(2)}, u32[]{:S(2)}) collective-permute-start(bf16[512,256]{1,0:T(8,128)(2,1)S(1)} %get-tuple-element.55), channel_id=1, source_target_pairs={{0,14},{1,15},{2,0},{3,1},{4,2},{5,3},{6,4},{7,5},{8,6},{9,7},{10,... | collective-permute-start | bytes 786440 | tf_op jit(solution)/shard_map/ppermute | solution.py:205
  105.9 8.0 %collective-permute-start.10 = (bf16[256,512]{1,0:T(8,128)(2,1)S(1)}, bf16[256,512]{1,0:T(8,128)(2,1)S(1)}, u32[]{:S(2)}, u32[]{:S(2)}) collective-permute-start(bf16[256,512]{1,0:T(8,128)(2,1)S(1)} %constant_dynamic-slice_fusion.1), channel_id=1, source_target_pairs={{0,1},{1,0},{2,3},{3,2},{4,5},{5,4},{6,7},{7,6},{8,9},{9,8},{10,11... | collective-permute-start | bytes 786440 | tf_op jit(solution)/shard_map/ppermute | solution.py:221
  113.8 0.7 copy-start.4
  114.8 2.2 %copy-start.1 = (bf16[16,256,512]{2,1,0:T(8,128)(2,1)S(1)}, bf16[16,256,512]{2,1,0:T(8,128)(2,1)}, u32[]{:S(2)}) copy-start(bf16[16,256,512]{2,1,0:T(8,128)(2,1)} %all-gather.6.cloned.1.call-done.kv_ref) | copy-start | bytes 12582916
  134.0 10.4 %collective-permute-start.14 = (bf16[512,256]{1,0:T(8,128)(2,1)S(1)}, bf16[512,256]{1,0:T(8,128)(2,1)S(1)}, u32[]{:S(2)}, u32[]{:S(2)}) collective-permute-start(bf16[512,256]{1,0:T(8,128)(2,1)S(1)} %shard_map.73), channel_id=1, source_target_pairs={{0,2},{1,3},{2,4},{3,5},{4,6},{5,7},{6,8},{7,9},{8,10},{9,11},{10,... | collective-permute-start | bytes 786440 | tf_op jit(solution)/shard_map/ppermute | solution.py:202
  134.7 9.7 %collective-permute-start.15 = (bf16[512,256]{1,0:T(8,128)(2,1)S(1)}, bf16[512,256]{1,0:T(8,128)(2,1)S(1)}, u32[]{:S(2)}, u32[]{:S(2)}) collective-permute-start(bf16[512,256]{1,0:T(8,128)(2,1)S(1)} %shard_map.73), channel_id=1, source_target_pairs={{0,14},{1,15},{2,0},{3,1},{4,2},{5,3},{6,4},{7,5},{8,6},{9,7},{10,... | collective-permute-start | bytes 786440 | tf_op jit(solution)/shard_map/ppermute | solution.py:205
  144.4 9.4 %collective-permute-start.16 = (bf16[512,256]{1,0:T(8,128)(2,1)S(1)}, bf16[512,256]{1,0:T(8,128)(2,1)S(1)}, u32[]{:S(2)}, u32[]{:S(2)}) collective-permute-start(bf16[512,256]{1,0:T(8,128)(2,1)S(1)} %collective-permute-done.14), channel_id=1, source_target_pairs={{0,2},{1,3},{2,4},{3,5},{4,6},{5,7},{6,8},{7,9},{8,10},{9,11},{10,... | collective-permute-start | bytes 786440 | tf_op jit(solution)/shard_map/ppermute | solution.py:202
  144.4 9.4 %collective-permute-start.17 = (bf16[512,256]{1,0:T(8,128)(2,1)S(1)}, bf16[512,256]{1,0:T(8,128)(2,1)S(1)}, u32[]{:S(2)}, u32[]{:S(2)}) collective-permute-start(bf16[512,256]{1,0:T(8,128)(2,1)S(1)} %collective-permute-done.15), channel_id=1, source_target_pairs={{0,14},{1,15},{2,0},{3,1},{4,2},{5,3},{6,4},{7,5},{8,6},{9,7},{10,... | collective-permute-start | bytes 786440 | tf_op jit(solution)/shard_map/ppermute | solution.py:205
  152.7 8.8 %copy-start.3 = (bf16[2048,512]{1,0:T(8,128)(2,1)S(1)}, bf16[2048,512]{1,0:T(8,128)(2,1)}, u32[]{:S(2)}) copy-start(bf16[2048,512]{1,0:T(8,128)(2,1)} %all-gather.10.cloned.1.call-done) | copy-start | bytes 6291460
  153.8 8.3 %collective-permute-start.18 = (bf16[512,256]{1,0:T(8,128)(2,1)S(1)}, bf16[512,256]{1,0:T(8,128)(2,1)S(1)}, u32[]{:S(2)}, u32[]{:S(2)}) collective-permute-start(bf16[512,256]{1,0:T(8,128)(2,1)S(1)} %collective-permute-done.16), channel_id=1, source_target_pairs={{0,2},{1,3},{2,4},{3,5},{4,6},{5,7},{6,8},{7,9},{8,10},{9,11},{10,... | collective-permute-start | bytes 786440 | tf_op jit(solution)/shard_map/ppermute | solution.py:202
  153.8 8.3 %collective-permute-start.19 = (bf16[512,256]{1,0:T(8,128)(2,1)S(1)}, bf16[512,256]{1,0:T(8,128)(2,1)S(1)}, u32[]{:S(2)}, u32[]{:S(2)}) collective-permute-start(bf16[512,256]{1,0:T(8,128)(2,1)S(1)} %collective-permute-done.17), channel_id=1, source_target_pairs={{0,14},{1,15},{2,0},{3,1},{4,2},{5,3},{6,4},{7,5},{8,6},{9,7},{10,... | collective-permute-start | bytes 786440 | tf_op jit(solution)/shard_map/ppermute | solution.py:205
  162.2 6.3 %collective-permute-start.20 = (bf16[512,128]{1,0:T(8,128)(2,1)S(1)}, bf16[512,128]{1,0:T(8,128)(2,1)S(1)}, u32[]{:S(2)}, u32[]{:S(2)}) collective-permute-start(bf16[512,128]{1,0:T(8,128)(2,1)S(1)} %slice.54), channel_id=1, source_target_pairs={{0,2},{1,3},{2,4},{3,5},{4,6},{5,7},{6,8},{7,9},{8,10},{9,11},{10,... | collective-permute-start | bytes 393224 | tf_op jit(solution)/shard_map/ppermute | solution.py:202
  162.3 6.4 %collective-permute-start.21 = (bf16[512,128]{1,0:T(8,128)(2,1)S(1)}, bf16[512,128]{1,0:T(8,128)(2,1)S(1)}, u32[]{:S(2)}, u32[]{:S(2)}) collective-permute-start(bf16[512,128]{1,0:T(8,128)(2,1)S(1)} %slice.55), channel_id=1, source_target_pairs={{0,14},{1,15},{2,0},{3,1},{4,2},{5,3},{6,4},{7,5},{8,6},{9,7},{10,... | collective-permute-start | bytes 393224 | tf_op jit(solution)/shard_map/ppermute | solution.py:205
  169.5 10.8 %collective-permute-start.22 = (bf16[512,512]{1,0:T(8,128)(2,1)S(1)}, bf16[512,512]{1,0:T(8,128)(2,1)S(1)}, u32[]{:S(2)}, u32[]{:S(2)}) collective-permute-start(bf16[512,512]{1,0:T(8,128)(2,1)S(1)} %fusion.19), channel_id=1, source_target_pairs={{0,1},{1,0},{2,3},{3,2},{4,5},{5,4},{6,7},{7,6},{8,9},{9,8},{10,11... | collective-permute-start | bytes 1572872 | tf_op jit(solution)/shard_map/ppermute | solution.py:250
Sparse Core Ops, SparseCore 0:
  18.1 29.2 all-gather.7
  70.0 34.8 all-gather.5
  114.7 23.3 all-gather.9

commit v4 on v3

--- a/solution.py
+++ b/solution.py
@@ -15,9 +15,9 @@
 EPSILON = 1e-05
 MASKED_SCORE = -1e30
 EXP_SCALE = HD ** (-0.5) * 1.4426950408889634
-KEY_BLOCK = 256
+KEY_BLOCK = 1024
 ROW_TILE = 512
-TILES_AT_ONCE = 1
+ATTENTION_VMEM = 32 * 1024 * 1024
 
 
 def z_shift(dz):
@@ -35,99 +35,120 @@
     return [(z * 2 + y, target(z) * 2 + y) for z in range(ZN) for y in range(2)]
 
 
-def attention_kernel(info_ref, q_ref, kv_ref, o_ref, qt_ref, peak_ref, total_ref, acc_ref):
-    shard = pl.program_id(0)
-    rows = q_ref.shape[0]
-    own = info_ref[pl.num_programs(0)]
-    count = info_ref[shard]
-    own_count = info_ref[own]
-    tiles = rows // ROW_TILE
-    lanes = 2 * ROW_TILE
-
-    @pl.when(shard == 0)
-    def _():
-        for tile in range(tiles):
-            for head in range(2):
-                block = q_ref[tile * ROW_TILE : (tile + 1) * ROW_TILE, head * HD : (head + 1) * HD]
-                qt_ref[tile, :, head * ROW_TILE : (head + 1) * ROW_TILE] = (
-                    block.astype(jnp.float32).T.astype(jnp.bfloat16)
-                )
-        peak_ref[...] = jnp.full_like(peak_ref, MASKED_SCORE)
-        total_ref[...] = jnp.zeros_like(total_ref)
-        acc_ref[...] = jnp.zeros_like(acc_ref)
-
-    def update(tile, start, masked):
-        keys = kv_ref[0, :HD, start : start + KEY_BLOCK]
-        values = kv_ref[0, HD:, start : start + KEY_BLOCK]
-        scores = lax.dot_general(
-            keys, qt_ref[tile], (((0,), (0,)), ((), ())), preferred_element_type=jnp.float32
-        )
-        if masked:
-            slot = tile * ROW_TILE + lax.broadcasted_iota(jnp.int32, (1, lanes), 1) % ROW_TILE
-            limit = jnp.where(shard < own, count, jnp.minimum(count, slot + 1)) - start
-            key_slot = lax.broadcasted_iota(jnp.int32, scores.shape, 0)
-            scores = jnp.where(key_slot < limit, scores, MASKED_SCORE)
-        peak = peak_ref[tile]
-        new_peak = jnp.maximum(peak, jnp.max(scores, axis=0, keepdims=True))
-        weights = jnp.exp2(scores - new_peak)
-        rescale = jnp.exp2(peak - new_peak)
-        total_ref[tile] = total_ref[tile] * rescale + jnp.sum(weights, axis=0, keepdims=True)
-        acc_ref[tile] = acc_ref[tile] * rescale + jnp.dot(
-            values, weights.astype(jnp.bfloat16), preferred_element_type=jnp.float32
-        )
-        peak_ref[tile] = new_peak
-
-    for start in range(0, rows, KEY_BLOCK):
-        whole = (shard < own) & (start + KEY_BLOCK <= count)
-        some = (shard <= own) & (start < count) & jnp.logical_not(whole)
-        for pair in range(tiles // TILES_AT_ONCE):
-            first = pair * TILES_AT_ONCE
-            used = first * ROW_TILE < own_count
-            reached = (shard < own) | ((first + TILES_AT_ONCE) * ROW_TILE > start)
-
-            @pl.when(whole & used)
+def attention_kernel(info_ref, q_ref, kv_ref, o_ref, qa_ref, ka_ref, v_ref):
+    shards_n, rows, _ = kv_ref.shape
+    own = info_ref[shards_n]
+    count = info_ref[own]
+    first = pl.multiple_of(info_ref[shards_n + 1 + own], 16)
+
+    def pack(step, _):
+        start = pl.multiple_of(info_ref[shards_n + 1 + step], 16)
+        slot = lax.broadcasted_iota(jnp.int32, (rows, HD), 0)
+        ka_ref[pl.ds(start, rows), :HD] = kv_ref[step, :, :HD]
+        ka_ref[pl.ds(start, rows), HD:] = jnp.where(slot < info_ref[step], 0.0, MASKED_SCORE).astype(jnp.bfloat16)
+        v_ref[pl.ds(start, rows), :] = kv_ref[step, :, HD:]
+
+    lax.fori_loop(0, own + 1, pack, None)
+    tail = pl.multiple_of(first + rows, 16)
+    ka_ref[pl.ds(tail, KEY_BLOCK), :] = jnp.zeros((KEY_BLOCK, 2 * HD), jnp.bfloat16)
+    v_ref[pl.ds(tail, KEY_BLOCK), :] = jnp.zeros((KEY_BLOCK, HD), jnp.bfloat16)
+    one = (lax.broadcasted_iota(jnp.int32, (rows, HD), 1) == 0).astype(jnp.bfloat16)
+    for head in range(2):
+        qa_ref[head, :, :HD] = q_ref[:, head * HD : (head + 1) * HD]
+        qa_ref[head, :, HD:] = one
+    open_blocks = first // KEY_BLOCK
+    blocks = (first + count + KEY_BLOCK - 1) // KEY_BLOCK
+
+    def lane_tiles(array):
+        return [array[:, i * HD : (i + 1) * HD] for i in range(KEY_BLOCK // HD)]
+
+    def tile_work(tile):
+        base = tile * ROW_TILE
+
+        def scores(block, head, masked):
+            start = pl.multiple_of(block * KEY_BLOCK, KEY_BLOCK)
+            out = lax.dot_general(
+                qa_ref[head, base : base + ROW_TILE, :],
+                ka_ref[pl.ds(start, KEY_BLOCK), :],
+                (((1,), (1,)), ((), ())),
+                preferred_element_type=jnp.float32,
+            )
+            if masked:
+                key = lax.broadcasted_iota(jnp.int32, out.shape, 1)
+                query = lax.broadcasted_iota(jnp.int32, out.shape, 0)
+                out = jnp.where(key - query <= first + base - start, out, MASKED_SCORE)
+            return out
+
+        def body(masked):
+            def run(block, state):
+                start = pl.multiple_of(block * KEY_BLOCK, KEY_BLOCK)
+                new = []
+                for head in range(2):
+                    peak, total, acc = state[3 * head : 3 * head + 3]
+                    score = scores(block, head, masked)
+                    lanes = functools.reduce(jnp.maximum, lane_tiles(score))
+                    new_peak = jnp.maximum(peak, jnp.max(lanes, axis=1, keepdims=True))
+                    weights = jnp.exp2(score - new_peak)
+                    rescale = jnp.exp2(peak - new_peak)
+                    new.append(new_peak)
+                    new.append(functools.reduce(jnp.add, lane_tiles(weights), total * rescale))
+                    new.append(
+                        acc * rescale
+                        + jnp.dot(
+                            weights.astype(jnp.bfloat16),
+                            v_ref[pl.ds(start, KEY_BLOCK), :],
+                            preferred_element_type=jnp.float32,
+                        )
+                    )
+                return tuple(new)
+
+            return run
+
+        zero = jnp.zeros((ROW_TILE, HD), jnp.float32)
+        state = (jnp.full((ROW_TILE, 1), MASKED_SCORE, jnp.float32), zero, zero) * 2
+        state = lax.fori_loop(0, open_blocks, body(False), state)
+        state = lax.fori_loop(open_blocks, blocks, body(True), state)
+        for head in range(2):
+            total = jnp.sum(state[3 * head + 1], axis=1, keepdims=True)
+            o_ref[base : base + ROW_TILE, head * HD : (head + 1) * HD] = (state[3 * head + 2] / total).astype(
+                jnp.bfloat16
+            )
+
+    for tile in range(rows // ROW_TILE):
+        if tile == 0:
+            tile_work(tile)
+        else:
+
+            @pl.when(tile * ROW_TILE < count)
             def _():
-                for tile in range(first, first + TILES_AT_ONCE):
-                    update(tile, start, False)
-
-            @pl.when(some & used & reached)
+                tile_work(tile)
+
+            @pl.when(tile * ROW_TILE >= count)
             def _():
-                for tile in range(first, first + TILES_AT_ONCE):
-                    update(tile, start, True)
-
-    @pl.when(shard == pl.num_programs(0) - 1)
-    def _():
-        for tile in range(tiles):
-            total = total_ref[tile]
-            mixed = acc_ref[tile] / jnp.where(total > 0.0, total, 1.0)
-            for head in range(2):
-                o_ref[tile * ROW_TILE : (tile + 1) * ROW_TILE, head * HD : (head + 1) * HD] = mixed[
-                    :, head * ROW_TILE : (head + 1) * ROW_TILE
-                ].T.astype(jnp.bfloat16)
-
-
-def attention(info, queries, kv):
-    shards_n, _, rows = kv.shape
-    tiles, lanes = rows // ROW_TILE, 2 * ROW_TILE
+                o_ref[tile * ROW_TILE : (tile + 1) * ROW_TILE, :] = jnp.zeros((ROW_TILE, 2 * HD), jnp.bfloat16)
+
+
+def attention(counts, own, queries, kv):
+    shards_n, rows, _ = kv.shape
+    packed = (counts + 15) // 16 * 16
+    first = jnp.cumsum(packed) - packed
+    info = jnp.concatenate([counts, own[None], first]).astype(jnp.int32)
+    capacity = shards_n * (rows // 2 + 16) + rows + KEY_BLOCK
     return pl.pallas_call(
         attention_kernel,
         out_shape=jax.ShapeDtypeStruct(queries.shape, jnp.bfloat16),
         grid_spec=pltpu.PrefetchScalarGridSpec(
             num_scalar_prefetch=1,
-            grid=(shards_n,),
-            in_specs=[
-                pl.BlockSpec(queries.shape, lambda s, info: (0, 0)),
-                pl.BlockSpec((1, 2 * HD, rows), lambda s, info: (jnp.minimum(s, info[shards_n]), 0, 0)),
-            ],
-            out_specs=pl.BlockSpec(queries.shape, lambda s, info: (0, 0)),
+            grid=(),
+            in_specs=[pl.BlockSpec(memory_space=pltpu.VMEM)] * 2,
+            out_specs=pl.BlockSpec(memory_space=pltpu.VMEM),
             scratch_shapes=[
-                pltpu.VMEM((tiles, HD, lanes), jnp.bfloat16),
-                pltpu.VMEM((tiles, 1, lanes), jnp.float32),
-                pltpu.VMEM((tiles, 1, lanes), jnp.float32),
-                pltpu.VMEM((tiles, HD, lanes), jnp.float32),
+                pltpu.VMEM((2, rows, 2 * HD), jnp.bfloat16),
+                pltpu.VMEM((capacity, 2 * HD), jnp.bfloat16),
+                pltpu.VMEM((capacity, HD), jnp.bfloat16),
             ],
         ),
-        compiler_params=pltpu.CompilerParams(vmem_limit_bytes=32 * 1024 * 1024),
+        compiler_params=pltpu.CompilerParams(vmem_limit_bytes=ATTENTION_VMEM),
         cost_estimate=pl.CostEstimate(
             flops=4 * 2 * rows * HD * shards_n * rows, bytes_accessed=kv.size * 2, transcendentals=rows * rows * shards_n
         ),
@@ -190,7 +211,7 @@
     piece, wq_in, x_in, query_own = lax.optimization_barrier((piece, wq_in, x_in, query_own))
     pieces = [lax.ppermute(piece, "tp", quad_shift(k)) for k in (3, 2, 1)] + [piece]
     ordered = jnp.stack(pieces + pieces[:3])
-    kv_own = lax.dynamic_slice_in_dim(ordered, (3 - z % 4) % 4, 4, 0).reshape(2 * HD, rows)
+    kv_own = lax.dynamic_slice_in_dim(ordered, (3 - z % 4) % 4, 4, 0).reshape(2 * HD, rows).T
     kv_all = lax.all_gather(kv_own, "ctx", axis=0, tiled=False)
 
     def query_part(offset):
@@ -229,8 +250,7 @@
     wo_in = share(wo_got).reshape(wo_rows, width)
 
     counts = jnp.sum((kept_rows < tokens).astype(jnp.int32), axis=1)
-    info = jnp.concatenate([counts, shard[None].astype(jnp.int32)])
-    mixed = attention(info, queries, kv_all)
+    mixed = attention(counts, shard, queries, kv_all)
 
     def project(piece, offset, low, high):
         start = ((z + offset) % ZN) * chunk + low
@@ -248,7 +268,8 @@
     terms.append(project(left(from_right[:, cut:]), 4, cut, chunk))
     for_partner = functools.reduce(jnp.add, [t[1] for t in terms])
     received = lax.ppermute(for_partner.astype(bf16), "tp", y_swap())
-    projected = functools.reduce(jnp.add, [t[0] for t in terms]) + received
+    own_sum, received = lax.optimization_barrier((functools.reduce(jnp.add, [t[0] for t in terms]), received))
+    projected = own_sum + received
     row_update = (jax.nn.sigmoid(router_logit)[:, None] * projected).astype(bf16)
     return lax.dot_general(select, row_update, (((0,), (0,)), ((), ())), preferred_element_type=jnp.float32).astype(
         bf16

time: 193 us -> 191 us (0.990)
  matrix products: 41.7 us -> 34.2 us
  local copies, waits for them, and re-layouts: 7.46 us -> 14.3 us
  Pallas kernels: 17 us -> 10.2 us
  starting transfers between devices: 46.2 us -> 48.7 us
  waiting for transfers between devices: 58.3 us -> 60.8 us
    pallas_call x1, Pallas kernels: 17 us -> 10.2 us  [attention(): pl.pallas_call(attention_kernel, out_shape=jax.ShapeDtypeStruct(queries.s...]
    all_gather x0 -> x1, local copies, waits for them, and re-layouts: none -> 6.46 us  [shards(): kv_all = lax.all_gather(kv_own, 'ctx', axis=0, tiled=False)]
    ppermute x8, starting transfers between devices: 20.4 us -> 25.4 us  [left(): return lax.ppermute(a.astype(bf16), 'tp', z_shift(-1))]
    dot_general x27 -> x28, matrix products: 35.9 us -> 31.4 us  [dot(): return jnp.dot(a, b, preferred_element_type=jnp.float32)]
    ppermute x8, waiting for transfers between devices: 6.34 us -> 2.67 us  [left(): return lax.ppermute(a.astype(bf16), 'tp', z_shift(-1))]
    ppermute x1, waiting for transfers between devices: 3.58 us -> 6.76 us  [shards(): received = lax.ppermute(for_partner.astype(bf16), 'tp', y_swap())]
    dot_general x1, matrix products: 5.05 us -> 1.99 us  [shards(): lax.dot_general(select, row_update, (((0,), (0,)), ((), ())), preferred_e...]
    ppermute x8, waiting for transfers between devices: 15.7 us -> 18.1 us  [right(): return lax.ppermute(a.astype(bf16), 'tp', z_shift(1))]
  transfers between devices with their start and end apart: 27 -> 27, of which waited for: 15 -> 16; matrix products, arithmetic and copies ran while one was open for 24% -> 25% of each run, Pallas kernels for 9% -> 5%
where the time goes in v4:
time: 191 us; the launch traced here: 190 us
  waiting for transfers between devices  60.8 us (32%)
  starting transfers between devices  48.7 us (25%)
  matrix products  34.2 us (18%)
  local copies, waits for them, and re-layouts  14.3 us (7%)
  between operations  13.8 us (7%)
  Pallas kernels  10.2 us (5%)
  other arithmetic  7.7 us (4%)
    dot_general x28, matrix products, dot(): return jnp.dot(a, b, preferred_element_type=jnp.float32)  31.4 us
    ppermute x8, starting transfers between devices, left(): return lax.ppermute(a.astype(bf16), 'tp', z_shift(-1))  25.4 us
    all_to_all x1, waiting for transfers between devices, shards(): lax.all_to_all(sent, 'tp', 0, 0, tiled=True).astype(jnp.float32)  23.1 us
    ppermute x8, waiting for transfers between devices, right(): return lax.ppermute(a.astype(bf16), 'tp', z_shift(1))  18.1 us
    all_to_all x1, starting transfers between devices, shards(): lax.all_to_all(sent, 'tp', 0, 0, tiled=True).astype(jnp.float32)  10.3 us
    pallas_call x1, Pallas kernels, attention(): pl.pallas_call(attention_kernel, out_shape=jax.ShapeDtypeStruct(queries.s...  10.2 us
    ppermute x1, waiting for transfers between devices, shards(): received = lax.ppermute(for_partner.astype(bf16), 'tp', y_swap())  6.76 us
    all_gather x1, local copies, waits for them, and re-layouts, shards(): kv_all = lax.all_gather(kv_own, 'ctx', axis=0, tiled=False)  6.46 us
  transfers between devices with their start and end apart: 27, of which 16 were waited for; matrix products, arithmetic and copies ran while one was open for 25% of the time, Pallas kernels for 5%

profile of v4, /device:TPU:14, one launch (start us, length us, event | category | flops | bytes accessed | tf_op | source)
XLA Modules:
  0.0 189.7 jit_solution(9450726796618647607)
XLA Ops:
  7.6 2.4 %collective-permute-start = (bf16[512,256]{1,0:T(8,128)(2,1)S(1)}, bf16[512,256]{1,0:T(8,128)(2,1)S(1)}, u32[]{:S(2)}, u32[]{:S(2)}) collective-permute-start(bf16[512,256]{1,0:T(8,128)(2,1)S(1)} %constant_dynamic-slice_fusion.2), channel_id=1, source_target_pairs={{0,1},{1,0},{2,3},{3,2},{4,5},{5,4},{6,7},{7,6},{8,9},{9,8},{10,11... | collective-permute-start | bytes 786440 | tf_op jit(solution)/shard_map/ppermute | solution.py:181
  12.1 2.2 %multiply_reduce_fusion.1 = (f32[512]{0:T(512)S(1)}, f32[512]{0:T(512)S(1)}, bf16[512,512]{0,1:T(8,128)(2,1)S(1)}) fusion(f32[512]{0:T(512)S(1)} %convert_element_type.89, f32[512]{0:T(512)S(1)} %convert_element_type.85, bf16[1024,512]{1,0:T(8,128)(2,1)} %param.7, s32[512]{0:T(512)S(1)} %bitcast.116), kind=kOutput, calls=%fused_computation.28 | convolution fusion | flops 538967040 | bytes 1583104 | tf_op jit(solution)/shard_map/dot_general | solution.py:159
  18.0 10.3 %all-to-all-start = ((bf16[16,72,512]{2,1,0:T(8,128)(2,1)}), bf16[16,72,512]{2,1,0:T(8,128)(2,1)S(1)}, u32[]{:S(2)}, u32[]{:S(2)}) async-start(bf16[16,72,512]{2,1,0:T(8,128)(2,1)} %pad_maximum_fusion), calls=%async_computation | async-start | bytes 2359296 | tf_op jit(solution)/shard_map/all_to_all | solution.py:206
  28.3 3.5 %collective-permute-start.1 = (bf16[512,512]{0,1:T(8,128)(2,1)S(1)}, bf16[512,512]{0,1:T(8,128)(2,1)S(1)}, u32[]{:S(2)}, u32[]{:S(2)}) collective-permute-start(bf16[512,512]{0,1:T(8,128)(2,1)S(1)} %get-tuple-element.61), channel_id=1, source_target_pairs={{0,1},{1,0},{2,3},{3,2},{4,5},{5,4},{6,7},{7,6},{8,9},{9,8},{10,11... | collective-permute-start | bytes 1572872 | tf_op jit(solution)/shard_map/ppermute | solution.py:189
  31.8 5.0 %fusion = f32[512,2048]{1,0:T(8,128)} fusion(bf16[512,512]{0,1:T(8,128)(2,1)S(1)} %get-tuple-element.61, bf16[512,4096]{1,0:T(8,128)(2,1)} %param.10, s32[]{:T(128)S(6)} %select_n.196), kind=kOutput, calls=%fused_computation.1 | convolution fusion | flops 1073741824 | bytes 6815748 | tf_op jit(solution)/shard_map/dot_general | solution.py:159
  36.8 23.1 %all-to-all-done = bf16[16,72,512]{2,1,0:T(8,128)(2,1)S(1)} async-done(((bf16[16,72,512]{2,1,0:T(8,128)(2,1)}), bf16[16,72,512]{2,1,0:T(8,128)(2,1)S(1)}, u32[]{:S(2)}, u32[]{:S(2)}) %all-to-all-start) | async-done | bytes 1179680 | tf_op jit(solution)/shard_map/all_to_all | solution.py:206
  60.2 1.9 %collective-permute-start.11 = (bf16[64,512]{1,0:T(8,128)(2,1)S(1)}, bf16[64,512]{1,0:T(8,128)(2,1)S(1)}, u32[]{:S(2)}, u32[]{:S(2)}) collective-permute-start(bf16[64,512]{1,0:T(8,128)(2,1)S(1)} %fusion.80), channel_id=1, source_target_pairs={{0,6},{1,7},{2,0},{3,1},{4,2},{5,3},{6,4},{7,5},{8,14},{9,15},{10,... | collective-permute-start | bytes 196616 | tf_op jit(solution)/shard_map/ppermute | solution.py:212
  63.3 1.3 collective-permute-done.11
  64.6 4.4 %collective-permute-done.12 = bf16[64,512]{1,0:T(8,128)(2,1)S(1)} collective-permute-done((bf16[64,512]{1,0:T(8,128)(2,1)S(1)}, bf16[64,512]{1,0:T(8,128)(2,1)S(1)}, u32[]{:S(2)}, u32[]{:S(2)}) %collective-permute-start.12) | collective-permute-done | bytes 65568 | tf_op jit(solution)/shard_map/ppermute | solution.py:212
  70.2 1.6 dynamic-slice_add_fusion.1
  72.0 1.4 add_convert_fusion.4
  73.5 3.2 %collective-permute-start.3 = (bf16[512,128]{1,0:T(8,128)(2,1)S(1)}, bf16[512,128]{1,0:T(8,128)(2,1)S(1)}, u32[]{:S(2)}, u32[]{:S(2)}) collective-permute-start(bf16[512,128]{1,0:T(8,128)(2,1)S(1)} %get-tuple-element.62), channel_id=1, source_target_pairs={{0,14},{1,15},{2,0},{3,1},{4,2},{5,3},{6,4},{7,5},{8,6},{9,7},{10,... | collective-permute-start | bytes 393224 | tf_op jit(solution)/shard_map/ppermute | solution.py:226
  76.7 1.4 dynamic-slice_add_fusion
  78.1 1.5 collective-permute-done.2
  80.8 2.6 %collective-permute-start.5 = (bf16[512,256]{1,0:T(8,128)(2,1)S(1)}, bf16[512,256]{1,0:T(8,128)(2,1)S(1)}, u32[]{:S(2)}, u32[]{:S(2)}) collective-permute-start(bf16[512,256]{1,0:T(8,128)(2,1)S(1)} %pad_maximum_fusion.2), channel_id=1, source_target_pairs={{0,14},{1,15},{2,0},{3,1},{4,2},{5,3},{6,4},{7,5},{8,6},{9,7},{10,... | collective-permute-start | bytes 786440 | tf_op jit(solution)/shard_map/ppermute | solution.py:226
  83.7 3.7 %collective-permute-done.4 = bf16[512,256]{1,0:T(8,128)(2,1)S(1)} collective-permute-done((bf16[512,256]{1,0:T(8,128)(2,1)S(1)}, bf16[512,256]{1,0:T(8,128)(2,1)S(1)}, u32[]{:S(2)}, u32[]{:S(2)}) %collective-permute-start.4) | collective-permute-done | bytes 262176 | tf_op jit(solution)/shard_map/ppermute | solution.py:223
  87.4 1.4 add_convert_fusion.3
  89.6 1.8 add_convert_fusion.2
  91.4 2.9 %collective-permute-start.7 = (bf16[512,256]{1,0:T(8,128)(2,1)}, bf16[512,256]{1,0:T(8,128)(2,1)S(1)}, u32[]{:S(2)}, u32[]{:S(2)}) collective-permute-start(bf16[512,256]{1,0:T(8,128)(2,1)} %add_convert_fusion.2), channel_id=1, source_target_pairs={{0,14},{1,15},{2,0},{3,1},{4,2},{5,3},{6,4},{7,5},{8,6},{9,7},{10,... | collective-permute-start | bytes 786440 | tf_op jit(solution)/shard_map/ppermute | solution.py:226
  95.0 1.8 collective-permute-done.6
  96.8 1.7 collective-permute-done.7
  98.5 1.4 add_convert_fusion
  101.1 2.6 %collective-permute-start.9 = (bf16[512,256]{1,0:T(8,128)(2,1)S(1)}, bf16[512,256]{1,0:T(8,128)(2,1)S(1)}, u32[]{:S(2)}, u32[]{:S(2)}) collective-permute-start(bf16[512,256]{1,0:T(8,128)(2,1)S(1)} %get-tuple-element.59), channel_id=1, source_target_pairs={{0,14},{1,15},{2,0},{3,1},{4,2},{5,3},{6,4},{7,5},{8,6},{9,7},{10,... | collective-permute-start | bytes 786440 | tf_op jit(solution)/shard_map/ppermute | solution.py:226
  105.4 1.3 fusion.46
  106.7 1.2 collective-permute-done.8
  109.1 3.6 %collective-permute-done.10 = bf16[256,512]{1,0:T(8,128)(2,1)S(1)} collective-permute-done((bf16[256,512]{1,0:T(8,128)(2,1)S(1)}, bf16[256,512]{1,0:T(8,128)(2,1)S(1)}, u32[]{:S(2)}, u32[]{:S(2)}) %collective-permute-start.10) | collective-permute-done | bytes 262176 | tf_op jit(solution)/shard_map/ppermute | solution.py:242
  113.9 6.5 %copy.24 = bf16[8192,256]{1,0:T(8,128)(2,1)} copy(bf16[8192,256]{0,1:T(8,128)(2,1)} %all-gather.9.cloned.1.call-done) | data formatting | bytes 8388608 | tf_op jit(solution)/shard_map/all_gather | solution.py:215
  120.4 2.3 %copy-done.1 = bf16[8192,256]{1,0:T(8,128)(2,1)S(1)} copy-done((bf16[8192,256]{1,0:T(8,128)(2,1)S(1)}, bf16[8192,256]{1,0:T(8,128)(2,1)}, u32[]{:S(2)}) %copy-start.1) | copy-done | bytes 4194328
  122.6 10.2 %shard_map.73 = bf16[512,256]{1,0:T(8,128)(2,1)S(1)} custom-call(s32[33]{0:T(128)S(1)} %pad_add_fusion.info_ref, bf16[512,256]{1,0:T(8,128)(2,1)S(1)} %multiply_convert_fusion.3.q_ref, bf16[16,512,256]{2,1,0:T(8,128)(2,1)S(1)} %bitcast.102), custom_call_target="tpu_custom_call" | custom-call | flops 4294967296 | bytes 4194304 | tf_op jit(solution)/shard_map/pallas_call | solution.py:137
  133.0 3.2 %collective-permute-start.15 = (bf16[512,256]{1,0:T(8,128)(2,1)S(1)}, bf16[512,256]{1,0:T(8,128)(2,1)S(1)}, u32[]{:S(2)}, u32[]{:S(2)}) collective-permute-start(bf16[512,256]{1,0:T(8,128)(2,1)S(1)} %shard_map.73), channel_id=1, source_target_pairs={{0,14},{1,15},{2,0},{3,1},{4,2},{5,3},{6,4},{7,5},{8,6},{9,7},{10,... | collective-permute-start | bytes 786440 | tf_op jit(solution)/shard_map/ppermute | solution.py:226
  136.2 5.0 %collective-permute-done.14 = bf16[512,256]{1,0:T(8,128)(2,1)S(1)} collective-permute-done((bf16[512,256]{1,0:T(8,128)(2,1)S(1)}, bf16[512,256]{1,0:T(8,128)(2,1)S(1)}, u32[]{:S(2)}, u32[]{:S(2)}) %collective-permute-start.14) | collective-permute-done | bytes 262176 | tf_op jit(solution)/shard_map/ppermute | solution.py:223
  141.2 3.5 %collective-permute-start.17 = (bf16[512,256]{1,0:T(8,128)(2,1)S(1)}, bf16[512,256]{1,0:T(8,128)(2,1)S(1)}, u32[]{:S(2)}, u32[]{:S(2)}) collective-permute-start(bf16[512,256]{1,0:T(8,128)(2,1)S(1)} %collective-permute-done.15), channel_id=1, source_target_pairs={{0,14},{1,15},{2,0},{3,1},{4,2},{5,3},{6,4},{7,5},{8,6},{9,7},{10,... | collective-permute-start | bytes 786440 | tf_op jit(solution)/shard_map/ppermute | solution.py:226
  144.7 1.2 fusion.69
  145.9 1.3 convolution_add_fusion.3
  147.2 1.3 fusion.58
  148.5 1.3 convolution_add_fusion.1
  150.3 3.6 %collective-permute-start.19 = (bf16[512,256]{1,0:T(8,128)(2,1)S(1)}, bf16[512,256]{1,0:T(8,128)(2,1)S(1)}, u32[]{:S(2)}, u32[]{:S(2)}) collective-permute-start(bf16[512,256]{1,0:T(8,128)(2,1)S(1)} %collective-permute-done.17), channel_id=1, source_target_pairs={{0,14},{1,15},{2,0},{3,1},{4,2},{5,3},{6,4},{7,5},{8,6},{9,7},{10,... | collective-permute-start | bytes 786440 | tf_op jit(solution)/shard_map/ppermute | solution.py:226
  153.9 1.2 fusion.64
  155.1 1.2 fusion.66
  157.0 1.2 collective-permute-done.18
  159.2 3.8 %collective-permute-start.21 = (bf16[512,128]{1,0:T(8,128)(2,1)S(1)}, bf16[512,128]{1,0:T(8,128)(2,1)S(1)}, u32[]{:S(2)}, u32[]{:S(2)}) collective-permute-start(bf16[512,128]{1,0:T(8,128)(2,1)S(1)} %slice.55), channel_id=1, source_target_pairs={{0,14},{1,15},{2,0},{3,1},{4,2},{5,3},{6,4},{7,5},{8,6},{9,7},{10,... | collective-permute-start | bytes 393224 | tf_op jit(solution)/shard_map/ppermute | solution.py:226
  163.1 1.2 fusion.60
  164.3 1.3 fusion.62
  166.2 3.1 %collective-permute-done.20 = bf16[512,128]{1,0:T(8,128)(2,1)S(1)} collective-permute-done((bf16[512,128]{1,0:T(8,128)(2,1)S(1)}, bf16[512,128]{1,0:T(8,128)(2,1)S(1)}, u32[]{:S(2)}, u32[]{:S(2)}) %collective-permute-start.20) | collective-permute-done | bytes 131104 | tf_op jit(solution)/shard_map/ppermute | solution.py:223
  170.5 1.2 fusion.85
  172.9 1.5 fusion.11
  174.4 6.8 %collective-permute-done.22 = bf16[512,512]{1,0:T(8,128)(2,1)S(1)} collective-permute-done((bf16[512,512]{1,0:T(8,128)(2,1)S(1)}, bf16[512,512]{1,0:T(8,128)(2,1)S(1)}, u32[]{:S(2)}, u32[]{:S(2)}) %collective-permute-start.22) | collective-permute-done | bytes 524320 | tf_op jit(solution)/shard_map/ppermute | solution.py:270
  181.2 2.0 %fusion.4 = bf16[1024,512]{1,0:T(8,128)(2,1)} fusion(s32[512]{0:T(512)S(1)} %bitcast.117, f32[512,512]{1,0:T(8,128)S(1)} %fusion.11, bf16[512,512]{1,0:T(8,128)(2,1)S(1)} %collective-permute-done.22, f32[512]{0:T(512)S(1)} %bitcast.118), kind=kOutput, calls=%fused_computation.6 | convolution fusion | flops 538968064 | bytes 2625536 | tf_op jit(solution)/shard_map/dot_general | solution.py:274
  (98 shorter events, 22.9 us)
Async XLA Ops:
  6.5 7.7 %copy-start = (bf16[2,512,512]{2,1,0:T(8,128)(2,1)S(1)}, bf16[2,512,512]{2,1,0:T(8,128)(2,1)}, u32[]{:S(2)}) copy-start(bf16[2,512,512]{2,1,0:T(8,128)(2,1)} %param.11) | copy-start | bytes 3145732
  6.5 53.7 %all-gather.7.cloned.1.call-start = ((), (), s32[]{:S(2)}) async-start(), calls=%async_computation.1 | async-start | bytes 2359296 | tf_op jit(solution)/shard_map/all_gather | solution.py:178
  7.6 9.6 %collective-permute-start = (bf16[512,256]{1,0:T(8,128)(2,1)S(1)}, bf16[512,256]{1,0:T(8,128)(2,1)S(1)}, u32[]{:S(2)}, u32[]{:S(2)}) collective-permute-start(bf16[512,256]{1,0:T(8,128)(2,1)S(1)} %constant_dynamic-slice_fusion.2), channel_id=1, source_target_pairs={{0,1},{1,0},{2,3},{3,2},{4,5},{5,4},{6,7},{7,6},{8,9},{9,8},{10,11... | collective-permute-start | bytes 786440 | tf_op jit(solution)/shard_map/ppermute | solution.py:181
  17.2 0.7 copy-start.5
  18.0 42.0 %all-to-all-start = ((bf16[16,72,512]{2,1,0:T(8,128)(2,1)}), bf16[16,72,512]{2,1,0:T(8,128)(2,1)S(1)}, u32[]{:S(2)}, u32[]{:S(2)}) async-start(bf16[16,72,512]{2,1,0:T(8,128)(2,1)} %pad_maximum_fusion), calls=%async_computation | async-start | bytes 2359296 | tf_op jit(solution)/shard_map/all_to_all | solution.py:206
  28.3 85.6 %all-gather.9.cloned.1.call-start = ((), (), s32[]{:S(2)}) async-start(), calls=%async_computation.2 | async-start | bytes 4456448 | tf_op jit(solution)/shard_map/all_gather | solution.py:215
  28.3 31.9 %collective-permute-start.1 = (bf16[512,512]{0,1:T(8,128)(2,1)S(1)}, bf16[512,512]{0,1:T(8,128)(2,1)S(1)}, u32[]{:S(2)}, u32[]{:S(2)}) collective-permute-start(bf16[512,512]{0,1:T(8,128)(2,1)S(1)} %get-tuple-element.61), channel_id=1, source_target_pairs={{0,1},{1,0},{2,3},{3,2},{4,5},{5,4},{6,7},{7,6},{8,9},{9,8},{10,11... | collective-permute-start | bytes 1572872 | tf_op jit(solution)/shard_map/ppermute | solution.py:189
  60.2 4.4 %collective-permute-start.11 = (bf16[64,512]{1,0:T(8,128)(2,1)S(1)}, bf16[64,512]{1,0:T(8,128)(2,1)S(1)}, u32[]{:S(2)}, u32[]{:S(2)}) collective-permute-start(bf16[64,512]{1,0:T(8,128)(2,1)S(1)} %fusion.80), channel_id=1, source_target_pairs={{0,6},{1,7},{2,0},{3,1},{4,2},{5,3},{6,4},{7,5},{8,14},{9,15},{10,... | collective-permute-start | bytes 196616 | tf_op jit(solution)/shard_map/ppermute | solution.py:212
  62.2 6.9 %collective-permute-start.12 = (bf16[64,512]{1,0:T(8,128)(2,1)S(1)}, bf16[64,512]{1,0:T(8,128)(2,1)S(1)}, u32[]{:S(2)}, u32[]{:S(2)}) collective-permute-start(bf16[64,512]{1,0:T(8,128)(2,1)S(1)} %fusion.80), channel_id=1, source_target_pairs={{0,4},{1,5},{2,6},{3,7},{4,0},{5,1},{6,2},{7,3},{8,12},{9,13},{10,... | collective-permute-start | bytes 196616 | tf_op jit(solution)/shard_map/ppermute | solution.py:212
  62.2 6.9 %collective-permute-start.13 = (bf16[64,512]{1,0:T(8,128)(2,1)S(1)}, bf16[64,512]{1,0:T(8,128)(2,1)S(1)}, u32[]{:S(2)}, u32[]{:S(2)}) collective-permute-start(bf16[64,512]{1,0:T(8,128)(2,1)S(1)} %fusion.80), channel_id=1, source_target_pairs={{0,2},{1,3},{2,4},{3,5},{4,6},{5,7},{6,0},{7,1},{8,10},{9,11},{10,... | collective-permute-start | bytes 196616 | tf_op jit(solution)/shard_map/ppermute | solution.py:212
  69.9 77.3 %all-gather.11.cloned.1.call-start = ((), (), s32[]{:S(2)}) async-start(), calls=%async_computation.3 | async-start | bytes 2359296 | tf_op jit(solution)/shard_map/all_gather | solution.py:178
  70.2 1.8 copy-start.2
  73.4 6.3 %collective-permute-start.2 = (bf16[512,128]{1,0:T(8,128)(2,1)S(1)}, bf16[512,128]{1,0:T(8,128)(2,1)S(1)}, u32[]{:S(2)}, u32[]{:S(2)}) collective-permute-start(bf16[512,128]{1,0:T(8,128)(2,1)S(1)} %get-tuple-element.63), channel_id=1, source_target_pairs={{0,2},{1,3},{2,4},{3,5},{4,6},{5,7},{6,8},{7,9},{8,10},{9,11},{10,... | collective-permute-start | bytes 393224 | tf_op jit(solution)/shard_map/ppermute | solution.py:223
  73.5 6.2 %collective-permute-start.3 = (bf16[512,128]{1,0:T(8,128)(2,1)S(1)}, bf16[512,128]{1,0:T(8,128)(2,1)S(1)}, u32[]{:S(2)}, u32[]{:S(2)}) collective-permute-start(bf16[512,128]{1,0:T(8,128)(2,1)S(1)} %get-tuple-element.62), channel_id=1, source_target_pairs={{0,14},{1,15},{2,0},{3,1},{4,2},{5,3},{6,4},{7,5},{8,6},{9,7},{10,... | collective-permute-start | bytes 393224 | tf_op jit(solution)/shard_map/ppermute | solution.py:226
  79.7 7.7 %collective-permute-start.4 = (bf16[512,256]{1,0:T(8,128)(2,1)S(1)}, bf16[512,256]{1,0:T(8,128)(2,1)S(1)}, u32[]{:S(2)}, u32[]{:S(2)}) collective-permute-start(bf16[512,256]{1,0:T(8,128)(2,1)S(1)} %pad_maximum_fusion.1), channel_id=1, source_target_pairs={{0,2},{1,3},{2,4},{3,5},{4,6},{5,7},{6,8},{7,9},{8,10},{9,11},{10,... | collective-permute-start | bytes 786440 | tf_op jit(solution)/shard_map/ppermute | solution.py:223
  80.8 6.7 %collective-permute-start.5 = (bf16[512,256]{1,0:T(8,128)(2,1)S(1)}, bf16[512,256]{1,0:T(8,128)(2,1)S(1)}, u32[]{:S(2)}, u32[]{:S(2)}) collective-permute-start(bf16[512,256]{1,0:T(8,128)(2,1)S(1)} %pad_maximum_fusion.2), channel_id=1, source_target_pairs={{0,14},{1,15},{2,0},{3,1},{4,2},{5,3},{6,4},{7,5},{8,6},{9,7},{10,... | collective-permute-start | bytes 786440 | tf_op jit(solution)/shard_map/ppermute | solution.py:226
  88.8 8.0 %collective-permute-start.6 = (bf16[512,256]{1,0:T(8,128)(2,1)S(1)}, bf16[512,256]{1,0:T(8,128)(2,1)S(1)}, u32[]{:S(2)}, u32[]{:S(2)}) collective-permute-start(bf16[512,256]{1,0:T(8,128)(2,1)S(1)} %add_convert_fusion.3), channel_id=1, source_target_pairs={{0,2},{1,3},{2,4},{3,5},{4,6},{5,7},{6,8},{7,9},{8,10},{9,11},{10,... | collective-permute-start | bytes 786440 | tf_op jit(solution)/shard_map/ppermute | solution.py:223
  91.4 7.1 %collective-permute-start.7 = (bf16[512,256]{1,0:T(8,128)(2,1)}, bf16[512,256]{1,0:T(8,128)(2,1)S(1)}, u32[]{:S(2)}, u32[]{:S(2)}) collective-permute-start(bf16[512,256]{1,0:T(8,128)(2,1)} %add_convert_fusion.2), channel_id=1, source_target_pairs={{0,14},{1,15},{2,0},{3,1},{4,2},{5,3},{6,4},{7,5},{8,6},{9,7},{10,... | collective-permute-start | bytes 786440 | tf_op jit(solution)/shard_map/ppermute | solution.py:226
  99.9 13.5 %copy-start.6 = (s32[16,512]{1,0:T(8,128)S(1)}, s32[16,512]{1,0:T(8,128)}, u32[]{:S(2)}) copy-start(s32[16,512]{1,0:T(8,128)} %param.13) | copy-start | bytes 98308
  99.9 8.0 %collective-permute-start.8 = (bf16[512,256]{1,0:T(8,128)(2,1)S(1)}, bf16[512,256]{1,0:T(8,128)(2,1)S(1)}, u32[]{:S(2)}, u32[]{:S(2)}) collective-permute-start(bf16[512,256]{1,0:T(8,128)(2,1)S(1)} %get-tuple-element.60), channel_id=1, source_target_pairs={{0,2},{1,3},{2,4},{3,5},{4,6},{5,7},{6,8},{7,9},{8,10},{9,11},{10,... | collective-permute-start | bytes 786440 | tf_op jit(solution)/shard_map/ppermute | solution.py:223
  101.1 6.8 %collective-permute-start.9 = (bf16[512,256]{1,0:T(8,128)(2,1)S(1)}, bf16[512,256]{1,0:T(8,128)(2,1)S(1)}, u32[]{:S(2)}, u32[]{:S(2)}) collective-permute-start(bf16[512,256]{1,0:T(8,128)(2,1)S(1)} %get-tuple-element.59), channel_id=1, source_target_pairs={{0,14},{1,15},{2,0},{3,1},{4,2},{5,3},{6,4},{7,5},{8,6},{9,7},{10,... | collective-permute-start | bytes 786440 | tf_op jit(solution)/shard_map/ppermute | solution.py:226
  104.7 8.0 %collective-permute-start.10 = (bf16[256,512]{1,0:T(8,128)(2,1)S(1)}, bf16[256,512]{1,0:T(8,128)(2,1)S(1)}, u32[]{:S(2)}, u32[]{:S(2)}) collective-permute-start(bf16[256,512]{1,0:T(8,128)(2,1)S(1)} %constant_dynamic-slice_fusion.1), channel_id=1, source_target_pairs={{0,1},{1,0},{2,3},{3,2},{4,5},{5,4},{6,7},{7,6},{8,9},{9,8},{10,11... | collective-permute-start | bytes 786440 | tf_op jit(solution)/shard_map/ppermute | solution.py:242
  112.7 0.7 copy-start.4
  120.4 2.3 %copy-start.1 = (bf16[8192,256]{1,0:T(8,128)(2,1)S(1)}, bf16[8192,256]{1,0:T(8,128)(2,1)}, u32[]{:S(2)}) copy-start(bf16[8192,256]{1,0:T(8,128)(2,1)} %copy.24) | copy-start | bytes 12582916
  132.9 8.3 %collective-permute-start.14 = (bf16[512,256]{1,0:T(8,128)(2,1)S(1)}, bf16[512,256]{1,0:T(8,128)(2,1)S(1)}, u32[]{:S(2)}, u32[]{:S(2)}) collective-permute-start(bf16[512,256]{1,0:T(8,128)(2,1)S(1)} %shard_map.73), channel_id=1, source_target_pairs={{0,2},{1,3},{2,4},{3,5},{4,6},{5,7},{6,8},{7,9},{8,10},{9,11},{10,... | collective-permute-start | bytes 786440 | tf_op jit(solution)/shard_map/ppermute | solution.py:223
  133.0 8.2 %collective-permute-start.15 = (bf16[512,256]{1,0:T(8,128)(2,1)S(1)}, bf16[512,256]{1,0:T(8,128)(2,1)S(1)}, u32[]{:S(2)}, u32[]{:S(2)}) collective-permute-start(bf16[512,256]{1,0:T(8,128)(2,1)S(1)} %shard_map.73), channel_id=1, source_target_pairs={{0,14},{1,15},{2,0},{3,1},{4,2},{5,3},{6,4},{7,5},{8,6},{9,7},{10,... | collective-permute-start | bytes 786440 | tf_op jit(solution)/shard_map/ppermute | solution.py:226
  141.2 9.2 %collective-permute-start.16 = (bf16[512,256]{1,0:T(8,128)(2,1)S(1)}, bf16[512,256]{1,0:T(8,128)(2,1)S(1)}, u32[]{:S(2)}, u32[]{:S(2)}) collective-permute-start(bf16[512,256]{1,0:T(8,128)(2,1)S(1)} %collective-permute-done.14), channel_id=1, source_target_pairs={{0,2},{1,3},{2,4},{3,5},{4,6},{5,7},{6,8},{7,9},{8,10},{9,11},{10,... | collective-permute-start | bytes 786440 | tf_op jit(solution)/shard_map/ppermute | solution.py:223
  141.2 9.2 %collective-permute-start.17 = (bf16[512,256]{1,0:T(8,128)(2,1)S(1)}, bf16[512,256]{1,0:T(8,128)(2,1)S(1)}, u32[]{:S(2)}, u32[]{:S(2)}) collective-permute-start(bf16[512,256]{1,0:T(8,128)(2,1)S(1)} %collective-permute-done.15), channel_id=1, source_target_pairs={{0,14},{1,15},{2,0},{3,1},{4,2},{5,3},{6,4},{7,5},{8,6},{9,7},{10,... | collective-permute-start | bytes 786440 | tf_op jit(solution)/shard_map/ppermute | solution.py:226
  149.7 6.7 %copy-start.3 = (bf16[2048,512]{1,0:T(8,128)(2,1)S(1)}, bf16[2048,512]{1,0:T(8,128)(2,1)}, u32[]{:S(2)}) copy-start(bf16[2048,512]{1,0:T(8,128)(2,1)} %all-gather.11.cloned.1.call-done) | copy-start | bytes 6291460
  150.3 7.9 %collective-permute-start.18 = (bf16[512,256]{1,0:T(8,128)(2,1)S(1)}, bf16[512,256]{1,0:T(8,128)(2,1)S(1)}, u32[]{:S(2)}, u32[]{:S(2)}) collective-permute-start(bf16[512,256]{1,0:T(8,128)(2,1)S(1)} %collective-permute-done.16), channel_id=1, source_target_pairs={{0,2},{1,3},{2,4},{3,5},{4,6},{5,7},{6,8},{7,9},{8,10},{9,11},{10,... | collective-permute-start | bytes 786440 | tf_op jit(solution)/shard_map/ppermute | solution.py:223
  150.3 8.9 %collective-permute-start.19 = (bf16[512,256]{1,0:T(8,128)(2,1)S(1)}, bf16[512,256]{1,0:T(8,128)(2,1)S(1)}, u32[]{:S(2)}, u32[]{:S(2)}) collective-permute-start(bf16[512,256]{1,0:T(8,128)(2,1)S(1)} %collective-permute-done.17), channel_id=1, source_target_pairs={{0,14},{1,15},{2,0},{3,1},{4,2},{5,3},{6,4},{7,5},{8,6},{9,7},{10,... | collective-permute-start | bytes 786440 | tf_op jit(solution)/shard_map/ppermute | solution.py:226
  159.2 10.3 %collective-permute-start.21 = (bf16[512,128]{1,0:T(8,128)(2,1)S(1)}, bf16[512,128]{1,0:T(8,128)(2,1)S(1)}, u32[]{:S(2)}, u32[]{:S(2)}) collective-permute-start(bf16[512,128]{1,0:T(8,128)(2,1)S(1)} %slice.55), channel_id=1, source_target_pairs={{0,14},{1,15},{2,0},{3,1},{4,2},{5,3},{6,4},{7,5},{8,6},{9,7},{10,... | collective-permute-start | bytes 393224 | tf_op jit(solution)/shard_map/ppermute | solution.py:226
  163.0 6.3 %collective-permute-start.20 = (bf16[512,128]{1,0:T(8,128)(2,1)S(1)}, bf16[512,128]{1,0:T(8,128)(2,1)S(1)}, u32[]{:S(2)}, u32[]{:S(2)}) collective-permute-start(bf16[512,128]{1,0:T(8,128)(2,1)S(1)} %slice.54), channel_id=1, source_target_pairs={{0,2},{1,3},{2,4},{3,5},{4,6},{5,7},{6,8},{7,9},{8,10},{9,11},{10,... | collective-permute-start | bytes 393224 | tf_op jit(solution)/shard_map/ppermute | solution.py:223
  170.4 10.8 %collective-permute-start.22 = (bf16[512,512]{1,0:T(8,128)(2,1)S(1)}, bf16[512,512]{1,0:T(8,128)(2,1)S(1)}, u32[]{:S(2)}, u32[]{:S(2)}) collective-permute-start(bf16[512,512]{1,0:T(8,128)(2,1)S(1)} %fusion.17), channel_id=1, source_target_pairs={{0,1},{1,0},{2,3},{3,2},{4,5},{5,4},{6,7},{7,6},{8,9},{9,8},{10,11... | collective-permute-start | bytes 1572872 | tf_op jit(solution)/shard_map/ppermute | solution.py:270
Sparse Core Ops, SparseCore 0:
  18.1 29.2 all-gather.6
  70.0 34.8 all-gather.8
  113.5 23.8 all-gather.10

commit v5 on v4

--- a/solution.py
+++ b/solution.py
@@ -35,20 +35,25 @@
     return [(z * 2 + y, target(z) * 2 + y) for z in range(ZN) for y in range(2)]
 
 
-def attention_kernel(info_ref, q_ref, kv_ref, o_ref, qa_ref, ka_ref, v_ref):
-    shards_n, rows, _ = kv_ref.shape
-    own = info_ref[shards_n]
-    count = info_ref[own]
-    first = pl.multiple_of(info_ref[shards_n + 1 + own], 16)
-
-    def pack(step, _):
-        start = pl.multiple_of(info_ref[shards_n + 1 + step], 16)
-        slot = lax.broadcasted_iota(jnp.int32, (rows, HD), 0)
-        ka_ref[pl.ds(start, rows), :HD] = kv_ref[step, :, :HD]
-        ka_ref[pl.ds(start, rows), HD:] = jnp.where(slot < info_ref[step], 0.0, MASKED_SCORE).astype(jnp.bfloat16)
-        v_ref[pl.ds(start, rows), :] = kv_ref[step, :, HD:]
-
-    lax.fori_loop(0, own + 1, pack, None)
+def attention_kernel(info_ref, q_ref, *refs):
+    kv_refs, (o_ref, qa_ref, ka_ref, v_ref) = refs[:-4], refs[-4:]
+    blocks_each, rows, _ = kv_refs[0].shape
+    order = [(array, place) for array in range(len(kv_refs)) for place in range(blocks_each)]
+    order = order[1:] + order[:1]
+    count = info_ref[len(order) - 1, 1]
+    first = pl.multiple_of(info_ref[len(order) - 1, 2], 16)
+
+    for index, (array, place) in enumerate(order):
+
+        @pl.when(info_ref[index, 0] > 0)
+        def _():
+            start = pl.multiple_of(info_ref[index, 2], 16)
+            slot = lax.broadcasted_iota(jnp.int32, (rows, HD), 0)
+            bias = jnp.where(slot < info_ref[index, 1], 0.0, MASKED_SCORE)
+            ka_ref[pl.ds(start, rows), :HD] = kv_refs[array][place, :, :HD]
+            ka_ref[pl.ds(start, rows), HD:] = bias.astype(jnp.bfloat16)
+            v_ref[pl.ds(start, rows), :] = kv_refs[array][place, :, HD:]
+
     tail = pl.multiple_of(first + rows, 16)
     ka_ref[pl.ds(tail, KEY_BLOCK), :] = jnp.zeros((KEY_BLOCK, 2 * HD), jnp.bfloat16)
     v_ref[pl.ds(tail, KEY_BLOCK), :] = jnp.zeros((KEY_BLOCK, HD), jnp.bfloat16)
@@ -128,31 +133,84 @@
                 o_ref[tile * ROW_TILE : (tile + 1) * ROW_TILE, :] = jnp.zeros((ROW_TILE, 2 * HD), jnp.bfloat16)
 
 
-def attention(counts, own, queries, kv):
-    shards_n, rows, _ = kv.shape
-    packed = (counts + 15) // 16 * 16
-    first = jnp.cumsum(packed) - packed
-    info = jnp.concatenate([counts, own[None], first]).astype(jnp.int32)
+def attention(counts, own, queries, ids, kv):
+    blocks_each, rows, _ = kv[0].shape
+    shards_n = blocks_each * len(kv)
+    ids = jnp.concatenate([ids[1:], ids[:1]])
+    used = ids <= own
+    held = jnp.sum(jnp.where(ids[:, None] == jnp.arange(shards_n)[None, :], counts[None, :], 0), axis=1)
+    packed = jnp.where(used, (held + 15) // 16 * 16, 0)
+    before = jnp.arange(shards_n)[None, :] < jnp.arange(shards_n)[:, None]
+    first = jnp.sum(jnp.where(before, packed[None, :], 0), axis=1)
+    info = jnp.stack([used.astype(jnp.int32), held, first], axis=1).astype(jnp.int32)
     capacity = shards_n * (rows // 2 + 16) + rows + KEY_BLOCK
     return pl.pallas_call(
         attention_kernel,
         out_shape=jax.ShapeDtypeStruct(queries.shape, jnp.bfloat16),
+        in_specs=[pl.BlockSpec(memory_space=pltpu.SMEM)]
+        + [pl.BlockSpec(memory_space=pltpu.VMEM)] * (1 + len(kv)),
+        out_specs=pl.BlockSpec(memory_space=pltpu.VMEM),
+        scratch_shapes=[
+            pltpu.VMEM((2, rows, 2 * HD), jnp.bfloat16),
+            pltpu.VMEM((capacity, 2 * HD), jnp.bfloat16),
+            pltpu.VMEM((capacity, HD), jnp.bfloat16),
+        ],
+        compiler_params=pltpu.CompilerParams(vmem_limit_bytes=ATTENTION_VMEM),
+        cost_estimate=pl.CostEstimate(
+            flops=4 * 2 * rows * HD * shards_n * rows,
+            bytes_accessed=shards_n * rows * HD * 4,
+            transcendentals=rows * rows * shards_n,
+        ),
+    )(info, queries, *kv)
+
+
+def query_kernel(y_ref, x_own_ref, x_in_ref, w_own_ref, w_in_ref, o_ref):
+    o_ref[0] = (dot(x_own_ref[...], w_own_ref[...]) + dot(x_in_ref[...], w_in_ref[0])).astype(jnp.bfloat16)
+
+
+def query_parts(y, x_own, x_in, query_weight, wq_in):
+    chunks, width, chunk = wq_in.shape
+    rows = x_own.shape[0]
+    return pl.pallas_call(
+        query_kernel,
+        out_shape=jax.ShapeDtypeStruct((chunks, rows, chunk), jnp.bfloat16),
         grid_spec=pltpu.PrefetchScalarGridSpec(
             num_scalar_prefetch=1,
-            grid=(),
-            in_specs=[pl.BlockSpec(memory_space=pltpu.VMEM)] * 2,
-            out_specs=pl.BlockSpec(memory_space=pltpu.VMEM),
-            scratch_shapes=[
-                pltpu.VMEM((2, rows, 2 * HD), jnp.bfloat16),
-                pltpu.VMEM((capacity, 2 * HD), jnp.bfloat16),
-                pltpu.VMEM((capacity, HD), jnp.bfloat16),
+            grid=(chunks,),
+            in_specs=[
+                pl.BlockSpec((rows, width), lambda d, y: (0, 0)),
+                pl.BlockSpec((rows, width), lambda d, y: (0, 0)),
+                pl.BlockSpec((width, chunk), lambda d, y: (0, y[0] * chunks + d)),
+                pl.BlockSpec((1, width, chunk), lambda d, y: (d, 0, 0)),
             ],
+            out_specs=pl.BlockSpec((1, rows, chunk), lambda d, y: (d, 0, 0)),
         ),
-        compiler_params=pltpu.CompilerParams(vmem_limit_bytes=ATTENTION_VMEM),
+        compiler_params=pltpu.CompilerParams(vmem_limit_bytes=16 * 1024 * 1024),
         cost_estimate=pl.CostEstimate(
-            flops=4 * 2 * rows * HD * shards_n * rows, bytes_accessed=kv.size * 2, transcendentals=rows * rows * shards_n
+            flops=4 * chunks * rows * width * chunk, bytes_accessed=chunks * chunk * (4 * width + 2 * rows), transcendentals=0
         ),
-    )(info, queries, kv)
+    )(y[None].astype(jnp.int32), x_own, x_in, query_weight, wq_in)
+
+
+def order_kernel(at_ref, *refs):
+    pieces, o_ref, scratch_ref = refs[:4], refs[4], refs[5]
+    depth = pieces[0].shape[0]
+    for k in range(4):
+        place = lax.rem(at_ref[0] - k + 4, 4)
+        scratch_ref[pl.ds(pl.multiple_of(place * depth, depth), depth), :] = pieces[k][...].astype(jnp.float32)
+    o_ref[...] = scratch_ref[...].T.astype(jnp.bfloat16)
+
+
+def ordered_rows(at, pieces):
+    depth, rows = pieces[0].shape
+    return pl.pallas_call(
+        order_kernel,
+        out_shape=jax.ShapeDtypeStruct((rows, 4 * depth), jnp.bfloat16),
+        in_specs=[pl.BlockSpec(memory_space=pltpu.SMEM)] + [pl.BlockSpec(memory_space=pltpu.VMEM)] * 4,
+        out_specs=pl.BlockSpec(memory_space=pltpu.VMEM),
+        scratch_shapes=[pltpu.VMEM((4 * depth, rows), jnp.float32)],
+        cost_estimate=pl.CostEstimate(flops=0, bytes_accessed=16 * depth * rows, transcendentals=0),
+    )(at[None].astype(jnp.int32), *pieces)
 
 
 def dot(a, b):
@@ -201,23 +259,52 @@
     sent = jnp.concatenate([kv_part, jnp.broadcast_to(stats_rows[None], (2 * ZN, 8, rows))], axis=1)
     sent, wq_got = lax.optimization_barrier((sent, wq_got))
     wq_in = share(wq_got)
-    own_weights = lax.dynamic_slice(query_weight, (0, y * half_cols), (width, half_cols))
-    query_own = dot(x_own, own_weights)
-    summed = jnp.sum(lax.all_to_all(sent, "tp", 0, 0, tiled=True).astype(jnp.float32), axis=0)
+    exchanged = lax.all_to_all(sent, "tp", 0, 0, tiled=True)
+    part = query_parts(y, x_own, x_in, query_weight, wq_in)
+    exchanged, part = lax.optimization_barrier((exchanged, part))
+    query_sum = lax.psum_scatter(
+        part, "tp", scatter_dimension=0, axis_index_groups=[[2 * k + h for k in range(ZN)] for h in range(2)]
+    )
+    summed = jnp.sum(exchanged.astype(jnp.float32), axis=0)
     square_sum = summed[HD // 2] + summed[HD // 2 + 2]
     router_logit = summed[HD // 2 + 1] + summed[HD // 2 + 3]
     inverse_rms = lax.rsqrt(square_sum / D + EPSILON)
     piece = (summed[: HD // 2] * inverse_rms[None, :]).astype(bf16)
-    piece, wq_in, x_in, query_own = lax.optimization_barrier((piece, wq_in, x_in, query_own))
-    pieces = [lax.ppermute(piece, "tp", quad_shift(k)) for k in (3, 2, 1)] + [piece]
-    ordered = jnp.stack(pieces + pieces[:3])
-    kv_own = lax.dynamic_slice_in_dim(ordered, (3 - z % 4) % 4, 4, 0).reshape(2 * HD, rows).T
-    kv_all = lax.all_gather(kv_own, "ctx", axis=0, tiled=False)
-
-    def query_part(offset):
-        d = (z + offset) % ZN
-        own = lax.dynamic_slice(query_own, (0, d * chunk), (rows, chunk))
-        return own + dot(x_in, lax.dynamic_index_in_dim(wq_in, d, 0, keepdims=False))
+    pieces = [lax.ppermute(piece, "tp", quad_shift(k)) for k in (1, 2, 3)]
+    pieces = [piece] + pieces
+    kv_own = ordered_rows(z % 4, pieces)
+
+    x_n = shard_n // 4
+
+    def along(step):
+        return [(c, c // (2 * x_n) * (2 * x_n) + (c + 2 * step) % (2 * x_n)) for c in range(shard_n)]
+
+    def x_hop(block, step):
+        return lax.ppermute(block, "ctx", along(step))
+
+    middle = rows // 2
+    over = lax.ppermute(kv_own, "ctx", [(c, (c + shard_n // 2) % shard_n) for c in range(shard_n)])
+    near_left, near_right, over = lax.optimization_barrier((x_hop(kv_own, 1), x_hop(kv_own, -1), over))
+    first_half = jnp.stack([kv_own, near_left, near_right, over])
+    far = x_hop(near_left[:middle], 1), x_hop(near_right[middle:], -1)
+    over_left, over_right = x_hop(over, 1), x_hop(over, -1)
+    wo_rows = out_weight.shape[0] // 2
+    wo_start = (1 - y) * wo_rows + mine * chunk
+    near_left, wo_start = lax.optimization_barrier((near_left, wo_start))
+    wo_got = lax.ppermute(lax.dynamic_slice(out_weight, (wo_start, 0), (chunk, width)), "tp", y_swap())
+    over_left, over_right, far, wo_got = lax.optimization_barrier((over_left, over_right, far, wo_got))
+    wo_in = share(wo_got).reshape(wo_rows, width)
+    over_far = x_hop(over_left[:middle], 1), x_hop(over_right[middle:], -1)
+    second_half = jnp.stack([over_left, over_right, jnp.concatenate(far), jnp.concatenate(over_far)])
+
+    def core_hop(block):
+        return lax.ppermute(block, "ctx", [(c, c ^ 1) for c in range(shard_n)])
+
+    kv_all = [first_half, second_half, core_hop(first_half), core_hop(second_half)]
+    at_y, at_x, core = shard // (2 * x_n), shard // 2 % x_n, shard % 2
+    offsets = [(0, 0), (-1, 0), (1, 0), (0, 1), (-1, 1), (1, 1), (2, 0), (2, 1)]
+    ids = [(at_y + dy) % 2 * (2 * x_n) + (at_x + dx) % x_n * 2 for dx, dy in offsets]
+    ids = jnp.stack([i + core for i in ids] + [i + 1 - core for i in ids])
 
     def right(a):
         return lax.ppermute(a.astype(bf16), "tp", z_shift(1))
@@ -229,28 +316,10 @@
         return lax.optimization_barrier((right(going_right), left(going_left)))
 
     cut = chunk // 2
-    far = query_part(4)
-    going_right, going_left = both(far[:, :cut], far[:, cut:])
-    part_right, part_left = query_part(3), query_part(-3)
-    going_right, going_left = both(
-        jnp.concatenate([part_right[:, :cut] + going_right, part_right[:, cut:]], axis=1),
-        jnp.concatenate([part_left[:, :cut], part_left[:, cut:] + going_left], axis=1),
-    )
-    wo_rows = out_weight.shape[0] // 2
-    wo_start = (1 - y) * wo_rows + mine * chunk
-    going_right, wo_start = lax.optimization_barrier((going_right, wo_start))
-    wo_got = lax.ppermute(
-        lax.dynamic_slice(out_weight, (wo_start, 0), (chunk, width)), "tp", y_swap()
-    )
-    for step in (2, 1):
-        going_right, going_left = both(query_part(step) + going_right, query_part(-step) + going_left)
-    queries = (query_part(0) + going_right + going_left) * (inverse_rms * EXP_SCALE)[:, None]
-
-    queries, wo_got = lax.optimization_barrier((queries.astype(bf16), wo_got))
-    wo_in = share(wo_got).reshape(wo_rows, width)
+    queries = (query_sum.astype(jnp.float32) * (inverse_rms * EXP_SCALE)[:, None]).astype(bf16)
 
     counts = jnp.sum((kept_rows < tokens).astype(jnp.int32), axis=1)
-    mixed = attention(counts, shard, queries, kv_all)
+    mixed = attention(counts, shard, queries, ids, kv_all)
 
     def project(piece, offset, low, high):
         start = ((z + offset) % ZN) * chunk + low

time: 191 us -> 188 us (0.984)
  matrix products: 34.2 us -> 24.6 us
  Pallas kernels: 10.2 us -> 18.4 us
  local copies, waits for them, and re-layouts: 14.3 us -> 11.9 us
    all_to_all x1, waiting for transfers between devices: 23.1 us -> 4.45 us  [shards(): exchanged = lax.all_to_all(sent, 'tp', 0, 0, tiled=True)]
    ppermute x3 -> x14, waiting for transfers between devices: 5.71 us -> 21.1 us  [the longest x8 14.8 us: x_hop(): return lax.ppermute(block, 'ctx', along(step))]
    ppermute x1, waiting for transfers between devices: 0.01 us -> 13.9 us  [shards(): x_in = lax.ppermute(x_own, 'tp', y_swap())]
    ppermute x3 -> x14, starting transfers between devices: 3.09 us -> 16.6 us  [the longest x8 10.6 us: x_hop(): return lax.ppermute(block, 'ctx', along(step))]
    dot_general x28 -> x19, matrix products: 31.4 us -> 21.9 us  [dot(): return jnp.dot(a, b, preferred_element_type=jnp.float32)]
    ppermute x8 -> x4, starting transfers between devices: 25.4 us -> 16 us  [left(): return lax.ppermute(a.astype(bf16), 'tp', z_shift(-1))]
    pallas_call x0 -> x2, Pallas kernels: none -> 7.05 us  [the longest x1 5.24 us: query_parts(): pl.pallas_call(query_kernel, out_shape=jax.ShapeDtypeStruct((chunks, rows...]
    all_gather x1 -> x0, local copies, waits for them, and re-layouts: 6.46 us -> none  [shards(): kv_all = lax.all_gather(kv_own, 'ctx', axis=0, tiled=False)]
  transfers between devices with their start and end apart: 27 -> 30, of which waited for: 16 -> 18; matrix products, arithmetic and copies ran while one was open for 25% -> 18% of each run, Pallas kernels for 5% -> 10%
where the time goes in v5:
time: 188 us
  waiting for transfers between devices  62 us (33%)
  starting transfers between devices  50.3 us (27%)
  matrix products  24.6 us (13%)
  Pallas kernels  18.4 us (10%)
  between operations  13.7 us (7%)
  local copies, waits for them, and re-layouts  11.9 us (6%)
  other arithmetic  6.83 us (4%)
    dot_general x19, matrix products, dot(): return jnp.dot(a, b, preferred_element_type=jnp.float32)  21.9 us
    ppermute x4, starting transfers between devices, left(): return lax.ppermute(a.astype(bf16), 'tp', z_shift(-1))  16 us
    ppermute x8, waiting for transfers between devices, x_hop(): return lax.ppermute(block, 'ctx', along(step))  14.8 us
    ppermute x1, waiting for transfers between devices, shards(): x_in = lax.ppermute(x_own, 'tp', y_swap())  13.9 us
    ppermute x4, waiting for transfers between devices, right(): return lax.ppermute(a.astype(bf16), 'tp', z_shift(1))  11.9 us
    pallas_call x1, Pallas kernels, attention(): pl.pallas_call(attention_kernel, out_shape=jax.ShapeDtypeStruct(queries.s...  11.3 us
    ppermute x8, starting transfers between devices, x_hop(): return lax.ppermute(block, 'ctx', along(step))  10.6 us
    all_to_all x1, starting transfers between devices, shards(): exchanged = lax.all_to_all(sent, 'tp', 0, 0, tiled=True)  9.25 us
  transfers between devices with their start and end apart: 30, of which 18 were waited for; matrix products, arithmetic and copies ran while one was open for 18% of the time, Pallas kernels for 10%

profile of v5, /device:TPU:14, one launch (start us, length us, event | category | flops | bytes accessed | tf_op | source)
XLA Modules:
  0.0 187.7 jit_solution(8633961275217589808)
XLA Ops:
  7.6 2.4 %collective-permute-start = (bf16[512,256]{1,0:T(8,128)(2,1)S(1)}, bf16[512,256]{1,0:T(8,128)(2,1)S(1)}, u32[]{:S(2)}, u32[]{:S(2)}) collective-permute-start(bf16[512,256]{1,0:T(8,128)(2,1)S(1)} %constant_dynamic-slice_fusion.1), channel_id=1, source_target_pairs={{0,1},{1,0},{2,3},{3,2},{4,5},{5,4},{6,7},{7,6},{8,9},{9,8},{10,11... | collective-permute-start | bytes 786440 | tf_op jit(solution)/shard_map/ppermute | solution.py:239
  11.4 3.1 %multiply_reduce_fusion.1 = (f32[512]{0:T(512)S(1)}, f32[512]{0:T(512)S(1)}, f32[512,512]{0,1:T(8,128)}) fusion(f32[512]{0:T(512)S(1)} %convert_element_type.65, bf16[1024,512]{1,0:T(8,128)(2,1)} %param.7, s32[512]{0:T(512)S(1)} %bitcast.95), kind=kOutput, calls=%fused_computation.28 | convolution fusion | flops 538442752 | bytes 2105344 | tf_op jit(solution)/shard_map/dot_general | solution.py:217
  14.5 1.6 copy.21
  19.1 9.3 %all-to-all-start = ((bf16[16,72,512]{2,1,0:T(8,128)(2,1)}), bf16[16,72,512]{2,1,0:T(8,128)(2,1)S(1)}, u32[]{:S(2)}, u32[]{:S(2)}) async-start(bf16[16,72,512]{2,1,0:T(8,128)(2,1)} %pad_maximum_fusion), calls=%async_computation | async-start | bytes 2359296 | tf_op jit(solution)/shard_map/all_to_all | solution.py:262
  28.4 3.5 %collective-permute-start.1 = (bf16[512,512]{1,0:T(8,128)(2,1)S(1)}, bf16[512,512]{1,0:T(8,128)(2,1)S(1)}, u32[]{:S(2)}, u32[]{:S(2)}) collective-permute-start(bf16[512,512]{1,0:T(8,128)(2,1)S(1)} %multiply_convert_fusion.1.x_own_ref), channel_id=1, source_target_pairs={{0,1},{1,0},{2,3},{3,2},{4,5},{5,4},{6,7},{7,6},{8,9},{9,8},{10,11... | collective-permute-start | bytes 1572872 | tf_op jit(solution)/shard_map/ppermute | solution.py:247
  31.9 13.9 %collective-permute-done.1.x_in_ref = bf16[512,512]{1,0:T(8,128)(2,1)S(1)} collective-permute-done((bf16[512,512]{1,0:T(8,128)(2,1)S(1)}, bf16[512,512]{1,0:T(8,128)(2,1)S(1)}, u32[]{:S(2)}, u32[]{:S(2)}) %collective-permute-start.1) | collective-permute-done | bytes 524320 | tf_op jit(solution)/shard_map/ppermute | solution.py:247
  45.9 1.5 all-gather.5.cloned.1.call-done
  47.3 2.2 %copy-done.1 = bf16[512,4096]{1,0:T(8,128)(2,1)S(1)} copy-done((bf16[512,4096]{1,0:T(8,128)(2,1)S(1)}, bf16[512,4096]{1,0:T(8,128)(2,1)}, u32[]{:S(2)}) %copy-start.1) | copy-done | bytes 4194328
  49.5 1.6 copy-done.2
  51.1 5.2 %shard_map.73 = bf16[8,512,256]{2,1,0:T(8,128)(2,1)} custom-call(s32[1]{0:T(128)} %bitcast.8.y_ref, bf16[512,512]{1,0:T(8,128)(2,1)S(1)} %multiply_convert_fusion.1.x_own_ref, bf16[512,512]{1,0:T(8,128)(2,1)S(1)} %collective-permute-done.1.x_in_ref, bf16[512,4096]{1,0:T(8,128)(2,1)S(1)} %copy-done.1, bf16[8,512,256]{2,1,0:T(8,128)(2,1)S(1)} %bitcast.84), custom_call_target="tpu_custom_call" | custom-call | flops 2147483648 | bytes 6291456 | tf_op jit(solution)/shard_map/pallas_call | solution.py:174
  56.4 4.5 %all-to-all-done = bf16[16,72,512]{2,1,0:T(8,128)(2,1)S(1)} async-done(((bf16[16,72,512]{2,1,0:T(8,128)(2,1)}), bf16[16,72,512]{2,1,0:T(8,128)(2,1)S(1)}, u32[]{:S(2)}, u32[]{:S(2)}) %all-to-all-start) | async-done | bytes 1179680 | tf_op jit(solution)/shard_map/all_to_all | solution.py:262
  61.2 5.0 %collective-permute-start.3 = (bf16[64,512]{1,0:T(8,128)(2,1)S(1)}, bf16[64,512]{1,0:T(8,128)(2,1)S(1)}, u32[]{:S(2)}, u32[]{:S(2)}) collective-permute-start(bf16[64,512]{1,0:T(8,128)(2,1)S(1)} %fusion.49.refs_0_), channel_id=1, source_target_pairs={{0,4},{1,5},{2,6},{3,7},{4,0},{5,1},{6,2},{7,3},{8,12},{9,13},{10,... | collective-permute-start | bytes 196616 | tf_op jit(solution)/shard_map/ppermute | solution.py:273
  66.2 1.7 collective-permute-done.2.refs_1_
  67.9 1.4 collective-permute-done.3.refs_2_
  71.1 1.8 shard_map.74
  73.3 1.5 collective-permute-start.6
  75.7 4.9 %collective-permute-done.5 = bf16[512,256]{1,0:T(8,128)(2,1)S(1)} collective-permute-done((bf16[512,256]{1,0:T(8,128)(2,1)}, bf16[512,256]{1,0:T(8,128)(2,1)S(1)}, u32[]{:S(2)}, u32[]{:S(2)}) %collective-permute-start.5) | collective-permute-done | bytes 262176 | tf_op jit(solution)/shard_map/ppermute | solution.py:283
  81.9 1.3 collective-permute-start.8
  84.9 1.2 collective-permute-start.12
  86.2 2.9 %collective-permute-start.10 = (bf16[256,256]{1,0:T(8,128)(2,1)S(1)}, bf16[256,256]{1,0:T(8,128)(2,1)S(1)}, u32[]{:S(2)}, u32[]{:S(2)}) collective-permute-start(bf16[256,256]{1,0:T(8,128)(2,1)S(1)} %slice.38), channel_id=1, source_target_pairs={{0,32},{16,48},{32,64},{48,80},{64,96},{80,112},{96,0},{112,16},{1... | collective-permute-start | bytes 393224 | tf_op jit(solution)/shard_map/ppermute | solution.py:283
  89.3 2.2 %collective-permute-done.10 = bf16[256,256]{1,0:T(8,128)(2,1)S(1)} collective-permute-done((bf16[256,256]{1,0:T(8,128)(2,1)S(1)}, bf16[256,256]{1,0:T(8,128)(2,1)S(1)}, u32[]{:S(2)}, u32[]{:S(2)}) %collective-permute-start.10) | collective-permute-done | bytes 131104 | tf_op jit(solution)/shard_map/ppermute | solution.py:283
  91.6 5.3 %collective-permute-done.11 = bf16[256,256]{1,0:T(8,128)(2,1)S(1)} collective-permute-done((bf16[256,256]{1,0:T(8,128)(2,1)S(1)}, bf16[256,256]{1,0:T(8,128)(2,1)S(1)}, u32[]{:S(2)}, u32[]{:S(2)}) %collective-permute-start.11) | collective-permute-done | bytes 131104 | tf_op jit(solution)/shard_map/ppermute | solution.py:283
  100.5 3.3 %collective-permute-start.13 = (bf16[256,256]{1,0:T(8,128)(2,1)S(1)}, bf16[256,256]{1,0:T(8,128)(2,1)S(1)}, u32[]{:S(2)}, u32[]{:S(2)}) collective-permute-start(bf16[256,256]{1,0:T(8,128)(2,1)S(1)} %slice.40), channel_id=1, source_target_pairs={{0,32},{16,48},{32,64},{48,80},{64,96},{80,112},{96,0},{112,16},{1... | collective-permute-start | bytes 393224 | tf_op jit(solution)/shard_map/ppermute | solution.py:283
  105.0 1.6 collective-permute-done.14
  109.3 1.4 collective-permute-done.16.refs_3_
  110.7 11.3 %shard_map.75 = bf16[512,256]{1,0:T(8,128)(2,1)S(1)} custom-call(s32[16,3]{1,0:T(8,128)S(1)} %copy.24.info_ref, bf16[512,256]{1,0:T(8,128)(2,1)S(1)} %fusion.20.q_ref, bf16[4,512,256]{2,1,0:T(8,128)(2,1)S(1)} %pad_maximum_fusion.1.refs_0_, bf16[4,512,256]{2,1,0:T(8,128)(2,1)S(1)} %pad_maximum_fusion.2.refs_1_, ...), custom_call_target="tpu_custom_call" | custom-call | flops 4294967296 | bytes 4194304 | tf_op jit(solution)/shard_map/pallas_call | solution.py:147
  122.1 7.0 %collective-permute-start.18 = (bf16[512,256]{1,0:T(8,128)(2,1)S(1)}, bf16[512,256]{1,0:T(8,128)(2,1)}, u32[]{:S(2)}, u32[]{:S(2)}) collective-permute-start(bf16[512,256]{1,0:T(8,128)(2,1)S(1)} %shard_map.75), channel_id=1, source_target_pairs={{0,14},{1,15},{2,0},{3,1},{4,2},{5,3},{6,4},{7,5},{8,6},{9,7},{10,... | collective-permute-start | bytes 786440 | tf_op jit(solution)/shard_map/ppermute | solution.py:313
  129.1 5.8 %collective-permute-done.17 = bf16[512,256]{1,0:T(8,128)(2,1)} collective-permute-done((bf16[512,256]{1,0:T(8,128)(2,1)S(1)}, bf16[512,256]{1,0:T(8,128)(2,1)}, u32[]{:S(2)}, u32[]{:S(2)}) %collective-permute-start.17) | collective-permute-done | bytes 262176 | tf_op jit(solution)/shard_map/ppermute | solution.py:310
  134.9 3.6 %collective-permute-start.20 = (bf16[512,256]{1,0:T(8,128)(2,1)}, bf16[512,256]{1,0:T(8,128)(2,1)}, u32[]{:S(2)}, u32[]{:S(2)}) collective-permute-start(bf16[512,256]{1,0:T(8,128)(2,1)} %collective-permute-done.18), channel_id=1, source_target_pairs={{0,14},{1,15},{2,0},{3,1},{4,2},{5,3},{6,4},{7,5},{8,6},{9,7},{10,... | collective-permute-start | bytes 786440 | tf_op jit(solution)/shard_map/ppermute | solution.py:313
  138.6 1.3 fusion.44
  139.9 1.3 fusion.46
  141.3 1.3 fusion.32
  142.6 1.5 fusion.34
  144.1 1.8 collective-permute-done.19
  146.9 2.3 %collective-permute-start.22 = (bf16[512,256]{1,0:T(8,128)(2,1)}, bf16[512,256]{1,0:T(8,128)(2,1)S(1)}, u32[]{:S(2)}, u32[]{:S(2)}) collective-permute-start(bf16[512,256]{1,0:T(8,128)(2,1)} %collective-permute-done.20), channel_id=1, source_target_pairs={{0,14},{1,15},{2,0},{3,1},{4,2},{5,3},{6,4},{7,5},{8,6},{9,7},{10,... | collective-permute-start | bytes 786440 | tf_op jit(solution)/shard_map/ppermute | solution.py:313
  149.2 1.3 fusion.40
  150.5 1.3 fusion.42
  151.9 1.2 fusion.28
  153.1 1.2 fusion.30
  154.3 1.5 collective-permute-done.21
  155.9 3.0 %collective-permute-start.24 = (bf16[512,128]{1,0:T(8,128)(2,1)S(1)}, bf16[512,128]{1,0:T(8,128)(2,1)S(1)}, u32[]{:S(2)}, u32[]{:S(2)}) collective-permute-start(bf16[512,128]{1,0:T(8,128)(2,1)S(1)} %slice.43), channel_id=1, source_target_pairs={{0,14},{1,15},{2,0},{3,1},{4,2},{5,3},{6,4},{7,5},{8,6},{9,7},{10,... | collective-permute-start | bytes 393224 | tf_op jit(solution)/shard_map/ppermute | solution.py:313
  159.0 1.2 fusion.36
  160.3 1.3 fusion.38
  162.4 2.8 %collective-permute-done.23 = bf16[512,128]{1,0:T(8,128)(2,1)S(1)} collective-permute-done((bf16[512,128]{1,0:T(8,128)(2,1)S(1)}, bf16[512,128]{1,0:T(8,128)(2,1)S(1)}, u32[]{:S(2)}, u32[]{:S(2)}) %collective-permute-start.23) | collective-permute-done | bytes 131104 | tf_op jit(solution)/shard_map/ppermute | solution.py:310
  167.4 1.2 fusion.56
  168.5 1.6 fusion.10
  170.2 9.1 %collective-permute-done.25 = bf16[512,512]{1,0:T(8,128)(2,1)S(1)} collective-permute-done((bf16[512,512]{1,0:T(8,128)(2,1)S(1)}, bf16[512,512]{1,0:T(8,128)(2,1)S(1)}, u32[]{:S(2)}, u32[]{:S(2)}) %collective-permute-start.25) | collective-permute-done | bytes 524320 | tf_op jit(solution)/shard_map/ppermute | solution.py:339
  179.2 2.0 %fusion.2 = bf16[1024,512]{1,0:T(8,128)(2,1)} fusion(s32[512]{0:T(512)S(1)} %bitcast.96, f32[512,512]{1,0:T(8,128)S(1)} %fusion.10, bf16[512,512]{1,0:T(8,128)(2,1)S(1)} %collective-permute-done.25, f32[512]{0:T(512)S(1)} %bitcast.98), kind=kOutput, calls=%fused_computation.4 | convolution fusion | flops 538968064 | bytes 2625536 | tf_op jit(solution)/shard_map/dot_general | solution.py:343
  (113 shorter events, 23.7 us)
Async XLA Ops:
  6.5 9.7 %copy-start = (bf16[2,512,512]{2,1,0:T(8,128)(2,1)S(1)}, bf16[2,512,512]{2,1,0:T(8,128)(2,1)}, u32[]{:S(2)}) copy-start(bf16[2,512,512]{2,1,0:T(8,128)(2,1)} %param.11) | copy-start | bytes 3145732
  6.5 40.8 %all-gather.5.cloned.1.call-start = ((), (), s32[]{:S(2)}) async-start(), calls=%async_computation.3 | async-start | bytes 2359296 | tf_op jit(solution)/shard_map/all_gather | solution.py:236
  7.6 10.8 %collective-permute-start = (bf16[512,256]{1,0:T(8,128)(2,1)S(1)}, bf16[512,256]{1,0:T(8,128)(2,1)S(1)}, u32[]{:S(2)}, u32[]{:S(2)}) collective-permute-start(bf16[512,256]{1,0:T(8,128)(2,1)S(1)} %constant_dynamic-slice_fusion.1), channel_id=1, source_target_pairs={{0,1},{1,0},{2,3},{3,2},{4,5},{5,4},{6,7},{7,6},{8,9},{9,8},{10,11... | collective-permute-start | bytes 786440 | tf_op jit(solution)/shard_map/ppermute | solution.py:239
  11.4 4.7 %copy-start.16 = (bf16[512]{0:T(512)(128)(2,1)S(1)}, bf16[512]{0:T(512)(128)(2,1)}, u32[]{:S(2)}) copy-start(bf16[512]{0:T(512)(128)(2,1)} %param.8) | copy-start | bytes 3076
  18.4 0.7 copy-start.9
  19.1 41.7 %all-to-all-start = ((bf16[16,72,512]{2,1,0:T(8,128)(2,1)}), bf16[16,72,512]{2,1,0:T(8,128)(2,1)S(1)}, u32[]{:S(2)}, u32[]{:S(2)}) async-start(bf16[16,72,512]{2,1,0:T(8,128)(2,1)} %pad_maximum_fusion), calls=%async_computation | async-start | bytes 2359296 | tf_op jit(solution)/shard_map/all_to_all | solution.py:262
  28.4 79.8 %reduce-scatter.2.cloned.1.call-start = ((), (), s32[]{:S(2)}) async-start(), calls=%async_computation.2 | async-start | bytes 2359296 | tf_op jit(solution)/shard_map/reduce_scatter | solution.py:265
  28.4 17.4 %collective-permute-start.1 = (bf16[512,512]{1,0:T(8,128)(2,1)S(1)}, bf16[512,512]{1,0:T(8,128)(2,1)S(1)}, u32[]{:S(2)}, u32[]{:S(2)}) collective-permute-start(bf16[512,512]{1,0:T(8,128)(2,1)S(1)} %multiply_convert_fusion.1.x_own_ref), channel_id=1, source_target_pairs={{0,1},{1,0},{2,3},{3,2},{4,5},{5,4},{6,7},{7,6},{8,9},{9,8},{10,11... | collective-permute-start | bytes 1572872 | tf_op jit(solution)/shard_map/ppermute | solution.py:247
  47.3 2.2 %copy-start.1 = (bf16[512,4096]{1,0:T(8,128)(2,1)S(1)}, bf16[512,4096]{1,0:T(8,128)(2,1)}, u32[]{:S(2)}) copy-start(bf16[512,4096]{1,0:T(8,128)(2,1)} %w_own_ref.1) | copy-start | bytes 12582916
  49.5 1.6 copy-start.2
  60.8 80.4 %all-gather.7.cloned.1.call-start = ((), (), s32[]{:S(2)}) async-start(), calls=%async_computation.4 | async-start | bytes 2359296 | tf_op jit(solution)/shard_map/all_gather | solution.py:236
  61.1 9.3 %copy-start.7 = (bf16[64,512]{1,0:T(8,128)(2,1)}, bf16[64,512]{1,0:T(8,128)(2,1)S(1)}, u32[]{:S(2)}) copy-start(bf16[64,512]{1,0:T(8,128)(2,1)S(1)} %fusion.49.refs_0_) | copy-start | bytes 196612
  61.1 6.8 %collective-permute-start.2 = (bf16[64,512]{1,0:T(8,128)(2,1)S(1)}, bf16[64,512]{1,0:T(8,128)(2,1)S(1)}, u32[]{:S(2)}, u32[]{:S(2)}) collective-permute-start(bf16[64,512]{1,0:T(8,128)(2,1)S(1)} %fusion.49.refs_0_), channel_id=1, source_target_pairs={{0,2},{1,3},{2,4},{3,5},{4,6},{5,7},{6,0},{7,1},{8,10},{9,11},{10,... | collective-permute-start | bytes 196616 | tf_op jit(solution)/shard_map/ppermute | solution.py:273
  61.2 8.1 %collective-permute-start.3 = (bf16[64,512]{1,0:T(8,128)(2,1)S(1)}, bf16[64,512]{1,0:T(8,128)(2,1)S(1)}, u32[]{:S(2)}, u32[]{:S(2)}) collective-permute-start(bf16[64,512]{1,0:T(8,128)(2,1)S(1)} %fusion.49.refs_0_), channel_id=1, source_target_pairs={{0,4},{1,5},{2,6},{3,7},{4,0},{5,1},{6,2},{7,3},{8,12},{9,13},{10,... | collective-permute-start | bytes 196616 | tf_op jit(solution)/shard_map/ppermute | solution.py:273
  66.2 4.3 %collective-permute-start.4 = (bf16[64,512]{1,0:T(8,128)(2,1)S(1)}, bf16[64,512]{1,0:T(8,128)(2,1)S(1)}, u32[]{:S(2)}, u32[]{:S(2)}) collective-permute-start(bf16[64,512]{1,0:T(8,128)(2,1)S(1)} %fusion.49.refs_0_), channel_id=1, source_target_pairs={{0,6},{1,7},{2,0},{3,1},{4,2},{5,3},{6,4},{7,5},{8,14},{9,15},{10,... | collective-permute-start | bytes 196616 | tf_op jit(solution)/shard_map/ppermute | solution.py:273
  67.9 2.6 %copy-start.13 = (bf16[64,512]{1,0:T(8,128)(2,1)}, bf16[64,512]{1,0:T(8,128)(2,1)S(1)}, u32[]{:S(2)}) copy-start(bf16[64,512]{1,0:T(8,128)(2,1)S(1)} %collective-permute-done.2.refs_1_) | copy-start | bytes 196612
  69.3 1.2 copy-start.14
  70.4 0.6 copy-start.15
  72.9 30.9 %copy-start.4 = (bf16[512,256]{1,0:T(8,128)(2,1)S(1)}, bf16[512,256]{1,0:T(8,128)(2,1)}, u32[]{:S(2)}) copy-start(bf16[512,256]{1,0:T(8,128)(2,1)} %shard_map.74) | copy-start | bytes 786436
  72.9 7.7 %collective-permute-start.5 = (bf16[512,256]{1,0:T(8,128)(2,1)}, bf16[512,256]{1,0:T(8,128)(2,1)S(1)}, u32[]{:S(2)}, u32[]{:S(2)}) collective-permute-start(bf16[512,256]{1,0:T(8,128)(2,1)} %shard_map.74), channel_id=1, source_target_pairs={{0,32},{16,48},{32,64},{48,80},{64,96},{80,112},{96,0},{112,16},{1... | collective-permute-start | bytes 786440 | tf_op jit(solution)/shard_map/ppermute | solution.py:283
  73.3 7.9 %collective-permute-start.6 = (bf16[512,256]{1,0:T(8,128)(2,1)}, bf16[512,256]{1,0:T(8,128)(2,1)S(1)}, u32[]{:S(2)}, u32[]{:S(2)}) collective-permute-start(bf16[512,256]{1,0:T(8,128)(2,1)} %shard_map.74), channel_id=1, source_target_pairs={{0,96},{16,112},{32,0},{48,16},{64,32},{80,48},{96,64},{112,80},{1... | collective-permute-start | bytes 786440 | tf_op jit(solution)/shard_map/ppermute | solution.py:283
  74.9 7.0 %collective-permute-start.7 = (bf16[512,256]{1,0:T(8,128)(2,1)}, bf16[512,256]{1,0:T(8,128)(2,1)S(1)}, u32[]{:S(2)}, u32[]{:S(2)}) collective-permute-start(bf16[512,256]{1,0:T(8,128)(2,1)} %shard_map.74), channel_id=1, source_target_pairs={{0,128},{16,144},{32,160},{48,176},{64,192},{80,208},{96,224},{112... | collective-permute-start | bytes 786440 | tf_op jit(solution)/shard_map/ppermute | solution.py:286
  81.9 21.9 %copy-start.10 = (bf16[512,256]{1,0:T(8,128)(2,1)}, bf16[512,256]{1,0:T(8,128)(2,1)S(1)}, u32[]{:S(2)}) copy-start(bf16[512,256]{1,0:T(8,128)(2,1)S(1)} %collective-permute-done.7) | copy-start | bytes 786436
  81.9 15.0 %collective-permute-start.8 = (bf16[512,256]{1,0:T(8,128)(2,1)S(1)}, bf16[512,256]{1,0:T(8,128)(2,1)S(1)}, u32[]{:S(2)}, u32[]{:S(2)}) collective-permute-start(bf16[512,256]{1,0:T(8,128)(2,1)S(1)} %collective-permute-done.7), channel_id=1, source_target_pairs={{0,32},{16,48},{32,64},{48,80},{64,96},{80,112},{96,0},{112,16},{1... | collective-permute-start | bytes 786440 | tf_op jit(solution)/shard_map/ppermute | solution.py:283
  83.2 13.7 %collective-permute-start.9 = (bf16[512,256]{1,0:T(8,128)(2,1)S(1)}, bf16[512,256]{1,0:T(8,128)(2,1)S(1)}, u32[]{:S(2)}, u32[]{:S(2)}) collective-permute-start(bf16[512,256]{1,0:T(8,128)(2,1)S(1)} %collective-permute-done.7), channel_id=1, source_target_pairs={{0,96},{16,112},{32,0},{48,16},{64,32},{80,48},{96,64},{112,80},{1... | collective-permute-start | bytes 786440 | tf_op jit(solution)/shard_map/ppermute | solution.py:283
  84.9 12.6 %collective-permute-start.12 = (bf16[256,512]{1,0:T(8,128)(2,1)S(1)}, bf16[256,512]{1,0:T(8,128)(2,1)S(1)}, u32[]{:S(2)}, u32[]{:S(2)}) collective-permute-start(bf16[256,512]{1,0:T(8,128)(2,1)S(1)} %constant_dynamic-slice_fusion), channel_id=1, source_target_pairs={{0,1},{1,0},{2,3},{3,2},{4,5},{5,4},{6,7},{7,6},{8,9},{9,8},{10,11... | collective-permute-start | bytes 786440 | tf_op jit(solution)/shard_map/ppermute | solution.py:294
  86.2 5.4 %collective-permute-start.10 = (bf16[256,256]{1,0:T(8,128)(2,1)S(1)}, bf16[256,256]{1,0:T(8,128)(2,1)S(1)}, u32[]{:S(2)}, u32[]{:S(2)}) collective-permute-start(bf16[256,256]{1,0:T(8,128)(2,1)S(1)} %slice.38), channel_id=1, source_target_pairs={{0,32},{16,48},{32,64},{48,80},{64,96},{80,112},{96,0},{112,16},{1... | collective-permute-start | bytes 393224 | tf_op jit(solution)/shard_map/ppermute | solution.py:283
  89.1 7.8 %collective-permute-start.11 = (bf16[256,256]{1,0:T(8,128)(2,1)S(1)}, bf16[256,256]{1,0:T(8,128)(2,1)S(1)}, u32[]{:S(2)}, u32[]{:S(2)}) collective-permute-start(bf16[256,256]{1,0:T(8,128)(2,1)S(1)} %slice.39), channel_id=1, source_target_pairs={{0,96},{16,112},{32,0},{48,16},{64,32},{80,48},{96,64},{112,80},{1... | collective-permute-start | bytes 393224 | tf_op jit(solution)/shard_map/ppermute | solution.py:283
  96.9 0.6 copy-start.11
  96.9 9.7 %copy-start.5 = (bf16[512,256]{1,0:T(8,128)(2,1)}, bf16[512,256]{1,0:T(8,128)(2,1)S(1)}, u32[]{:S(2)}) copy-start(bf16[512,256]{1,0:T(8,128)(2,1)S(1)} %collective-permute-done.8) | copy-start | bytes 786436
  97.5 9.1 %copy-start.6 = (bf16[512,256]{1,0:T(8,128)(2,1)}, bf16[512,256]{1,0:T(8,128)(2,1)S(1)}, u32[]{:S(2)}) copy-start(bf16[512,256]{1,0:T(8,128)(2,1)S(1)} %collective-permute-done.9) | copy-start | bytes 786436
  97.5 0.7 copy-start.8
  99.2 5.7 %copy-start.12 = (bf16[256,256]{1,0:T(8,128)(2,1)S(1)}, bf16[256,256]{1,0:T(8,128)(2,1)}, u32[]{:S(2)}) copy-start(bf16[256,256]{1,0:T(8,128)(2,1)} %copy-done.11) | copy-start | bytes 393220
  100.4 6.3 %collective-permute-start.14 = (bf16[256,256]{1,0:T(8,128)(2,1)S(1)}, bf16[256,256]{1,0:T(8,128)(2,1)S(1)}, u32[]{:S(2)}, u32[]{:S(2)}) collective-permute-start(bf16[256,256]{1,0:T(8,128)(2,1)S(1)} %slice.41), channel_id=1, source_target_pairs={{0,96},{16,112},{32,0},{48,16},{64,32},{80,48},{96,64},{112,80},{1... | collective-permute-start | bytes 393224 | tf_op jit(solution)/shard_map/ppermute | solution.py:283
  100.5 6.1 %collective-permute-start.13 = (bf16[256,256]{1,0:T(8,128)(2,1)S(1)}, bf16[256,256]{1,0:T(8,128)(2,1)S(1)}, u32[]{:S(2)}, u32[]{:S(2)}) collective-permute-start(bf16[256,256]{1,0:T(8,128)(2,1)S(1)} %slice.40), channel_id=1, source_target_pairs={{0,32},{16,48},{32,64},{48,80},{64,96},{80,112},{96,0},{112,16},{1... | collective-permute-start | bytes 393224 | tf_op jit(solution)/shard_map/ppermute | solution.py:283
  104.8 3.2 %copy-start.17 = (s32[16,1]{0,1:T(1,128)S(1)}, s32[16,1]{0,1:T(1,128)}, u32[]{:S(2)}) copy-start(s32[16,1]{0,1:T(1,128)} %concatenate.87) | copy-start | bytes 196
  104.9 4.4 %collective-permute-start.15 = (bf16[4,512,256]{2,1,0:T(8,128)(2,1)S(1)}, bf16[4,512,256]{2,1,0:T(8,128)(2,1)}, u32[]{:S(2)}, u32[]{:S(2)}) collective-permute-start(bf16[4,512,256]{2,1,0:T(8,128)(2,1)S(1)} %pad_maximum_fusion.1.refs_0_), channel_id=1, source_target_pairs={{0,16},{16,0},{32,48},{48,32},{64,80},{80,64},{96,112},{112,96},{1... | collective-permute-start | bytes 3145736 | tf_op jit(solution)/shard_map/ppermute | solution.py:301
  107.8 2.9 %collective-permute-start.16 = (bf16[4,512,256]{2,1,0:T(8,128)(2,1)S(1)}, bf16[4,512,256]{2,1,0:T(8,128)(2,1)}, u32[]{:S(2)}, u32[]{:S(2)}) collective-permute-start(bf16[4,512,256]{2,1,0:T(8,128)(2,1)S(1)} %pad_maximum_fusion.2.refs_1_), channel_id=1, source_target_pairs={{0,16},{16,0},{32,48},{48,32},{64,80},{80,64},{96,112},{112,96},{1... | collective-permute-start | bytes 3145736 | tf_op jit(solution)/shard_map/ppermute | solution.py:301
  122.0 12.9 %collective-permute-start.17 = (bf16[512,256]{1,0:T(8,128)(2,1)S(1)}, bf16[512,256]{1,0:T(8,128)(2,1)}, u32[]{:S(2)}, u32[]{:S(2)}) collective-permute-start(bf16[512,256]{1,0:T(8,128)(2,1)S(1)} %shard_map.75), channel_id=1, source_target_pairs={{0,2},{1,3},{2,4},{3,5},{4,6},{5,7},{6,8},{7,9},{8,10},{9,11},{10,... | collective-permute-start | bytes 786440 | tf_op jit(solution)/shard_map/ppermute | solution.py:310
  122.1 12.8 %collective-permute-start.18 = (bf16[512,256]{1,0:T(8,128)(2,1)S(1)}, bf16[512,256]{1,0:T(8,128)(2,1)}, u32[]{:S(2)}, u32[]{:S(2)}) collective-permute-start(bf16[512,256]{1,0:T(8,128)(2,1)S(1)} %shard_map.75), channel_id=1, source_target_pairs={{0,14},{1,15},{2,0},{3,1},{4,2},{5,3},{6,4},{7,5},{8,6},{9,7},{10,... | collective-permute-start | bytes 786440 | tf_op jit(solution)/shard_map/ppermute | solution.py:313
  134.9 10.9 %collective-permute-start.19 = (bf16[512,256]{1,0:T(8,128)(2,1)}, bf16[512,256]{1,0:T(8,128)(2,1)}, u32[]{:S(2)}, u32[]{:S(2)}) collective-permute-start(bf16[512,256]{1,0:T(8,128)(2,1)} %collective-permute-done.17), channel_id=1, source_target_pairs={{0,2},{1,3},{2,4},{3,5},{4,6},{5,7},{6,8},{7,9},{8,10},{9,11},{10,... | collective-permute-start | bytes 786440 | tf_op jit(solution)/shard_map/ppermute | solution.py:310
  134.9 10.9 %collective-permute-start.20 = (bf16[512,256]{1,0:T(8,128)(2,1)}, bf16[512,256]{1,0:T(8,128)(2,1)}, u32[]{:S(2)}, u32[]{:S(2)}) collective-permute-start(bf16[512,256]{1,0:T(8,128)(2,1)} %collective-permute-done.18), channel_id=1, source_target_pairs={{0,14},{1,15},{2,0},{3,1},{4,2},{5,3},{6,4},{7,5},{8,6},{9,7},{10,... | collective-permute-start | bytes 786440 | tf_op jit(solution)/shard_map/ppermute | solution.py:313
  142.6 9.3 %copy-start.3 = (bf16[2048,512]{1,0:T(8,128)(2,1)S(1)}, bf16[2048,512]{1,0:T(8,128)(2,1)}, u32[]{:S(2)}) copy-start(bf16[2048,512]{1,0:T(8,128)(2,1)} %all-gather.7.cloned.1.call-done) | copy-start | bytes 6291460
  145.9 10.0 %collective-permute-start.21 = (bf16[512,256]{1,0:T(8,128)(2,1)}, bf16[512,256]{1,0:T(8,128)(2,1)S(1)}, u32[]{:S(2)}, u32[]{:S(2)}) collective-permute-start(bf16[512,256]{1,0:T(8,128)(2,1)} %collective-permute-done.19), channel_id=1, source_target_pairs={{0,2},{1,3},{2,4},{3,5},{4,6},{5,7},{6,8},{7,9},{8,10},{9,11},{10,... | collective-permute-start | bytes 786440 | tf_op jit(solution)/shard_map/ppermute | solution.py:310
  146.9 9.0 %collective-permute-start.22 = (bf16[512,256]{1,0:T(8,128)(2,1)}, bf16[512,256]{1,0:T(8,128)(2,1)S(1)}, u32[]{:S(2)}, u32[]{:S(2)}) collective-permute-start(bf16[512,256]{1,0:T(8,128)(2,1)} %collective-permute-done.20), channel_id=1, source_target_pairs={{0,14},{1,15},{2,0},{3,1},{4,2},{5,3},{6,4},{7,5},{8,6},{9,7},{10,... | collective-permute-start | bytes 786440 | tf_op jit(solution)/shard_map/ppermute | solution.py:313
  155.9 6.2 %collective-permute-start.24 = (bf16[512,128]{1,0:T(8,128)(2,1)S(1)}, bf16[512,128]{1,0:T(8,128)(2,1)S(1)}, u32[]{:S(2)}, u32[]{:S(2)}) collective-permute-start(bf16[512,128]{1,0:T(8,128)(2,1)S(1)} %slice.43), channel_id=1, source_target_pairs={{0,14},{1,15},{2,0},{3,1},{4,2},{5,3},{6,4},{7,5},{8,6},{9,7},{10,... | collective-permute-start | bytes 393224 | tf_op jit(solution)/shard_map/ppermute | solution.py:313
  158.9 6.3 %collective-permute-start.23 = (bf16[512,128]{1,0:T(8,128)(2,1)S(1)}, bf16[512,128]{1,0:T(8,128)(2,1)S(1)}, u32[]{:S(2)}, u32[]{:S(2)}) collective-permute-start(bf16[512,128]{1,0:T(8,128)(2,1)S(1)} %slice.42), channel_id=1, source_target_pairs={{0,2},{1,3},{2,4},{3,5},{4,6},{5,7},{6,8},{7,9},{8,10},{9,11},{10,... | collective-permute-start | bytes 393224 | tf_op jit(solution)/shard_map/ppermute | solution.py:310
  166.1 13.2 %collective-permute-start.25 = (bf16[512,512]{1,0:T(8,128)(2,1)S(1)}, bf16[512,512]{1,0:T(8,128)(2,1)S(1)}, u32[]{:S(2)}, u32[]{:S(2)}) collective-permute-start(bf16[512,512]{1,0:T(8,128)(2,1)S(1)} %fusion.17), channel_id=1, source_target_pairs={{0,1},{1,0},{2,3},{3,2},{4,5},{5,4},{6,7},{7,6},{8,9},{9,8},{10,11... | collective-permute-start | bytes 1572872 | tf_op jit(solution)/shard_map/ppermute | solution.py:339
Sparse Core Ops, SparseCore 0:
  19.2 28.0 all-gather.4
  61.0 45.9 reduce-scatter.1
  108.8 25.7 all-gather.6

commit v6 on v5

--- a/solution.py
+++ b/solution.py
@@ -133,16 +133,20 @@
                 o_ref[tile * ROW_TILE : (tile + 1) * ROW_TILE, :] = jnp.zeros((ROW_TILE, 2 * HD), jnp.bfloat16)
 
 
-def attention(counts, own, queries, ids, kv):
-    blocks_each, rows, _ = kv[0].shape
-    shards_n = blocks_each * len(kv)
+def packing(counts, own, ids):
+    shards_n = ids.shape[0]
     ids = jnp.concatenate([ids[1:], ids[:1]])
     used = ids <= own
     held = jnp.sum(jnp.where(ids[:, None] == jnp.arange(shards_n)[None, :], counts[None, :], 0), axis=1)
     packed = jnp.where(used, (held + 15) // 16 * 16, 0)
     before = jnp.arange(shards_n)[None, :] < jnp.arange(shards_n)[:, None]
     first = jnp.sum(jnp.where(before, packed[None, :], 0), axis=1)
-    info = jnp.stack([used.astype(jnp.int32), held, first], axis=1).astype(jnp.int32)
+    return jnp.stack([used.astype(jnp.int32), held, first], axis=1).astype(jnp.int32)
+
+
+def attention(info, queries, kv):
+    blocks_each, rows, _ = kv[0].shape
+    shards_n = blocks_each * len(kv)
     capacity = shards_n * (rows // 2 + 16) + rows + KEY_BLOCK
     return pl.pallas_call(
         attention_kernel,
@@ -164,6 +168,53 @@
     )(info, queries, *kv)
 
 
+def rows_kernel(rows_ref, hidden_ref, gain_ref, router_ref, kv_ref, x_ref, sent_ref):
+    tokens, width = hidden_ref.shape
+    rows = rows_ref.shape[1]
+    token = lax.broadcasted_iota(jnp.int32, (tokens, rows), 0)
+    select = jnp.where(token == rows_ref[...], 1.0, 0.0).astype(jnp.bfloat16)
+    kept = lax.dot_general(select, hidden_ref[...], (((0,), (0,)), ((), ())), preferred_element_type=jnp.float32)
+    normed = kept * gain_ref[...].astype(jnp.float32)
+    x_ref[...] = normed.astype(jnp.bfloat16)
+
+    def feature_sum(array):
+        tiles = [array[:, i * HD : (i + 1) * HD] for i in range(width // HD)]
+        return jnp.sum(functools.reduce(jnp.add, tiles).T, axis=0, keepdims=True)
+
+    stats = jnp.concatenate([feature_sum(kept * kept), feature_sum(kept * router_ref[...].astype(jnp.float32))])
+    high = stats.astype(jnp.bfloat16).astype(jnp.float32)
+    stats = jnp.concatenate([high, stats - high, jnp.zeros((4, rows), jnp.float32)])
+    turned = normed.T.astype(jnp.bfloat16)
+    depth = sent_ref.shape[1] - stats.shape[0]
+    halves = HD // depth
+    for which in range(2):
+        sums = lax.dot_general(
+            kv_ref[which], turned, (((0,), (0,)), ((), ())), preferred_element_type=jnp.float32
+        )
+        for group in range(KVH):
+            for half in range(halves):
+                start = group * HD + half * depth
+                place = ((group % 2 * 2 + which) * halves + half) * 2 + group // 2
+                sent_ref[place] = jnp.concatenate([sums[start : start + depth], stats]).astype(jnp.bfloat16)
+
+
+def rows_and_sums(own_rows, hidden, norm_gain, router_weight, key_value_weight):
+    rows, (_, width) = own_rows.shape[1], hidden.shape
+    return pl.pallas_call(
+        rows_kernel,
+        out_shape=(
+            jax.ShapeDtypeStruct((rows, width), jnp.bfloat16),
+            jax.ShapeDtypeStruct((2 * ZN, HD // 2 + 8, rows), jnp.bfloat16),
+        ),
+        in_specs=[pl.BlockSpec(memory_space=pltpu.VMEM)] * 5,
+        out_specs=(pl.BlockSpec(memory_space=pltpu.VMEM),) * 2,
+        compiler_params=pltpu.CompilerParams(vmem_limit_bytes=24 * 1024 * 1024),
+        cost_estimate=pl.CostEstimate(
+            flops=4 * rows * width * hidden.shape[0], bytes_accessed=5 * 1024 * 1024, transcendentals=0
+        ),
+    )(own_rows, hidden, norm_gain.reshape(1, width), router_weight.reshape(1, width), key_value_weight)
+
+
 def query_kernel(y_ref, x_own_ref, x_in_ref, w_own_ref, w_in_ref, o_ref):
     o_ref[0] = (dot(x_own_ref[...], w_own_ref[...]) + dot(x_in_ref[...], w_in_ref[0])).astype(jnp.bfloat16)
 
@@ -238,30 +289,23 @@
     wq_sent = lax.dynamic_slice(query_weight, (0, (1 - y) * half_cols + mine * chunk), (width, chunk))
     wq_got = lax.ppermute(wq_sent, "tp", y_swap())
 
-    own_rows = lax.dynamic_index_in_dim(kept_rows, shard, 0, keepdims=False)
-    select = (own_rows[:, None] == jnp.arange(tokens, dtype=jnp.int32)[None, :]).astype(bf16)
-    kept = dot(select, hidden)
-    square_part = jnp.sum(kept * kept, axis=1)
-    router_part = jnp.sum(kept * router_weight.astype(jnp.float32)[None, :], axis=1)
-    x_own = (kept * norm_gain.astype(jnp.float32)[None, :]).astype(bf16)
+    own_rows = lax.dynamic_slice_in_dim(kept_rows, shard, 1, 0)
+    x_own, sent = rows_and_sums(own_rows, hidden, norm_gain, router_weight, key_value_weight)
+    x_own, sent, wq_got = lax.optimization_barrier((x_own, sent, wq_got))
     x_in = lax.ppermute(x_own, "tp", y_swap())
 
-    kv_part = lax.dot_general(
-        key_value_weight, x_own, (((1,), (1,)), ((), ())), preferred_element_type=jnp.float32
-    ).astype(bf16)
-    kv_part = (
-        kv_part.reshape(2, 2, 2, 2, HD // 2, rows).transpose(2, 0, 3, 1, 4, 5).reshape(2 * ZN, HD // 2, rows)
-    )
-    stats = jnp.stack([square_part, router_part])
-    stats_high = lax.reduce_precision(stats, 8, 7)
-    stats_low = stats - stats_high
-    stats_rows = jnp.concatenate([stats_high, stats_low, jnp.zeros((4, rows), jnp.float32)]).astype(bf16)
-    sent = jnp.concatenate([kv_part, jnp.broadcast_to(stats_rows[None], (2 * ZN, 8, rows))], axis=1)
-    sent, wq_got = lax.optimization_barrier((sent, wq_got))
+    sent, x_in = lax.optimization_barrier((sent, x_in))
     wq_in = share(wq_got)
     exchanged = lax.all_to_all(sent, "tp", 0, 0, tiled=True)
     part = query_parts(y, x_own, x_in, query_weight, wq_in)
-    exchanged, part = lax.optimization_barrier((exchanged, part))
+    x_n = shard_n // 4
+    at_y, at_x, core = shard // (2 * x_n), shard // 2 % x_n, shard % 2
+    offsets = [(0, 0), (-1, 0), (1, 0), (0, 1), (-1, 1), (1, 1), (2, 0), (2, 1)]
+    ids = [(at_y + dy) % 2 * (2 * x_n) + (at_x + dx) % x_n * 2 for dx, dy in offsets]
+    ids = jnp.stack([i + core for i in ids] + [i + 1 - core for i in ids])
+    counts = jnp.sum((kept_rows < tokens).astype(jnp.int32), axis=1)
+    info = packing(counts, shard, ids)
+    exchanged, part, info = lax.optimization_barrier((exchanged, part, info))
     query_sum = lax.psum_scatter(
         part, "tp", scatter_dimension=0, axis_index_groups=[[2 * k + h for k in range(ZN)] for h in range(2)]
     )
@@ -274,7 +318,6 @@
     pieces = [piece] + pieces
     kv_own = ordered_rows(z % 4, pieces)
 
-    x_n = shard_n // 4
 
     def along(step):
         return [(c, c // (2 * x_n) * (2 * x_n) + (c + 2 * step) % (2 * x_n)) for c in range(shard_n)]
@@ -301,11 +344,6 @@
         return lax.ppermute(block, "ctx", [(c, c ^ 1) for c in range(shard_n)])
 
     kv_all = [first_half, second_half, core_hop(first_half), core_hop(second_half)]
-    at_y, at_x, core = shard // (2 * x_n), shard // 2 % x_n, shard % 2
-    offsets = [(0, 0), (-1, 0), (1, 0), (0, 1), (-1, 1), (1, 1), (2, 0), (2, 1)]
-    ids = [(at_y + dy) % 2 * (2 * x_n) + (at_x + dx) % x_n * 2 for dx, dy in offsets]
-    ids = jnp.stack([i + core for i in ids] + [i + 1 - core for i in ids])
-
     def right(a):
         return lax.ppermute(a.astype(bf16), "tp", z_shift(1))
 
@@ -318,8 +356,7 @@
     cut = chunk // 2
     queries = (query_sum.astype(jnp.float32) * (inverse_rms * EXP_SCALE)[:, None]).astype(bf16)
 
-    counts = jnp.sum((kept_rows < tokens).astype(jnp.int32), axis=1)
-    mixed = attention(counts, shard, queries, ids, kv_all)
+    mixed = attention(info, queries, kv_all)
 
     def project(piece, offset, low, high):
         start = ((z + offset) % ZN) * chunk + low
@@ -333,13 +370,19 @@
         from_left, from_right = both(from_left, from_right)
         terms.append(project(from_left, -step, 0, chunk))
         terms.append(project(from_right, step, 0, chunk))
-    terms.append(project(right(from_left[:, :cut]), 4, 0, cut))
-    terms.append(project(left(from_right[:, cut:]), 4, cut, chunk))
-    for_partner = functools.reduce(jnp.add, [t[1] for t in terms])
-    received = lax.ppermute(for_partner.astype(bf16), "tp", y_swap())
-    own_sum, received = lax.optimization_barrier((functools.reduce(jnp.add, [t[0] for t in terms]), received))
-    projected = own_sum + received
+    for_partner = functools.reduce(jnp.add, [t[1] for t in terms]).astype(bf16)
+    far = right(from_left[:, :cut]), left(from_right[:, cut:])
+    received = lax.ppermute(for_partner, "tp", y_swap())
+    far = jnp.concatenate(far, axis=1)
+    far_in = lax.ppermute(far, "tp", y_swap())
+    far_start = (z + 4) % ZN * chunk
+    far_weights = lax.dynamic_slice(out_weight, (y * wo_rows + far_start, 0), (chunk, width))
+    far_in_weights = lax.dynamic_slice(out_weight, ((1 - y) * wo_rows + far_start, 0), (chunk, width))
+    own_sum = functools.reduce(jnp.add, [t[0] for t in terms]) + dot(far, far_weights)
+    own_sum, received, far_in, far_in_weights = lax.optimization_barrier((own_sum, received, far_in, far_in_weights))
+    projected = own_sum + received + dot(far_in, far_in_weights)
     row_update = (jax.nn.sigmoid(router_logit)[:, None] * projected).astype(bf16)
+    select = (own_rows.reshape(rows, 1) == jnp.arange(tokens, dtype=jnp.int32)[None, :]).astype(bf16)
     return lax.dot_general(select, row_update, (((0,), (0,)), ((), ())), preferred_element_type=jnp.float32).astype(
         bf16
     )

time: 188 us -> 198 us (1.053)
  waiting for transfers between devices: 62 us -> 77.4 us
  matrix products: 24.6 us -> 17.7 us
  other arithmetic: 6.83 us -> 3.06 us
  local copies, waits for them, and re-layouts: 11.9 us -> 14.4 us
  Pallas kernels: 18.4 us -> 20.8 us
    all_to_all x1, waiting for transfers between devices: 4.45 us -> 16 us  [shards(): exchanged = lax.all_to_all(sent, 'tp', 0, 0, tiled=True)]
    dot_general x19 -> x15, matrix products: 21.9 us -> 14.5 us  [dot(): return jnp.dot(a, b, preferred_element_type=jnp.float32)]
    ppermute x4, starting transfers between devices: 16 us -> 11.5 us  [left(): return lax.ppermute(a.astype(bf16), 'tp', z_shift(-1))]
    ppermute x1 -> x2, waiting for transfers between devices: 9.05 us -> 13.2 us  [the longest x1 13.2 us: shards(): far_in = lax.ppermute(far, 'tp', y_swap())]
    ppermute x1 -> x2, starting transfers between devices: 0.1 us -> 3.7 us  [the longest x1 3.1 us: shards(): received = lax.ppermute(for_partner, 'tp', y_swap())]
    unnamed x36 -> x35, local copies, waits for them, and re-layouts: 6.5 us -> 9.23 us
    all_gather x2, waiting for transfers between devices: 1.51 us -> 4.16 us  [share(): lax.all_gather(got, 'ctx', axis=0, tiled=False, axis_index_groups=groups)]
    pallas_call x0 -> x1, Pallas kernels: none -> 2.6 us  [rows_and_sums(): pl.pallas_call(rows_kernel, out_shape=(jax.ShapeDtypeStruct((rows, width)...]
  transfers between devices with their start and end apart: 30 -> 31, of which waited for: 18 -> 19; matrix products, arithmetic and copies ran while one was open for 18% -> 11% of each run, Pallas kernels for 10% -> 11%
where the time goes in v6:
time: 198 us; the launch traced here: 196 us
  waiting for transfers between devices  77.4 us (39%)
  starting transfers between devices  49.3 us (25%)
  Pallas kernels  20.8 us (11%)
  matrix products  17.7 us (9%)
  local copies, waits for them, and re-layouts  14.4 us (7%)
  between operations  13.6 us (7%)
  other arithmetic  3.06 us (2%)
    all_to_all x1, waiting for transfers between devices, shards(): exchanged = lax.all_to_all(sent, 'tp', 0, 0, tiled=True)  16 us
    ppermute x8, waiting for transfers between devices, x_hop(): return lax.ppermute(block, 'ctx', along(step))  14.8 us
    dot_general x15, matrix products, dot(): return jnp.dot(a, b, preferred_element_type=jnp.float32)  14.5 us
    ppermute x1, waiting for transfers between devices, shards(): far_in = lax.ppermute(far, 'tp', y_swap())  13.2 us
    ppermute x1, waiting for transfers between devices, shards(): x_in = lax.ppermute(x_own, 'tp', y_swap())  12.5 us
    ppermute x4, starting transfers between devices, left(): return lax.ppermute(a.astype(bf16), 'tp', z_shift(-1))  11.5 us
    pallas_call x1, Pallas kernels, attention(): pl.pallas_call(attention_kernel, out_shape=jax.ShapeDtypeStruct(queries.s...  11.1 us
    ppermute x4, waiting for transfers between devices, right(): return lax.ppermute(a.astype(bf16), 'tp', z_shift(1))  10.9 us
  transfers between devices with their start and end apart: 31, of which 19 were waited for; matrix products, arithmetic and copies ran while one was open for 11% of the time, Pallas kernels for 11%

profile of v6, /device:TPU:14, one launch (start us, length us, event | category | flops | bytes accessed | tf_op | source)
XLA Modules:
  0.0 196.3 jit_solution(4572576804988986228)
XLA Ops:
  7.5 2.4 %collective-permute-start = (bf16[512,256]{1,0:T(8,128)(2,1)S(1)}, bf16[512,256]{1,0:T(8,128)(2,1)S(1)}, u32[]{:S(2)}, u32[]{:S(2)}) collective-permute-start(bf16[512,256]{1,0:T(8,128)(2,1)S(1)} %constant_dynamic-slice_fusion.2), channel_id=1, source_target_pairs={{0,1},{1,0},{2,3},{3,2},{4,5},{5,4},{6,7},{7,6},{8,9},{9,8},{10,11... | collective-permute-start | bytes 786440 | tf_op jit(solution)/shard_map/ppermute | solution.py:290
  14.4 2.6 %shard_map.73 = (bf16[512,512]{1,0:T(8,128)(2,1)S(1)}, bf16[16,72,512]{2,1,0:T(8,128)(2,1)}) custom-call(s32[1,512]{1,0:T(1,128)S(1)} %constant_dynamic-slice_fusion.3.rows_ref, bf16[1024,512]{1,0:T(8,128)(2,1)S(1)} %copy-done.2, bf16[1,512]{1,0:T(2,128)(2,1)S(1)} %reshape.431.gain_ref, bf16[1,512]{1,0:T(2,128)(2,1)S(1)} %reshape.432.router_ref, ...), custom_call_target="tpu_custom_call" | custom-call | flops 1073741824 | bytes 5242880 | tf_op jit(solution)/shard_map/pallas_call | solution.py:203
  17.9 2.4 %collective-permute-start.1 = (bf16[512,512]{1,0:T(8,128)(2,1)S(1)}, bf16[512,512]{1,0:T(8,128)(2,1)S(1)}, u32[]{:S(2)}, u32[]{:S(2)}) collective-permute-start(bf16[512,512]{1,0:T(8,128)(2,1)S(1)} %get-tuple-element.37.x_own_ref), channel_id=1, source_target_pairs={{0,1},{1,0},{2,3},{3,2},{4,5},{5,4},{6,7},{7,6},{8,9},{9,8},{10,11... | collective-permute-start | bytes 1572872 | tf_op jit(solution)/shard_map/ppermute | solution.py:295
  20.3 12.5 %collective-permute-done.1.x_in_ref = bf16[512,512]{1,0:T(8,128)(2,1)S(1)} collective-permute-done((bf16[512,512]{1,0:T(8,128)(2,1)S(1)}, bf16[512,512]{1,0:T(8,128)(2,1)S(1)}, u32[]{:S(2)}, u32[]{:S(2)}) %collective-permute-start.1) | collective-permute-done | bytes 524320 | tf_op jit(solution)/shard_map/ppermute | solution.py:295
  32.7 9.8 %all-to-all-start = ((bf16[16,72,512]{2,1,0:T(8,128)(2,1)}), bf16[16,72,512]{2,1,0:T(8,128)(2,1)S(1)}, u32[]{:S(2)}, u32[]{:S(2)}) async-start(bf16[16,72,512]{2,1,0:T(8,128)(2,1)} %get-tuple-element.38), calls=%async_computation | async-start | bytes 2359296 | tf_op jit(solution)/shard_map/all_to_all | solution.py:299
  43.5 4.1 %all-gather.5.cloned.1.call-done = bf16[4096,256]{1,0:T(8,128)(2,1)} async-done(((bf16[512,256]{1,0:T(8,128)(2,1)}), bf16[4096,256]{1,0:T(8,128)(2,1)}) %all-gather.5.cloned.1.call-update) | async-done | bytes 2097168 | tf_op jit(solution)/shard_map/all_gather | solution.py:287
  47.6 2.2 %copy-done = bf16[512,4096]{1,0:T(8,128)(2,1)S(1)} copy-done((bf16[512,4096]{1,0:T(8,128)(2,1)S(1)}, bf16[512,4096]{1,0:T(8,128)(2,1)}, u32[]{:S(2)}) %copy-start) | copy-done | bytes 4194328
  49.8 1.6 copy-done.1
  51.4 5.3 %shard_map.74 = bf16[8,512,256]{2,1,0:T(8,128)(2,1)} custom-call(s32[1]{0:T(128)} %bitcast.1.y_ref, bf16[512,512]{1,0:T(8,128)(2,1)S(1)} %get-tuple-element.37.x_own_ref, bf16[512,512]{1,0:T(8,128)(2,1)S(1)} %collective-permute-done.1.x_in_ref, bf16[512,4096]{1,0:T(8,128)(2,1)S(1)} %copy-done, bf16[8,512,256]{2,1,0:T(8,128)(2,1)S(1)} %bitcast.70), custom_call_target="tpu_custom_call" | custom-call | flops 2147483648 | bytes 6291456 | tf_op jit(solution)/shard_map/pallas_call | solution.py:225
  56.6 16.0 %all-to-all-done = bf16[16,72,512]{2,1,0:T(8,128)(2,1)S(1)} async-done(((bf16[16,72,512]{2,1,0:T(8,128)(2,1)}), bf16[16,72,512]{2,1,0:T(8,128)(2,1)S(1)}, u32[]{:S(2)}, u32[]{:S(2)}) %all-to-all-start) | async-done | bytes 1179680 | tf_op jit(solution)/shard_map/all_to_all | solution.py:299
  73.0 3.1 %collective-permute-start.3 = (bf16[64,512]{1,0:T(8,128)(2,1)S(1)}, bf16[64,512]{1,0:T(8,128)(2,1)S(1)}, u32[]{:S(2)}, u32[]{:S(2)}) collective-permute-start(bf16[64,512]{1,0:T(8,128)(2,1)S(1)} %fusion.47.refs_0_), channel_id=1, source_target_pairs={{0,4},{1,5},{2,6},{3,7},{4,0},{5,1},{6,2},{7,3},{8,12},{9,13},{10,... | collective-permute-start | bytes 196616 | tf_op jit(solution)/shard_map/ppermute | solution.py:317
  76.1 1.5 collective-permute-start.4
  77.7 1.6 collective-permute-done.2.refs_1_
  79.3 1.4 collective-permute-done.3.refs_2_
  81.9 1.8 shard_map.75
  84.2 1.5 collective-permute-start.6
  85.7 1.3 collective-permute-start.7
  87.1 4.6 %collective-permute-done.5 = bf16[512,256]{1,0:T(8,128)(2,1)S(1)} collective-permute-done((bf16[512,256]{1,0:T(8,128)(2,1)}, bf16[512,256]{1,0:T(8,128)(2,1)S(1)}, u32[]{:S(2)}, u32[]{:S(2)}) %collective-permute-start.5) | collective-permute-done | bytes 262176 | tf_op jit(solution)/shard_map/ppermute | solution.py:326
  91.7 1.4 collective-permute-done.6
  93.1 1.7 collective-permute-start.8
  95.2 1.8 constant_dynamic-slice_fusion
  97.7 3.0 %collective-permute-start.10 = (bf16[256,256]{1,0:T(8,128)(2,1)S(1)}, bf16[256,256]{1,0:T(8,128)(2,1)S(1)}, u32[]{:S(2)}, u32[]{:S(2)}) collective-permute-start(bf16[256,256]{1,0:T(8,128)(2,1)S(1)} %slice.38), channel_id=1, source_target_pairs={{0,32},{16,48},{32,64},{48,80},{64,96},{80,112},{96,0},{112,16},{1... | collective-permute-start | bytes 393224 | tf_op jit(solution)/shard_map/ppermute | solution.py:326
  101.0 2.2 %collective-permute-done.10 = bf16[256,256]{1,0:T(8,128)(2,1)S(1)} collective-permute-done((bf16[256,256]{1,0:T(8,128)(2,1)S(1)}, bf16[256,256]{1,0:T(8,128)(2,1)S(1)}, u32[]{:S(2)}, u32[]{:S(2)}) %collective-permute-start.10) | collective-permute-done | bytes 131104 | tf_op jit(solution)/shard_map/ppermute | solution.py:326
  103.2 3.9 %collective-permute-done.11 = bf16[256,256]{1,0:T(8,128)(2,1)S(1)} collective-permute-done((bf16[256,256]{1,0:T(8,128)(2,1)S(1)}, bf16[256,256]{1,0:T(8,128)(2,1)S(1)}, u32[]{:S(2)}, u32[]{:S(2)}) %collective-permute-start.11) | collective-permute-done | bytes 131104 | tf_op jit(solution)/shard_map/ppermute | solution.py:326
  108.1 3.3 %collective-permute-start.13 = (bf16[256,256]{1,0:T(8,128)(2,1)S(1)}, bf16[256,256]{1,0:T(8,128)(2,1)S(1)}, u32[]{:S(2)}, u32[]{:S(2)}) collective-permute-start(bf16[256,256]{1,0:T(8,128)(2,1)S(1)} %slice.40), channel_id=1, source_target_pairs={{0,32},{16,48},{32,64},{48,80},{64,96},{80,112},{96,0},{112,16},{1... | collective-permute-start | bytes 393224 | tf_op jit(solution)/shard_map/ppermute | solution.py:326
  111.6 2.6 %collective-permute-done.14 = bf16[256,256]{1,0:T(8,128)(2,1)S(1)} collective-permute-done((bf16[256,256]{1,0:T(8,128)(2,1)S(1)}, bf16[256,256]{1,0:T(8,128)(2,1)S(1)}, u32[]{:S(2)}, u32[]{:S(2)}) %collective-permute-start.14) | collective-permute-done | bytes 131104 | tf_op jit(solution)/shard_map/ppermute | solution.py:326
  116.7 1.6 collective-permute-done.16.refs_3_
  118.3 11.1 %shard_map.76 = bf16[512,256]{1,0:T(8,128)(2,1)S(1)} custom-call(s32[16,3]{1,0:T(8,128)S(1)} %copy.11.info_ref, bf16[512,256]{1,0:T(8,128)(2,1)S(1)} %fusion.17.q_ref, bf16[4,512,256]{2,1,0:T(8,128)(2,1)S(1)} %pad_maximum_fusion.refs_0_, bf16[4,512,256]{2,1,0:T(8,128)(2,1)S(1)} %pad_maximum_fusion.1.refs_1_, ...), custom_call_target="tpu_custom_call" | custom-call | flops 4294967296 | bytes 4194304 | tf_op jit(solution)/shard_map/pallas_call | solution.py:151
  129.4 1.6 collective-permute-start.17
  131.0 1.7 collective-permute-start.18
  132.7 5.7 %collective-permute-done.17 = bf16[512,256]{1,0:T(8,128)(2,1)S(1)} collective-permute-done((bf16[512,256]{1,0:T(8,128)(2,1)S(1)}, bf16[512,256]{1,0:T(8,128)(2,1)S(1)}, u32[]{:S(2)}, u32[]{:S(2)}) %collective-permute-start.17) | collective-permute-done | bytes 262176 | tf_op jit(solution)/shard_map/ppermute | solution.py:348
  139.0 3.2 %collective-permute-start.20 = (bf16[512,256]{1,0:T(8,128)(2,1)S(1)}, bf16[512,256]{1,0:T(8,128)(2,1)S(1)}, u32[]{:S(2)}, u32[]{:S(2)}) collective-permute-start(bf16[512,256]{1,0:T(8,128)(2,1)S(1)} %collective-permute-done.18), channel_id=1, source_target_pairs={{0,14},{1,15},{2,0},{3,1},{4,2},{5,3},{6,4},{7,5},{8,6},{9,7},{10,... | collective-permute-start | bytes 786440 | tf_op jit(solution)/shard_map/ppermute | solution.py:351
  143.5 1.2 fusion.44
  144.8 1.2 fusion.28
  146.0 1.4 fusion.30
  147.4 2.0 %collective-permute-done.19 = bf16[512,256]{1,0:T(8,128)(2,1)S(1)} collective-permute-done((bf16[512,256]{1,0:T(8,128)(2,1)S(1)}, bf16[512,256]{1,0:T(8,128)(2,1)S(1)}, u32[]{:S(2)}, u32[]{:S(2)}) %collective-permute-start.19) | collective-permute-done | bytes 262176 | tf_op jit(solution)/shard_map/ppermute | solution.py:348
  149.4 3.2 %collective-permute-start.22 = (bf16[512,256]{1,0:T(8,128)(2,1)S(1)}, bf16[512,256]{1,0:T(8,128)(2,1)S(1)}, u32[]{:S(2)}, u32[]{:S(2)}) collective-permute-start(bf16[512,256]{1,0:T(8,128)(2,1)S(1)} %collective-permute-done.20), channel_id=1, source_target_pairs={{0,14},{1,15},{2,0},{3,1},{4,2},{5,3},{6,4},{7,5},{8,6},{9,7},{10,... | collective-permute-start | bytes 786440 | tf_op jit(solution)/shard_map/ppermute | solution.py:351
  152.6 1.2 fusion.38
  153.9 1.3 fusion.40
  155.7 3.2 %collective-permute-done.21 = bf16[512,256]{1,0:T(8,128)(2,1)S(1)} collective-permute-done((bf16[512,256]{1,0:T(8,128)(2,1)S(1)}, bf16[512,256]{1,0:T(8,128)(2,1)S(1)}, u32[]{:S(2)}, u32[]{:S(2)}) %collective-permute-start.21) | collective-permute-done | bytes 262176 | tf_op jit(solution)/shard_map/ppermute | solution.py:348
  159.1 3.3 %collective-permute-start.24 = (bf16[512,128]{1,0:T(8,128)(2,1)S(1)}, bf16[512,128]{1,0:T(8,128)(2,1)S(1)}, u32[]{:S(2)}, u32[]{:S(2)}) collective-permute-start(bf16[512,128]{1,0:T(8,128)(2,1)S(1)} %slice.43), channel_id=1, source_target_pairs={{0,14},{1,15},{2,0},{3,1},{4,2},{5,3},{6,4},{7,5},{8,6},{9,7},{10,... | collective-permute-start | bytes 393224 | tf_op jit(solution)/shard_map/ppermute | solution.py:351
  162.4 1.2 fusion.34
  164.7 1.2 fusion.36
  165.9 3.1 %collective-permute-start.25 = (bf16[512,512]{1,0:T(8,128)(2,1)S(1)}, bf16[512,512]{1,0:T(8,128)(2,1)S(1)}, u32[]{:S(2)}, u32[]{:S(2)}) collective-permute-start(bf16[512,512]{1,0:T(8,128)(2,1)S(1)} %fusion.13), channel_id=1, source_target_pairs={{0,1},{1,0},{2,3},{3,2},{4,5},{5,4},{6,7},{7,6},{8,9},{9,8},{10,11... | collective-permute-start | bytes 1572872 | tf_op jit(solution)/shard_map/ppermute | solution.py:375
  169.7 1.2 fusion.32
  170.9 1.5 fusion.8
  172.5 13.2 %collective-permute-done.26 = bf16[512,256]{1,0:T(8,128)(2,1)S(1)} collective-permute-done((bf16[512,256]{1,0:T(8,128)(2,1)S(1)}, bf16[512,256]{1,0:T(8,128)(2,1)S(1)}, u32[]{:S(2)}, u32[]{:S(2)}) %collective-permute-start.26) | collective-permute-done | bytes 262176 | tf_op jit(solution)/shard_map/ppermute | solution.py:377
  186.6 3.1 %fusion.1 = bf16[1024,512]{1,0:T(8,128)(2,1)} fusion(s32[512]{0:T(512)S(1)} %bitcast.71, f32[512,512]{1,0:T(8,128)S(1)} %fusion.8, bf16[512,512]{1,0:T(8,128)(2,1)} %copy-done.15, bf16[512,256]{1,0:T(8,128)(2,1)} %copy-done.16, bf16[256,512]{1,0:T(8,128)(2,1)} %get-tuple-element.62, f32[512]{0:T(512)S(1)} %bitcast.81), kind=kOutput, calls=%fused_computation.3 | convolution fusion | flops 673447936 | bytes 3149824 | tf_op jit(solution)/shard_map/dot_general | solution.py:386
  (102 shorter events, 19.3 us)
Async XLA Ops:
  6.5 41.1 %all-gather.5.cloned.1.call-start = ((), (), s32[]{:S(2)}) async-start(), calls=%async_computation.3 | async-start | bytes 2359296 | tf_op jit(solution)/shard_map/all_gather | solution.py:287
  7.5 9.6 %collective-permute-start = (bf16[512,256]{1,0:T(8,128)(2,1)S(1)}, bf16[512,256]{1,0:T(8,128)(2,1)S(1)}, u32[]{:S(2)}, u32[]{:S(2)}) collective-permute-start(bf16[512,256]{1,0:T(8,128)(2,1)S(1)} %constant_dynamic-slice_fusion.2), channel_id=1, source_target_pairs={{0,1},{1,0},{2,3},{3,2},{4,5},{5,4},{6,7},{7,6},{8,9},{9,8},{10,11... | collective-permute-start | bytes 786440 | tf_op jit(solution)/shard_map/ppermute | solution.py:290
  12.0 1.2 copy-start.2
  13.2 1.2 copy-start.3
  17.0 26.0 %copy-start.14 = (s32[16,512]{1,0:T(8,128)S(1)}, s32[16,512]{1,0:T(8,128)}, u32[]{:S(2)}) copy-start(s32[16,512]{1,0:T(8,128)} %param.13) | copy-start | bytes 98308
  17.1 0.7 copy-start.10
  17.9 14.9 %collective-permute-start.1 = (bf16[512,512]{1,0:T(8,128)(2,1)S(1)}, bf16[512,512]{1,0:T(8,128)(2,1)S(1)}, u32[]{:S(2)}, u32[]{:S(2)}) collective-permute-start(bf16[512,512]{1,0:T(8,128)(2,1)S(1)} %get-tuple-element.37.x_own_ref), channel_id=1, source_target_pairs={{0,1},{1,0},{2,3},{3,2},{4,5},{5,4},{6,7},{7,6},{8,9},{9,8},{10,11... | collective-permute-start | bytes 1572872 | tf_op jit(solution)/shard_map/ppermute | solution.py:295
  32.7 39.9 %all-to-all-start = ((bf16[16,72,512]{2,1,0:T(8,128)(2,1)}), bf16[16,72,512]{2,1,0:T(8,128)(2,1)S(1)}, u32[]{:S(2)}, u32[]{:S(2)}) async-start(bf16[16,72,512]{2,1,0:T(8,128)(2,1)} %get-tuple-element.38), calls=%async_computation | async-start | bytes 2359296 | tf_op jit(solution)/shard_map/all_to_all | solution.py:299
  42.6 73.0 %reduce-scatter.2.cloned.1.call-start = ((), (), s32[]{:S(2)}) async-start(), calls=%async_computation.2 | async-start | bytes 2359296 | tf_op jit(solution)/shard_map/reduce_scatter | solution.py:309
  47.6 2.2 %copy-start = (bf16[512,4096]{1,0:T(8,128)(2,1)S(1)}, bf16[512,4096]{1,0:T(8,128)(2,1)}, u32[]{:S(2)}) copy-start(bf16[512,4096]{1,0:T(8,128)(2,1)} %w_own_ref.1) | copy-start | bytes 12582916
  49.8 1.6 copy-start.1
  72.6 72.1 %all-gather.7.cloned.1.call-start = ((), (), s32[]{:S(2)}) async-start(), calls=%async_computation.4 | async-start | bytes 2359296 | tf_op jit(solution)/shard_map/all_gather | solution.py:287
  72.9 8.4 %copy-start.8 = (bf16[64,512]{1,0:T(8,128)(2,1)}, bf16[64,512]{1,0:T(8,128)(2,1)S(1)}, u32[]{:S(2)}) copy-start(bf16[64,512]{1,0:T(8,128)(2,1)S(1)} %fusion.47.refs_0_) | copy-start | bytes 196612
  72.9 6.4 %collective-permute-start.2 = (bf16[64,512]{1,0:T(8,128)(2,1)S(1)}, bf16[64,512]{1,0:T(8,128)(2,1)S(1)}, u32[]{:S(2)}, u32[]{:S(2)}) collective-permute-start(bf16[64,512]{1,0:T(8,128)(2,1)S(1)} %fusion.47.refs_0_), channel_id=1, source_target_pairs={{0,2},{1,3},{2,4},{3,5},{4,6},{5,7},{6,0},{7,1},{8,10},{9,11},{10,... | collective-permute-start | bytes 196616 | tf_op jit(solution)/shard_map/ppermute | solution.py:317
  73.0 7.7 %collective-permute-start.3 = (bf16[64,512]{1,0:T(8,128)(2,1)S(1)}, bf16[64,512]{1,0:T(8,128)(2,1)S(1)}, u32[]{:S(2)}, u32[]{:S(2)}) collective-permute-start(bf16[64,512]{1,0:T(8,128)(2,1)S(1)} %fusion.47.refs_0_), channel_id=1, source_target_pairs={{0,4},{1,5},{2,6},{3,7},{4,0},{5,1},{6,2},{7,3},{8,12},{9,13},{10,... | collective-permute-start | bytes 196616 | tf_op jit(solution)/shard_map/ppermute | solution.py:317
  76.1 5.1 %collective-permute-start.4 = (bf16[64,512]{1,0:T(8,128)(2,1)S(1)}, bf16[64,512]{1,0:T(8,128)(2,1)S(1)}, u32[]{:S(2)}, u32[]{:S(2)}) collective-permute-start(bf16[64,512]{1,0:T(8,128)(2,1)S(1)} %fusion.47.refs_0_), channel_id=1, source_target_pairs={{0,6},{1,7},{2,0},{3,1},{4,2},{5,3},{6,4},{7,5},{8,14},{9,15},{10,... | collective-permute-start | bytes 196616 | tf_op jit(solution)/shard_map/ppermute | solution.py:317
  79.3 2.0 copy-start.11
  80.6 0.6 copy-start.12
  81.2 0.6 copy-start.13
  83.7 27.7 %copy-start.5 = (bf16[512,256]{1,0:T(8,128)(2,1)S(1)}, bf16[512,256]{1,0:T(8,128)(2,1)}, u32[]{:S(2)}) copy-start(bf16[512,256]{1,0:T(8,128)(2,1)} %shard_map.75) | copy-start | bytes 786436
  83.7 8.0 %collective-permute-start.5 = (bf16[512,256]{1,0:T(8,128)(2,1)}, bf16[512,256]{1,0:T(8,128)(2,1)S(1)}, u32[]{:S(2)}, u32[]{:S(2)}) collective-permute-start(bf16[512,256]{1,0:T(8,128)(2,1)} %shard_map.75), channel_id=1, source_target_pairs={{0,32},{16,48},{32,64},{48,80},{64,96},{80,112},{96,0},{112,16},{1... | collective-permute-start | bytes 786440 | tf_op jit(solution)/shard_map/ppermute | solution.py:326
  84.2 8.9 %collective-permute-start.6 = (bf16[512,256]{1,0:T(8,128)(2,1)}, bf16[512,256]{1,0:T(8,128)(2,1)S(1)}, u32[]{:S(2)}, u32[]{:S(2)}) collective-permute-start(bf16[512,256]{1,0:T(8,128)(2,1)} %shard_map.75), channel_id=1, source_target_pairs={{0,96},{16,112},{32,0},{48,16},{64,32},{80,48},{96,64},{112,80},{1... | collective-permute-start | bytes 786440 | tf_op jit(solution)/shard_map/ppermute | solution.py:326
  85.7 7.4 %collective-permute-start.7 = (bf16[512,256]{1,0:T(8,128)(2,1)}, bf16[512,256]{1,0:T(8,128)(2,1)S(1)}, u32[]{:S(2)}, u32[]{:S(2)}) collective-permute-start(bf16[512,256]{1,0:T(8,128)(2,1)} %shard_map.75), channel_id=1, source_target_pairs={{0,128},{16,144},{32,160},{48,176},{64,192},{80,208},{96,224},{112... | collective-permute-start | bytes 786440 | tf_op jit(solution)/shard_map/ppermute | solution.py:329
  93.1 14.0 %collective-permute-start.8 = (bf16[512,256]{1,0:T(8,128)(2,1)S(1)}, bf16[512,256]{1,0:T(8,128)(2,1)S(1)}, u32[]{:S(2)}, u32[]{:S(2)}) collective-permute-start(bf16[512,256]{1,0:T(8,128)(2,1)S(1)} %collective-permute-done.7), channel_id=1, source_target_pairs={{0,32},{16,48},{32,64},{48,80},{64,96},{80,112},{96,0},{112,16},{1... | collective-permute-start | bytes 786440 | tf_op jit(solution)/shard_map/ppermute | solution.py:326
  94.8 12.3 %collective-permute-start.9 = (bf16[512,256]{1,0:T(8,128)(2,1)S(1)}, bf16[512,256]{1,0:T(8,128)(2,1)S(1)}, u32[]{:S(2)}, u32[]{:S(2)}) collective-permute-start(bf16[512,256]{1,0:T(8,128)(2,1)S(1)} %collective-permute-done.7), channel_id=1, source_target_pairs={{0,96},{16,112},{32,0},{48,16},{64,32},{80,48},{96,64},{112,80},{1... | collective-permute-start | bytes 786440 | tf_op jit(solution)/shard_map/ppermute | solution.py:326
  96.9 10.2 %collective-permute-start.12 = (bf16[256,512]{1,0:T(8,128)(2,1)S(1)}, bf16[256,512]{1,0:T(8,128)(2,1)S(1)}, u32[]{:S(2)}, u32[]{:S(2)}) collective-permute-start(bf16[256,512]{1,0:T(8,128)(2,1)S(1)} %get-tuple-element.64), channel_id=1, source_target_pairs={{0,1},{1,0},{2,3},{3,2},{4,5},{5,4},{6,7},{7,6},{8,9},{9,8},{10,11... | collective-permute-start | bytes 786440 | tf_op jit(solution)/shard_map/ppermute | solution.py:337
  97.7 5.5 %collective-permute-start.10 = (bf16[256,256]{1,0:T(8,128)(2,1)S(1)}, bf16[256,256]{1,0:T(8,128)(2,1)S(1)}, u32[]{:S(2)}, u32[]{:S(2)}) collective-permute-start(bf16[256,256]{1,0:T(8,128)(2,1)S(1)} %slice.38), channel_id=1, source_target_pairs={{0,32},{16,48},{32,64},{48,80},{64,96},{80,112},{96,0},{112,16},{1... | collective-permute-start | bytes 393224 | tf_op jit(solution)/shard_map/ppermute | solution.py:326
  100.7 6.4 %collective-permute-start.11 = (bf16[256,256]{1,0:T(8,128)(2,1)S(1)}, bf16[256,256]{1,0:T(8,128)(2,1)S(1)}, u32[]{:S(2)}, u32[]{:S(2)}) collective-permute-start(bf16[256,256]{1,0:T(8,128)(2,1)S(1)} %slice.39), channel_id=1, source_target_pairs={{0,96},{16,112},{32,0},{48,16},{64,32},{80,48},{96,64},{112,80},{1... | collective-permute-start | bytes 393224 | tf_op jit(solution)/shard_map/ppermute | solution.py:326
  107.1 7.1 %copy-start.6 = (bf16[512,256]{1,0:T(8,128)(2,1)}, bf16[512,256]{1,0:T(8,128)(2,1)S(1)}, u32[]{:S(2)}) copy-start(bf16[512,256]{1,0:T(8,128)(2,1)S(1)} %collective-permute-done.8) | copy-start | bytes 786436
  107.1 7.1 %copy-start.7 = (bf16[512,256]{1,0:T(8,128)(2,1)}, bf16[512,256]{1,0:T(8,128)(2,1)S(1)}, u32[]{:S(2)}) copy-start(bf16[512,256]{1,0:T(8,128)(2,1)S(1)} %collective-permute-done.9) | copy-start | bytes 786436
  107.2 0.7 copy-start.9
  108.0 6.3 %collective-permute-start.14 = (bf16[256,256]{1,0:T(8,128)(2,1)S(1)}, bf16[256,256]{1,0:T(8,128)(2,1)S(1)}, u32[]{:S(2)}, u32[]{:S(2)}) collective-permute-start(bf16[256,256]{1,0:T(8,128)(2,1)S(1)} %slice.41), channel_id=1, source_target_pairs={{0,96},{16,112},{32,0},{48,16},{64,32},{80,48},{96,64},{112,80},{1... | collective-permute-start | bytes 393224 | tf_op jit(solution)/shard_map/ppermute | solution.py:326
  108.1 6.1 %collective-permute-start.13 = (bf16[256,256]{1,0:T(8,128)(2,1)S(1)}, bf16[256,256]{1,0:T(8,128)(2,1)S(1)}, u32[]{:S(2)}, u32[]{:S(2)}) collective-permute-start(bf16[256,256]{1,0:T(8,128)(2,1)S(1)} %slice.40), channel_id=1, source_target_pairs={{0,32},{16,48},{32,64},{48,80},{64,96},{80,112},{96,0},{112,16},{1... | collective-permute-start | bytes 393224 | tf_op jit(solution)/shard_map/ppermute | solution.py:326
  111.5 5.2 %collective-permute-start.15 = (bf16[4,512,256]{2,1,0:T(8,128)(2,1)S(1)}, bf16[4,512,256]{2,1,0:T(8,128)(2,1)S(1)}, u32[]{:S(2)}, u32[]{:S(2)}) collective-permute-start(bf16[4,512,256]{2,1,0:T(8,128)(2,1)S(1)} %pad_maximum_fusion.refs_0_), channel_id=1, source_target_pairs={{0,16},{16,0},{32,48},{48,32},{64,80},{80,64},{96,112},{112,96},{1... | collective-permute-start | bytes 3145736 | tf_op jit(solution)/shard_map/ppermute | solution.py:344
  115.4 2.9 %collective-permute-start.16 = (bf16[4,512,256]{2,1,0:T(8,128)(2,1)S(1)}, bf16[4,512,256]{2,1,0:T(8,128)(2,1)}, u32[]{:S(2)}, u32[]{:S(2)}) collective-permute-start(bf16[4,512,256]{2,1,0:T(8,128)(2,1)S(1)} %pad_maximum_fusion.1.refs_1_), channel_id=1, source_target_pairs={{0,16},{16,0},{32,48},{48,32},{64,80},{80,64},{96,112},{112,96},{1... | collective-permute-start | bytes 3145736 | tf_op jit(solution)/shard_map/ppermute | solution.py:344
  129.4 9.0 %collective-permute-start.17 = (bf16[512,256]{1,0:T(8,128)(2,1)S(1)}, bf16[512,256]{1,0:T(8,128)(2,1)S(1)}, u32[]{:S(2)}, u32[]{:S(2)}) collective-permute-start(bf16[512,256]{1,0:T(8,128)(2,1)S(1)} %shard_map.76), channel_id=1, source_target_pairs={{0,2},{1,3},{2,4},{3,5},{4,6},{5,7},{6,8},{7,9},{8,10},{9,11},{10,... | collective-permute-start | bytes 786440 | tf_op jit(solution)/shard_map/ppermute | solution.py:348
  131.0 8.0 %collective-permute-start.18 = (bf16[512,256]{1,0:T(8,128)(2,1)S(1)}, bf16[512,256]{1,0:T(8,128)(2,1)S(1)}, u32[]{:S(2)}, u32[]{:S(2)}) collective-permute-start(bf16[512,256]{1,0:T(8,128)(2,1)S(1)} %shard_map.76), channel_id=1, source_target_pairs={{0,14},{1,15},{2,0},{3,1},{4,2},{5,3},{6,4},{7,5},{8,6},{9,7},{10,... | collective-permute-start | bytes 786440 | tf_op jit(solution)/shard_map/ppermute | solution.py:351
  139.0 10.4 %collective-permute-start.19 = (bf16[512,256]{1,0:T(8,128)(2,1)S(1)}, bf16[512,256]{1,0:T(8,128)(2,1)S(1)}, u32[]{:S(2)}, u32[]{:S(2)}) collective-permute-start(bf16[512,256]{1,0:T(8,128)(2,1)S(1)} %collective-permute-done.17), channel_id=1, source_target_pairs={{0,2},{1,3},{2,4},{3,5},{4,6},{5,7},{6,8},{7,9},{8,10},{9,11},{10,... | collective-permute-start | bytes 786440 | tf_op jit(solution)/shard_map/ppermute | solution.py:348
  139.0 10.4 %collective-permute-start.20 = (bf16[512,256]{1,0:T(8,128)(2,1)S(1)}, bf16[512,256]{1,0:T(8,128)(2,1)S(1)}, u32[]{:S(2)}, u32[]{:S(2)}) collective-permute-start(bf16[512,256]{1,0:T(8,128)(2,1)S(1)} %collective-permute-done.18), channel_id=1, source_target_pairs={{0,14},{1,15},{2,0},{3,1},{4,2},{5,3},{6,4},{7,5},{8,6},{9,7},{10,... | collective-permute-start | bytes 786440 | tf_op jit(solution)/shard_map/ppermute | solution.py:351
  146.0 9.1 %copy-start.4 = (bf16[2048,512]{1,0:T(8,128)(2,1)S(1)}, bf16[2048,512]{1,0:T(8,128)(2,1)}, u32[]{:S(2)}) copy-start(bf16[2048,512]{1,0:T(8,128)(2,1)} %all-gather.7.cloned.1.call-done) | copy-start | bytes 6291460
  149.4 9.5 %collective-permute-start.21 = (bf16[512,256]{1,0:T(8,128)(2,1)S(1)}, bf16[512,256]{1,0:T(8,128)(2,1)S(1)}, u32[]{:S(2)}, u32[]{:S(2)}) collective-permute-start(bf16[512,256]{1,0:T(8,128)(2,1)S(1)} %collective-permute-done.19), channel_id=1, source_target_pairs={{0,2},{1,3},{2,4},{3,5},{4,6},{5,7},{6,8},{7,9},{8,10},{9,11},{10,... | collective-permute-start | bytes 786440 | tf_op jit(solution)/shard_map/ppermute | solution.py:348
  149.4 9.5 %collective-permute-start.22 = (bf16[512,256]{1,0:T(8,128)(2,1)S(1)}, bf16[512,256]{1,0:T(8,128)(2,1)S(1)}, u32[]{:S(2)}, u32[]{:S(2)}) collective-permute-start(bf16[512,256]{1,0:T(8,128)(2,1)S(1)} %collective-permute-done.20), channel_id=1, source_target_pairs={{0,14},{1,15},{2,0},{3,1},{4,2},{5,3},{6,4},{7,5},{8,6},{9,7},{10,... | collective-permute-start | bytes 786440 | tf_op jit(solution)/shard_map/ppermute | solution.py:351
  159.0 10.1 %collective-permute-start.23 = (bf16[512,128]{1,0:T(8,128)(2,1)S(1)}, bf16[512,128]{1,0:T(8,128)(2,1)S(1)}, u32[]{:S(2)}, u32[]{:S(2)}) collective-permute-start(bf16[512,128]{1,0:T(8,128)(2,1)S(1)} %slice.42), channel_id=1, source_target_pairs={{0,2},{1,3},{2,4},{3,5},{4,6},{5,7},{6,8},{7,9},{8,10},{9,11},{10,... | collective-permute-start | bytes 393224 | tf_op jit(solution)/shard_map/ppermute | solution.py:348
  159.1 10.0 %collective-permute-start.24 = (bf16[512,128]{1,0:T(8,128)(2,1)S(1)}, bf16[512,128]{1,0:T(8,128)(2,1)S(1)}, u32[]{:S(2)}, u32[]{:S(2)}) collective-permute-start(bf16[512,128]{1,0:T(8,128)(2,1)S(1)} %slice.43), channel_id=1, source_target_pairs={{0,14},{1,15},{2,0},{3,1},{4,2},{5,3},{6,4},{7,5},{8,6},{9,7},{10,... | collective-permute-start | bytes 393224 | tf_op jit(solution)/shard_map/ppermute | solution.py:351
  165.9 19.8 %collective-permute-start.25 = (bf16[512,512]{1,0:T(8,128)(2,1)S(1)}, bf16[512,512]{1,0:T(8,128)(2,1)S(1)}, u32[]{:S(2)}, u32[]{:S(2)}) collective-permute-start(bf16[512,512]{1,0:T(8,128)(2,1)S(1)} %fusion.13), channel_id=1, source_target_pairs={{0,1},{1,0},{2,3},{3,2},{4,5},{5,4},{6,7},{7,6},{8,9},{9,8},{10,11... | collective-permute-start | bytes 1572872 | tf_op jit(solution)/shard_map/ppermute | solution.py:375
  169.1 16.6 %collective-permute-start.26 = (bf16[512,256]{1,0:T(8,128)(2,1)S(1)}, bf16[512,256]{1,0:T(8,128)(2,1)S(1)}, u32[]{:S(2)}, u32[]{:S(2)}) collective-permute-start(bf16[512,256]{1,0:T(8,128)(2,1)S(1)} %constant_dynamic-update-slice_fusion), channel_id=1, source_target_pairs={{0,1},{1,0},{2,3},{3,2},{4,5},{5,4},{6,7},{7,6},{8,9},{9,8},{10,11... | collective-permute-start | bytes 786440 | tf_op jit(solution)/shard_map/ppermute | solution.py:377
  185.7 0.9 copy-start.16
  185.7 0.8 copy-start.15
Sparse Core Ops, SparseCore 0:
  18.0 29.5 all-gather.4
  72.7 38.6 reduce-scatter.1
  113.3 25.7 all-gather.6

commit v7 on v6

--- a/solution.py
+++ b/solution.py
@@ -291,10 +291,9 @@
 
     own_rows = lax.dynamic_slice_in_dim(kept_rows, shard, 1, 0)
     x_own, sent = rows_and_sums(own_rows, hidden, norm_gain, router_weight, key_value_weight)
-    x_own, sent, wq_got = lax.optimization_barrier((x_own, sent, wq_got))
     x_in = lax.ppermute(x_own, "tp", y_swap())
 
-    sent, x_in = lax.optimization_barrier((sent, x_in))
+    sent, wq_got = lax.optimization_barrier((sent, wq_got))
     wq_in = share(wq_got)
     exchanged = lax.all_to_all(sent, "tp", 0, 0, tiled=True)
     part = query_parts(y, x_own, x_in, query_weight, wq_in)
@@ -305,17 +304,19 @@
     ids = jnp.stack([i + core for i in ids] + [i + 1 - core for i in ids])
     counts = jnp.sum((kept_rows < tokens).astype(jnp.int32), axis=1)
     info = packing(counts, shard, ids)
-    exchanged, part, info = lax.optimization_barrier((exchanged, part, info))
-    query_sum = lax.psum_scatter(
-        part, "tp", scatter_dimension=0, axis_index_groups=[[2 * k + h for k in range(ZN)] for h in range(2)]
-    )
+    wo_rows = out_weight.shape[0] // 2
+    wo_sent = lax.dynamic_slice(out_weight, ((1 - y) * wo_rows + mine * chunk, 0), (chunk, width))
+    exchanged, info, wo_sent = lax.optimization_barrier((exchanged, info, wo_sent))
     summed = jnp.sum(exchanged.astype(jnp.float32), axis=0)
     square_sum = summed[HD // 2] + summed[HD // 2 + 2]
     router_logit = summed[HD // 2 + 1] + summed[HD // 2 + 3]
     inverse_rms = lax.rsqrt(square_sum / D + EPSILON)
     piece = (summed[: HD // 2] * inverse_rms[None, :]).astype(bf16)
     pieces = [lax.ppermute(piece, "tp", quad_shift(k)) for k in (1, 2, 3)]
-    pieces = [piece] + pieces
+    pieces, part = lax.optimization_barrier(([piece] + pieces, part))
+    query_sum = lax.psum_scatter(
+        part, "tp", scatter_dimension=0, axis_index_groups=[[2 * k + h for k in range(ZN)] for h in range(2)]
+    )
     kv_own = ordered_rows(z % 4, pieces)
 
 
@@ -327,16 +328,14 @@
 
     middle = rows // 2
     over = lax.ppermute(kv_own, "ctx", [(c, (c + shard_n // 2) % shard_n) for c in range(shard_n)])
-    near_left, near_right, over = lax.optimization_barrier((x_hop(kv_own, 1), x_hop(kv_own, -1), over))
+    kv_own, wo_sent = lax.optimization_barrier((kv_own, wo_sent))
+    wo_got = lax.ppermute(wo_sent, "tp", y_swap())
+    near_left, near_right, over, wo_got = lax.optimization_barrier((x_hop(kv_own, 1), x_hop(kv_own, -1), over, wo_got))
+    wo_in = share(wo_got).reshape(wo_rows, width)
     first_half = jnp.stack([kv_own, near_left, near_right, over])
     far = x_hop(near_left[:middle], 1), x_hop(near_right[middle:], -1)
     over_left, over_right = x_hop(over, 1), x_hop(over, -1)
-    wo_rows = out_weight.shape[0] // 2
-    wo_start = (1 - y) * wo_rows + mine * chunk
-    near_left, wo_start = lax.optimization_barrier((near_left, wo_start))
-    wo_got = lax.ppermute(lax.dynamic_slice(out_weight, (wo_start, 0), (chunk, width)), "tp", y_swap())
-    over_left, over_right, far, wo_got = lax.optimization_barrier((over_left, over_right, far, wo_got))
-    wo_in = share(wo_got).reshape(wo_rows, width)
+    over_left, over_right, far = lax.optimization_barrier((over_left, over_right, far))
     over_far = x_hop(over_left[:middle], 1), x_hop(over_right[middle:], -1)
     second_half = jnp.stack([over_left, over_right, jnp.concatenate(far), jnp.concatenate(over_far)])
 
@@ -370,17 +369,12 @@
         from_left, from_right = both(from_left, from_right)
         terms.append(project(from_left, -step, 0, chunk))
         terms.append(project(from_right, step, 0, chunk))
-    for_partner = functools.reduce(jnp.add, [t[1] for t in terms]).astype(bf16)
-    far = right(from_left[:, :cut]), left(from_right[:, cut:])
-    received = lax.ppermute(for_partner, "tp", y_swap())
-    far = jnp.concatenate(far, axis=1)
-    far_in = lax.ppermute(far, "tp", y_swap())
-    far_start = (z + 4) % ZN * chunk
-    far_weights = lax.dynamic_slice(out_weight, (y * wo_rows + far_start, 0), (chunk, width))
-    far_in_weights = lax.dynamic_slice(out_weight, ((1 - y) * wo_rows + far_start, 0), (chunk, width))
-    own_sum = functools.reduce(jnp.add, [t[0] for t in terms]) + dot(far, far_weights)
-    own_sum, received, far_in, far_in_weights = lax.optimization_barrier((own_sum, received, far_in, far_in_weights))
-    projected = own_sum + received + dot(far_in, far_in_weights)
+    terms.append(project(right(from_left[:, :cut]), 4, 0, cut))
+    terms.append(project(left(from_right[:, cut:]), 4, cut, chunk))
+    for_partner = functools.reduce(jnp.add, [t[1] for t in terms])
+    received = lax.ppermute(for_partner.astype(bf16), "tp", y_swap())
+    own_sum, received = lax.optimization_barrier((functools.reduce(jnp.add, [t[0] for t in terms]), received))
+    projected = own_sum + received
     row_update = (jax.nn.sigmoid(router_logit)[:, None] * projected).astype(bf16)
     select = (own_rows.reshape(rows, 1) == jnp.arange(tokens, dtype=jnp.int32)[None, :]).astype(bf16)
     return lax.dot_general(select, row_update, (((0,), (0,)), ((), ())), preferred_element_type=jnp.float32).astype(

time: 198 us -> 187 us (0.944)
  waiting for transfers between devices: 77.4 us -> 66.6 us
    ppermute x1, waiting for transfers between devices: 12.5 us -> 0.01 us  [shards(): x_in = lax.ppermute(x_own, 'tp', y_swap())]
    all_to_all x1, waiting for transfers between devices: 16 us -> 26.5 us  [shards(): exchanged = lax.all_to_all(sent, 'tp', 0, 0, tiled=True)]
    ppermute x3 -> x2, waiting for transfers between devices: 13.2 us -> 7.6 us  [the longest x1 5.23 us: shards(): received = lax.ppermute(for_partner.astype(bf16), 'tp', y_swap())]
    all_gather x2, waiting for transfers between devices: 4.16 us -> 0.02 us  [share(): lax.all_gather(got, 'ctx', axis=0, tiled=False, axis_index_groups=groups)]
    reduce_scatter x1, waiting for transfers between devices: 0.01 us -> 3.87 us  [shards(): lax.psum_scatter(part, 'tp', scatter_dimension=0, axis_index_groups=[[2 *...]
    ppermute x3, waiting for transfers between devices: 3.57 us -> 0.01 us  [shards(): pieces = [lax.ppermute(piece, 'tp', quad_shift(k)) for k in (1, 2, 3)]]
    ppermute x1, waiting for transfers between devices: 0.06 us -> 2.38 us  [shards(): lax.ppermute(kv_own, 'ctx', [(c, (c + shard_n // 2) % shard_n) for c in r...]
    ppermute x4, starting transfers between devices: 11.5 us -> 9.48 us  [left(): return lax.ppermute(a.astype(bf16), 'tp', z_shift(-1))]
  transfers between devices with their start and end apart: 31 -> 30, of which waited for: 19 -> 16; matrix products, arithmetic and copies ran while one was open for 11% -> 12% of each run, Pallas kernels for 11% -> 11%
where the time goes in v7:
time: 187 us; the launch traced here: 184 us
  waiting for transfers between devices  66.6 us (36%)
  starting transfers between devices  49.5 us (26%)
  Pallas kernels  20.8 us (11%)
  matrix products  18.4 us (10%)
  between operations  13.5 us (7%)
  local copies, waits for them, and re-layouts  12.6 us (7%)
  other arithmetic  2.98 us (2%)
    all_to_all x1, waiting for transfers between devices, shards(): exchanged = lax.all_to_all(sent, 'tp', 0, 0, tiled=True)  26.5 us
    dot_general x18, matrix products, dot(): return jnp.dot(a, b, preferred_element_type=jnp.float32)  16.4 us
    ppermute x8, waiting for transfers between devices, x_hop(): return lax.ppermute(block, 'ctx', along(step))  13.5 us
    ppermute x4, waiting for transfers between devices, right(): return lax.ppermute(a.astype(bf16), 'tp', z_shift(1))  12.6 us
    pallas_call x1, Pallas kernels, attention(): pl.pallas_call(attention_kernel, out_shape=jax.ShapeDtypeStruct(queries.s...  11.1 us
    ppermute x8, starting transfers between devices, x_hop(): return lax.ppermute(block, 'ctx', along(step))  10.7 us
    all_to_all x1, starting transfers between devices, shards(): exchanged = lax.all_to_all(sent, 'tp', 0, 0, tiled=True)  10.3 us
    ppermute x4, starting transfers between devices, left(): return lax.ppermute(a.astype(bf16), 'tp', z_shift(-1))  9.48 us
  transfers between devices with their start and end apart: 30, of which 16 were waited for; matrix products, arithmetic and copies ran while one was open for 12% of the time, Pallas kernels for 11%

profile of v7, /device:TPU:14, one launch (start us, length us, event | category | flops | bytes accessed | tf_op | source)
XLA Modules:
  0.0 184.3 jit_solution(10634305676957783919)
XLA Ops:
  7.5 2.4 %collective-permute-start = (bf16[512,256]{1,0:T(8,128)(2,1)S(1)}, bf16[512,256]{1,0:T(8,128)(2,1)S(1)}, u32[]{:S(2)}, u32[]{:S(2)}) collective-permute-start(bf16[512,256]{1,0:T(8,128)(2,1)S(1)} %constant_dynamic-slice_fusion.1), channel_id=1, source_target_pairs={{0,1},{1,0},{2,3},{3,2},{4,5},{5,4},{6,7},{7,6},{8,9},{9,8},{10,11... | collective-permute-start | bytes 786440 | tf_op jit(solution)/shard_map/ppermute | solution.py:290
  12.0 1.2 copy-done.2
  13.2 1.2 copy-done.3
  14.4 2.6 %shard_map.73 = (bf16[512,512]{1,0:T(8,128)(2,1)S(1)}, bf16[16,72,512]{2,1,0:T(8,128)(2,1)}) custom-call(s32[1,512]{1,0:T(1,128)S(1)} %constant_dynamic-slice_fusion.2.rows_ref, bf16[1024,512]{1,0:T(8,128)(2,1)S(1)} %copy-done.2, bf16[1,512]{1,0:T(2,128)(2,1)S(1)} %reshape.431.gain_ref, bf16[1,512]{1,0:T(2,128)(2,1)S(1)} %reshape.432.router_ref, ...), custom_call_target="tpu_custom_call" | custom-call | flops 1073741824 | bytes 5242880 | tf_op jit(solution)/shard_map/pallas_call | solution.py:203
  17.9 10.3 %all-to-all-start = ((bf16[16,72,512]{2,1,0:T(8,128)(2,1)}), bf16[16,72,512]{2,1,0:T(8,128)(2,1)S(1)}, u32[]{:S(2)}, u32[]{:S(2)}) async-start(bf16[16,72,512]{2,1,0:T(8,128)(2,1)} %get-tuple-element.36), calls=%async_computation | async-start | bytes 2359296 | tf_op jit(solution)/shard_map/all_to_all | solution.py:298
  28.2 3.5 %collective-permute-start.4 = (bf16[512,512]{1,0:T(8,128)(2,1)S(1)}, bf16[512,512]{1,0:T(8,128)(2,1)S(1)}, u32[]{:S(2)}, u32[]{:S(2)}) collective-permute-start(bf16[512,512]{1,0:T(8,128)(2,1)S(1)} %get-tuple-element.39.x_own_ref), channel_id=1, source_target_pairs={{0,1},{1,0},{2,3},{3,2},{4,5},{5,4},{6,7},{7,6},{8,9},{9,8},{10,11... | collective-permute-start | bytes 1572872 | tf_op jit(solution)/shard_map/ppermute | solution.py:294
  33.4 26.5 %all-to-all-done = bf16[16,72,512]{2,1,0:T(8,128)(2,1)S(1)} async-done(((bf16[16,72,512]{2,1,0:T(8,128)(2,1)}), bf16[16,72,512]{2,1,0:T(8,128)(2,1)S(1)}, u32[]{:S(2)}, u32[]{:S(2)}) %all-to-all-start) | async-done | bytes 1179680 | tf_op jit(solution)/shard_map/all_to_all | solution.py:298
  60.2 2.4 %collective-permute-start.2 = (bf16[64,512]{1,0:T(8,128)(2,1)S(1)}, bf16[64,512]{1,0:T(8,128)(2,1)S(1)}, u32[]{:S(2)}, u32[]{:S(2)}) collective-permute-start(bf16[64,512]{1,0:T(8,128)(2,1)S(1)} %fusion.46.refs_0_), channel_id=1, source_target_pairs={{0,4},{1,5},{2,6},{3,7},{4,0},{5,1},{6,2},{7,3},{8,12},{9,13},{10,... | collective-permute-start | bytes 196616 | tf_op jit(solution)/shard_map/ppermute | solution.py:315
  62.6 1.5 collective-permute-start.3
  64.1 2.2 %copy-done = bf16[512,4096]{1,0:T(8,128)(2,1)S(1)} copy-done((bf16[512,4096]{1,0:T(8,128)(2,1)S(1)}, bf16[512,4096]{1,0:T(8,128)(2,1)}, u32[]{:S(2)}) %copy-start) | copy-done | bytes 4194328
  66.3 1.6 copy-done.1
  67.9 5.3 %shard_map.74 = bf16[8,512,256]{2,1,0:T(8,128)(2,1)} custom-call(s32[1]{0:T(128)} %bitcast.37.y_ref, bf16[512,512]{1,0:T(8,128)(2,1)S(1)} %get-tuple-element.39.x_own_ref, bf16[512,512]{1,0:T(8,128)(2,1)S(1)} %collective-permute-done.4.x_in_ref, bf16[512,4096]{1,0:T(8,128)(2,1)S(1)} %copy-done, bf16[8,512,256]{2,1,0:T(8,128)(2,1)S(1)} %bitcast.71), custom_call_target="tpu_custom_call" | custom-call | flops 2147483648 | bytes 6291456 | tf_op jit(solution)/shard_map/pallas_call | solution.py:225
  73.8 1.8 shard_map.75
  76.1 1.5 collective-permute-start.6
  77.7 1.3 collective-permute-start.7
  79.0 3.2 %collective-permute-done.5 = bf16[512,256]{1,0:T(8,128)(2,1)S(1)} collective-permute-done((bf16[512,256]{1,0:T(8,128)(2,1)}, bf16[512,256]{1,0:T(8,128)(2,1)S(1)}, u32[]{:S(2)}, u32[]{:S(2)}) %collective-permute-start.5) | collective-permute-done | bytes 262176 | tf_op jit(solution)/shard_map/ppermute | solution.py:327
  82.2 1.7 collective-permute-done.6
  83.9 2.4 %collective-permute-done.7 = bf16[512,256]{1,0:T(8,128)(2,1)S(1)} collective-permute-done((bf16[512,256]{1,0:T(8,128)(2,1)}, bf16[512,256]{1,0:T(8,128)(2,1)S(1)}, u32[]{:S(2)}, u32[]{:S(2)}) %collective-permute-start.7) | collective-permute-done | bytes 262176 | tf_op jit(solution)/shard_map/ppermute | solution.py:330
  86.3 2.4 %collective-permute-done.8 = bf16[256,512]{1,0:T(8,128)(2,1)S(1)} collective-permute-done((bf16[256,512]{1,0:T(8,128)(2,1)S(1)}, bf16[256,512]{1,0:T(8,128)(2,1)S(1)}, u32[]{:S(2)}, u32[]{:S(2)}) %collective-permute-start.8) | collective-permute-done | bytes 262176 | tf_op jit(solution)/shard_map/ppermute | solution.py:332
  89.4 1.8 collective-permute-start.9
  91.5 3.0 %collective-permute-start.11 = (bf16[256,256]{1,0:T(8,128)(2,1)S(1)}, bf16[256,256]{1,0:T(8,128)(2,1)S(1)}, u32[]{:S(2)}, u32[]{:S(2)}) collective-permute-start(bf16[256,256]{1,0:T(8,128)(2,1)S(1)} %slice.38), channel_id=1, source_target_pairs={{0,32},{16,48},{32,64},{48,80},{64,96},{80,112},{96,0},{112,16},{1... | collective-permute-start | bytes 393224 | tf_op jit(solution)/shard_map/ppermute | solution.py:327
  94.8 2.5 %collective-permute-done.11 = bf16[256,256]{1,0:T(8,128)(2,1)S(1)} collective-permute-done((bf16[256,256]{1,0:T(8,128)(2,1)S(1)}, bf16[256,256]{1,0:T(8,128)(2,1)S(1)}, u32[]{:S(2)}, u32[]{:S(2)}) %collective-permute-start.11) | collective-permute-done | bytes 131104 | tf_op jit(solution)/shard_map/ppermute | solution.py:327
  97.2 4.5 %collective-permute-done.12 = bf16[256,256]{1,0:T(8,128)(2,1)S(1)} collective-permute-done((bf16[256,256]{1,0:T(8,128)(2,1)S(1)}, bf16[256,256]{1,0:T(8,128)(2,1)S(1)}, u32[]{:S(2)}, u32[]{:S(2)}) %collective-permute-start.12) | collective-permute-done | bytes 131104 | tf_op jit(solution)/shard_map/ppermute | solution.py:327
  101.9 3.3 %collective-permute-start.13 = (bf16[256,256]{1,0:T(8,128)(2,1)S(1)}, bf16[256,256]{1,0:T(8,128)(2,1)S(1)}, u32[]{:S(2)}, u32[]{:S(2)}) collective-permute-start(bf16[256,256]{1,0:T(8,128)(2,1)S(1)} %slice.40), channel_id=1, source_target_pairs={{0,32},{16,48},{32,64},{48,80},{64,96},{80,112},{96,0},{112,16},{1... | collective-permute-start | bytes 393224 | tf_op jit(solution)/shard_map/ppermute | solution.py:327
  106.4 1.6 collective-permute-done.14
  108.4 3.9 %reduce-scatter.2.cloned.1.call-done = bf16[1,512,256]{2,1,0:T(8,128)(2,1)} async-done(((bf16[8,512,256]{2,1,0:T(8,128)(2,1)}), bf16[1,512,256]{2,1,0:T(8,128)(2,1)}) %reduce-scatter.2.cloned.1.call-update) | async-done | bytes 262160 | tf_op jit(solution)/shard_map/reduce_scatter | solution.py:317
  113.4 11.1 %shard_map.76 = bf16[512,256]{1,0:T(8,128)(2,1)S(1)} custom-call(s32[16,3]{1,0:T(8,128)S(1)} %copy.11.info_ref, bf16[512,256]{1,0:T(8,128)(2,1)S(1)} %fusion.18.q_ref, bf16[4,512,256]{2,1,0:T(8,128)(2,1)S(1)} %pad_maximum_fusion.refs_0_, bf16[4,512,256]{2,1,0:T(8,128)(2,1)S(1)} %pad_maximum_fusion.1.refs_1_, ...), custom_call_target="tpu_custom_call" | custom-call | flops 4294967296 | bytes 4194304 | tf_op jit(solution)/shard_map/pallas_call | solution.py:151
  124.5 1.3 collective-permute-start.17
  125.8 2.0 %collective-permute-start.18 = (bf16[512,256]{1,0:T(8,128)(2,1)S(1)}, bf16[512,256]{1,0:T(8,128)(2,1)S(1)}, u32[]{:S(2)}, u32[]{:S(2)}) collective-permute-start(bf16[512,256]{1,0:T(8,128)(2,1)S(1)} %shard_map.76), channel_id=1, source_target_pairs={{0,14},{1,15},{2,0},{3,1},{4,2},{5,3},{6,4},{7,5},{8,6},{9,7},{10,... | collective-permute-start | bytes 786440 | tf_op jit(solution)/shard_map/ppermute | solution.py:350
  127.8 6.3 %collective-permute-done.17 = bf16[512,256]{1,0:T(8,128)(2,1)S(1)} collective-permute-done((bf16[512,256]{1,0:T(8,128)(2,1)S(1)}, bf16[512,256]{1,0:T(8,128)(2,1)S(1)}, u32[]{:S(2)}, u32[]{:S(2)}) %collective-permute-start.17) | collective-permute-done | bytes 262176 | tf_op jit(solution)/shard_map/ppermute | solution.py:347
  134.6 2.7 %collective-permute-start.20 = (bf16[512,256]{1,0:T(8,128)(2,1)S(1)}, bf16[512,256]{1,0:T(8,128)(2,1)S(1)}, u32[]{:S(2)}, u32[]{:S(2)}) collective-permute-start(bf16[512,256]{1,0:T(8,128)(2,1)S(1)} %collective-permute-done.18), channel_id=1, source_target_pairs={{0,14},{1,15},{2,0},{3,1},{4,2},{5,3},{6,4},{7,5},{8,6},{9,7},{10,... | collective-permute-start | bytes 786440 | tf_op jit(solution)/shard_map/ppermute | solution.py:350
  137.3 1.2 fusion.41
  138.6 1.2 fusion.43
  139.8 1.2 fusion.29
  141.1 1.4 fusion.31
  142.7 1.5 collective-permute-start.21
  144.2 1.7 collective-permute-start.22
  146.0 1.2 fusion.37
  147.2 1.2 fusion.39
  149.1 3.3 %collective-permute-done.21 = bf16[512,256]{1,0:T(8,128)(2,1)S(1)} collective-permute-done((bf16[512,256]{1,0:T(8,128)(2,1)S(1)}, bf16[512,256]{1,0:T(8,128)(2,1)S(1)}, u32[]{:S(2)}, u32[]{:S(2)}) %collective-permute-start.21) | collective-permute-done | bytes 262176 | tf_op jit(solution)/shard_map/ppermute | solution.py:347
  152.4 3.1 %collective-permute-start.24 = (bf16[512,128]{1,0:T(8,128)(2,1)S(1)}, bf16[512,128]{1,0:T(8,128)(2,1)S(1)}, u32[]{:S(2)}, u32[]{:S(2)}) collective-permute-start(bf16[512,128]{1,0:T(8,128)(2,1)S(1)} %slice.43), channel_id=1, source_target_pairs={{0,14},{1,15},{2,0},{3,1},{4,2},{5,3},{6,4},{7,5},{8,6},{9,7},{10,... | collective-permute-start | bytes 393224 | tf_op jit(solution)/shard_map/ppermute | solution.py:350
  155.6 1.2 fusion.33
  156.8 1.2 fusion.35
  159.0 2.8 %collective-permute-done.23 = bf16[512,128]{1,0:T(8,128)(2,1)S(1)} collective-permute-done((bf16[512,128]{1,0:T(8,128)(2,1)S(1)}, bf16[512,128]{1,0:T(8,128)(2,1)S(1)}, u32[]{:S(2)}, u32[]{:S(2)}) %collective-permute-start.23) | collective-permute-done | bytes 131104 | tf_op jit(solution)/shard_map/ppermute | solution.py:347
  162.6 3.9 %collective-permute-start.25 = (bf16[512,512]{1,0:T(8,128)(2,1)S(1)}, bf16[512,512]{1,0:T(8,128)(2,1)S(1)}, u32[]{:S(2)}, u32[]{:S(2)}) collective-permute-start(bf16[512,512]{1,0:T(8,128)(2,1)S(1)} %fusion.16), channel_id=1, source_target_pairs={{0,1},{1,0},{2,3},{3,2},{4,5},{5,4},{6,7},{7,6},{8,9},{9,8},{10,11... | collective-permute-start | bytes 1572872 | tf_op jit(solution)/shard_map/ppermute | solution.py:375
  168.9 1.6 fusion.9
  170.6 5.2 %collective-permute-done.25 = bf16[512,512]{1,0:T(8,128)(2,1)S(1)} collective-permute-done((bf16[512,512]{1,0:T(8,128)(2,1)S(1)}, bf16[512,512]{1,0:T(8,128)(2,1)S(1)}, u32[]{:S(2)}, u32[]{:S(2)}) %collective-permute-start.25) | collective-permute-done | bytes 524320 | tf_op jit(solution)/shard_map/ppermute | solution.py:375
  175.8 2.0 %fusion.1 = bf16[1024,512]{1,0:T(8,128)(2,1)} fusion(s32[512]{0:T(512)S(1)} %bitcast.72, f32[512,512]{1,0:T(8,128)S(1)} %fusion.9, bf16[512,512]{1,0:T(8,128)(2,1)S(1)} %collective-permute-done.25, f32[512]{0:T(512)S(1)} %bitcast.82), kind=kOutput, calls=%fused_computation.3 | convolution fusion | flops 538968064 | bytes 2625536 | tf_op jit(solution)/shard_map/dot_general | solution.py:380
  (91 shorter events, 16.7 us)
Async XLA Ops:
  6.5 57.6 %all-gather.5.cloned.1.call-start = ((), (), s32[]{:S(2)}) async-start(), calls=%async_computation.3 | async-start | bytes 2359296 | tf_op jit(solution)/shard_map/all_gather | solution.py:287
  7.5 9.6 %collective-permute-start = (bf16[512,256]{1,0:T(8,128)(2,1)S(1)}, bf16[512,256]{1,0:T(8,128)(2,1)S(1)}, u32[]{:S(2)}, u32[]{:S(2)}) collective-permute-start(bf16[512,256]{1,0:T(8,128)(2,1)S(1)} %constant_dynamic-slice_fusion.1), channel_id=1, source_target_pairs={{0,1},{1,0},{2,3},{3,2},{4,5},{5,4},{6,7},{7,6},{8,9},{9,8},{10,11... | collective-permute-start | bytes 786440 | tf_op jit(solution)/shard_map/ppermute | solution.py:290
  12.0 1.2 copy-start.2
  13.2 1.2 copy-start.3
  17.0 14.9 %copy-start.11 = (s32[16,512]{1,0:T(8,128)S(1)}, s32[16,512]{1,0:T(8,128)}, u32[]{:S(2)}) copy-start(s32[16,512]{1,0:T(8,128)} %param.13) | copy-start | bytes 98308
  17.1 0.7 copy-start.7
  17.9 42.0 %all-to-all-start = ((bf16[16,72,512]{2,1,0:T(8,128)(2,1)}), bf16[16,72,512]{2,1,0:T(8,128)(2,1)S(1)}, u32[]{:S(2)}, u32[]{:S(2)}) async-start(bf16[16,72,512]{2,1,0:T(8,128)(2,1)} %get-tuple-element.36), calls=%async_computation | async-start | bytes 2359296 | tf_op jit(solution)/shard_map/all_to_all | solution.py:298
  28.2 84.1 %reduce-scatter.2.cloned.1.call-start = ((), (), s32[]{:S(2)}) async-start(), calls=%async_computation.2 | async-start | bytes 2359296 | tf_op jit(solution)/shard_map/reduce_scatter | solution.py:317
  28.2 35.9 %collective-permute-start.4 = (bf16[512,512]{1,0:T(8,128)(2,1)S(1)}, bf16[512,512]{1,0:T(8,128)(2,1)S(1)}, u32[]{:S(2)}, u32[]{:S(2)}) collective-permute-start(bf16[512,512]{1,0:T(8,128)(2,1)S(1)} %get-tuple-element.39.x_own_ref), channel_id=1, source_target_pairs={{0,1},{1,0},{2,3},{3,2},{4,5},{5,4},{6,7},{7,6},{8,9},{9,8},{10,11... | collective-permute-start | bytes 1572872 | tf_op jit(solution)/shard_map/ppermute | solution.py:294
  60.1 13.1 %copy-start.5 = (bf16[64,512]{1,0:T(8,128)(2,1)}, bf16[64,512]{1,0:T(8,128)(2,1)S(1)}, u32[]{:S(2)}) copy-start(bf16[64,512]{1,0:T(8,128)(2,1)S(1)} %fusion.46.refs_0_) | copy-start | bytes 196612
  60.1 13.1 %collective-permute-start.1 = (bf16[64,512]{1,0:T(8,128)(2,1)S(1)}, bf16[64,512]{1,0:T(8,128)(2,1)S(1)}, u32[]{:S(2)}, u32[]{:S(2)}) collective-permute-start(bf16[64,512]{1,0:T(8,128)(2,1)S(1)} %fusion.46.refs_0_), channel_id=1, source_target_pairs={{0,2},{1,3},{2,4},{3,5},{4,6},{5,7},{6,0},{7,1},{8,10},{9,11},{10,... | collective-permute-start | bytes 196616 | tf_op jit(solution)/shard_map/ppermute | solution.py:315
  60.2 13.0 %collective-permute-start.2 = (bf16[64,512]{1,0:T(8,128)(2,1)S(1)}, bf16[64,512]{1,0:T(8,128)(2,1)S(1)}, u32[]{:S(2)}, u32[]{:S(2)}) collective-permute-start(bf16[64,512]{1,0:T(8,128)(2,1)S(1)} %fusion.46.refs_0_), channel_id=1, source_target_pairs={{0,4},{1,5},{2,6},{3,7},{4,0},{5,1},{6,2},{7,3},{8,12},{9,13},{10,... | collective-permute-start | bytes 196616 | tf_op jit(solution)/shard_map/ppermute | solution.py:315
  62.6 10.6 %collective-permute-start.3 = (bf16[64,512]{1,0:T(8,128)(2,1)S(1)}, bf16[64,512]{1,0:T(8,128)(2,1)S(1)}, u32[]{:S(2)}, u32[]{:S(2)}) collective-permute-start(bf16[64,512]{1,0:T(8,128)(2,1)S(1)} %fusion.46.refs_0_), channel_id=1, source_target_pairs={{0,6},{1,7},{2,0},{3,1},{4,2},{5,3},{6,4},{7,5},{8,14},{9,15},{10,... | collective-permute-start | bytes 196616 | tf_op jit(solution)/shard_map/ppermute | solution.py:315
  64.1 2.2 %copy-start = (bf16[512,4096]{1,0:T(8,128)(2,1)S(1)}, bf16[512,4096]{1,0:T(8,128)(2,1)}, u32[]{:S(2)}) copy-start(bf16[512,4096]{1,0:T(8,128)(2,1)} %w_own_ref.1) | copy-start | bytes 12582916
  66.3 1.6 copy-start.1
  73.2 0.6 copy-start.8
  73.2 0.6 copy-start.9
  73.2 0.6 copy-start.10
  73.2 66.6 %all-gather.7.cloned.1.call-start = ((), (), s32[]{:S(2)}) async-start(), calls=%async_computation.4 | async-start | bytes 2359296 | tf_op jit(solution)/shard_map/all_gather | solution.py:287
  75.6 6.6 %collective-permute-start.5 = (bf16[512,256]{1,0:T(8,128)(2,1)}, bf16[512,256]{1,0:T(8,128)(2,1)S(1)}, u32[]{:S(2)}, u32[]{:S(2)}) collective-permute-start(bf16[512,256]{1,0:T(8,128)(2,1)} %shard_map.75), channel_id=1, source_target_pairs={{0,32},{16,48},{32,64},{48,80},{64,96},{80,112},{96,0},{112,16},{1... | collective-permute-start | bytes 786440 | tf_op jit(solution)/shard_map/ppermute | solution.py:327
  76.1 7.8 %collective-permute-start.6 = (bf16[512,256]{1,0:T(8,128)(2,1)}, bf16[512,256]{1,0:T(8,128)(2,1)S(1)}, u32[]{:S(2)}, u32[]{:S(2)}) collective-permute-start(bf16[512,256]{1,0:T(8,128)(2,1)} %shard_map.75), channel_id=1, source_target_pairs={{0,96},{16,112},{32,0},{48,16},{64,32},{80,48},{96,64},{112,80},{1... | collective-permute-start | bytes 786440 | tf_op jit(solution)/shard_map/ppermute | solution.py:327
  77.7 8.6 %collective-permute-start.7 = (bf16[512,256]{1,0:T(8,128)(2,1)}, bf16[512,256]{1,0:T(8,128)(2,1)S(1)}, u32[]{:S(2)}, u32[]{:S(2)}) collective-permute-start(bf16[512,256]{1,0:T(8,128)(2,1)} %shard_map.75), channel_id=1, source_target_pairs={{0,128},{16,144},{32,160},{48,176},{64,192},{80,208},{96,224},{112... | collective-permute-start | bytes 786440 | tf_op jit(solution)/shard_map/ppermute | solution.py:330
  79.0 9.6 %collective-permute-start.8 = (bf16[256,512]{1,0:T(8,128)(2,1)S(1)}, bf16[256,512]{1,0:T(8,128)(2,1)S(1)}, u32[]{:S(2)}, u32[]{:S(2)}) collective-permute-start(bf16[256,512]{1,0:T(8,128)(2,1)S(1)} %constant_dynamic-slice_fusion), channel_id=1, source_target_pairs={{0,1},{1,0},{2,3},{3,2},{4,5},{5,4},{6,7},{7,6},{8,9},{9,8},{10,11... | collective-permute-start | bytes 786440 | tf_op jit(solution)/shard_map/ppermute | solution.py:332
  88.7 0.7 copy-start.6
  89.4 12.4 %collective-permute-start.9 = (bf16[512,256]{1,0:T(8,128)(2,1)S(1)}, bf16[512,256]{1,0:T(8,128)(2,1)S(1)}, u32[]{:S(2)}, u32[]{:S(2)}) collective-permute-start(bf16[512,256]{1,0:T(8,128)(2,1)S(1)} %collective-permute-done.7), channel_id=1, source_target_pairs={{0,32},{16,48},{32,64},{48,80},{64,96},{80,112},{96,0},{112,16},{1... | collective-permute-start | bytes 786440 | tf_op jit(solution)/shard_map/ppermute | solution.py:327
  91.2 10.6 %collective-permute-start.10 = (bf16[512,256]{1,0:T(8,128)(2,1)S(1)}, bf16[512,256]{1,0:T(8,128)(2,1)S(1)}, u32[]{:S(2)}, u32[]{:S(2)}) collective-permute-start(bf16[512,256]{1,0:T(8,128)(2,1)S(1)} %collective-permute-done.7), channel_id=1, source_target_pairs={{0,96},{16,112},{32,0},{48,16},{64,32},{80,48},{96,64},{112,80},{1... | collective-permute-start | bytes 786440 | tf_op jit(solution)/shard_map/ppermute | solution.py:327
  91.5 5.7 %collective-permute-start.11 = (bf16[256,256]{1,0:T(8,128)(2,1)S(1)}, bf16[256,256]{1,0:T(8,128)(2,1)S(1)}, u32[]{:S(2)}, u32[]{:S(2)}) collective-permute-start(bf16[256,256]{1,0:T(8,128)(2,1)S(1)} %slice.38), channel_id=1, source_target_pairs={{0,32},{16,48},{32,64},{48,80},{64,96},{80,112},{96,0},{112,16},{1... | collective-permute-start | bytes 393224 | tf_op jit(solution)/shard_map/ppermute | solution.py:327
  94.5 7.3 %collective-permute-start.12 = (bf16[256,256]{1,0:T(8,128)(2,1)S(1)}, bf16[256,256]{1,0:T(8,128)(2,1)S(1)}, u32[]{:S(2)}, u32[]{:S(2)}) collective-permute-start(bf16[256,256]{1,0:T(8,128)(2,1)S(1)} %slice.39), channel_id=1, source_target_pairs={{0,96},{16,112},{32,0},{48,16},{64,32},{80,48},{96,64},{112,80},{1... | collective-permute-start | bytes 393224 | tf_op jit(solution)/shard_map/ppermute | solution.py:327
  101.8 6.3 %collective-permute-start.14 = (bf16[256,256]{1,0:T(8,128)(2,1)S(1)}, bf16[256,256]{1,0:T(8,128)(2,1)S(1)}, u32[]{:S(2)}, u32[]{:S(2)}) collective-permute-start(bf16[256,256]{1,0:T(8,128)(2,1)S(1)} %slice.41), channel_id=1, source_target_pairs={{0,96},{16,112},{32,0},{48,16},{64,32},{80,48},{96,64},{112,80},{1... | collective-permute-start | bytes 393224 | tf_op jit(solution)/shard_map/ppermute | solution.py:327
  101.9 6.1 %collective-permute-start.13 = (bf16[256,256]{1,0:T(8,128)(2,1)S(1)}, bf16[256,256]{1,0:T(8,128)(2,1)S(1)}, u32[]{:S(2)}, u32[]{:S(2)}) collective-permute-start(bf16[256,256]{1,0:T(8,128)(2,1)S(1)} %slice.40), channel_id=1, source_target_pairs={{0,32},{16,48},{32,64},{48,80},{64,96},{80,112},{96,0},{112,16},{1... | collective-permute-start | bytes 393224 | tf_op jit(solution)/shard_map/ppermute | solution.py:327
  106.3 7.1 %collective-permute-start.15 = (bf16[4,512,256]{2,1,0:T(8,128)(2,1)S(1)}, bf16[4,512,256]{2,1,0:T(8,128)(2,1)S(1)}, u32[]{:S(2)}, u32[]{:S(2)}) collective-permute-start(bf16[4,512,256]{2,1,0:T(8,128)(2,1)S(1)} %pad_maximum_fusion.refs_0_), channel_id=1, source_target_pairs={{0,16},{16,0},{32,48},{48,32},{64,80},{80,64},{96,112},{112,96},{1... | collective-permute-start | bytes 3145736 | tf_op jit(solution)/shard_map/ppermute | solution.py:343
  108.2 5.2 %collective-permute-start.16 = (bf16[4,512,256]{2,1,0:T(8,128)(2,1)S(1)}, bf16[4,512,256]{2,1,0:T(8,128)(2,1)}, u32[]{:S(2)}, u32[]{:S(2)}) collective-permute-start(bf16[4,512,256]{2,1,0:T(8,128)(2,1)S(1)} %pad_maximum_fusion.1.refs_1_), channel_id=1, source_target_pairs={{0,16},{16,0},{32,48},{48,32},{64,80},{80,64},{96,112},{112,96},{1... | collective-permute-start | bytes 3145736 | tf_op jit(solution)/shard_map/ppermute | solution.py:343
  124.5 9.6 %collective-permute-start.17 = (bf16[512,256]{1,0:T(8,128)(2,1)S(1)}, bf16[512,256]{1,0:T(8,128)(2,1)S(1)}, u32[]{:S(2)}, u32[]{:S(2)}) collective-permute-start(bf16[512,256]{1,0:T(8,128)(2,1)S(1)} %shard_map.76), channel_id=1, source_target_pairs={{0,2},{1,3},{2,4},{3,5},{4,6},{5,7},{6,8},{7,9},{8,10},{9,11},{10,... | collective-permute-start | bytes 786440 | tf_op jit(solution)/shard_map/ppermute | solution.py:347
  125.8 8.3 %collective-permute-start.18 = (bf16[512,256]{1,0:T(8,128)(2,1)S(1)}, bf16[512,256]{1,0:T(8,128)(2,1)S(1)}, u32[]{:S(2)}, u32[]{:S(2)}) collective-permute-start(bf16[512,256]{1,0:T(8,128)(2,1)S(1)} %shard_map.76), channel_id=1, source_target_pairs={{0,14},{1,15},{2,0},{3,1},{4,2},{5,3},{6,4},{7,5},{8,6},{9,7},{10,... | collective-permute-start | bytes 786440 | tf_op jit(solution)/shard_map/ppermute | solution.py:350
  134.1 8.7 %collective-permute-start.19 = (bf16[512,256]{1,0:T(8,128)(2,1)S(1)}, bf16[512,256]{1,0:T(8,128)(2,1)S(1)}, u32[]{:S(2)}, u32[]{:S(2)}) collective-permute-start(bf16[512,256]{1,0:T(8,128)(2,1)S(1)} %collective-permute-done.17), channel_id=1, source_target_pairs={{0,2},{1,3},{2,4},{3,5},{4,6},{5,7},{6,8},{7,9},{8,10},{9,11},{10,... | collective-permute-start | bytes 786440 | tf_op jit(solution)/shard_map/ppermute | solution.py:347
  134.6 8.1 %collective-permute-start.20 = (bf16[512,256]{1,0:T(8,128)(2,1)S(1)}, bf16[512,256]{1,0:T(8,128)(2,1)S(1)}, u32[]{:S(2)}, u32[]{:S(2)}) collective-permute-start(bf16[512,256]{1,0:T(8,128)(2,1)S(1)} %collective-permute-done.18), channel_id=1, source_target_pairs={{0,14},{1,15},{2,0},{3,1},{4,2},{5,3},{6,4},{7,5},{8,6},{9,7},{10,... | collective-permute-start | bytes 786440 | tf_op jit(solution)/shard_map/ppermute | solution.py:350
  141.1 7.4 %copy-start.4 = (bf16[2048,512]{1,0:T(8,128)(2,1)S(1)}, bf16[2048,512]{1,0:T(8,128)(2,1)}, u32[]{:S(2)}) copy-start(bf16[2048,512]{1,0:T(8,128)(2,1)} %all-gather.7.cloned.1.call-done) | copy-start | bytes 6291460
  142.7 9.6 %collective-permute-start.21 = (bf16[512,256]{1,0:T(8,128)(2,1)S(1)}, bf16[512,256]{1,0:T(8,128)(2,1)S(1)}, u32[]{:S(2)}, u32[]{:S(2)}) collective-permute-start(bf16[512,256]{1,0:T(8,128)(2,1)S(1)} %collective-permute-done.19), channel_id=1, source_target_pairs={{0,2},{1,3},{2,4},{3,5},{4,6},{5,7},{6,8},{7,9},{8,10},{9,11},{10,... | collective-permute-start | bytes 786440 | tf_op jit(solution)/shard_map/ppermute | solution.py:347
  144.2 8.2 %collective-permute-start.22 = (bf16[512,256]{1,0:T(8,128)(2,1)S(1)}, bf16[512,256]{1,0:T(8,128)(2,1)S(1)}, u32[]{:S(2)}, u32[]{:S(2)}) collective-permute-start(bf16[512,256]{1,0:T(8,128)(2,1)S(1)} %collective-permute-done.20), channel_id=1, source_target_pairs={{0,14},{1,15},{2,0},{3,1},{4,2},{5,3},{6,4},{7,5},{8,6},{9,7},{10,... | collective-permute-start | bytes 786440 | tf_op jit(solution)/shard_map/ppermute | solution.py:350
  152.4 6.3 %collective-permute-start.24 = (bf16[512,128]{1,0:T(8,128)(2,1)S(1)}, bf16[512,128]{1,0:T(8,128)(2,1)S(1)}, u32[]{:S(2)}, u32[]{:S(2)}) collective-permute-start(bf16[512,128]{1,0:T(8,128)(2,1)S(1)} %slice.43), channel_id=1, source_target_pairs={{0,14},{1,15},{2,0},{3,1},{4,2},{5,3},{6,4},{7,5},{8,6},{9,7},{10,... | collective-permute-start | bytes 393224 | tf_op jit(solution)/shard_map/ppermute | solution.py:350
  155.5 6.3 %collective-permute-start.23 = (bf16[512,128]{1,0:T(8,128)(2,1)S(1)}, bf16[512,128]{1,0:T(8,128)(2,1)S(1)}, u32[]{:S(2)}, u32[]{:S(2)}) collective-permute-start(bf16[512,128]{1,0:T(8,128)(2,1)S(1)} %slice.42), channel_id=1, source_target_pairs={{0,2},{1,3},{2,4},{3,5},{4,6},{5,7},{6,8},{7,9},{8,10},{9,11},{10,... | collective-permute-start | bytes 393224 | tf_op jit(solution)/shard_map/ppermute | solution.py:347
  162.6 13.2 %collective-permute-start.25 = (bf16[512,512]{1,0:T(8,128)(2,1)S(1)}, bf16[512,512]{1,0:T(8,128)(2,1)S(1)}, u32[]{:S(2)}, u32[]{:S(2)}) collective-permute-start(bf16[512,512]{1,0:T(8,128)(2,1)S(1)} %fusion.16), channel_id=1, source_target_pairs={{0,1},{1,0},{2,3},{3,2},{4,5},{5,4},{6,7},{7,6},{8,9},{9,8},{10,11... | collective-permute-start | bytes 1572872 | tf_op jit(solution)/shard_map/ppermute | solution.py:375
Sparse Core Ops, SparseCore 0:
  18.0 29.2 all-gather.4
  73.4 38.8 reduce-scatter.1
  114.1 25.4 all-gather.6

commit v8 on v7

--- a/solution.py
+++ b/solution.py
@@ -18,6 +18,7 @@
 KEY_BLOCK = 1024
 ROW_TILE = 512
 ATTENTION_VMEM = 32 * 1024 * 1024
+WHOLE_VMEM = 58 * 1024 * 1024
 
 
 def z_shift(dz):
@@ -168,11 +169,16 @@
     )(info, queries, *kv)
 
 
-def rows_kernel(rows_ref, hidden_ref, gain_ref, router_ref, kv_ref, x_ref, sent_ref):
+def rows_kernel(rows_ref, hidden_hbm, gain_ref, router_ref, kv_hbm, x_ref, sent_ref, hidden_ref, kv_ref, sem):
+    hidden_copy = pltpu.make_async_copy(hidden_hbm, hidden_ref, sem.at[0])
+    kv_copy = pltpu.make_async_copy(kv_hbm, kv_ref, sem.at[1])
+    hidden_copy.start()
+    kv_copy.start()
     tokens, width = hidden_ref.shape
     rows = rows_ref.shape[1]
     token = lax.broadcasted_iota(jnp.int32, (tokens, rows), 0)
     select = jnp.where(token == rows_ref[...], 1.0, 0.0).astype(jnp.bfloat16)
+    hidden_copy.wait()
     kept = lax.dot_general(select, hidden_ref[...], (((0,), (0,)), ((), ())), preferred_element_type=jnp.float32)
     normed = kept * gain_ref[...].astype(jnp.float32)
     x_ref[...] = normed.astype(jnp.bfloat16)
@@ -187,6 +193,7 @@
     turned = normed.T.astype(jnp.bfloat16)
     depth = sent_ref.shape[1] - stats.shape[0]
     halves = HD // depth
+    kv_copy.wait()
     for which in range(2):
         sums = lax.dot_general(
             kv_ref[which], turned, (((0,), (0,)), ((), ())), preferred_element_type=jnp.float32
@@ -206,9 +213,20 @@
             jax.ShapeDtypeStruct((rows, width), jnp.bfloat16),
             jax.ShapeDtypeStruct((2 * ZN, HD // 2 + 8, rows), jnp.bfloat16),
         ),
-        in_specs=[pl.BlockSpec(memory_space=pltpu.VMEM)] * 5,
+        in_specs=[
+            pl.BlockSpec(memory_space=pltpu.VMEM),
+            pl.BlockSpec(memory_space=pl.ANY),
+            pl.BlockSpec(memory_space=pltpu.VMEM),
+            pl.BlockSpec(memory_space=pltpu.VMEM),
+            pl.BlockSpec(memory_space=pl.ANY),
+        ],
         out_specs=(pl.BlockSpec(memory_space=pltpu.VMEM),) * 2,
-        compiler_params=pltpu.CompilerParams(vmem_limit_bytes=24 * 1024 * 1024),
+        scratch_shapes=[
+            pltpu.VMEM(hidden.shape, jnp.bfloat16),
+            pltpu.VMEM(key_value_weight.shape, jnp.bfloat16),
+            pltpu.SemaphoreType.DMA((2,)),
+        ],
+        compiler_params=pltpu.CompilerParams(vmem_limit_bytes=WHOLE_VMEM),
         cost_estimate=pl.CostEstimate(
             flops=4 * rows * width * hidden.shape[0], bytes_accessed=5 * 1024 * 1024, transcendentals=0
         ),
@@ -236,7 +254,7 @@
             ],
             out_specs=pl.BlockSpec((1, rows, chunk), lambda d, y: (d, 0, 0)),
         ),
-        compiler_params=pltpu.CompilerParams(vmem_limit_bytes=16 * 1024 * 1024),
+        compiler_params=pltpu.CompilerParams(vmem_limit_bytes=WHOLE_VMEM),
         cost_estimate=pl.CostEstimate(
             flops=4 * chunks * rows * width * chunk, bytes_accessed=chunks * chunk * (4 * width + 2 * rows), transcendentals=0
         ),
@@ -312,11 +330,15 @@
     router_logit = summed[HD // 2 + 1] + summed[HD // 2 + 3]
     inverse_rms = lax.rsqrt(square_sum / D + EPSILON)
     piece = (summed[: HD // 2] * inverse_rms[None, :]).astype(bf16)
+    piece, wo_sent = lax.optimization_barrier((piece, wo_sent))
     pieces = [lax.ppermute(piece, "tp", quad_shift(k)) for k in (1, 2, 3)]
-    pieces, part = lax.optimization_barrier(([piece] + pieces, part))
+    wo_got = lax.ppermute(wo_sent, "tp", y_swap())
+    pieces, part, wo_got = lax.optimization_barrier(([piece] + pieces, part, wo_got))
     query_sum = lax.psum_scatter(
         part, "tp", scatter_dimension=0, axis_index_groups=[[2 * k + h for k in range(ZN)] for h in range(2)]
     )
+    query_sum, wo_got = lax.optimization_barrier((query_sum, wo_got))
+    wo_in = share(wo_got).reshape(wo_rows, width)
     kv_own = ordered_rows(z % 4, pieces)
 
 
@@ -328,10 +350,7 @@
 
     middle = rows // 2
     over = lax.ppermute(kv_own, "ctx", [(c, (c + shard_n // 2) % shard_n) for c in range(shard_n)])
-    kv_own, wo_sent = lax.optimization_barrier((kv_own, wo_sent))
-    wo_got = lax.ppermute(wo_sent, "tp", y_swap())
-    near_left, near_right, over, wo_got = lax.optimization_barrier((x_hop(kv_own, 1), x_hop(kv_own, -1), over, wo_got))
-    wo_in = share(wo_got).reshape(wo_rows, width)
+    near_left, near_right, over = lax.optimization_barrier((x_hop(kv_own, 1), x_hop(kv_own, -1), over))
     first_half = jnp.stack([kv_own, near_left, near_right, over])
     far = x_hop(near_left[:middle], 1), x_hop(near_right[middle:], -1)
     over_left, over_right = x_hop(over, 1), x_hop(over, -1)

time: 187 us -> 202 us (1.080)
  waiting for transfers between devices: 66.6 us -> 78.3 us
  Pallas kernels: 20.8 us -> 25.6 us
  matrix products: 18.4 us -> 22.5 us
  starting transfers between devices: 49.5 us -> 46.2 us
  local copies, waits for them, and re-layouts: 12.6 us -> 9.52 us
    reduce_scatter x1, waiting for transfers between devices: 3.87 us -> 12.6 us  [shards(): lax.psum_scatter(part, 'tp', scatter_dimension=0, axis_index_groups=[[2 *...]
    unnamed x24 -> x58, local copies, waits for them, and re-layouts: 8.17 us -> 2.71 us
    ppermute x1, waiting for transfers between devices: 5.23 us -> 9.53 us  [shards(): received = lax.ppermute(for_partner.astype(bf16), 'tp', y_swap())]
    dot_general x18, matrix products: 16.4 us -> 20.6 us  [dot(): return jnp.dot(a, b, preferred_element_type=jnp.float32)]
    pallas_call x1, Pallas kernels: 5.26 us -> 7.99 us  [query_parts(): pl.pallas_call(query_kernel, out_shape=jax.ShapeDtypeStruct((chunks, rows...]
    ppermute x1, waiting for transfers between devices: 2.36 us -> 0.01 us  [shards(): wo_got = lax.ppermute(wo_sent, 'tp', y_swap())]
    pallas_call x1, Pallas kernels: 2.62 us -> 4.78 us  [rows_and_sums(): pl.pallas_call(rows_kernel, out_shape=(jax.ShapeDtypeStruct((rows, width)...]
    ppermute x1, waiting for transfers between devices: 2.38 us -> 0.34 us  [shards(): lax.ppermute(kv_own, 'ctx', [(c, (c + shard_n // 2) % shard_n) for c in r...]
  transfers between devices with their start and end apart: 30 -> 30, of which waited for: 16 -> 14; matrix products, arithmetic and copies ran while one was open for 12% -> 15% of each run, Pallas kernels for 11% -> 13%
where the time goes in v8:
time: 202 us; the launch traced here: 201 us
  waiting for transfers between devices  78.3 us (39%)
  starting transfers between devices  46.2 us (23%)
  Pallas kernels  25.6 us (13%)
  matrix products  22.5 us (11%)
  between operations  13.7 us (7%)
  local copies, waits for them, and re-layouts  9.52 us (5%)
  other arithmetic  4.91 us (2%)
    all_to_all x1, waiting for transfers between devices, shards(): exchanged = lax.all_to_all(sent, 'tp', 0, 0, tiled=True)  27.2 us
    dot_general x18, matrix products, dot(): return jnp.dot(a, b, preferred_element_type=jnp.float32)  20.6 us
    ppermute x4, waiting for transfers between devices, right(): return lax.ppermute(a.astype(bf16), 'tp', z_shift(1))  13.1 us
    ppermute x8, waiting for transfers between devices, x_hop(): return lax.ppermute(block, 'ctx', along(step))  13.1 us
    reduce_scatter x1, waiting for transfers between devices, shards(): lax.psum_scatter(part, 'tp', scatter_dimension=0, axis_index_groups=[[2 *...  12.6 us
    pallas_call x1, Pallas kernels, attention(): pl.pallas_call(attention_kernel, out_shape=jax.ShapeDtypeStruct(queries.s...  11 us
    ppermute x8, starting transfers between devices, x_hop(): return lax.ppermute(block, 'ctx', along(step))  10.7 us
    ppermute x1, waiting for transfers between devices, shards(): received = lax.ppermute(for_partner.astype(bf16), 'tp', y_swap())  9.53 us
  transfers between devices with their start and end apart: 30, of which 14 were waited for; matrix products, arithmetic and copies ran while one was open for 15% of the time, Pallas kernels for 13%

profile of v8, /device:TPU:14, one launch (start us, length us, event | category | flops | bytes accessed | tf_op | source)
XLA Modules:
  0.0 200.8 jit_solution(687482838365321554)
XLA Ops:
  7.5 2.4 %collective-permute-start = (bf16[512,256]{1,0:T(8,128)(2,1)S(1)}, bf16[512,256]{1,0:T(8,128)(2,1)S(1)}, u32[]{:S(2)}, u32[]{:S(2)}) collective-permute-start(bf16[512,256]{1,0:T(8,128)(2,1)S(1)} %constant_dynamic-slice_fusion.1), channel_id=1, source_target_pairs={{0,1},{1,0},{2,3},{3,2},{4,5},{5,4},{6,7},{7,6},{8,9},{9,8},{10,11... | collective-permute-start | bytes 786440 | tf_op jit(solution)/shard_map/ppermute | solution.py:308
  9.9 1.3 reshape.429.gain_ref
  11.2 1.3 reshape.430.router_ref
  12.4 1.3 constant_dynamic-slice_fusion.2.rows_ref
  13.7 4.8 %shard_map.73 = (bf16[512,512]{1,0:T(8,128)(2,1)}, bf16[16,72,512]{2,1,0:T(8,128)(2,1)}) custom-call(s32[1,512]{1,0:T(1,128)} %constant_dynamic-slice_fusion.2.rows_ref, bf16[1024,512]{1,0:T(8,128)(2,1)} %hidden_hbm.1, bf16[1,512]{1,0:T(2,128)(2,1)} %reshape.429.gain_ref, bf16[1,512]{1,0:T(2,128)(2,1)} %reshape.430.router_ref, bf16[2,512,512]{2,1,0:T(8,128)(2,1)} %kv_hbm.1), custom_call_target="tpu_custom_call" | custom-call | flops 1073741824 | bytes 5242880 | tf_op jit(solution)/shard_map/pallas_call | solution.py:210
  19.3 9.2 %all-to-all-start = ((bf16[16,72,512]{2,1,0:T(8,128)(2,1)}), bf16[16,72,512]{2,1,0:T(8,128)(2,1)S(1)}, u32[]{:S(2)}, u32[]{:S(2)}) async-start(bf16[16,72,512]{2,1,0:T(8,128)(2,1)} %get-tuple-element.38), calls=%async_computation | async-start | bytes 2359296 | tf_op jit(solution)/shard_map/all_to_all | solution.py:316
  28.6 3.5 %collective-permute-start.4 = (bf16[512,512]{1,0:T(8,128)(2,1)S(1)}, bf16[512,512]{1,0:T(8,128)(2,1)S(1)}, u32[]{:S(2)}, u32[]{:S(2)}) collective-permute-start(bf16[512,512]{1,0:T(8,128)(2,1)S(1)} %copy-done.17), channel_id=1, source_target_pairs={{0,1},{1,0},{2,3},{3,2},{4,5},{5,4},{6,7},{7,6},{8,9},{9,8},{10,11... | collective-permute-start | bytes 1572872 | tf_op jit(solution)/shard_map/ppermute | solution.py:312
  33.8 27.2 %all-to-all-done = bf16[16,72,512]{2,1,0:T(8,128)(2,1)S(1)} async-done(((bf16[16,72,512]{2,1,0:T(8,128)(2,1)}), bf16[16,72,512]{2,1,0:T(8,128)(2,1)S(1)}, u32[]{:S(2)}, u32[]{:S(2)}) %all-to-all-start) | async-done | bytes 1179680 | tf_op jit(solution)/shard_map/all_to_all | solution.py:316
  61.9 2.2 %collective-permute-start.2 = (bf16[64,512]{1,0:T(8,128)(2,1)S(1)}, bf16[64,512]{1,0:T(8,128)(2,1)S(1)}, u32[]{:S(2)}, u32[]{:S(2)}) collective-permute-start(bf16[64,512]{1,0:T(8,128)(2,1)S(1)} %fusion.45.refs_0_), channel_id=1, source_target_pairs={{0,4},{1,5},{2,6},{3,7},{4,0},{5,1},{6,2},{7,3},{8,12},{9,13},{10,... | collective-permute-start | bytes 196616 | tf_op jit(solution)/shard_map/ppermute | solution.py:334
  64.1 1.6 collective-permute-start.3
  66.5 8.0 %shard_map.74 = bf16[8,512,256]{2,1,0:T(8,128)(2,1)} custom-call(s32[1]{0:T(128)} %bitcast.37.y_ref, bf16[512,512]{1,0:T(8,128)(2,1)} %get-tuple-element.43.x_own_ref, bf16[512,512]{1,0:T(8,128)(2,1)} %copy-done.18, bf16[512,4096]{1,0:T(8,128)(2,1)} %w_own_ref.1, bf16[8,512,256]{2,1,0:T(8,128)(2,1)} %bitcast.69), custom_call_target="tpu_custom_call" | custom-call | flops 2147483648 | bytes 6291456 | tf_op jit(solution)/shard_map/pallas_call | solution.py:243
  75.2 1.8 shard_map.75
  77.5 1.6 collective-permute-start.7
  79.7 3.9 %collective-permute-done.6 = bf16[512,256]{1,0:T(8,128)(2,1)S(1)} collective-permute-done((bf16[512,256]{1,0:T(8,128)(2,1)}, bf16[512,256]{1,0:T(8,128)(2,1)S(1)}, u32[]{:S(2)}, u32[]{:S(2)}) %collective-permute-start.6) | collective-permute-done | bytes 262176 | tf_op jit(solution)/shard_map/ppermute | solution.py:349
  83.6 1.7 collective-permute-done.7
  85.6 1.7 collective-permute-start.9
  87.6 3.0 %collective-permute-start.11 = (bf16[256,256]{1,0:T(8,128)(2,1)S(1)}, bf16[256,256]{1,0:T(8,128)(2,1)S(1)}, u32[]{:S(2)}, u32[]{:S(2)}) collective-permute-start(bf16[256,256]{1,0:T(8,128)(2,1)S(1)} %slice.38), channel_id=1, source_target_pairs={{0,32},{16,48},{32,64},{48,80},{64,96},{80,112},{96,0},{112,16},{1... | collective-permute-start | bytes 393224 | tf_op jit(solution)/shard_map/ppermute | solution.py:349
  90.9 2.5 %collective-permute-done.11 = bf16[256,256]{1,0:T(8,128)(2,1)S(1)} collective-permute-done((bf16[256,256]{1,0:T(8,128)(2,1)S(1)}, bf16[256,256]{1,0:T(8,128)(2,1)S(1)}, u32[]{:S(2)}, u32[]{:S(2)}) %collective-permute-start.11) | collective-permute-done | bytes 131104 | tf_op jit(solution)/shard_map/ppermute | solution.py:349
  93.4 5.0 %collective-permute-done.12 = bf16[256,256]{1,0:T(8,128)(2,1)S(1)} collective-permute-done((bf16[256,256]{1,0:T(8,128)(2,1)S(1)}, bf16[256,256]{1,0:T(8,128)(2,1)S(1)}, u32[]{:S(2)}, u32[]{:S(2)}) %collective-permute-start.12) | collective-permute-done | bytes 131104 | tf_op jit(solution)/shard_map/ppermute | solution.py:349
  98.5 3.3 %collective-permute-start.13 = (bf16[256,256]{1,0:T(8,128)(2,1)S(1)}, bf16[256,256]{1,0:T(8,128)(2,1)}, u32[]{:S(2)}, u32[]{:S(2)}) collective-permute-start(bf16[256,256]{1,0:T(8,128)(2,1)S(1)} %slice.40), channel_id=1, source_target_pairs={{0,32},{16,48},{32,64},{48,80},{64,96},{80,112},{96,0},{112,16},{1... | collective-permute-start | bytes 393224 | tf_op jit(solution)/shard_map/ppermute | solution.py:349
  101.8 1.1 pad_maximum_fusion.refs_0_
  103.0 12.6 %reduce-scatter.2.cloned.1.call-done = bf16[1,512,256]{2,1,0:T(8,128)(2,1)} async-done(((bf16[8,512,256]{2,1,0:T(8,128)(2,1)}), bf16[1,512,256]{2,1,0:T(8,128)(2,1)}) %reduce-scatter.2.cloned.1.call-update) | async-done | bytes 262160 | tf_op jit(solution)/shard_map/reduce_scatter | solution.py:337
  116.6 1.2 pad_maximum_fusion.1.refs_1_
  119.1 1.6 collective-permute-done.16.refs_3_
  120.7 11.0 %shard_map.76 = bf16[512,256]{1,0:T(8,128)(2,1)S(1)} custom-call(s32[16,3]{1,0:T(8,128)S(1)} %copy.11.info_ref, bf16[512,256]{1,0:T(8,128)(2,1)S(1)} %multiply_convert_fusion.2.q_ref, bf16[4,512,256]{2,1,0:T(8,128)(2,1)S(1)} %pad_maximum_fusion.refs_0_, bf16[4,512,256]{2,1,0:T(8,128)(2,1)S(1)} %pad_maximum_fusion.1.refs_1_, ...), custom_call_target="tpu_custom_call" | custom-call | flops 4294967296 | bytes 4194304 | tf_op jit(solution)/shard_map/pallas_call | solution.py:152
  131.7 1.4 collective-permute-start.17
  133.1 1.9 collective-permute-start.18
  135.0 5.7 %collective-permute-done.17 = bf16[512,256]{1,0:T(8,128)(2,1)S(1)} collective-permute-done((bf16[512,256]{1,0:T(8,128)(2,1)S(1)}, bf16[512,256]{1,0:T(8,128)(2,1)S(1)}, u32[]{:S(2)}, u32[]{:S(2)}) %collective-permute-start.17) | collective-permute-done | bytes 262176 | tf_op jit(solution)/shard_map/ppermute | solution.py:366
  142.0 2.3 %collective-permute-start.20 = (bf16[512,256]{1,0:T(8,128)(2,1)S(1)}, bf16[512,256]{1,0:T(8,128)(2,1)S(1)}, u32[]{:S(2)}, u32[]{:S(2)}) collective-permute-start(bf16[512,256]{1,0:T(8,128)(2,1)S(1)} %collective-permute-done.18), channel_id=1, source_target_pairs={{0,14},{1,15},{2,0},{3,1},{4,2},{5,3},{6,4},{7,5},{8,6},{9,7},{10,... | collective-permute-start | bytes 786440 | tf_op jit(solution)/shard_map/ppermute | solution.py:369
  144.4 1.2 fusion.40
  145.6 1.3 fusion.42
  146.9 4.4 %collective-permute-done.19 = bf16[512,256]{1,0:T(8,128)(2,1)S(1)} collective-permute-done((bf16[512,256]{1,0:T(8,128)(2,1)S(1)}, bf16[512,256]{1,0:T(8,128)(2,1)S(1)}, u32[]{:S(2)}, u32[]{:S(2)}) %collective-permute-start.19) | collective-permute-done | bytes 262176 | tf_op jit(solution)/shard_map/ppermute | solution.py:366
  151.5 1.7 collective-permute-start.21
  153.3 1.6 collective-permute-start.22
  154.9 1.2 fusion.36
  156.1 2.2 %fusion.38 = f32[512,512]{1,0:T(8,128)} fusion(bf16[512,256]{1,0:T(8,128)(2,1)S(1)} %collective-permute-done.19, bf16[4096,512]{1,0:T(8,128)(2,1)} %param.12, s32[]{:T(128)S(6)} %select_n.223), kind=kOutput, calls=%fused_computation.48 | convolution fusion | flops 134217728 | bytes 1572868 | tf_op jit(solution)/shard_map/dot_general | solution.py:286
  158.3 3.0 %collective-permute-done.21 = bf16[512,256]{1,0:T(8,128)(2,1)S(1)} collective-permute-done((bf16[512,256]{1,0:T(8,128)(2,1)S(1)}, bf16[512,256]{1,0:T(8,128)(2,1)S(1)}, u32[]{:S(2)}, u32[]{:S(2)}) %collective-permute-start.21) | collective-permute-done | bytes 262176 | tf_op jit(solution)/shard_map/ppermute | solution.py:366
  161.4 3.1 %collective-permute-start.24 = (bf16[512,128]{1,0:T(8,128)(2,1)S(1)}, bf16[512,128]{1,0:T(8,128)(2,1)S(1)}, u32[]{:S(2)}, u32[]{:S(2)}) collective-permute-start(bf16[512,128]{1,0:T(8,128)(2,1)S(1)} %slice.43), channel_id=1, source_target_pairs={{0,14},{1,15},{2,0},{3,1},{4,2},{5,3},{6,4},{7,5},{8,6},{9,7},{10,... | collective-permute-start | bytes 393224 | tf_op jit(solution)/shard_map/ppermute | solution.py:369
  165.2 2.2 %fusion.32 = f32[512,512]{1,0:T(8,128)} fusion(bf16[512,256]{1,0:T(8,128)(2,1)S(1)} %collective-permute-done.22, bf16[4096,512]{1,0:T(8,128)(2,1)} %param.12, s32[]{:T(128)S(6)} %select_n.229), kind=kOutput, calls=%fused_computation.42 | convolution fusion | flops 134217728 | bytes 1572868 | tf_op jit(solution)/shard_map/dot_general | solution.py:286
  167.4 2.2 %fusion.34 = f32[512,512]{1,0:T(8,128)} fusion(bf16[512,256]{1,0:T(8,128)(2,1)S(1)} %collective-permute-done.21, bf16[4096,512]{1,0:T(8,128)(2,1)} %param.12, s32[]{:T(128)S(6)} %select_n.227), kind=kOutput, calls=%fused_computation.44 | convolution fusion | flops 134217728 | bytes 1572868 | tf_op jit(solution)/shard_map/dot_general | solution.py:286
  170.3 2.2 %fusion.50 = f32[512,512]{1,0:T(8,128)} fusion(bf16[512,128]{1,0:T(8,128)(2,1)S(1)} %collective-permute-done.24, bf16[4096,512]{1,0:T(8,128)(2,1)} %param.12, s32[]{:T(128)S(6)} %select_n.232), kind=kOutput, calls=%fused_computation.61 | convolution fusion | flops 67108864 | bytes 1310724 | tf_op jit(solution)/shard_map/dot_general | solution.py:286
  172.5 1.5 fusion.20
  174.0 1.4 fusion.22
  177.8 2.0 %collective-permute-start.25 = (bf16[512,512]{1,0:T(8,128)(2,1)S(1)}, bf16[512,512]{1,0:T(8,128)(2,1)S(1)}, u32[]{:S(2)}, u32[]{:S(2)}) collective-permute-start(bf16[512,512]{1,0:T(8,128)(2,1)S(1)} %fusion.16), channel_id=1, source_target_pairs={{0,1},{1,0},{2,3},{3,2},{4,5},{5,4},{6,7},{7,6},{8,9},{9,8},{10,11... | collective-permute-start | bytes 1572872 | tf_op jit(solution)/shard_map/ppermute | solution.py:394
  179.8 1.2 fusion.52
  181.1 1.6 fusion.9
  182.7 9.5 %collective-permute-done.25 = bf16[512,512]{1,0:T(8,128)(2,1)S(1)} collective-permute-done((bf16[512,512]{1,0:T(8,128)(2,1)S(1)}, bf16[512,512]{1,0:T(8,128)(2,1)S(1)}, u32[]{:S(2)}, u32[]{:S(2)}) %collective-permute-start.25) | collective-permute-done | bytes 524320 | tf_op jit(solution)/shard_map/ppermute | solution.py:394
  192.3 2.0 fusion.1
  (125 shorter events, 15.5 us)
Async XLA Ops:
  6.5 59.2 %all-gather.5.cloned.1.call-start = ((), (), s32[]{:S(2)}) async-start(), calls=%async_computation.3 | async-start | bytes 2359296 | tf_op jit(solution)/shard_map/all_gather | solution.py:305
  7.5 11.1 %collective-permute-start = (bf16[512,256]{1,0:T(8,128)(2,1)S(1)}, bf16[512,256]{1,0:T(8,128)(2,1)S(1)}, u32[]{:S(2)}, u32[]{:S(2)}) collective-permute-start(bf16[512,256]{1,0:T(8,128)(2,1)S(1)} %constant_dynamic-slice_fusion.1), channel_id=1, source_target_pairs={{0,1},{1,0},{2,3},{3,2},{4,5},{5,4},{6,7},{7,6},{8,9},{9,8},{10,11... | collective-permute-start | bytes 786440 | tf_op jit(solution)/shard_map/ppermute | solution.py:308
  18.5 10.0 %copy-start.17 = (bf16[512,512]{1,0:T(8,128)(2,1)S(1)}, bf16[512,512]{1,0:T(8,128)(2,1)}, u32[]{:S(2)}) copy-start(bf16[512,512]{1,0:T(8,128)(2,1)} %get-tuple-element.43.x_own_ref) | copy-start | bytes 1572868
  18.6 13.8 %copy-start.27 = (s32[16,512]{1,0:T(8,128)S(1)}, s32[16,512]{1,0:T(8,128)}, u32[]{:S(2)}) copy-start(s32[16,512]{1,0:T(8,128)} %param.13) | copy-start | bytes 98308
  19.3 41.7 %all-to-all-start = ((bf16[16,72,512]{2,1,0:T(8,128)(2,1)}), bf16[16,72,512]{2,1,0:T(8,128)(2,1)S(1)}, u32[]{:S(2)}, u32[]{:S(2)}) async-start(bf16[16,72,512]{2,1,0:T(8,128)(2,1)} %get-tuple-element.38), calls=%async_computation | async-start | bytes 2359296 | tf_op jit(solution)/shard_map/all_to_all | solution.py:316
  28.5 87.1 %reduce-scatter.2.cloned.1.call-start = ((), (), s32[]{:S(2)}) async-start(), calls=%async_computation.2 | async-start | bytes 2359296 | tf_op jit(solution)/shard_map/reduce_scatter | solution.py:337
  28.6 37.1 %collective-permute-start.4 = (bf16[512,512]{1,0:T(8,128)(2,1)S(1)}, bf16[512,512]{1,0:T(8,128)(2,1)S(1)}, u32[]{:S(2)}, u32[]{:S(2)}) collective-permute-start(bf16[512,512]{1,0:T(8,128)(2,1)S(1)} %copy-done.17), channel_id=1, source_target_pairs={{0,1},{1,0},{2,3},{3,2},{4,5},{5,4},{6,7},{7,6},{8,9},{9,8},{10,11... | collective-permute-start | bytes 1572872 | tf_op jit(solution)/shard_map/ppermute | solution.py:312
  61.2 13.5 %copy-start.21 = (bf16[64,512]{1,0:T(8,128)(2,1)}, bf16[64,512]{1,0:T(8,128)(2,1)S(1)}, u32[]{:S(2)}) copy-start(bf16[64,512]{1,0:T(8,128)(2,1)S(1)} %fusion.45.refs_0_) | copy-start | bytes 196612
  61.2 13.3 %collective-permute-start.5 = (bf16[256,512]{1,0:T(8,128)(2,1)S(1)}, bf16[256,512]{1,0:T(8,128)(2,1)S(1)}, u32[]{:S(2)}, u32[]{:S(2)}) collective-permute-start(bf16[256,512]{1,0:T(8,128)(2,1)S(1)} %constant_dynamic-slice_fusion), channel_id=1, source_target_pairs={{0,1},{1,0},{2,3},{3,2},{4,5},{5,4},{6,7},{7,6},{8,9},{9,8},{10,11... | collective-permute-start | bytes 786440 | tf_op jit(solution)/shard_map/ppermute | solution.py:335
  61.9 12.6 %collective-permute-start.1 = (bf16[64,512]{1,0:T(8,128)(2,1)S(1)}, bf16[64,512]{1,0:T(8,128)(2,1)S(1)}, u32[]{:S(2)}, u32[]{:S(2)}) collective-permute-start(bf16[64,512]{1,0:T(8,128)(2,1)S(1)} %fusion.45.refs_0_), channel_id=1, source_target_pairs={{0,2},{1,3},{2,4},{3,5},{4,6},{5,7},{6,0},{7,1},{8,10},{9,11},{10,... | collective-permute-start | bytes 196616 | tf_op jit(solution)/shard_map/ppermute | solution.py:334
  61.9 12.6 %collective-permute-start.2 = (bf16[64,512]{1,0:T(8,128)(2,1)S(1)}, bf16[64,512]{1,0:T(8,128)(2,1)S(1)}, u32[]{:S(2)}, u32[]{:S(2)}) collective-permute-start(bf16[64,512]{1,0:T(8,128)(2,1)S(1)} %fusion.45.refs_0_), channel_id=1, source_target_pairs={{0,4},{1,5},{2,6},{3,7},{4,0},{5,1},{6,2},{7,3},{8,12},{9,13},{10,... | collective-permute-start | bytes 196616 | tf_op jit(solution)/shard_map/ppermute | solution.py:334
  64.1 10.4 %collective-permute-start.3 = (bf16[64,512]{1,0:T(8,128)(2,1)S(1)}, bf16[64,512]{1,0:T(8,128)(2,1)S(1)}, u32[]{:S(2)}, u32[]{:S(2)}) collective-permute-start(bf16[64,512]{1,0:T(8,128)(2,1)S(1)} %fusion.45.refs_0_), channel_id=1, source_target_pairs={{0,6},{1,7},{2,0},{3,1},{4,2},{5,3},{6,4},{7,5},{8,14},{9,15},{10,... | collective-permute-start | bytes 196616 | tf_op jit(solution)/shard_map/ppermute | solution.py:334
  74.5 28.4 %copy-start.22 = (bf16[256,512]{1,0:T(8,128)(2,1)}, bf16[256,512]{1,0:T(8,128)(2,1)S(1)}, u32[]{:S(2)}) copy-start(bf16[256,512]{1,0:T(8,128)(2,1)S(1)} %collective-permute-done.5) | copy-start | bytes 786436
  74.6 97.9 %all-gather.7.cloned.1.call-start = ((), (), s32[]{:S(2)}) async-start(), calls=%async_computation.4 | async-start | bytes 2359296 | tf_op jit(solution)/shard_map/all_gather | solution.py:305
  77.0 6.6 %collective-permute-start.6 = (bf16[512,256]{1,0:T(8,128)(2,1)}, bf16[512,256]{1,0:T(8,128)(2,1)S(1)}, u32[]{:S(2)}, u32[]{:S(2)}) collective-permute-start(bf16[512,256]{1,0:T(8,128)(2,1)} %shard_map.75), channel_id=1, source_target_pairs={{0,32},{16,48},{32,64},{48,80},{64,96},{80,112},{96,0},{112,16},{1... | collective-permute-start | bytes 786440 | tf_op jit(solution)/shard_map/ppermute | solution.py:349
  77.5 7.8 %collective-permute-start.7 = (bf16[512,256]{1,0:T(8,128)(2,1)}, bf16[512,256]{1,0:T(8,128)(2,1)S(1)}, u32[]{:S(2)}, u32[]{:S(2)}) collective-permute-start(bf16[512,256]{1,0:T(8,128)(2,1)} %shard_map.75), channel_id=1, source_target_pairs={{0,96},{16,112},{32,0},{48,16},{64,32},{80,48},{96,64},{112,80},{1... | collective-permute-start | bytes 786440 | tf_op jit(solution)/shard_map/ppermute | solution.py:349
  79.0 6.6 %collective-permute-start.8 = (bf16[512,256]{1,0:T(8,128)(2,1)}, bf16[512,256]{1,0:T(8,128)(2,1)S(1)}, u32[]{:S(2)}, u32[]{:S(2)}) collective-permute-start(bf16[512,256]{1,0:T(8,128)(2,1)} %shard_map.75), channel_id=1, source_target_pairs={{0,128},{16,144},{32,160},{48,176},{64,192},{80,208},{96,224},{112... | collective-permute-start | bytes 786440 | tf_op jit(solution)/shard_map/ppermute | solution.py:352
  85.6 12.8 %collective-permute-start.9 = (bf16[512,256]{1,0:T(8,128)(2,1)S(1)}, bf16[512,256]{1,0:T(8,128)(2,1)S(1)}, u32[]{:S(2)}, u32[]{:S(2)}) collective-permute-start(bf16[512,256]{1,0:T(8,128)(2,1)S(1)} %collective-permute-done.8), channel_id=1, source_target_pairs={{0,32},{16,48},{32,64},{48,80},{64,96},{80,112},{96,0},{112,16},{1... | collective-permute-start | bytes 786440 | tf_op jit(solution)/shard_map/ppermute | solution.py:349
  87.3 11.1 %collective-permute-start.10 = (bf16[512,256]{1,0:T(8,128)(2,1)S(1)}, bf16[512,256]{1,0:T(8,128)(2,1)S(1)}, u32[]{:S(2)}, u32[]{:S(2)}) collective-permute-start(bf16[512,256]{1,0:T(8,128)(2,1)S(1)} %collective-permute-done.8), channel_id=1, source_target_pairs={{0,96},{16,112},{32,0},{48,16},{64,32},{80,48},{96,64},{112,80},{1... | collective-permute-start | bytes 786440 | tf_op jit(solution)/shard_map/ppermute | solution.py:349
  87.6 5.7 %collective-permute-start.11 = (bf16[256,256]{1,0:T(8,128)(2,1)S(1)}, bf16[256,256]{1,0:T(8,128)(2,1)S(1)}, u32[]{:S(2)}, u32[]{:S(2)}) collective-permute-start(bf16[256,256]{1,0:T(8,128)(2,1)S(1)} %slice.38), channel_id=1, source_target_pairs={{0,32},{16,48},{32,64},{48,80},{64,96},{80,112},{96,0},{112,16},{1... | collective-permute-start | bytes 393224 | tf_op jit(solution)/shard_map/ppermute | solution.py:349
  90.6 7.7 %collective-permute-start.12 = (bf16[256,256]{1,0:T(8,128)(2,1)S(1)}, bf16[256,256]{1,0:T(8,128)(2,1)S(1)}, u32[]{:S(2)}, u32[]{:S(2)}) collective-permute-start(bf16[256,256]{1,0:T(8,128)(2,1)S(1)} %slice.39), channel_id=1, source_target_pairs={{0,96},{16,112},{32,0},{48,16},{64,32},{80,48},{96,64},{112,80},{1... | collective-permute-start | bytes 393224 | tf_op jit(solution)/shard_map/ppermute | solution.py:349
  98.4 18.2 %copy-start.15 = (bf16[512,256]{1,0:T(8,128)(2,1)}, bf16[512,256]{1,0:T(8,128)(2,1)S(1)}, u32[]{:S(2)}) copy-start(bf16[512,256]{1,0:T(8,128)(2,1)S(1)} %collective-permute-done.9) | copy-start | bytes 786436
  98.4 18.2 %copy-start.16 = (bf16[512,256]{1,0:T(8,128)(2,1)}, bf16[512,256]{1,0:T(8,128)(2,1)S(1)}, u32[]{:S(2)}) copy-start(bf16[512,256]{1,0:T(8,128)(2,1)S(1)} %collective-permute-done.10) | copy-start | bytes 786436
  98.4 17.3 %collective-permute-start.14 = (bf16[256,256]{1,0:T(8,128)(2,1)S(1)}, bf16[256,256]{1,0:T(8,128)(2,1)S(1)}, u32[]{:S(2)}, u32[]{:S(2)}) collective-permute-start(bf16[256,256]{1,0:T(8,128)(2,1)S(1)} %slice.41), channel_id=1, source_target_pairs={{0,96},{16,112},{32,0},{48,16},{64,32},{80,48},{96,64},{112,80},{1... | collective-permute-start | bytes 393224 | tf_op jit(solution)/shard_map/ppermute | solution.py:349
  98.5 17.2 %collective-permute-start.13 = (bf16[256,256]{1,0:T(8,128)(2,1)S(1)}, bf16[256,256]{1,0:T(8,128)(2,1)}, u32[]{:S(2)}, u32[]{:S(2)}) collective-permute-start(bf16[256,256]{1,0:T(8,128)(2,1)S(1)} %slice.40), channel_id=1, source_target_pairs={{0,32},{16,48},{32,64},{48,80},{64,96},{80,112},{96,0},{112,16},{1... | collective-permute-start | bytes 393224 | tf_op jit(solution)/shard_map/ppermute | solution.py:349
  102.9 16.2 %collective-permute-start.15 = (bf16[4,512,256]{2,1,0:T(8,128)(2,1)S(1)}, bf16[4,512,256]{2,1,0:T(8,128)(2,1)S(1)}, u32[]{:S(2)}, u32[]{:S(2)}) collective-permute-start(bf16[4,512,256]{2,1,0:T(8,128)(2,1)S(1)} %pad_maximum_fusion.refs_0_), channel_id=1, source_target_pairs={{0,16},{16,0},{32,48},{48,32},{64,80},{80,64},{96,112},{112,96},{1... | collective-permute-start | bytes 3145736 | tf_op jit(solution)/shard_map/ppermute | solution.py:362
  117.8 2.9 %collective-permute-start.16 = (bf16[4,512,256]{2,1,0:T(8,128)(2,1)S(1)}, bf16[4,512,256]{2,1,0:T(8,128)(2,1)}, u32[]{:S(2)}, u32[]{:S(2)}) collective-permute-start(bf16[4,512,256]{2,1,0:T(8,128)(2,1)S(1)} %pad_maximum_fusion.1.refs_1_), channel_id=1, source_target_pairs={{0,16},{16,0},{32,48},{48,32},{64,80},{80,64},{96,112},{112,96},{1... | collective-permute-start | bytes 3145736 | tf_op jit(solution)/shard_map/ppermute | solution.py:362
  131.7 9.0 %collective-permute-start.17 = (bf16[512,256]{1,0:T(8,128)(2,1)S(1)}, bf16[512,256]{1,0:T(8,128)(2,1)S(1)}, u32[]{:S(2)}, u32[]{:S(2)}) collective-permute-start(bf16[512,256]{1,0:T(8,128)(2,1)S(1)} %shard_map.76), channel_id=1, source_target_pairs={{0,2},{1,3},{2,4},{3,5},{4,6},{5,7},{6,8},{7,9},{8,10},{9,11},{10,... | collective-permute-start | bytes 786440 | tf_op jit(solution)/shard_map/ppermute | solution.py:366
  133.1 8.1 %collective-permute-start.18 = (bf16[512,256]{1,0:T(8,128)(2,1)S(1)}, bf16[512,256]{1,0:T(8,128)(2,1)S(1)}, u32[]{:S(2)}, u32[]{:S(2)}) collective-permute-start(bf16[512,256]{1,0:T(8,128)(2,1)S(1)} %shard_map.76), channel_id=1, source_target_pairs={{0,14},{1,15},{2,0},{3,1},{4,2},{5,3},{6,4},{7,5},{8,6},{9,7},{10,... | collective-permute-start | bytes 786440 | tf_op jit(solution)/shard_map/ppermute | solution.py:369
  140.7 12.6 %copy-start.7 = (bf16[512,256]{1,0:T(8,128)(2,1)}, bf16[512,256]{1,0:T(8,128)(2,1)S(1)}, u32[]{:S(2)}) copy-start(bf16[512,256]{1,0:T(8,128)(2,1)S(1)} %collective-permute-done.17) | copy-start | bytes 786436
  141.2 12.1 %copy-start.9 = (bf16[512,256]{1,0:T(8,128)(2,1)}, bf16[512,256]{1,0:T(8,128)(2,1)S(1)}, u32[]{:S(2)}) copy-start(bf16[512,256]{1,0:T(8,128)(2,1)S(1)} %collective-permute-done.18) | copy-start | bytes 786436
  141.2 10.1 %collective-permute-start.19 = (bf16[512,256]{1,0:T(8,128)(2,1)S(1)}, bf16[512,256]{1,0:T(8,128)(2,1)S(1)}, u32[]{:S(2)}, u32[]{:S(2)}) collective-permute-start(bf16[512,256]{1,0:T(8,128)(2,1)S(1)} %collective-permute-done.17), channel_id=1, source_target_pairs={{0,2},{1,3},{2,4},{3,5},{4,6},{5,7},{6,8},{7,9},{8,10},{9,11},{10,... | collective-permute-start | bytes 786440 | tf_op jit(solution)/shard_map/ppermute | solution.py:366
  142.0 9.5 %collective-permute-start.20 = (bf16[512,256]{1,0:T(8,128)(2,1)S(1)}, bf16[512,256]{1,0:T(8,128)(2,1)S(1)}, u32[]{:S(2)}, u32[]{:S(2)}) collective-permute-start(bf16[512,256]{1,0:T(8,128)(2,1)S(1)} %collective-permute-done.18), channel_id=1, source_target_pairs={{0,14},{1,15},{2,0},{3,1},{4,2},{5,3},{6,4},{7,5},{8,6},{9,7},{10,... | collective-permute-start | bytes 786440 | tf_op jit(solution)/shard_map/ppermute | solution.py:369
  151.2 16.1 %copy-start.11 = (bf16[512,256]{1,0:T(8,128)(2,1)}, bf16[512,256]{1,0:T(8,128)(2,1)S(1)}, u32[]{:S(2)}) copy-start(bf16[512,256]{1,0:T(8,128)(2,1)S(1)} %collective-permute-done.19) | copy-start | bytes 786436
  151.5 15.8 %copy-start.13 = (bf16[512,256]{1,0:T(8,128)(2,1)}, bf16[512,256]{1,0:T(8,128)(2,1)S(1)}, u32[]{:S(2)}) copy-start(bf16[512,256]{1,0:T(8,128)(2,1)S(1)} %collective-permute-done.20) | copy-start | bytes 786436
  151.5 9.8 %collective-permute-start.21 = (bf16[512,256]{1,0:T(8,128)(2,1)S(1)}, bf16[512,256]{1,0:T(8,128)(2,1)S(1)}, u32[]{:S(2)}, u32[]{:S(2)}) collective-permute-start(bf16[512,256]{1,0:T(8,128)(2,1)S(1)} %collective-permute-done.19), channel_id=1, source_target_pairs={{0,2},{1,3},{2,4},{3,5},{4,6},{5,7},{6,8},{7,9},{8,10},{9,11},{10,... | collective-permute-start | bytes 786440 | tf_op jit(solution)/shard_map/ppermute | solution.py:366
  153.3 8.1 %collective-permute-start.22 = (bf16[512,256]{1,0:T(8,128)(2,1)S(1)}, bf16[512,256]{1,0:T(8,128)(2,1)S(1)}, u32[]{:S(2)}, u32[]{:S(2)}) collective-permute-start(bf16[512,256]{1,0:T(8,128)(2,1)S(1)} %collective-permute-done.20), channel_id=1, source_target_pairs={{0,14},{1,15},{2,0},{3,1},{4,2},{5,3},{6,4},{7,5},{8,6},{9,7},{10,... | collective-permute-start | bytes 786440 | tf_op jit(solution)/shard_map/ppermute | solution.py:369
  161.4 6.0 %copy-start.5 = (bf16[512,256]{1,0:T(8,128)(2,1)}, bf16[512,256]{1,0:T(8,128)(2,1)S(1)}, u32[]{:S(2)}) copy-start(bf16[512,256]{1,0:T(8,128)(2,1)S(1)} %collective-permute-done.21) | copy-start | bytes 786436
  161.4 8.3 %copy-start.6 = (bf16[512,256]{1,0:T(8,128)(2,1)}, bf16[512,256]{1,0:T(8,128)(2,1)S(1)}, u32[]{:S(2)}) copy-start(bf16[512,256]{1,0:T(8,128)(2,1)S(1)} %collective-permute-done.22) | copy-start | bytes 786436
  161.4 8.3 %collective-permute-start.24 = (bf16[512,128]{1,0:T(8,128)(2,1)S(1)}, bf16[512,128]{1,0:T(8,128)(2,1)S(1)}, u32[]{:S(2)}, u32[]{:S(2)}) collective-permute-start(bf16[512,128]{1,0:T(8,128)(2,1)S(1)} %slice.43), channel_id=1, source_target_pairs={{0,14},{1,15},{2,0},{3,1},{4,2},{5,3},{6,4},{7,5},{8,6},{9,7},{10,... | collective-permute-start | bytes 393224 | tf_op jit(solution)/shard_map/ppermute | solution.py:369
  165.2 11.7 %collective-permute-start.23 = (bf16[512,128]{1,0:T(8,128)(2,1)}, bf16[512,128]{1,0:T(8,128)(2,1)S(1)}, u32[]{:S(2)}, u32[]{:S(2)}) collective-permute-start(bf16[512,128]{1,0:T(8,128)(2,1)} %slice.42), channel_id=1, source_target_pairs={{0,2},{1,3},{2,4},{3,5},{4,6},{5,7},{6,8},{7,9},{8,10},{9,11},{10,... | collective-permute-start | bytes 393224 | tf_op jit(solution)/shard_map/ppermute | solution.py:366
  172.5 3.2 %copy-start.12 = (bf16[512,256]{1,0:T(8,128)(2,1)S(1)}, bf16[512,256]{1,0:T(8,128)(2,1)}, u32[]{:S(2)}) copy-start(bf16[512,256]{1,0:T(8,128)(2,1)} %copy-done.11) | copy-start | bytes 786436
  177.2 3.8 %copy-start = (f32[512,512]{1,0:T(8,128)S(1)}, f32[512,512]{1,0:T(8,128)}, u32[]{:S(2)}) copy-start(f32[512,512]{1,0:T(8,128)} %fusion.38) | copy-start | bytes 3145732
  177.2 3.8 %copy-start.1 = (f32[512,512]{1,0:T(8,128)S(1)}, f32[512,512]{1,0:T(8,128)}, u32[]{:S(2)}) copy-start(f32[512,512]{1,0:T(8,128)} %fusion.32) | copy-start | bytes 3145732
  177.2 3.8 %copy-start.2 = (f32[512,512]{1,0:T(8,128)S(1)}, f32[512,512]{1,0:T(8,128)}, u32[]{:S(2)}) copy-start(f32[512,512]{1,0:T(8,128)} %fusion.34) | copy-start | bytes 3145732
  177.2 3.8 %copy-start.3 = (f32[512,512]{1,0:T(8,128)S(1)}, f32[512,512]{1,0:T(8,128)}, u32[]{:S(2)}) copy-start(f32[512,512]{1,0:T(8,128)} %fusion.50) | copy-start | bytes 3145732
  177.8 14.4 %collective-permute-start.25 = (bf16[512,512]{1,0:T(8,128)(2,1)S(1)}, bf16[512,512]{1,0:T(8,128)(2,1)S(1)}, u32[]{:S(2)}, u32[]{:S(2)}) collective-permute-start(bf16[512,512]{1,0:T(8,128)(2,1)S(1)} %fusion.16), channel_id=1, source_target_pairs={{0,1},{1,0},{2,3},{3,2},{4,5},{5,4},{6,7},{7,6},{8,9},{9,8},{10,11... | collective-permute-start | bytes 1572872 | tf_op jit(solution)/shard_map/ppermute | solution.py:394
  181.1 11.2 %copy-start.28 = (s32[1,512]{1,0:T(1,128)S(1)}, s32[1,512]{1,0:T(1,128)}, u32[]{:S(2)}) copy-start(s32[1,512]{1,0:T(1,128)} %constant_dynamic-slice_fusion.2.rows_ref) | copy-start | bytes 6148
  (11 other events, 13.7 us)
Sparse Core Ops, SparseCore 0:
  19.4 28.0 all-gather.4
  74.7 40.8 reduce-scatter.1
  117.5 25.7 all-gather.6

commit v9 on v7

--- a/solution.py
+++ b/solution.py
@@ -215,34 +215,6 @@
     )(own_rows, hidden, norm_gain.reshape(1, width), router_weight.reshape(1, width), key_value_weight)
 
 
-def query_kernel(y_ref, x_own_ref, x_in_ref, w_own_ref, w_in_ref, o_ref):
-    o_ref[0] = (dot(x_own_ref[...], w_own_ref[...]) + dot(x_in_ref[...], w_in_ref[0])).astype(jnp.bfloat16)
-
-
-def query_parts(y, x_own, x_in, query_weight, wq_in):
-    chunks, width, chunk = wq_in.shape
-    rows = x_own.shape[0]
-    return pl.pallas_call(
-        query_kernel,
-        out_shape=jax.ShapeDtypeStruct((chunks, rows, chunk), jnp.bfloat16),
-        grid_spec=pltpu.PrefetchScalarGridSpec(
-            num_scalar_prefetch=1,
-            grid=(chunks,),
-            in_specs=[
-                pl.BlockSpec((rows, width), lambda d, y: (0, 0)),
-                pl.BlockSpec((rows, width), lambda d, y: (0, 0)),
-                pl.BlockSpec((width, chunk), lambda d, y: (0, y[0] * chunks + d)),
-                pl.BlockSpec((1, width, chunk), lambda d, y: (d, 0, 0)),
-            ],
-            out_specs=pl.BlockSpec((1, rows, chunk), lambda d, y: (d, 0, 0)),
-        ),
-        compiler_params=pltpu.CompilerParams(vmem_limit_bytes=16 * 1024 * 1024),
-        cost_estimate=pl.CostEstimate(
-            flops=4 * chunks * rows * width * chunk, bytes_accessed=chunks * chunk * (4 * width + 2 * rows), transcendentals=0
-        ),
-    )(y[None].astype(jnp.int32), x_own, x_in, query_weight, wq_in)
-
-
 def order_kernel(at_ref, *refs):
     pieces, o_ref, scratch_ref = refs[:4], refs[4], refs[5]
     depth = pieces[0].shape[0]
@@ -268,6 +240,56 @@
     return jnp.dot(a, b, preferred_element_type=jnp.float32)
 
 
+def own_kernel(y_ref, x_ref, w_ref, o_ref):
+    o_ref[0] = dot(x_ref[...], w_ref[...]).astype(jnp.bfloat16)
+
+
+def in_kernel(x_ref, w_ref, own_ref, o_ref):
+    o_ref[0] = (dot(x_ref[...], w_ref[0]) + own_ref[0].astype(jnp.float32)).astype(jnp.bfloat16)
+
+
+def own_parts(y, x_own, query_weight, chunks):
+    rows, width = x_own.shape
+    chunk = query_weight.shape[1] // 2 // chunks
+    return pl.pallas_call(
+        own_kernel,
+        out_shape=jax.ShapeDtypeStruct((chunks, rows, chunk), jnp.bfloat16),
+        grid_spec=pltpu.PrefetchScalarGridSpec(
+            num_scalar_prefetch=1,
+            grid=(chunks,),
+            in_specs=[
+                pl.BlockSpec((rows, width), lambda d, y: (0, 0)),
+                pl.BlockSpec((width, chunk), lambda d, y: (0, y[0] * chunks + d)),
+            ],
+            out_specs=pl.BlockSpec((1, rows, chunk), lambda d, y: (d, 0, 0)),
+        ),
+        compiler_params=pltpu.CompilerParams(vmem_limit_bytes=16 * 1024 * 1024),
+        cost_estimate=pl.CostEstimate(
+            flops=2 * chunks * rows * width * chunk, bytes_accessed=chunks * chunk * 2 * (width + rows), transcendentals=0
+        ),
+    )(y[None].astype(jnp.int32), x_own, query_weight)
+
+
+def all_parts(x_in, wq_in, own):
+    chunks, rows, chunk = own.shape
+    width = x_in.shape[1]
+    return pl.pallas_call(
+        in_kernel,
+        out_shape=jax.ShapeDtypeStruct(own.shape, jnp.bfloat16),
+        grid=(chunks,),
+        in_specs=[
+            pl.BlockSpec((rows, width), lambda d: (0, 0)),
+            pl.BlockSpec((1, width, chunk), lambda d: (d, 0, 0)),
+            pl.BlockSpec((1, rows, chunk), lambda d: (d, 0, 0)),
+        ],
+        out_specs=pl.BlockSpec((1, rows, chunk), lambda d: (d, 0, 0)),
+        compiler_params=pltpu.CompilerParams(vmem_limit_bytes=16 * 1024 * 1024),
+        cost_estimate=pl.CostEstimate(
+            flops=2 * chunks * rows * width * chunk, bytes_accessed=chunks * chunk * 2 * (width + 2 * rows), transcendentals=0
+        ),
+    )(x_in, wq_in, own)
+
+
 def shards(hidden, norm_gain, router_weight, query_weight, key_value_weight, out_weight, kept_rows):
     bf16 = jnp.bfloat16
     shard = lax.axis_index("ctx")
@@ -296,7 +318,7 @@
     sent, wq_got = lax.optimization_barrier((sent, wq_got))
     wq_in = share(wq_got)
     exchanged = lax.all_to_all(sent, "tp", 0, 0, tiled=True)
-    part = query_parts(y, x_own, x_in, query_weight, wq_in)
+    part = own_parts(y, x_own, query_weight, ZN)
     x_n = shard_n // 4
     at_y, at_x, core = shard // (2 * x_n), shard // 2 % x_n, shard % 2
     offsets = [(0, 0), (-1, 0), (1, 0), (0, 1), (-1, 1), (1, 1), (2, 0), (2, 1)]
@@ -306,17 +328,22 @@
     info = packing(counts, shard, ids)
     wo_rows = out_weight.shape[0] // 2
     wo_sent = lax.dynamic_slice(out_weight, ((1 - y) * wo_rows + mine * chunk, 0), (chunk, width))
-    exchanged, info, wo_sent = lax.optimization_barrier((exchanged, info, wo_sent))
+    exchanged, info, wo_sent, part, wq_in = lax.optimization_barrier((exchanged, info, wo_sent, part, wq_in))
+    part = all_parts(x_in, wq_in, part)
     summed = jnp.sum(exchanged.astype(jnp.float32), axis=0)
     square_sum = summed[HD // 2] + summed[HD // 2 + 2]
     router_logit = summed[HD // 2 + 1] + summed[HD // 2 + 3]
     inverse_rms = lax.rsqrt(square_sum / D + EPSILON)
     piece = (summed[: HD // 2] * inverse_rms[None, :]).astype(bf16)
-    pieces = [lax.ppermute(piece, "tp", quad_shift(k)) for k in (1, 2, 3)]
-    pieces, part = lax.optimization_barrier(([piece] + pieces, part))
+    piece, wo_sent, part = lax.optimization_barrier((piece, wo_sent, part))
     query_sum = lax.psum_scatter(
         part, "tp", scatter_dimension=0, axis_index_groups=[[2 * k + h for k in range(ZN)] for h in range(2)]
     )
+    pieces = [lax.ppermute(piece, "tp", quad_shift(k)) for k in (1, 2, 3)]
+    wo_got = lax.ppermute(wo_sent, "tp", y_swap())
+    pieces, wo_got = lax.optimization_barrier(([piece] + pieces, wo_got))
+    query_sum, wo_got = lax.optimization_barrier((query_sum, wo_got))
+    wo_in = share(wo_got).reshape(wo_rows, width)
     kv_own = ordered_rows(z % 4, pieces)
 
 
@@ -328,10 +355,7 @@
 
     middle = rows // 2
     over = lax.ppermute(kv_own, "ctx", [(c, (c + shard_n // 2) % shard_n) for c in range(shard_n)])
-    kv_own, wo_sent = lax.optimization_barrier((kv_own, wo_sent))
-    wo_got = lax.ppermute(wo_sent, "tp", y_swap())
-    near_left, near_right, over, wo_got = lax.optimization_barrier((x_hop(kv_own, 1), x_hop(kv_own, -1), over, wo_got))
-    wo_in = share(wo_got).reshape(wo_rows, width)
+    near_left, near_right, over = lax.optimization_barrier((x_hop(kv_own, 1), x_hop(kv_own, -1), over))
     first_half = jnp.stack([kv_own, near_left, near_right, over])
     far = x_hop(near_left[:middle], 1), x_hop(near_right[middle:], -1)
     over_left, over_right = x_hop(over, 1), x_hop(over, -1)

time: 187 us -> 190 us (1.016)
  matrix products: 18.4 us -> 23.3 us
  waiting for transfers between devices: 66.6 us -> 62.7 us
  Pallas kernels: 20.8 us -> 23 us
    all_to_all x1, waiting for transfers between devices: 26.5 us -> 21.3 us  [shards(): exchanged = lax.all_to_all(sent, 'tp', 0, 0, tiled=True)]
    dot_general x18, matrix products: 16.4 us -> 21.3 us  [dot(): return jnp.dot(a, b, preferred_element_type=jnp.float32)]
    ppermute x1, waiting for transfers between devices: 5.23 us -> 8.69 us  [shards(): received = lax.ppermute(for_partner.astype(bf16), 'tp', y_swap())]
    ppermute x3, waiting for transfers between devices: 0.01 us -> 3.36 us  [shards(): pieces = [lax.ppermute(piece, 'tp', quad_shift(k)) for k in (1, 2, 3)]]
    ppermute x1, waiting for transfers between devices: 2.36 us -> 0.01 us  [shards(): wo_got = lax.ppermute(wo_sent, 'tp', y_swap())]
    ppermute x1, waiting for transfers between devices: 2.38 us -> 0.06 us  [shards(): lax.ppermute(kv_own, 'ctx', [(c, (c + shard_n // 2) % shard_n) for c in r...]
    ppermute x2, waiting for transfers between devices: 0.01 us -> 2 us  [core_hop(): return lax.ppermute(block, 'ctx', [(c, c ^ 1) for c in range(shard_n)])]
    pallas_call x1 -> x2, Pallas kernels: 5.26 us -> 7.16 us  [the longest x1 4.38 us: all_parts(): pl.pallas_call(in_kernel, out_shape=jax.ShapeDtypeStruct(own.shape, jnp.b...]
  transfers between devices with their start and end apart: 30 -> 30, of which waited for: 16 -> 18; matrix products, arithmetic and copies ran while one was open for 12% -> 15% of each run, Pallas kernels for 11% -> 10%
where the time goes in v9:
time: 190 us; the launch traced here: 189 us
  waiting for transfers between devices  62.7 us (33%)
  starting transfers between devices  48.4 us (25%)
  matrix products  23.3 us (12%)
  Pallas kernels  23 us (12%)
  local copies, waits for them, and re-layouts  14.2 us (7%)
  between operations  13.6 us (7%)
  other arithmetic  3.31 us (2%)
    dot_general x18, matrix products, dot(): return jnp.dot(a, b, preferred_element_type=jnp.float32)  21.3 us
    all_to_all x1, waiting for transfers between devices, shards(): exchanged = lax.all_to_all(sent, 'tp', 0, 0, tiled=True)  21.3 us
    ppermute x4, waiting for transfers between devices, right(): return lax.ppermute(a.astype(bf16), 'tp', z_shift(1))  11.9 us
    ppermute x8, waiting for transfers between devices, x_hop(): return lax.ppermute(block, 'ctx', along(step))  11.9 us
    pallas_call x1, Pallas kernels, attention(): pl.pallas_call(attention_kernel, out_shape=jax.ShapeDtypeStruct(queries.s...  11.4 us
    ppermute x8, starting transfers between devices, x_hop(): return lax.ppermute(block, 'ctx', along(step))  10.7 us
    all_to_all x1, starting transfers between devices, shards(): exchanged = lax.all_to_all(sent, 'tp', 0, 0, tiled=True)  10.4 us
    unnamed x48, local copies, waits for them, and re-layouts  9.11 us
  transfers between devices with their start and end apart: 30, of which 18 were waited for; matrix products, arithmetic and copies ran while one was open for 15% of the time, Pallas kernels for 10%

profile of v9, /device:TPU:14, one launch (start us, length us, event | category | flops | bytes accessed | tf_op | source)
XLA Modules:
  0.0 188.5 jit_solution(898096556444677514)
XLA Ops:
  7.5 2.4 %collective-permute-start = (bf16[512,256]{1,0:T(8,128)(2,1)S(1)}, bf16[512,256]{1,0:T(8,128)(2,1)S(1)}, u32[]{:S(2)}, u32[]{:S(2)}) collective-permute-start(bf16[512,256]{1,0:T(8,128)(2,1)S(1)} %constant_dynamic-slice_fusion.1), channel_id=1, source_target_pairs={{0,1},{1,0},{2,3},{3,2},{4,5},{5,4},{6,7},{7,6},{8,9},{9,8},{10,11... | collective-permute-start | bytes 786440 | tf_op jit(solution)/shard_map/ppermute | solution.py:312
  12.0 1.2 copy-done.2
  14.4 2.6 %shard_map.73 = (bf16[512,512]{1,0:T(8,128)(2,1)S(1)}, bf16[16,72,512]{2,1,0:T(8,128)(2,1)}) custom-call(s32[1,512]{1,0:T(1,128)S(1)} %constant_dynamic-slice_fusion.2.rows_ref, bf16[1024,512]{1,0:T(8,128)(2,1)S(1)} %copy-done.2, bf16[1,512]{1,0:T(2,128)(2,1)S(1)} %reshape.429.gain_ref, bf16[1,512]{1,0:T(2,128)(2,1)S(1)} %reshape.430.router_ref, ...), custom_call_target="tpu_custom_call" | custom-call | flops 1073741824 | bytes 5242880 | tf_op jit(solution)/shard_map/pallas_call | solution.py:203
  17.9 10.4 %all-to-all-start = ((bf16[16,72,512]{2,1,0:T(8,128)(2,1)}), bf16[16,72,512]{2,1,0:T(8,128)(2,1)}, u32[]{:S(2)}, u32[]{:S(2)}) async-start(bf16[16,72,512]{2,1,0:T(8,128)(2,1)} %get-tuple-element.40), calls=%async_computation | async-start | bytes 2359296 | tf_op jit(solution)/shard_map/all_to_all | solution.py:320
  28.3 3.5 %collective-permute-start.1 = (bf16[512,512]{1,0:T(8,128)(2,1)S(1)}, bf16[512,512]{1,0:T(8,128)(2,1)S(1)}, u32[]{:S(2)}, u32[]{:S(2)}) collective-permute-start(bf16[512,512]{1,0:T(8,128)(2,1)S(1)} %get-tuple-element.41.x_ref), channel_id=1, source_target_pairs={{0,1},{1,0},{2,3},{3,2},{4,5},{5,4},{6,7},{7,6},{8,9},{9,8},{10,11... | collective-permute-start | bytes 1572872 | tf_op jit(solution)/shard_map/ppermute | solution.py:316
  32.0 2.4 %copy-done = bf16[512,4096]{1,0:T(8,128)(2,1)S(1)} copy-done((bf16[512,4096]{1,0:T(8,128)(2,1)S(1)}, bf16[512,4096]{1,0:T(8,128)(2,1)}, u32[]{:S(2)}) %copy-start) | copy-done | bytes 4194328
  34.4 2.8 %shard_map.74.own_ref = bf16[8,512,256]{2,1,0:T(8,128)(2,1)S(1)} custom-call(s32[1]{0:T(128)} %bitcast.35.y_ref, bf16[512,512]{1,0:T(8,128)(2,1)S(1)} %get-tuple-element.41.x_ref, bf16[512,4096]{1,0:T(8,128)(2,1)S(1)} %copy-done), custom_call_target="tpu_custom_call" | custom-call | flops 1073741824 | bytes 4194304 | tf_op jit(solution)/shard_map/pallas_call | solution.py:254
  38.7 21.3 %all-to-all-done = bf16[16,72,512]{2,1,0:T(8,128)(2,1)} async-done(((bf16[16,72,512]{2,1,0:T(8,128)(2,1)}), bf16[16,72,512]{2,1,0:T(8,128)(2,1)}, u32[]{:S(2)}, u32[]{:S(2)}) %all-to-all-start) | async-done | bytes 1179680 | tf_op jit(solution)/shard_map/all_to_all | solution.py:320
  60.0 1.4 convert_reduce_fusion
  61.5 1.6 copy-done.1
  63.1 4.4 %shard_map.75 = bf16[8,512,256]{2,1,0:T(8,128)(2,1)} custom-call(bf16[512,512]{1,0:T(8,128)(2,1)S(1)} %collective-permute-done.1.x_ref, bf16[8,512,256]{2,1,0:T(8,128)(2,1)S(1)} %bitcast.69, bf16[8,512,256]{2,1,0:T(8,128)(2,1)S(1)} %shard_map.74.own_ref), custom_call_target="tpu_custom_call" | custom-call | flops 1073741824 | bytes 6291456 | tf_op jit(solution)/shard_map/pallas_call | solution.py:276
  68.4 2.3 %collective-permute-start.3 = (bf16[64,512]{1,0:T(8,128)(2,1)S(1)}, bf16[64,512]{1,0:T(8,128)(2,1)S(1)}, u32[]{:S(2)}, u32[]{:S(2)}) collective-permute-start(bf16[64,512]{1,0:T(8,128)(2,1)S(1)} %fusion.45.refs_0_), channel_id=1, source_target_pairs={{0,4},{1,5},{2,6},{3,7},{4,0},{5,1},{6,2},{7,3},{8,12},{9,13},{10,... | collective-permute-start | bytes 196616 | tf_op jit(solution)/shard_map/ppermute | solution.py:342
  70.6 1.6 collective-permute-start.4
  72.2 2.4 %collective-permute-done.2.refs_1_ = bf16[64,512]{1,0:T(8,128)(2,1)S(1)} collective-permute-done((bf16[64,512]{1,0:T(8,128)(2,1)S(1)}, bf16[64,512]{1,0:T(8,128)(2,1)S(1)}, u32[]{:S(2)}, u32[]{:S(2)}) %collective-permute-start.2) | collective-permute-done | bytes 65568 | tf_op jit(solution)/shard_map/ppermute | solution.py:342
  76.2 1.8 shard_map.76
  78.5 1.5 collective-permute-start.7
  80.1 1.3 collective-permute-start.8
  81.4 4.2 %collective-permute-done.6 = bf16[512,256]{1,0:T(8,128)(2,1)S(1)} collective-permute-done((bf16[512,256]{1,0:T(8,128)(2,1)}, bf16[512,256]{1,0:T(8,128)(2,1)S(1)}, u32[]{:S(2)}, u32[]{:S(2)}) %collective-permute-start.6) | collective-permute-done | bytes 262176 | tf_op jit(solution)/shard_map/ppermute | solution.py:354
  85.6 1.4 collective-permute-done.7
  87.1 1.7 collective-permute-start.9
  89.1 3.0 %collective-permute-start.11 = (bf16[256,256]{1,0:T(8,128)(2,1)S(1)}, bf16[256,256]{1,0:T(8,128)(2,1)S(1)}, u32[]{:S(2)}, u32[]{:S(2)}) collective-permute-start(bf16[256,256]{1,0:T(8,128)(2,1)S(1)} %slice.38), channel_id=1, source_target_pairs={{0,32},{16,48},{32,64},{48,80},{64,96},{80,112},{96,0},{112,16},{1... | collective-permute-start | bytes 393224 | tf_op jit(solution)/shard_map/ppermute | solution.py:354
  92.4 3.7 %collective-permute-done.11 = bf16[256,256]{1,0:T(8,128)(2,1)S(1)} collective-permute-done((bf16[256,256]{1,0:T(8,128)(2,1)S(1)}, bf16[256,256]{1,0:T(8,128)(2,1)S(1)}, u32[]{:S(2)}, u32[]{:S(2)}) %collective-permute-start.11) | collective-permute-done | bytes 131104 | tf_op jit(solution)/shard_map/ppermute | solution.py:354
  96.1 2.5 %collective-permute-done.12 = bf16[256,256]{1,0:T(8,128)(2,1)S(1)} collective-permute-done((bf16[256,256]{1,0:T(8,128)(2,1)S(1)}, bf16[256,256]{1,0:T(8,128)(2,1)S(1)}, u32[]{:S(2)}, u32[]{:S(2)}) %collective-permute-start.12) | collective-permute-done | bytes 131104 | tf_op jit(solution)/shard_map/ppermute | solution.py:354
  98.8 3.3 %collective-permute-start.13 = (bf16[256,256]{1,0:T(8,128)(2,1)S(1)}, bf16[256,256]{1,0:T(8,128)(2,1)S(1)}, u32[]{:S(2)}, u32[]{:S(2)}) collective-permute-start(bf16[256,256]{1,0:T(8,128)(2,1)S(1)} %slice.40), channel_id=1, source_target_pairs={{0,32},{16,48},{32,64},{48,80},{64,96},{80,112},{96,0},{112,16},{1... | collective-permute-start | bytes 393224 | tf_op jit(solution)/shard_map/ppermute | solution.py:354
  103.3 2.4 %reduce-scatter.2.cloned.1.call-done = bf16[1,512,256]{2,1,0:T(8,128)(2,1)} async-done(((bf16[8,512,256]{2,1,0:T(8,128)(2,1)}), bf16[1,512,256]{2,1,0:T(8,128)(2,1)}) %reduce-scatter.2.cloned.1.call-update) | async-done | bytes 262160 | tf_op jit(solution)/shard_map/reduce_scatter | solution.py:339
  106.8 2.0 %collective-permute-done.16.refs_3_ = bf16[4,512,256]{2,1,0:T(8,128)(2,1)} collective-permute-done((bf16[4,512,256]{2,1,0:T(8,128)(2,1)S(1)}, bf16[4,512,256]{2,1,0:T(8,128)(2,1)}, u32[]{:S(2)}, u32[]{:S(2)}) %collective-permute-start.16) | collective-permute-done | bytes 1048608 | tf_op jit(solution)/shard_map/ppermute | solution.py:367
  108.8 11.4 %shard_map.77 = bf16[512,256]{1,0:T(8,128)(2,1)S(1)} custom-call(s32[16,3]{1,0:T(8,128)S(1)} %copy.11.info_ref, bf16[512,256]{1,0:T(8,128)(2,1)S(1)} %multiply_convert_fusion.2.q_ref, bf16[4,512,256]{2,1,0:T(8,128)(2,1)S(1)} %pad_maximum_fusion.refs_0_, bf16[4,512,256]{2,1,0:T(8,128)(2,1)S(1)} %pad_maximum_fusion.1.refs_1_, ...), custom_call_target="tpu_custom_call" | custom-call | flops 4294967296 | bytes 4194304 | tf_op jit(solution)/shard_map/pallas_call | solution.py:151
  120.2 1.3 collective-permute-start.17
  121.5 2.0 %collective-permute-start.18 = (bf16[512,256]{1,0:T(8,128)(2,1)S(1)}, bf16[512,256]{1,0:T(8,128)(2,1)S(1)}, u32[]{:S(2)}, u32[]{:S(2)}) collective-permute-start(bf16[512,256]{1,0:T(8,128)(2,1)S(1)} %shard_map.77), channel_id=1, source_target_pairs={{0,14},{1,15},{2,0},{3,1},{4,2},{5,3},{6,4},{7,5},{8,6},{9,7},{10,... | collective-permute-start | bytes 786440 | tf_op jit(solution)/shard_map/ppermute | solution.py:374
  123.5 5.7 %collective-permute-done.17 = bf16[512,256]{1,0:T(8,128)(2,1)S(1)} collective-permute-done((bf16[512,256]{1,0:T(8,128)(2,1)S(1)}, bf16[512,256]{1,0:T(8,128)(2,1)S(1)}, u32[]{:S(2)}, u32[]{:S(2)}) %collective-permute-start.17) | collective-permute-done | bytes 262176 | tf_op jit(solution)/shard_map/ppermute | solution.py:371
  130.4 2.4 %collective-permute-start.20 = (bf16[512,256]{1,0:T(8,128)(2,1)S(1)}, bf16[512,256]{1,0:T(8,128)(2,1)S(1)}, u32[]{:S(2)}, u32[]{:S(2)}) collective-permute-start(bf16[512,256]{1,0:T(8,128)(2,1)S(1)} %collective-permute-done.18), channel_id=1, source_target_pairs={{0,14},{1,15},{2,0},{3,1},{4,2},{5,3},{6,4},{7,5},{8,6},{9,7},{10,... | collective-permute-start | bytes 786440 | tf_op jit(solution)/shard_map/ppermute | solution.py:374
  132.8 1.2 fusion.40
  134.0 1.2 fusion.42
  135.3 4.0 %collective-permute-done.19 = bf16[512,256]{1,0:T(8,128)(2,1)S(1)} collective-permute-done((bf16[512,256]{1,0:T(8,128)(2,1)S(1)}, bf16[512,256]{1,0:T(8,128)(2,1)S(1)}, u32[]{:S(2)}, u32[]{:S(2)}) %collective-permute-start.19) | collective-permute-done | bytes 262176 | tf_op jit(solution)/shard_map/ppermute | solution.py:371
  139.6 2.3 %collective-permute-start.21 = (bf16[512,256]{1,0:T(8,128)(2,1)S(1)}, bf16[512,256]{1,0:T(8,128)(2,1)S(1)}, u32[]{:S(2)}, u32[]{:S(2)}) collective-permute-start(bf16[512,256]{1,0:T(8,128)(2,1)S(1)} %collective-permute-done.19), channel_id=1, source_target_pairs={{0,2},{1,3},{2,4},{3,5},{4,6},{5,7},{6,8},{7,9},{8,10},{9,11},{10,... | collective-permute-start | bytes 786440 | tf_op jit(solution)/shard_map/ppermute | solution.py:371
  142.9 2.2 %fusion.36 = f32[512,512]{1,0:T(8,128)} fusion(bf16[512,256]{1,0:T(8,128)(2,1)S(1)} %collective-permute-done.20, bf16[4096,512]{1,0:T(8,128)(2,1)} %param.12, s32[]{:T(128)S(6)} %select_n.225), kind=kOutput, calls=%fused_computation.46 | convolution fusion | flops 134217728 | bytes 1572868 | tf_op jit(solution)/shard_map/dot_general | solution.py:240
  145.1 2.2 %fusion.38 = f32[512,512]{1,0:T(8,128)} fusion(bf16[512,256]{1,0:T(8,128)(2,1)S(1)} %collective-permute-done.19, bf16[4096,512]{1,0:T(8,128)(2,1)} %param.12, s32[]{:T(128)S(6)} %select_n.223), kind=kOutput, calls=%fused_computation.48 | convolution fusion | flops 134217728 | bytes 1572868 | tf_op jit(solution)/shard_map/dot_general | solution.py:240
  147.3 2.2 %collective-permute-done.21 = bf16[512,256]{1,0:T(8,128)(2,1)S(1)} collective-permute-done((bf16[512,256]{1,0:T(8,128)(2,1)S(1)}, bf16[512,256]{1,0:T(8,128)(2,1)S(1)}, u32[]{:S(2)}, u32[]{:S(2)}) %collective-permute-start.21) | collective-permute-done | bytes 262176 | tf_op jit(solution)/shard_map/ppermute | solution.py:371
  149.9 2.6 %collective-permute-start.24 = (bf16[512,128]{1,0:T(8,128)(2,1)S(1)}, bf16[512,128]{1,0:T(8,128)(2,1)S(1)}, u32[]{:S(2)}, u32[]{:S(2)}) collective-permute-start(bf16[512,128]{1,0:T(8,128)(2,1)S(1)} %slice.43), channel_id=1, source_target_pairs={{0,14},{1,15},{2,0},{3,1},{4,2},{5,3},{6,4},{7,5},{8,6},{9,7},{10,... | collective-permute-start | bytes 393224 | tf_op jit(solution)/shard_map/ppermute | solution.py:374
  153.2 2.2 %fusion.32 = f32[512,512]{1,0:T(8,128)} fusion(bf16[512,256]{1,0:T(8,128)(2,1)S(1)} %collective-permute-done.22, bf16[4096,512]{1,0:T(8,128)(2,1)} %param.12, s32[]{:T(128)S(6)} %select_n.229), kind=kOutput, calls=%fused_computation.42 | convolution fusion | flops 134217728 | bytes 1572868 | tf_op jit(solution)/shard_map/dot_general | solution.py:240
  155.4 2.2 %fusion.34 = f32[512,512]{1,0:T(8,128)} fusion(bf16[512,256]{1,0:T(8,128)(2,1)S(1)} %collective-permute-done.21, bf16[4096,512]{1,0:T(8,128)(2,1)} %param.12, s32[]{:T(128)S(6)} %select_n.227), kind=kOutput, calls=%fused_computation.44 | convolution fusion | flops 134217728 | bytes 1572868 | tf_op jit(solution)/shard_map/dot_general | solution.py:240
  158.3 2.1 %fusion.50 = f32[512,512]{1,0:T(8,128)} fusion(bf16[512,128]{1,0:T(8,128)(2,1)S(1)} %collective-permute-done.24, bf16[4096,512]{1,0:T(8,128)(2,1)} %param.12, s32[]{:T(128)S(6)} %select_n.232), kind=kOutput, calls=%fused_computation.61 | convolution fusion | flops 67108864 | bytes 1310724 | tf_op jit(solution)/shard_map/dot_general | solution.py:240
  160.4 1.4 fusion.20
  161.8 1.2 fusion.22
  165.6 2.9 %collective-permute-start.25 = (bf16[512,512]{1,0:T(8,128)(2,1)S(1)}, bf16[512,512]{1,0:T(8,128)(2,1)S(1)}, u32[]{:S(2)}, u32[]{:S(2)}) collective-permute-start(bf16[512,512]{1,0:T(8,128)(2,1)S(1)} %fusion.16), channel_id=1, source_target_pairs={{0,1},{1,0},{2,3},{3,2},{4,5},{5,4},{6,7},{7,6},{8,9},{9,8},{10,11... | collective-permute-start | bytes 1572872 | tf_op jit(solution)/shard_map/ppermute | solution.py:399
  169.7 1.6 fusion.9
  171.3 8.7 %collective-permute-done.25 = bf16[512,512]{1,0:T(8,128)(2,1)S(1)} collective-permute-done((bf16[512,512]{1,0:T(8,128)(2,1)S(1)}, bf16[512,512]{1,0:T(8,128)(2,1)S(1)}, u32[]{:S(2)}, u32[]{:S(2)}) %collective-permute-start.25) | collective-permute-done | bytes 524320 | tf_op jit(solution)/shard_map/ppermute | solution.py:399
  180.0 2.0 %fusion.1 = bf16[1024,512]{1,0:T(8,128)(2,1)} fusion(s32[512]{0:T(512)S(1)} %bitcast.70, f32[512,512]{1,0:T(8,128)S(1)} %fusion.9, bf16[512,512]{1,0:T(8,128)(2,1)S(1)} %collective-permute-done.25, f32[512]{0:T(512)S(1)} %bitcast.81), kind=kOutput, calls=%fused_computation.3 | convolution fusion | flops 538968064 | bytes 2625536 | tf_op jit(solution)/shard_map/dot_general | solution.py:404
  (116 shorter events, 20.6 us)
Async XLA Ops:
  6.5 53.5 %all-gather.5.cloned.1.call-start = ((), (), s32[]{:S(2)}) async-start(), calls=%async_computation.3 | async-start | bytes 2359296 | tf_op jit(solution)/shard_map/all_gather | solution.py:309
  7.5 9.6 %collective-permute-start = (bf16[512,256]{1,0:T(8,128)(2,1)S(1)}, bf16[512,256]{1,0:T(8,128)(2,1)S(1)}, u32[]{:S(2)}, u32[]{:S(2)}) collective-permute-start(bf16[512,256]{1,0:T(8,128)(2,1)S(1)} %constant_dynamic-slice_fusion.1), channel_id=1, source_target_pairs={{0,1},{1,0},{2,3},{3,2},{4,5},{5,4},{6,7},{7,6},{8,9},{9,8},{10,11... | collective-permute-start | bytes 786440 | tf_op jit(solution)/shard_map/ppermute | solution.py:312
  12.0 1.2 copy-start.2
  13.2 1.2 copy-start.3
  17.9 42.1 %all-to-all-start = ((bf16[16,72,512]{2,1,0:T(8,128)(2,1)}), bf16[16,72,512]{2,1,0:T(8,128)(2,1)}, u32[]{:S(2)}, u32[]{:S(2)}) async-start(bf16[16,72,512]{2,1,0:T(8,128)(2,1)} %get-tuple-element.40), calls=%async_computation | async-start | bytes 2359296 | tf_op jit(solution)/shard_map/all_to_all | solution.py:320
  28.2 77.4 %reduce-scatter.2.cloned.1.call-start = ((), (), s32[]{:S(2)}) async-start(), calls=%async_computation.2 | async-start | bytes 2359296 | tf_op jit(solution)/shard_map/reduce_scatter | solution.py:339
  28.3 33.2 %collective-permute-start.1 = (bf16[512,512]{1,0:T(8,128)(2,1)S(1)}, bf16[512,512]{1,0:T(8,128)(2,1)S(1)}, u32[]{:S(2)}, u32[]{:S(2)}) collective-permute-start(bf16[512,512]{1,0:T(8,128)(2,1)S(1)} %get-tuple-element.41.x_ref), channel_id=1, source_target_pairs={{0,1},{1,0},{2,3},{3,2},{4,5},{5,4},{6,7},{7,6},{8,9},{9,8},{10,11... | collective-permute-start | bytes 1572872 | tf_op jit(solution)/shard_map/ppermute | solution.py:316
  32.0 2.5 %copy-start = (bf16[512,4096]{1,0:T(8,128)(2,1)S(1)}, bf16[512,4096]{1,0:T(8,128)(2,1)}, u32[]{:S(2)}) copy-start(bf16[512,4096]{1,0:T(8,128)(2,1)} %w_ref.1) | copy-start | bytes 12582916
  34.4 2.8 %copy-start.23 = (s32[16,512]{1,0:T(8,128)S(1)}, s32[16,512]{1,0:T(8,128)}, u32[]{:S(2)}) copy-start(s32[16,512]{1,0:T(8,128)} %param.13) | copy-start | bytes 98308
  61.5 9.2 %copy-start.16 = (bf16[64,512]{1,0:T(8,128)(2,1)}, bf16[64,512]{1,0:T(8,128)(2,1)S(1)}, u32[]{:S(2)}) copy-start(bf16[64,512]{1,0:T(8,128)(2,1)S(1)} %fusion.45.refs_0_) | copy-start | bytes 196612
  61.5 1.6 copy-start.1
  67.5 92.9 %all-gather.7.cloned.1.call-start = ((), (), s32[]{:S(2)}) async-start(), calls=%async_computation.4 | async-start | bytes 2359296 | tf_op jit(solution)/shard_map/all_gather | solution.py:309
  67.6 8.0 %collective-permute-start.5 = (bf16[256,512]{1,0:T(8,128)(2,1)S(1)}, bf16[256,512]{1,0:T(8,128)(2,1)S(1)}, u32[]{:S(2)}, u32[]{:S(2)}) collective-permute-start(bf16[256,512]{1,0:T(8,128)(2,1)S(1)} %constant_dynamic-slice_fusion), channel_id=1, source_target_pairs={{0,1},{1,0},{2,3},{3,2},{4,5},{5,4},{6,7},{7,6},{8,9},{9,8},{10,11... | collective-permute-start | bytes 786440 | tf_op jit(solution)/shard_map/ppermute | solution.py:343
  68.4 6.2 %collective-permute-start.2 = (bf16[64,512]{1,0:T(8,128)(2,1)S(1)}, bf16[64,512]{1,0:T(8,128)(2,1)S(1)}, u32[]{:S(2)}, u32[]{:S(2)}) collective-permute-start(bf16[64,512]{1,0:T(8,128)(2,1)S(1)} %fusion.45.refs_0_), channel_id=1, source_target_pairs={{0,2},{1,3},{2,4},{3,5},{4,6},{5,7},{6,0},{7,1},{8,10},{9,11},{10,... | collective-permute-start | bytes 196616 | tf_op jit(solution)/shard_map/ppermute | solution.py:342
  68.4 7.2 %collective-permute-start.3 = (bf16[64,512]{1,0:T(8,128)(2,1)S(1)}, bf16[64,512]{1,0:T(8,128)(2,1)S(1)}, u32[]{:S(2)}, u32[]{:S(2)}) collective-permute-start(bf16[64,512]{1,0:T(8,128)(2,1)S(1)} %fusion.45.refs_0_), channel_id=1, source_target_pairs={{0,4},{1,5},{2,6},{3,7},{4,0},{5,1},{6,2},{7,3},{8,12},{9,13},{10,... | collective-permute-start | bytes 196616 | tf_op jit(solution)/shard_map/ppermute | solution.py:342
  70.6 4.9 %collective-permute-start.4 = (bf16[64,512]{1,0:T(8,128)(2,1)S(1)}, bf16[64,512]{1,0:T(8,128)(2,1)S(1)}, u32[]{:S(2)}, u32[]{:S(2)}) collective-permute-start(bf16[64,512]{1,0:T(8,128)(2,1)S(1)} %fusion.45.refs_0_), channel_id=1, source_target_pairs={{0,6},{1,7},{2,0},{3,1},{4,2},{5,3},{6,4},{7,5},{8,14},{9,15},{10,... | collective-permute-start | bytes 196616 | tf_op jit(solution)/shard_map/ppermute | solution.py:342
  74.6 1.0 copy-start.20
  75.6 27.7 %copy-start.17 = (bf16[256,512]{1,0:T(8,128)(2,1)}, bf16[256,512]{1,0:T(8,128)(2,1)S(1)}, u32[]{:S(2)}) copy-start(bf16[256,512]{1,0:T(8,128)(2,1)S(1)} %collective-permute-done.5) | copy-start | bytes 786436
  78.1 7.6 %collective-permute-start.6 = (bf16[512,256]{1,0:T(8,128)(2,1)}, bf16[512,256]{1,0:T(8,128)(2,1)S(1)}, u32[]{:S(2)}, u32[]{:S(2)}) collective-permute-start(bf16[512,256]{1,0:T(8,128)(2,1)} %shard_map.76), channel_id=1, source_target_pairs={{0,32},{16,48},{32,64},{48,80},{64,96},{80,112},{96,0},{112,16},{1... | collective-permute-start | bytes 786440 | tf_op jit(solution)/shard_map/ppermute | solution.py:354
  78.5 8.5 %collective-permute-start.7 = (bf16[512,256]{1,0:T(8,128)(2,1)}, bf16[512,256]{1,0:T(8,128)(2,1)S(1)}, u32[]{:S(2)}, u32[]{:S(2)}) collective-permute-start(bf16[512,256]{1,0:T(8,128)(2,1)} %shard_map.76), channel_id=1, source_target_pairs={{0,96},{16,112},{32,0},{48,16},{64,32},{80,48},{96,64},{112,80},{1... | collective-permute-start | bytes 786440 | tf_op jit(solution)/shard_map/ppermute | solution.py:354
  80.1 7.0 %collective-permute-start.8 = (bf16[512,256]{1,0:T(8,128)(2,1)}, bf16[512,256]{1,0:T(8,128)(2,1)S(1)}, u32[]{:S(2)}, u32[]{:S(2)}) collective-permute-start(bf16[512,256]{1,0:T(8,128)(2,1)} %shard_map.76), channel_id=1, source_target_pairs={{0,128},{16,144},{32,160},{48,176},{64,192},{80,208},{96,224},{112... | collective-permute-start | bytes 786440 | tf_op jit(solution)/shard_map/ppermute | solution.py:357
  87.1 11.5 %collective-permute-start.9 = (bf16[512,256]{1,0:T(8,128)(2,1)S(1)}, bf16[512,256]{1,0:T(8,128)(2,1)S(1)}, u32[]{:S(2)}, u32[]{:S(2)}) collective-permute-start(bf16[512,256]{1,0:T(8,128)(2,1)S(1)} %collective-permute-done.8), channel_id=1, source_target_pairs={{0,32},{16,48},{32,64},{48,80},{64,96},{80,112},{96,0},{112,16},{1... | collective-permute-start | bytes 786440 | tf_op jit(solution)/shard_map/ppermute | solution.py:354
  88.8 9.9 %collective-permute-start.10 = (bf16[512,256]{1,0:T(8,128)(2,1)S(1)}, bf16[512,256]{1,0:T(8,128)(2,1)S(1)}, u32[]{:S(2)}, u32[]{:S(2)}) collective-permute-start(bf16[512,256]{1,0:T(8,128)(2,1)S(1)} %collective-permute-done.8), channel_id=1, source_target_pairs={{0,96},{16,112},{32,0},{48,16},{64,32},{80,48},{96,64},{112,80},{1... | collective-permute-start | bytes 786440 | tf_op jit(solution)/shard_map/ppermute | solution.py:354
  89.1 7.0 %collective-permute-start.11 = (bf16[256,256]{1,0:T(8,128)(2,1)S(1)}, bf16[256,256]{1,0:T(8,128)(2,1)S(1)}, u32[]{:S(2)}, u32[]{:S(2)}) collective-permute-start(bf16[256,256]{1,0:T(8,128)(2,1)S(1)} %slice.38), channel_id=1, source_target_pairs={{0,32},{16,48},{32,64},{48,80},{64,96},{80,112},{96,0},{112,16},{1... | collective-permute-start | bytes 393224 | tf_op jit(solution)/shard_map/ppermute | solution.py:354
  92.1 6.5 %collective-permute-start.12 = (bf16[256,256]{1,0:T(8,128)(2,1)S(1)}, bf16[256,256]{1,0:T(8,128)(2,1)S(1)}, u32[]{:S(2)}, u32[]{:S(2)}) collective-permute-start(bf16[256,256]{1,0:T(8,128)(2,1)S(1)} %slice.39), channel_id=1, source_target_pairs={{0,96},{16,112},{32,0},{48,16},{64,32},{80,48},{96,64},{112,80},{1... | collective-permute-start | bytes 393224 | tf_op jit(solution)/shard_map/ppermute | solution.py:354
  98.7 7.0 %collective-permute-start.14 = (bf16[256,256]{1,0:T(8,128)(2,1)S(1)}, bf16[256,256]{1,0:T(8,128)(2,1)S(1)}, u32[]{:S(2)}, u32[]{:S(2)}) collective-permute-start(bf16[256,256]{1,0:T(8,128)(2,1)S(1)} %slice.41), channel_id=1, source_target_pairs={{0,96},{16,112},{32,0},{48,16},{64,32},{80,48},{96,64},{112,80},{1... | collective-permute-start | bytes 393224 | tf_op jit(solution)/shard_map/ppermute | solution.py:354
  98.8 6.9 %collective-permute-start.13 = (bf16[256,256]{1,0:T(8,128)(2,1)S(1)}, bf16[256,256]{1,0:T(8,128)(2,1)S(1)}, u32[]{:S(2)}, u32[]{:S(2)}) collective-permute-start(bf16[256,256]{1,0:T(8,128)(2,1)S(1)} %slice.40), channel_id=1, source_target_pairs={{0,32},{16,48},{32,64},{48,80},{64,96},{80,112},{96,0},{112,16},{1... | collective-permute-start | bytes 393224 | tf_op jit(solution)/shard_map/ppermute | solution.py:354
  103.1 3.6 %collective-permute-start.15 = (bf16[4,512,256]{2,1,0:T(8,128)(2,1)S(1)}, bf16[4,512,256]{2,1,0:T(8,128)(2,1)}, u32[]{:S(2)}, u32[]{:S(2)}) collective-permute-start(bf16[4,512,256]{2,1,0:T(8,128)(2,1)S(1)} %pad_maximum_fusion.refs_0_), channel_id=1, source_target_pairs={{0,16},{16,0},{32,48},{48,32},{64,80},{80,64},{96,112},{112,96},{1... | collective-permute-start | bytes 3145736 | tf_op jit(solution)/shard_map/ppermute | solution.py:367
  105.9 2.9 %collective-permute-start.16 = (bf16[4,512,256]{2,1,0:T(8,128)(2,1)S(1)}, bf16[4,512,256]{2,1,0:T(8,128)(2,1)}, u32[]{:S(2)}, u32[]{:S(2)}) collective-permute-start(bf16[4,512,256]{2,1,0:T(8,128)(2,1)S(1)} %pad_maximum_fusion.1.refs_1_), channel_id=1, source_target_pairs={{0,16},{16,0},{32,48},{48,32},{64,80},{80,64},{96,112},{112,96},{1... | collective-permute-start | bytes 3145736 | tf_op jit(solution)/shard_map/ppermute | solution.py:367
  120.2 9.0 %collective-permute-start.17 = (bf16[512,256]{1,0:T(8,128)(2,1)S(1)}, bf16[512,256]{1,0:T(8,128)(2,1)S(1)}, u32[]{:S(2)}, u32[]{:S(2)}) collective-permute-start(bf16[512,256]{1,0:T(8,128)(2,1)S(1)} %shard_map.77), channel_id=1, source_target_pairs={{0,2},{1,3},{2,4},{3,5},{4,6},{5,7},{6,8},{7,9},{8,10},{9,11},{10,... | collective-permute-start | bytes 786440 | tf_op jit(solution)/shard_map/ppermute | solution.py:371
  121.5 8.0 %collective-permute-start.18 = (bf16[512,256]{1,0:T(8,128)(2,1)S(1)}, bf16[512,256]{1,0:T(8,128)(2,1)S(1)}, u32[]{:S(2)}, u32[]{:S(2)}) collective-permute-start(bf16[512,256]{1,0:T(8,128)(2,1)S(1)} %shard_map.77), channel_id=1, source_target_pairs={{0,14},{1,15},{2,0},{3,1},{4,2},{5,3},{6,4},{7,5},{8,6},{9,7},{10,... | collective-permute-start | bytes 786440 | tf_op jit(solution)/shard_map/ppermute | solution.py:374
  129.5 9.8 %collective-permute-start.19 = (bf16[512,256]{1,0:T(8,128)(2,1)S(1)}, bf16[512,256]{1,0:T(8,128)(2,1)S(1)}, u32[]{:S(2)}, u32[]{:S(2)}) collective-permute-start(bf16[512,256]{1,0:T(8,128)(2,1)S(1)} %collective-permute-done.17), channel_id=1, source_target_pairs={{0,2},{1,3},{2,4},{3,5},{4,6},{5,7},{6,8},{7,9},{8,10},{9,11},{10,... | collective-permute-start | bytes 786440 | tf_op jit(solution)/shard_map/ppermute | solution.py:371
  130.4 9.2 %collective-permute-start.20 = (bf16[512,256]{1,0:T(8,128)(2,1)S(1)}, bf16[512,256]{1,0:T(8,128)(2,1)S(1)}, u32[]{:S(2)}, u32[]{:S(2)}) collective-permute-start(bf16[512,256]{1,0:T(8,128)(2,1)S(1)} %collective-permute-done.18), channel_id=1, source_target_pairs={{0,14},{1,15},{2,0},{3,1},{4,2},{5,3},{6,4},{7,5},{8,6},{9,7},{10,... | collective-permute-start | bytes 786440 | tf_op jit(solution)/shard_map/ppermute | solution.py:374
  139.3 16.1 %copy-start.10 = (bf16[512,256]{1,0:T(8,128)(2,1)}, bf16[512,256]{1,0:T(8,128)(2,1)S(1)}, u32[]{:S(2)}) copy-start(bf16[512,256]{1,0:T(8,128)(2,1)S(1)} %collective-permute-done.19) | copy-start | bytes 786436
  139.6 15.8 %copy-start.12 = (bf16[512,256]{1,0:T(8,128)(2,1)}, bf16[512,256]{1,0:T(8,128)(2,1)S(1)}, u32[]{:S(2)}) copy-start(bf16[512,256]{1,0:T(8,128)(2,1)S(1)} %collective-permute-done.20) | copy-start | bytes 786436
  139.6 9.9 %collective-permute-start.21 = (bf16[512,256]{1,0:T(8,128)(2,1)S(1)}, bf16[512,256]{1,0:T(8,128)(2,1)S(1)}, u32[]{:S(2)}, u32[]{:S(2)}) collective-permute-start(bf16[512,256]{1,0:T(8,128)(2,1)S(1)} %collective-permute-done.19), channel_id=1, source_target_pairs={{0,2},{1,3},{2,4},{3,5},{4,6},{5,7},{6,8},{7,9},{8,10},{9,11},{10,... | collective-permute-start | bytes 786440 | tf_op jit(solution)/shard_map/ppermute | solution.py:371
  141.9 8.0 %collective-permute-start.22 = (bf16[512,256]{1,0:T(8,128)(2,1)S(1)}, bf16[512,256]{1,0:T(8,128)(2,1)S(1)}, u32[]{:S(2)}, u32[]{:S(2)}) collective-permute-start(bf16[512,256]{1,0:T(8,128)(2,1)S(1)} %collective-permute-done.20), channel_id=1, source_target_pairs={{0,14},{1,15},{2,0},{3,1},{4,2},{5,3},{6,4},{7,5},{8,6},{9,7},{10,... | collective-permute-start | bytes 786440 | tf_op jit(solution)/shard_map/ppermute | solution.py:374
  149.9 7.7 %collective-permute-start.24 = (bf16[512,128]{1,0:T(8,128)(2,1)S(1)}, bf16[512,128]{1,0:T(8,128)(2,1)S(1)}, u32[]{:S(2)}, u32[]{:S(2)}) collective-permute-start(bf16[512,128]{1,0:T(8,128)(2,1)S(1)} %slice.43), channel_id=1, source_target_pairs={{0,14},{1,15},{2,0},{3,1},{4,2},{5,3},{6,4},{7,5},{8,6},{9,7},{10,... | collective-permute-start | bytes 393224 | tf_op jit(solution)/shard_map/ppermute | solution.py:374
  153.2 11.5 %collective-permute-start.23 = (bf16[512,128]{1,0:T(8,128)(2,1)}, bf16[512,128]{1,0:T(8,128)(2,1)S(1)}, u32[]{:S(2)}, u32[]{:S(2)}) collective-permute-start(bf16[512,128]{1,0:T(8,128)(2,1)} %slice.42), channel_id=1, source_target_pairs={{0,2},{1,3},{2,4},{3,5},{4,6},{5,7},{6,8},{7,9},{8,10},{9,11},{10,... | collective-permute-start | bytes 393224 | tf_op jit(solution)/shard_map/ppermute | solution.py:371
  160.4 2.7 %copy-start.9 = (bf16[2048,512]{1,0:T(8,128)(2,1)S(1)}, bf16[2048,512]{1,0:T(8,128)(2,1)}, u32[]{:S(2)}) copy-start(bf16[2048,512]{1,0:T(8,128)(2,1)} %all-gather.7.cloned.1.call-done) | copy-start | bytes 6291460
  160.4 2.7 %copy-start.13 = (bf16[512,256]{1,0:T(8,128)(2,1)S(1)}, bf16[512,256]{1,0:T(8,128)(2,1)}, u32[]{:S(2)}) copy-start(bf16[512,256]{1,0:T(8,128)(2,1)} %copy-done.12) | copy-start | bytes 786436
  160.4 3.0 %copy-start.11 = (bf16[512,256]{1,0:T(8,128)(2,1)S(1)}, bf16[512,256]{1,0:T(8,128)(2,1)}, u32[]{:S(2)}) copy-start(bf16[512,256]{1,0:T(8,128)(2,1)} %copy-done.10) | copy-start | bytes 786436
  164.9 4.7 %copy-start.4 = (f32[512,512]{1,0:T(8,128)S(1)}, f32[512,512]{1,0:T(8,128)}, u32[]{:S(2)}) copy-start(f32[512,512]{1,0:T(8,128)} %fusion.36) | copy-start | bytes 3145732
  164.9 4.7 %copy-start.5 = (f32[512,512]{1,0:T(8,128)S(1)}, f32[512,512]{1,0:T(8,128)}, u32[]{:S(2)}) copy-start(f32[512,512]{1,0:T(8,128)} %fusion.38) | copy-start | bytes 3145732
  165.0 4.7 %copy-start.6 = (f32[512,512]{1,0:T(8,128)S(1)}, f32[512,512]{1,0:T(8,128)}, u32[]{:S(2)}) copy-start(f32[512,512]{1,0:T(8,128)} %fusion.32) | copy-start | bytes 3145732
  165.0 4.7 %copy-start.7 = (f32[512,512]{1,0:T(8,128)S(1)}, f32[512,512]{1,0:T(8,128)}, u32[]{:S(2)}) copy-start(f32[512,512]{1,0:T(8,128)} %fusion.34) | copy-start | bytes 3145732
  165.0 4.7 %copy-start.8 = (f32[512,512]{1,0:T(8,128)S(1)}, f32[512,512]{1,0:T(8,128)}, u32[]{:S(2)}) copy-start(f32[512,512]{1,0:T(8,128)} %fusion.50) | copy-start | bytes 3145732
  165.6 14.4 %collective-permute-start.25 = (bf16[512,512]{1,0:T(8,128)(2,1)S(1)}, bf16[512,512]{1,0:T(8,128)(2,1)S(1)}, u32[]{:S(2)}, u32[]{:S(2)}) collective-permute-start(bf16[512,512]{1,0:T(8,128)(2,1)S(1)} %fusion.16), channel_id=1, source_target_pairs={{0,1},{1,0},{2,3},{3,2},{4,5},{5,4},{6,7},{7,6},{8,9},{9,8},{10,11... | collective-permute-start | bytes 1572872 | tf_op jit(solution)/shard_map/ppermute | solution.py:399
  (6 other events, 4.5 us)
Sparse Core Ops, SparseCore 0:
  18.0 29.2 all-gather.4
  67.7 37.9 reduce-scatter.1
  107.5 25.5 all-gather.6

commit v10 on v9

--- a/solution.py
+++ b/solution.py
@@ -288,6 +288,50 @@
             flops=2 * chunks * rows * width * chunk, bytes_accessed=chunks * chunk * 2 * (width + 2 * rows), transcendentals=0
         ),
     )(x_in, wq_in, own)
+
+
+def project_kernel(starts_ref, w_hbm, *refs):
+    pieces, (o_ref, x_ref, w_ref, sem) = refs[:-4], refs[-4:]
+    copies, at = [], 0
+    for index, piece in enumerate(pieces):
+        depth = piece.shape[1]
+        start = pl.multiple_of(starts_ref[index], HD)
+        copies.append(
+            pltpu.make_async_copy(w_hbm.at[pl.ds(start, depth), :], w_ref.at[pl.ds(at, depth), :], sem.at[index])
+        )
+        at += depth
+    for copy in copies:
+        copy.start()
+    at = 0
+    for piece in pieces:
+        depth = piece.shape[1]
+        x_ref[:, at : at + depth] = piece[...]
+        at += depth
+    for copy in copies:
+        copy.wait()
+    o_ref[...] = dot(x_ref[...], w_ref[...]).astype(o_ref.dtype)
+
+
+def project(starts, weights, pieces, kind):
+    rows = pieces[0].shape[0]
+    depth = sum(piece.shape[1] for piece in pieces)
+    width = weights.shape[1]
+    return pl.pallas_call(
+        project_kernel,
+        out_shape=jax.ShapeDtypeStruct((rows, width), kind),
+        in_specs=[pl.BlockSpec(memory_space=pltpu.SMEM), pl.BlockSpec(memory_space=pl.ANY)]
+        + [pl.BlockSpec(memory_space=pltpu.VMEM)] * len(pieces),
+        out_specs=pl.BlockSpec(memory_space=pltpu.VMEM),
+        scratch_shapes=[
+            pltpu.VMEM((rows, depth), jnp.bfloat16),
+            pltpu.VMEM((depth, width), jnp.bfloat16),
+            pltpu.SemaphoreType.DMA((len(pieces),)),
+        ],
+        compiler_params=pltpu.CompilerParams(vmem_limit_bytes=24 * 1024 * 1024),
+        cost_estimate=pl.CostEstimate(
+            flops=2 * rows * depth * width, bytes_accessed=2 * depth * (rows + width) + 4 * rows * width, transcendentals=0
+        ),
+    )(starts, weights, *pieces)
 
 
 def shards(hidden, norm_gain, router_weight, query_weight, key_value_weight, out_weight, kept_rows):
@@ -381,23 +425,22 @@
 
     mixed = attention(info, queries, kv_all)
 
-    def project(piece, offset, low, high):
-        start = ((z + offset) % ZN) * chunk + low
-        own_w = lax.dynamic_slice(out_weight, (y * wo_rows + start, 0), (high - low, width))
-        in_w = lax.dynamic_slice(wo_in, (start, 0), (high - low, width))
-        return dot(piece, own_w), dot(piece, in_w)
-
-    terms = [project(mixed, 0, 0, chunk)]
+    pieces, starts = [mixed], [0]
     from_left, from_right = mixed, mixed
     for step in (1, 2, 3):
         from_left, from_right = both(from_left, from_right)
-        terms.append(project(from_left, -step, 0, chunk))
-        terms.append(project(from_right, step, 0, chunk))
-    terms.append(project(right(from_left[:, :cut]), 4, 0, cut))
-    terms.append(project(left(from_right[:, cut:]), 4, cut, chunk))
-    for_partner = functools.reduce(jnp.add, [t[1] for t in terms])
-    received = lax.ppermute(for_partner.astype(bf16), "tp", y_swap())
-    own_sum, received = lax.optimization_barrier((functools.reduce(jnp.add, [t[0] for t in terms]), received))
+        if step == 2:
+            from_left, from_right, wo_in = lax.optimization_barrier((from_left, from_right, wo_in))
+        pieces += [from_left, from_right]
+        starts += [-step, step]
+    pieces += [right(from_left[:, :cut]), left(from_right[:, cut:])]
+    starts = [(z + offset) % ZN * chunk for offset in starts] + [(z + 4) % ZN * chunk + low for low in (0, cut)]
+    starts = jnp.stack(starts).astype(jnp.int32)
+    for_partner = project(starts, wo_in, pieces, bf16)
+    received = lax.ppermute(for_partner, "tp", y_swap())
+    pieces, for_partner = lax.optimization_barrier((pieces, for_partner))
+    own_sum = project(starts + y * wo_rows, out_weight, pieces, jnp.float32)
+    own_sum, received = lax.optimization_barrier((own_sum, received))
     projected = own_sum + received
     row_update = (jax.nn.sigmoid(router_logit)[:, None] * projected).astype(bf16)
     select = (own_rows.reshape(rows, 1) == jnp.arange(tokens, dtype=jnp.int32)[None, :]).astype(bf16)

time: 190 us -> 223 us (1.17)
  waiting for transfers between devices: 62.7 us -> 111 us
  matrix products: 23.3 us -> 1.99 us
  Pallas kernels: 23 us -> 28.3 us
    reduce_scatter x1, waiting for transfers between devices: 2.39 us -> 28.7 us  [shards(): lax.psum_scatter(part, 'tp', scatter_dimension=0, axis_index_groups=[[2 *...]
    dot_general x18 -> x0, matrix products: 21.3 us -> none  [dot(): return jnp.dot(a, b, preferred_element_type=jnp.float32)]
    ppermute x4, waiting for transfers between devices: 11.9 us -> 21.1 us  [right(): return lax.ppermute(a.astype(bf16), 'tp', z_shift(1))]
    ppermute x4, waiting for transfers between devices: 1.04 us -> 7.67 us  [left(): return lax.ppermute(a.astype(bf16), 'tp', z_shift(-1))]
    pallas_call x0 -> x2, Pallas kernels: none -> 5.36 us  [project(): pl.pallas_call(project_kernel, out_shape=jax.ShapeDtypeStruct((rows, widt...]
    ppermute x4, starting transfers between devices: 4.44 us -> 0.01 us  [right(): return lax.ppermute(a.astype(bf16), 'tp', z_shift(1))]
    ppermute x4, starting transfers between devices: 7.98 us -> 12.4 us  [left(): return lax.ppermute(a.astype(bf16), 'tp', z_shift(-1))]
    ppermute x8, waiting for transfers between devices: 11.9 us -> 15.6 us  [x_hop(): return lax.ppermute(block, 'ctx', along(step))]
  transfers between devices with their start and end apart: 30 -> 30, of which waited for: 18 -> 20; matrix products, arithmetic and copies ran while one was open for 15% -> 3% of each run, Pallas kernels for 10% -> 10%
where the time goes in v10:
time: 223 us; the launch traced here: 222 us
  waiting for transfers between devices  111 us (50%)
  starting transfers between devices  48.6 us (22%)
  Pallas kernels  28.3 us (13%)
  local copies, waits for them, and re-layouts  15.5 us (7%)
  between operations  13.4 us (6%)
  other arithmetic  3.32 us (1%)
    reduce_scatter x1, waiting for transfers between devices, shards(): lax.psum_scatter(part, 'tp', scatter_dimension=0, axis_index_groups=[[2 *...  28.7 us
    all_to_all x1, waiting for transfers between devices, shards(): exchanged = lax.all_to_all(sent, 'tp', 0, 0, tiled=True)  21.3 us
    ppermute x4, waiting for transfers between devices, right(): return lax.ppermute(a.astype(bf16), 'tp', z_shift(1))  21.1 us
    ppermute x8, waiting for transfers between devices, x_hop(): return lax.ppermute(block, 'ctx', along(step))  15.6 us
    ppermute x8, starting transfers between devices, x_hop(): return lax.ppermute(block, 'ctx', along(step))  13.1 us
    ppermute x4, starting transfers between devices, left(): return lax.ppermute(a.astype(bf16), 'tp', z_shift(-1))  12.4 us
    pallas_call x1, Pallas kernels, attention(): pl.pallas_call(attention_kernel, out_shape=jax.ShapeDtypeStruct(queries.s...  11.4 us
    unnamed x28, local copies, waits for them, and re-layouts  11 us
  transfers between devices with their start and end apart: 30, of which 20 were waited for; matrix products, arithmetic and copies ran while one was open for 3% of the time, Pallas kernels for 10%

profile of v10, /device:TPU:14, one launch (start us, length us, event | category | flops | bytes accessed | tf_op | source)
XLA Modules:
  0.0 222.2 jit_solution(17192019603505418725)
XLA Ops:
  7.5 2.4 %collective-permute-start = (bf16[512,256]{1,0:T(8,128)(2,1)S(1)}, bf16[512,256]{1,0:T(8,128)(2,1)S(1)}, u32[]{:S(2)}, u32[]{:S(2)}) collective-permute-start(bf16[512,256]{1,0:T(8,128)(2,1)S(1)} %constant_dynamic-slice_fusion.1), channel_id=1, source_target_pairs={{0,1},{1,0},{2,3},{3,2},{4,5},{5,4},{6,7},{7,6},{8,9},{9,8},{10,11... | collective-permute-start | bytes 786440 | tf_op jit(solution)/shard_map/ppermute | solution.py:356
  12.0 1.2 copy-done.4
  13.2 1.2 copy-done.5
  14.4 2.6 %shard_map.73 = (bf16[512,512]{1,0:T(8,128)(2,1)S(1)}, bf16[16,72,512]{2,1,0:T(8,128)(2,1)}) custom-call(s32[1,512]{1,0:T(1,128)S(1)} %constant_dynamic-slice_fusion.2.rows_ref, bf16[1024,512]{1,0:T(8,128)(2,1)S(1)} %copy-done.4, bf16[1,512]{1,0:T(2,128)(2,1)S(1)} %reshape.429.gain_ref, bf16[1,512]{1,0:T(2,128)(2,1)S(1)} %reshape.430.router_ref, ...), custom_call_target="tpu_custom_call" | custom-call | flops 1073741824 | bytes 5242880 | tf_op jit(solution)/shard_map/pallas_call | solution.py:203
  17.9 10.4 %all-to-all-start = ((bf16[16,72,512]{2,1,0:T(8,128)(2,1)}), bf16[16,72,512]{2,1,0:T(8,128)(2,1)}, u32[]{:S(2)}, u32[]{:S(2)}) async-start(bf16[16,72,512]{2,1,0:T(8,128)(2,1)} %get-tuple-element.52), calls=%async_computation | async-start | bytes 2359296 | tf_op jit(solution)/shard_map/all_to_all | solution.py:364
  28.3 3.5 %collective-permute-start.1 = (bf16[512,512]{1,0:T(8,128)(2,1)S(1)}, bf16[512,512]{1,0:T(8,128)(2,1)S(1)}, u32[]{:S(2)}, u32[]{:S(2)}) collective-permute-start(bf16[512,512]{1,0:T(8,128)(2,1)S(1)} %get-tuple-element.53.x_ref), channel_id=1, source_target_pairs={{0,1},{1,0},{2,3},{3,2},{4,5},{5,4},{6,7},{7,6},{8,9},{9,8},{10,11... | collective-permute-start | bytes 1572872 | tf_op jit(solution)/shard_map/ppermute | solution.py:360
  32.0 2.4 %copy-done = bf16[512,4096]{1,0:T(8,128)(2,1)S(1)} copy-done((bf16[512,4096]{1,0:T(8,128)(2,1)S(1)}, bf16[512,4096]{1,0:T(8,128)(2,1)}, u32[]{:S(2)}) %copy-start) | copy-done | bytes 4194328
  34.4 2.8 %shard_map.74.own_ref = bf16[8,512,256]{2,1,0:T(8,128)(2,1)S(1)} custom-call(s32[1]{0:T(128)} %bitcast.35.y_ref, bf16[512,512]{1,0:T(8,128)(2,1)S(1)} %get-tuple-element.53.x_ref, bf16[512,4096]{1,0:T(8,128)(2,1)S(1)} %copy-done), custom_call_target="tpu_custom_call" | custom-call | flops 1073741824 | bytes 4194304 | tf_op jit(solution)/shard_map/pallas_call | solution.py:254
  37.7 1.0 constant_dynamic-slice_fusion
  38.7 21.3 %all-to-all-done = bf16[16,72,512]{2,1,0:T(8,128)(2,1)} async-done(((bf16[16,72,512]{2,1,0:T(8,128)(2,1)}), bf16[16,72,512]{2,1,0:T(8,128)(2,1)}, u32[]{:S(2)}, u32[]{:S(2)}) %all-to-all-start) | async-done | bytes 1179680 | tf_op jit(solution)/shard_map/all_to_all | solution.py:364
  60.0 1.4 convert_reduce_fusion
  61.5 1.6 copy-done.3
  63.1 4.3 %shard_map.75 = bf16[8,512,256]{2,1,0:T(8,128)(2,1)} custom-call(bf16[512,512]{1,0:T(8,128)(2,1)S(1)} %collective-permute-done.1.x_ref, bf16[8,512,256]{2,1,0:T(8,128)(2,1)S(1)} %bitcast.60, bf16[8,512,256]{2,1,0:T(8,128)(2,1)S(1)} %shard_map.74.own_ref), custom_call_target="tpu_custom_call" | custom-call | flops 1073741824 | bytes 6291456 | tf_op jit(solution)/shard_map/pallas_call | solution.py:276
  68.3 1.7 collective-permute-start.4
  70.0 1.1 collective-permute-start.2
  71.2 1.4 collective-permute-done.4.refs_3_
  72.6 4.1 %collective-permute-done.3.refs_2_ = bf16[64,512]{1,0:T(8,128)(2,1)S(1)} collective-permute-done((bf16[64,512]{1,0:T(8,128)(2,1)S(1)}, bf16[64,512]{1,0:T(8,128)(2,1)S(1)}, u32[]{:S(2)}, u32[]{:S(2)}) %collective-permute-start.3) | collective-permute-done | bytes 65568 | tf_op jit(solution)/shard_map/ppermute | solution.py:386
  76.7 28.7 %reduce-scatter.2.cloned.1.call-done = bf16[1,512,256]{2,1,0:T(8,128)(2,1)} async-done(((bf16[8,512,256]{2,1,0:T(8,128)(2,1)}), bf16[1,512,256]{2,1,0:T(8,128)(2,1)}) %reduce-scatter.2.cloned.1.call-update) | async-done | bytes 262160 | tf_op jit(solution)/shard_map/reduce_scatter | solution.py:383
  105.5 1.8 shard_map.76
  108.7 2.4 %collective-permute-start.6 = (bf16[512,256]{1,0:T(8,128)(2,1)}, bf16[512,256]{1,0:T(8,128)(2,1)S(1)}, u32[]{:S(2)}, u32[]{:S(2)}) collective-permute-start(bf16[512,256]{1,0:T(8,128)(2,1)} %shard_map.76), channel_id=1, source_target_pairs={{0,32},{16,48},{32,64},{48,80},{64,96},{80,112},{96,0},{112,16},{1... | collective-permute-start | bytes 786440 | tf_op jit(solution)/shard_map/ppermute | solution.py:398
  111.1 2.8 %collective-permute-done.8 = bf16[512,256]{1,0:T(8,128)(2,1)S(1)} collective-permute-done((bf16[512,256]{1,0:T(8,128)(2,1)}, bf16[512,256]{1,0:T(8,128)(2,1)S(1)}, u32[]{:S(2)}, u32[]{:S(2)}) %collective-permute-start.8) | collective-permute-done | bytes 262176 | tf_op jit(solution)/shard_map/ppermute | solution.py:401
  113.9 3.3 %collective-permute-done.7 = bf16[512,256]{1,0:T(8,128)(2,1)S(1)} collective-permute-done((bf16[512,256]{1,0:T(8,128)(2,1)}, bf16[512,256]{1,0:T(8,128)(2,1)S(1)}, u32[]{:S(2)}, u32[]{:S(2)}) %collective-permute-start.7) | collective-permute-done | bytes 262176 | tf_op jit(solution)/shard_map/ppermute | solution.py:398
  117.7 3.2 %collective-permute-start.9 = (bf16[512,256]{1,0:T(8,128)(2,1)S(1)}, bf16[512,256]{1,0:T(8,128)(2,1)S(1)}, u32[]{:S(2)}, u32[]{:S(2)}) collective-permute-start(bf16[512,256]{1,0:T(8,128)(2,1)S(1)} %collective-permute-done.8), channel_id=1, source_target_pairs={{0,32},{16,48},{32,64},{48,80},{64,96},{80,112},{96,0},{112,16},{1... | collective-permute-start | bytes 786440 | tf_op jit(solution)/shard_map/ppermute | solution.py:398
  121.1 3.2 %collective-permute-start.11 = (bf16[256,256]{1,0:T(8,128)(2,1)S(1)}, bf16[256,256]{1,0:T(8,128)(2,1)S(1)}, u32[]{:S(2)}, u32[]{:S(2)}) collective-permute-start(bf16[256,256]{1,0:T(8,128)(2,1)S(1)} %slice.38), channel_id=1, source_target_pairs={{0,32},{16,48},{32,64},{48,80},{64,96},{80,112},{96,0},{112,16},{1... | collective-permute-start | bytes 393224 | tf_op jit(solution)/shard_map/ppermute | solution.py:398
  124.3 8.5 %collective-permute-done.12 = bf16[256,256]{1,0:T(8,128)(2,1)S(1)} collective-permute-done((bf16[256,256]{1,0:T(8,128)(2,1)S(1)}, bf16[256,256]{1,0:T(8,128)(2,1)S(1)}, u32[]{:S(2)}, u32[]{:S(2)}) %collective-permute-start.12) | collective-permute-done | bytes 131104 | tf_op jit(solution)/shard_map/ppermute | solution.py:398
  132.8 1.5 collective-permute-done.11
  135.0 2.7 %collective-permute-start.13 = (bf16[256,256]{1,0:T(8,128)(2,1)S(1)}, bf16[256,256]{1,0:T(8,128)(2,1)S(1)}, u32[]{:S(2)}, u32[]{:S(2)}) collective-permute-start(bf16[256,256]{1,0:T(8,128)(2,1)S(1)} %slice.40), channel_id=1, source_target_pairs={{0,32},{16,48},{32,64},{48,80},{64,96},{80,112},{96,0},{112,16},{1... | collective-permute-start | bytes 393224 | tf_op jit(solution)/shard_map/ppermute | solution.py:398
  137.7 1.1 pad_maximum_fusion.refs_0_
  138.9 1.7 collective-permute-done.14
  141.7 2.0 collective-permute-done.16.refs_3_
  143.7 11.4 %shard_map.77.refs_0_ = bf16[512,256]{1,0:T(8,128)(2,1)S(1)} custom-call(s32[16,3]{1,0:T(8,128)S(1)} %copy.11.info_ref, bf16[512,256]{1,0:T(8,128)(2,1)S(1)} %multiply_convert_fusion.2.q_ref, bf16[4,512,256]{2,1,0:T(8,128)(2,1)S(1)} %pad_maximum_fusion.refs_0_, bf16[4,512,256]{2,1,0:T(8,128)(2,1)S(1)} %pad_maximum_fusion.1.refs_1_, ...), custom_call_target="tpu_custom_call" | custom-call | flops 4294967296 | bytes 4194304 | tf_op jit(solution)/shard_map/pallas_call | solution.py:151
  155.1 2.9 %collective-permute-start.18 = (bf16[512,256]{1,0:T(8,128)(2,1)S(1)}, bf16[512,256]{1,0:T(8,128)(2,1)S(1)}, u32[]{:S(2)}, u32[]{:S(2)}) collective-permute-start(bf16[512,256]{1,0:T(8,128)(2,1)S(1)} %shard_map.77.refs_0_), channel_id=1, source_target_pairs={{0,14},{1,15},{2,0},{3,1},{4,2},{5,3},{6,4},{7,5},{8,6},{9,7},{10,... | collective-permute-start | bytes 786440 | tf_op jit(solution)/shard_map/ppermute | solution.py:418
  158.0 5.2 %collective-permute-done.18.refs_2_ = bf16[512,256]{1,0:T(8,128)(2,1)S(1)} collective-permute-done((bf16[512,256]{1,0:T(8,128)(2,1)S(1)}, bf16[512,256]{1,0:T(8,128)(2,1)S(1)}, u32[]{:S(2)}, u32[]{:S(2)}) %collective-permute-start.18) | collective-permute-done | bytes 262176 | tf_op jit(solution)/shard_map/ppermute | solution.py:418
  163.2 4.0 %collective-permute-done.17.refs_1_ = bf16[512,256]{1,0:T(8,128)(2,1)S(1)} collective-permute-done((bf16[512,256]{1,0:T(8,128)(2,1)S(1)}, bf16[512,256]{1,0:T(8,128)(2,1)S(1)}, u32[]{:S(2)}, u32[]{:S(2)}) %collective-permute-start.17) | collective-permute-done | bytes 262176 | tf_op jit(solution)/shard_map/ppermute | solution.py:415
  167.3 3.2 %collective-permute-start.20 = (bf16[512,256]{1,0:T(8,128)(2,1)S(1)}, bf16[512,256]{1,0:T(8,128)(2,1)S(1)}, u32[]{:S(2)}, u32[]{:S(2)}) collective-permute-start(bf16[512,256]{1,0:T(8,128)(2,1)S(1)} %collective-permute-done.18.refs_2_), channel_id=1, source_target_pairs={{0,14},{1,15},{2,0},{3,1},{4,2},{5,3},{6,4},{7,5},{8,6},{9,7},{10,... | collective-permute-start | bytes 786440 | tf_op jit(solution)/shard_map/ppermute | solution.py:418
  170.5 7.2 %collective-permute-done.19.refs_3_ = bf16[512,256]{1,0:T(8,128)(2,1)S(1)} collective-permute-done((bf16[512,256]{1,0:T(8,128)(2,1)S(1)}, bf16[512,256]{1,0:T(8,128)(2,1)S(1)}, u32[]{:S(2)}, u32[]{:S(2)}) %collective-permute-start.19) | collective-permute-done | bytes 262176 | tf_op jit(solution)/shard_map/ppermute | solution.py:415
  177.7 3.2 %collective-permute-start.22 = (bf16[512,256]{1,0:T(8,128)(2,1)S(1)}, bf16[512,256]{1,0:T(8,128)(2,1)S(1)}, u32[]{:S(2)}, u32[]{:S(2)}) collective-permute-start(bf16[512,256]{1,0:T(8,128)(2,1)S(1)} %collective-permute-done.20.refs_4_), channel_id=1, source_target_pairs={{0,14},{1,15},{2,0},{3,1},{4,2},{5,3},{6,4},{7,5},{8,6},{9,7},{10,... | collective-permute-start | bytes 786440 | tf_op jit(solution)/shard_map/ppermute | solution.py:418
  180.9 6.3 %collective-permute-done.21.refs_5_ = bf16[512,256]{1,0:T(8,128)(2,1)S(1)} collective-permute-done((bf16[512,256]{1,0:T(8,128)(2,1)S(1)}, bf16[512,256]{1,0:T(8,128)(2,1)S(1)}, u32[]{:S(2)}, u32[]{:S(2)}) %collective-permute-start.21) | collective-permute-done | bytes 262176 | tf_op jit(solution)/shard_map/ppermute | solution.py:415
  187.2 3.0 %collective-permute-start.24 = (bf16[512,128]{1,0:T(8,128)(2,1)S(1)}, bf16[512,128]{1,0:T(8,128)(2,1)S(1)}, u32[]{:S(2)}, u32[]{:S(2)}) collective-permute-start(bf16[512,128]{1,0:T(8,128)(2,1)S(1)} %slice.43), channel_id=1, source_target_pairs={{0,14},{1,15},{2,0},{3,1},{4,2},{5,3},{6,4},{7,5},{8,6},{9,7},{10,... | collective-permute-start | bytes 393224 | tf_op jit(solution)/shard_map/ppermute | solution.py:418
  190.3 2.4 %collective-permute-done.24.refs_8_ = bf16[512,128]{1,0:T(8,128)(2,1)S(1)} collective-permute-done((bf16[512,128]{1,0:T(8,128)(2,1)S(1)}, bf16[512,128]{1,0:T(8,128)(2,1)S(1)}, u32[]{:S(2)}, u32[]{:S(2)}) %collective-permute-start.24) | collective-permute-done | bytes 131104 | tf_op jit(solution)/shard_map/ppermute | solution.py:418
  192.8 3.7 %collective-permute-done.23.refs_7_ = bf16[512,128]{1,0:T(8,128)(2,1)S(1)} collective-permute-done((bf16[512,128]{1,0:T(8,128)(2,1)S(1)}, bf16[512,128]{1,0:T(8,128)(2,1)S(1)}, u32[]{:S(2)}, u32[]{:S(2)}) %collective-permute-start.23) | collective-permute-done | bytes 131104 | tf_op jit(solution)/shard_map/ppermute | solution.py:415
  196.4 1.6 copy-done.2
  198.0 2.7 %shard_map.78 = bf16[512,512]{1,0:T(8,128)(2,1)S(1)} custom-call(s32[9]{0:T(128)S(1)} %stack.146.starts_ref, bf16[2048,512]{1,0:T(8,128)(2,1)S(1)} %copy-done.2, bf16[512,256]{1,0:T(8,128)(2,1)S(1)} %shard_map.77.refs_0_, bf16[512,256]{1,0:T(8,128)(2,1)S(1)} %collective-permute-done.17.refs_1_, bf16[512,256]{1,0:T(8,128)(2,1)S(1)} %collective-permute-done.18.refs_2_, ...), custom_call_target="tpu_custom_call" | custom-call | flops 1073741824 | bytes 5242880 | tf_op jit(solution)/shard_map/pallas_call | solution.py:319
  200.7 2.5 %collective-permute-start.25 = (bf16[512,512]{1,0:T(8,128)(2,1)S(1)}, bf16[512,512]{1,0:T(8,128)(2,1)S(1)}, u32[]{:S(2)}, u32[]{:S(2)}) collective-permute-start(bf16[512,512]{1,0:T(8,128)(2,1)S(1)} %shard_map.78), channel_id=1, source_target_pairs={{0,1},{1,0},{2,3},{3,2},{4,5},{5,4},{6,7},{7,6},{8,9},{9,8},{10,11... | collective-permute-start | bytes 1572872 | tf_op jit(solution)/shard_map/ppermute | solution.py:440
  203.2 2.2 copy-done.1
  205.4 2.7 %shard_map.79 = f32[512,512]{1,0:T(8,128)S(1)} custom-call(s32[9]{0:T(128)S(1)} %broadcast_add_fusion.starts_ref, bf16[4096,512]{1,0:T(8,128)(2,1)S(1)} %copy-done.1, bf16[512,256]{1,0:T(8,128)(2,1)S(1)} %shard_map.77.refs_0_, bf16[512,256]{1,0:T(8,128)(2,1)S(1)} %collective-permute-done.17.refs_1_, bf16[512,256]{1,0:T(8,128)(2,1)S(1)} %collective-permute-done.18.refs_2_, ...), custom_call_target="tpu_custom_call" | custom-call | flops 1073741824 | bytes 5242880 | tf_op jit(solution)/shard_map/pallas_call | solution.py:319
  208.1 5.6 %collective-permute-done.25 = bf16[512,512]{1,0:T(8,128)(2,1)S(1)} collective-permute-done((bf16[512,512]{1,0:T(8,128)(2,1)S(1)}, bf16[512,512]{1,0:T(8,128)(2,1)S(1)}, u32[]{:S(2)}, u32[]{:S(2)}) %collective-permute-start.25) | collective-permute-done | bytes 524320 | tf_op jit(solution)/shard_map/ppermute | solution.py:440
  213.7 2.0 fusion.1
  (82 shorter events, 9.5 us)
Async XLA Ops:
  6.5 53.5 %all-gather.5.cloned.1.call-start = ((), (), s32[]{:S(2)}) async-start(), calls=%async_computation.3 | async-start | bytes 2359296 | tf_op jit(solution)/shard_map/all_gather | solution.py:353
  7.5 9.6 %collective-permute-start = (bf16[512,256]{1,0:T(8,128)(2,1)S(1)}, bf16[512,256]{1,0:T(8,128)(2,1)S(1)}, u32[]{:S(2)}, u32[]{:S(2)}) collective-permute-start(bf16[512,256]{1,0:T(8,128)(2,1)S(1)} %constant_dynamic-slice_fusion.1), channel_id=1, source_target_pairs={{0,1},{1,0},{2,3},{3,2},{4,5},{5,4},{6,7},{7,6},{8,9},{9,8},{10,11... | collective-permute-start | bytes 786440 | tf_op jit(solution)/shard_map/ppermute | solution.py:356
  12.0 1.2 copy-start.4
  13.2 1.2 copy-start.5
  17.1 0.7 copy-start.7
  17.9 42.1 %all-to-all-start = ((bf16[16,72,512]{2,1,0:T(8,128)(2,1)}), bf16[16,72,512]{2,1,0:T(8,128)(2,1)}, u32[]{:S(2)}, u32[]{:S(2)}) async-start(bf16[16,72,512]{2,1,0:T(8,128)(2,1)} %get-tuple-element.52), calls=%async_computation | async-start | bytes 2359296 | tf_op jit(solution)/shard_map/all_to_all | solution.py:364
  28.2 77.2 %reduce-scatter.2.cloned.1.call-start = ((), (), s32[]{:S(2)}) async-start(), calls=%async_computation.2 | async-start | bytes 2359296 | tf_op jit(solution)/shard_map/reduce_scatter | solution.py:383
  28.3 33.2 %collective-permute-start.1 = (bf16[512,512]{1,0:T(8,128)(2,1)S(1)}, bf16[512,512]{1,0:T(8,128)(2,1)S(1)}, u32[]{:S(2)}, u32[]{:S(2)}) collective-permute-start(bf16[512,512]{1,0:T(8,128)(2,1)S(1)} %get-tuple-element.53.x_ref), channel_id=1, source_target_pairs={{0,1},{1,0},{2,3},{3,2},{4,5},{5,4},{6,7},{7,6},{8,9},{9,8},{10,11... | collective-permute-start | bytes 1572872 | tf_op jit(solution)/shard_map/ppermute | solution.py:360
  32.0 2.5 %copy-start = (bf16[512,4096]{1,0:T(8,128)(2,1)S(1)}, bf16[512,4096]{1,0:T(8,128)(2,1)}, u32[]{:S(2)}) copy-start(bf16[512,4096]{1,0:T(8,128)(2,1)} %w_ref.1) | copy-start | bytes 12582916
  34.4 2.8 %copy-start.13 = (s32[16,512]{1,0:T(8,128)S(1)}, s32[16,512]{1,0:T(8,128)}, u32[]{:S(2)}) copy-start(s32[16,512]{1,0:T(8,128)} %param.13) | copy-start | bytes 98308
  61.5 8.5 %copy-start.6 = (bf16[64,512]{1,0:T(8,128)(2,1)}, bf16[64,512]{1,0:T(8,128)(2,1)S(1)}, u32[]{:S(2)}) copy-start(bf16[64,512]{1,0:T(8,128)(2,1)S(1)} %fusion.4.refs_0_) | copy-start | bytes 196612
  61.5 1.6 copy-start.3
  67.5 110.2 %all-gather.7.cloned.1.call-start = ((), (), s32[]{:S(2)}) async-start(), calls=%async_computation.4 | async-start | bytes 2359296 | tf_op jit(solution)/shard_map/all_gather | solution.py:353
  67.5 9.2 %collective-permute-start.5 = (bf16[256,512]{1,0:T(8,128)(2,1)S(1)}, bf16[256,512]{1,0:T(8,128)(2,1)S(1)}, u32[]{:S(2)}, u32[]{:S(2)}) collective-permute-start(bf16[256,512]{1,0:T(8,128)(2,1)S(1)} %constant_dynamic-slice_fusion), channel_id=1, source_target_pairs={{0,1},{1,0},{2,3},{3,2},{4,5},{5,4},{6,7},{7,6},{8,9},{9,8},{10,11... | collective-permute-start | bytes 786440 | tf_op jit(solution)/shard_map/ppermute | solution.py:387
  68.3 4.3 %collective-permute-start.4 = (bf16[64,512]{1,0:T(8,128)(2,1)S(1)}, bf16[64,512]{1,0:T(8,128)(2,1)S(1)}, u32[]{:S(2)}, u32[]{:S(2)}) collective-permute-start(bf16[64,512]{1,0:T(8,128)(2,1)S(1)} %fusion.4.refs_0_), channel_id=1, source_target_pairs={{0,6},{1,7},{2,0},{3,1},{4,2},{5,3},{6,4},{7,5},{8,14},{9,15},{10,... | collective-permute-start | bytes 196616 | tf_op jit(solution)/shard_map/ppermute | solution.py:386
  70.0 6.7 %collective-permute-start.3 = (bf16[64,512]{1,0:T(8,128)(2,1)S(1)}, bf16[64,512]{1,0:T(8,128)(2,1)S(1)}, u32[]{:S(2)}, u32[]{:S(2)}) collective-permute-start(bf16[64,512]{1,0:T(8,128)(2,1)S(1)} %fusion.4.refs_0_), channel_id=1, source_target_pairs={{0,4},{1,5},{2,6},{3,7},{4,0},{5,1},{6,2},{7,3},{8,12},{9,13},{10,... | collective-permute-start | bytes 196616 | tf_op jit(solution)/shard_map/ppermute | solution.py:386
  70.0 6.7 %collective-permute-start.2 = (bf16[64,512]{1,0:T(8,128)(2,1)S(1)}, bf16[64,512]{1,0:T(8,128)(2,1)S(1)}, u32[]{:S(2)}, u32[]{:S(2)}) collective-permute-start(bf16[64,512]{1,0:T(8,128)(2,1)S(1)} %fusion.4.refs_0_), channel_id=1, source_target_pairs={{0,2},{1,3},{2,4},{3,5},{4,6},{5,7},{6,0},{7,1},{8,10},{9,11},{10,... | collective-permute-start | bytes 196616 | tf_op jit(solution)/shard_map/ppermute | solution.py:386
  72.6 32.9 %copy-start.10 = (bf16[64,512]{1,0:T(8,128)(2,1)}, bf16[64,512]{1,0:T(8,128)(2,1)S(1)}, u32[]{:S(2)}) copy-start(bf16[64,512]{1,0:T(8,128)(2,1)S(1)} %collective-permute-done.4.refs_3_) | copy-start | bytes 196612
  76.7 28.8 %copy-start.11 = (bf16[64,512]{1,0:T(8,128)(2,1)}, bf16[64,512]{1,0:T(8,128)(2,1)S(1)}, u32[]{:S(2)}) copy-start(bf16[64,512]{1,0:T(8,128)(2,1)S(1)} %collective-permute-done.3.refs_2_) | copy-start | bytes 196612
  76.7 28.8 %copy-start.12 = (bf16[64,512]{1,0:T(8,128)(2,1)}, bf16[64,512]{1,0:T(8,128)(2,1)S(1)}, u32[]{:S(2)}) copy-start(bf16[64,512]{1,0:T(8,128)(2,1)S(1)} %collective-permute-done.2.refs_1_) | copy-start | bytes 196612
  76.7 28.7 %copy-start.8 = (bf16[256,512]{1,0:T(8,128)(2,1)}, bf16[256,512]{1,0:T(8,128)(2,1)S(1)}, u32[]{:S(2)}) copy-start(bf16[256,512]{1,0:T(8,128)(2,1)S(1)} %collective-permute-done.5) | copy-start | bytes 786436
  107.3 6.6 %collective-permute-start.8 = (bf16[512,256]{1,0:T(8,128)(2,1)}, bf16[512,256]{1,0:T(8,128)(2,1)S(1)}, u32[]{:S(2)}, u32[]{:S(2)}) collective-permute-start(bf16[512,256]{1,0:T(8,128)(2,1)} %shard_map.76), channel_id=1, source_target_pairs={{0,128},{16,144},{32,160},{48,176},{64,192},{80,208},{96,224},{112... | collective-permute-start | bytes 786440 | tf_op jit(solution)/shard_map/ppermute | solution.py:401
  107.8 9.4 %collective-permute-start.7 = (bf16[512,256]{1,0:T(8,128)(2,1)}, bf16[512,256]{1,0:T(8,128)(2,1)S(1)}, u32[]{:S(2)}, u32[]{:S(2)}) collective-permute-start(bf16[512,256]{1,0:T(8,128)(2,1)} %shard_map.76), channel_id=1, source_target_pairs={{0,96},{16,112},{32,0},{48,16},{64,32},{80,48},{96,64},{112,80},{1... | collective-permute-start | bytes 786440 | tf_op jit(solution)/shard_map/ppermute | solution.py:398
  108.7 9.0 %collective-permute-start.6 = (bf16[512,256]{1,0:T(8,128)(2,1)}, bf16[512,256]{1,0:T(8,128)(2,1)S(1)}, u32[]{:S(2)}, u32[]{:S(2)}) collective-permute-start(bf16[512,256]{1,0:T(8,128)(2,1)} %shard_map.76), channel_id=1, source_target_pairs={{0,32},{16,48},{32,64},{48,80},{64,96},{80,112},{96,0},{112,16},{1... | collective-permute-start | bytes 786440 | tf_op jit(solution)/shard_map/ppermute | solution.py:398
  117.7 16.6 %collective-permute-start.10 = (bf16[512,256]{1,0:T(8,128)(2,1)S(1)}, bf16[512,256]{1,0:T(8,128)(2,1)S(1)}, u32[]{:S(2)}, u32[]{:S(2)}) collective-permute-start(bf16[512,256]{1,0:T(8,128)(2,1)S(1)} %collective-permute-done.8), channel_id=1, source_target_pairs={{0,96},{16,112},{32,0},{48,16},{64,32},{80,48},{96,64},{112,80},{1... | collective-permute-start | bytes 786440 | tf_op jit(solution)/shard_map/ppermute | solution.py:398
  117.7 16.6 %collective-permute-start.9 = (bf16[512,256]{1,0:T(8,128)(2,1)S(1)}, bf16[512,256]{1,0:T(8,128)(2,1)S(1)}, u32[]{:S(2)}, u32[]{:S(2)}) collective-permute-start(bf16[512,256]{1,0:T(8,128)(2,1)S(1)} %collective-permute-done.8), channel_id=1, source_target_pairs={{0,32},{16,48},{32,64},{48,80},{64,96},{80,112},{96,0},{112,16},{1... | collective-permute-start | bytes 786440 | tf_op jit(solution)/shard_map/ppermute | solution.py:398
  121.0 11.8 %collective-permute-start.12 = (bf16[256,256]{1,0:T(8,128)(2,1)S(1)}, bf16[256,256]{1,0:T(8,128)(2,1)S(1)}, u32[]{:S(2)}, u32[]{:S(2)}) collective-permute-start(bf16[256,256]{1,0:T(8,128)(2,1)S(1)} %slice.39), channel_id=1, source_target_pairs={{0,96},{16,112},{32,0},{48,16},{64,32},{80,48},{96,64},{112,80},{1... | collective-permute-start | bytes 393224 | tf_op jit(solution)/shard_map/ppermute | solution.py:398
  121.1 13.2 %collective-permute-start.11 = (bf16[256,256]{1,0:T(8,128)(2,1)S(1)}, bf16[256,256]{1,0:T(8,128)(2,1)S(1)}, u32[]{:S(2)}, u32[]{:S(2)}) collective-permute-start(bf16[256,256]{1,0:T(8,128)(2,1)S(1)} %slice.38), channel_id=1, source_target_pairs={{0,32},{16,48},{32,64},{48,80},{64,96},{80,112},{96,0},{112,16},{1... | collective-permute-start | bytes 393224 | tf_op jit(solution)/shard_map/ppermute | solution.py:398
  134.4 6.3 %collective-permute-start.14 = (bf16[256,256]{1,0:T(8,128)(2,1)S(1)}, bf16[256,256]{1,0:T(8,128)(2,1)S(1)}, u32[]{:S(2)}, u32[]{:S(2)}) collective-permute-start(bf16[256,256]{1,0:T(8,128)(2,1)S(1)} %slice.41), channel_id=1, source_target_pairs={{0,96},{16,112},{32,0},{48,16},{64,32},{80,48},{96,64},{112,80},{1... | collective-permute-start | bytes 393224 | tf_op jit(solution)/shard_map/ppermute | solution.py:398
  135.0 5.6 %collective-permute-start.13 = (bf16[256,256]{1,0:T(8,128)(2,1)S(1)}, bf16[256,256]{1,0:T(8,128)(2,1)S(1)}, u32[]{:S(2)}, u32[]{:S(2)}) collective-permute-start(bf16[256,256]{1,0:T(8,128)(2,1)S(1)} %slice.40), channel_id=1, source_target_pairs={{0,32},{16,48},{32,64},{48,80},{64,96},{80,112},{96,0},{112,16},{1... | collective-permute-start | bytes 393224 | tf_op jit(solution)/shard_map/ppermute | solution.py:398
  138.8 2.2 copy-start.9
  138.8 2.9 %collective-permute-start.15 = (bf16[4,512,256]{2,1,0:T(8,128)(2,1)S(1)}, bf16[4,512,256]{2,1,0:T(8,128)(2,1)}, u32[]{:S(2)}, u32[]{:S(2)}) collective-permute-start(bf16[4,512,256]{2,1,0:T(8,128)(2,1)S(1)} %pad_maximum_fusion.refs_0_), channel_id=1, source_target_pairs={{0,16},{16,0},{32,48},{48,32},{64,80},{80,64},{96,112},{112,96},{1... | collective-permute-start | bytes 3145736 | tf_op jit(solution)/shard_map/ppermute | solution.py:411
  140.8 2.9 %collective-permute-start.16 = (bf16[4,512,256]{2,1,0:T(8,128)(2,1)S(1)}, bf16[4,512,256]{2,1,0:T(8,128)(2,1)}, u32[]{:S(2)}, u32[]{:S(2)}) collective-permute-start(bf16[4,512,256]{2,1,0:T(8,128)(2,1)S(1)} %pad_maximum_fusion.1.refs_1_), channel_id=1, source_target_pairs={{0,16},{16,0},{32,48},{48,32},{64,80},{80,64},{96,112},{112,96},{1... | collective-permute-start | bytes 3145736 | tf_op jit(solution)/shard_map/ppermute | solution.py:411
  155.1 8.1 %collective-permute-start.18 = (bf16[512,256]{1,0:T(8,128)(2,1)S(1)}, bf16[512,256]{1,0:T(8,128)(2,1)S(1)}, u32[]{:S(2)}, u32[]{:S(2)}) collective-permute-start(bf16[512,256]{1,0:T(8,128)(2,1)S(1)} %shard_map.77.refs_0_), channel_id=1, source_target_pairs={{0,14},{1,15},{2,0},{3,1},{4,2},{5,3},{6,4},{7,5},{8,6},{9,7},{10,... | collective-permute-start | bytes 786440 | tf_op jit(solution)/shard_map/ppermute | solution.py:418
  158.0 9.2 %collective-permute-start.17 = (bf16[512,256]{1,0:T(8,128)(2,1)S(1)}, bf16[512,256]{1,0:T(8,128)(2,1)S(1)}, u32[]{:S(2)}, u32[]{:S(2)}) collective-permute-start(bf16[512,256]{1,0:T(8,128)(2,1)S(1)} %shard_map.77.refs_0_), channel_id=1, source_target_pairs={{0,2},{1,3},{2,4},{3,5},{4,6},{5,7},{6,8},{7,9},{8,10},{9,11},{10,... | collective-permute-start | bytes 786440 | tf_op jit(solution)/shard_map/ppermute | solution.py:415
  167.3 10.4 %collective-permute-start.19 = (bf16[512,256]{1,0:T(8,128)(2,1)S(1)}, bf16[512,256]{1,0:T(8,128)(2,1)S(1)}, u32[]{:S(2)}, u32[]{:S(2)}) collective-permute-start(bf16[512,256]{1,0:T(8,128)(2,1)S(1)} %collective-permute-done.17.refs_1_), channel_id=1, source_target_pairs={{0,2},{1,3},{2,4},{3,5},{4,6},{5,7},{6,8},{7,9},{8,10},{9,11},{10,... | collective-permute-start | bytes 786440 | tf_op jit(solution)/shard_map/ppermute | solution.py:415
  167.3 10.4 %collective-permute-start.20 = (bf16[512,256]{1,0:T(8,128)(2,1)S(1)}, bf16[512,256]{1,0:T(8,128)(2,1)S(1)}, u32[]{:S(2)}, u32[]{:S(2)}) collective-permute-start(bf16[512,256]{1,0:T(8,128)(2,1)S(1)} %collective-permute-done.18.refs_2_), channel_id=1, source_target_pairs={{0,14},{1,15},{2,0},{3,1},{4,2},{5,3},{6,4},{7,5},{8,6},{9,7},{10,... | collective-permute-start | bytes 786440 | tf_op jit(solution)/shard_map/ppermute | solution.py:418
  177.6 9.5 %collective-permute-start.21 = (bf16[512,256]{1,0:T(8,128)(2,1)S(1)}, bf16[512,256]{1,0:T(8,128)(2,1)S(1)}, u32[]{:S(2)}, u32[]{:S(2)}) collective-permute-start(bf16[512,256]{1,0:T(8,128)(2,1)S(1)} %collective-permute-done.19.refs_3_), channel_id=1, source_target_pairs={{0,2},{1,3},{2,4},{3,5},{4,6},{5,7},{6,8},{7,9},{8,10},{9,11},{10,... | collective-permute-start | bytes 786440 | tf_op jit(solution)/shard_map/ppermute | solution.py:415
  177.7 9.5 %collective-permute-start.22 = (bf16[512,256]{1,0:T(8,128)(2,1)S(1)}, bf16[512,256]{1,0:T(8,128)(2,1)S(1)}, u32[]{:S(2)}, u32[]{:S(2)}) collective-permute-start(bf16[512,256]{1,0:T(8,128)(2,1)S(1)} %collective-permute-done.20.refs_4_), channel_id=1, source_target_pairs={{0,14},{1,15},{2,0},{3,1},{4,2},{5,3},{6,4},{7,5},{8,6},{9,7},{10,... | collective-permute-start | bytes 786440 | tf_op jit(solution)/shard_map/ppermute | solution.py:418
  187.2 5.6 %collective-permute-start.24 = (bf16[512,128]{1,0:T(8,128)(2,1)S(1)}, bf16[512,128]{1,0:T(8,128)(2,1)S(1)}, u32[]{:S(2)}, u32[]{:S(2)}) collective-permute-start(bf16[512,128]{1,0:T(8,128)(2,1)S(1)} %slice.43), channel_id=1, source_target_pairs={{0,14},{1,15},{2,0},{3,1},{4,2},{5,3},{6,4},{7,5},{8,6},{9,7},{10,... | collective-permute-start | bytes 393224 | tf_op jit(solution)/shard_map/ppermute | solution.py:418
  190.2 6.2 %collective-permute-start.23 = (bf16[512,128]{1,0:T(8,128)(2,1)S(1)}, bf16[512,128]{1,0:T(8,128)(2,1)S(1)}, u32[]{:S(2)}, u32[]{:S(2)}) collective-permute-start(bf16[512,128]{1,0:T(8,128)(2,1)S(1)} %slice.42), channel_id=1, source_target_pairs={{0,2},{1,3},{2,4},{3,5},{4,6},{5,7},{6,8},{7,9},{8,10},{9,11},{10,... | collective-permute-start | bytes 393224 | tf_op jit(solution)/shard_map/ppermute | solution.py:415
  196.4 1.6 copy-start.2
  200.7 12.9 %collective-permute-start.25 = (bf16[512,512]{1,0:T(8,128)(2,1)S(1)}, bf16[512,512]{1,0:T(8,128)(2,1)S(1)}, u32[]{:S(2)}, u32[]{:S(2)}) collective-permute-start(bf16[512,512]{1,0:T(8,128)(2,1)S(1)} %shard_map.78), channel_id=1, source_target_pairs={{0,1},{1,0},{2,3},{3,2},{4,5},{5,4},{6,7},{7,6},{8,9},{9,8},{10,11... | collective-permute-start | bytes 1572872 | tf_op jit(solution)/shard_map/ppermute | solution.py:440
  203.2 2.2 copy-start.1
Sparse Core Ops, SparseCore 0:
  18.0 29.2 all-gather.4
  67.6 37.7 reduce-scatter.1
  107.3 28.4 all-gather.6

commit v11 on v10

--- a/solution.py
+++ b/solution.py
@@ -386,8 +386,6 @@
     pieces = [lax.ppermute(piece, "tp", quad_shift(k)) for k in (1, 2, 3)]
     wo_got = lax.ppermute(wo_sent, "tp", y_swap())
     pieces, wo_got = lax.optimization_barrier(([piece] + pieces, wo_got))
-    query_sum, wo_got = lax.optimization_barrier((query_sum, wo_got))
-    wo_in = share(wo_got).reshape(wo_rows, width)
     kv_own = ordered_rows(z % 4, pieces)
 
 
@@ -399,7 +397,8 @@
 
     middle = rows // 2
     over = lax.ppermute(kv_own, "ctx", [(c, (c + shard_n // 2) % shard_n) for c in range(shard_n)])
-    near_left, near_right, over = lax.optimization_barrier((x_hop(kv_own, 1), x_hop(kv_own, -1), over))
+    near_left, near_right, over, wo_got = lax.optimization_barrier((x_hop(kv_own, 1), x_hop(kv_own, -1), over, wo_got))
+    wo_in = share(wo_got).reshape(wo_rows, width)
     first_half = jnp.stack([kv_own, near_left, near_right, over])
     far = x_hop(near_left[:middle], 1), x_hop(near_right[middle:], -1)
     over_left, over_right = x_hop(over, 1), x_hop(over, -1)
@@ -429,17 +428,20 @@
     from_left, from_right = mixed, mixed
     for step in (1, 2, 3):
         from_left, from_right = both(from_left, from_right)
-        if step == 2:
-            from_left, from_right, wo_in = lax.optimization_barrier((from_left, from_right, wo_in))
         pieces += [from_left, from_right]
         starts += [-step, step]
     pieces += [right(from_left[:, :cut]), left(from_right[:, cut:])]
     starts = [(z + offset) % ZN * chunk for offset in starts] + [(z + 4) % ZN * chunk + low for low in (0, cut)]
-    starts = jnp.stack(starts).astype(jnp.int32)
-    for_partner = project(starts, wo_in, pieces, bf16)
+    for_partner = functools.reduce(
+        jnp.add,
+        [
+            dot(piece, lax.dynamic_slice(wo_in, (start, 0), (piece.shape[1], width)))
+            for piece, start in zip(pieces, starts)
+        ],
+    ).astype(bf16)
     received = lax.ppermute(for_partner, "tp", y_swap())
     pieces, for_partner = lax.optimization_barrier((pieces, for_partner))
-    own_sum = project(starts + y * wo_rows, out_weight, pieces, jnp.float32)
+    own_sum = project(jnp.stack(starts).astype(jnp.int32) + y * wo_rows, out_weight, pieces, jnp.float32)
     own_sum, received = lax.optimization_barrier((own_sum, received))
     projected = own_sum + received
     row_update = (jax.nn.sigmoid(router_logit)[:, None] * projected).astype(bf16)

time: 223 us -> 182 us (0.82)
  waiting for transfers between devices: 111 us -> 67.7 us
  matrix products: 1.99 us -> 6.94 us
  Pallas kernels: 28.3 us -> 25.6 us
    reduce_scatter x1, waiting for transfers between devices: 28.7 us -> 0.21 us  [shards(): lax.psum_scatter(part, 'tp', scatter_dimension=0, axis_index_groups=[[2 *...]
    ppermute x8, waiting for transfers between devices: 15.6 us -> 7.5 us  [x_hop(): return lax.ppermute(block, 'ctx', along(step))]
    dot_general x0 -> x9, matrix products: none -> 4.96 us  [dot(): return jnp.dot(a, b, preferred_element_type=jnp.float32)]
    ppermute x4, waiting for transfers between devices: 21.1 us -> 17.5 us  [right(): return lax.ppermute(a.astype(bf16), 'tp', z_shift(1))]
    ppermute x4, starting transfers between devices: 12.4 us -> 9.18 us  [left(): return lax.ppermute(a.astype(bf16), 'tp', z_shift(-1))]
    pallas_call x2 -> x1, Pallas kernels: 5.36 us -> 2.68 us  [project(): pl.pallas_call(project_kernel, out_shape=jax.ShapeDtypeStruct((rows, widt...]
    ppermute x4, starting transfers between devices: 0.01 us -> 2.62 us  [right(): return lax.ppermute(a.astype(bf16), 'tp', z_shift(1))]
    unnamed x28 -> x26, local copies, waits for them, and re-layouts: 11 us -> 10 us
  transfers between devices with their start and end apart: 30 -> 30, of which waited for: 20 -> 17; matrix products, arithmetic and copies ran while one was open for 3% -> 7% of each run, Pallas kernels for 10% -> 12%
where the time goes in v11:
time: 182 us
  waiting for transfers between devices  67.7 us (37%)
  starting transfers between devices  49.2 us (27%)
  Pallas kernels  25.6 us (14%)
  local copies, waits for them, and re-layouts  14.5 us (8%)
  between operations  13.4 us (7%)
  matrix products  6.94 us (4%)
  other arithmetic  4.27 us (2%)
    all_to_all x1, waiting for transfers between devices, shards(): exchanged = lax.all_to_all(sent, 'tp', 0, 0, tiled=True)  21.3 us
    ppermute x4, waiting for transfers between devices, right(): return lax.ppermute(a.astype(bf16), 'tp', z_shift(1))  17.5 us
    ppermute x8, starting transfers between devices, x_hop(): return lax.ppermute(block, 'ctx', along(step))  13.7 us
    pallas_call x1, Pallas kernels, attention(): pl.pallas_call(attention_kernel, out_shape=jax.ShapeDtypeStruct(queries.s...  11.4 us
    all_to_all x1, starting transfers between devices, shards(): exchanged = lax.all_to_all(sent, 'tp', 0, 0, tiled=True)  10.4 us
    unnamed x26, local copies, waits for them, and re-layouts  10 us
    ppermute x4, starting transfers between devices, left(): return lax.ppermute(a.astype(bf16), 'tp', z_shift(-1))  9.18 us
    ppermute x8, waiting for transfers between devices, x_hop(): return lax.ppermute(block, 'ctx', along(step))  7.5 us
  transfers between devices with their start and end apart: 30, of which 17 were waited for; matrix products, arithmetic and copies ran while one was open for 7% of the time, Pallas kernels for 12%

profile of v11, /device:TPU:14, one launch (start us, length us, event | category | flops | bytes accessed | tf_op | source)
XLA Modules:
  0.0 181.7 jit_solution(1061765445934839379)
XLA Ops:
  7.5 2.4 %collective-permute-start = (bf16[512,256]{1,0:T(8,128)(2,1)S(1)}, bf16[512,256]{1,0:T(8,128)(2,1)S(1)}, u32[]{:S(2)}, u32[]{:S(2)}) collective-permute-start(bf16[512,256]{1,0:T(8,128)(2,1)S(1)} %constant_dynamic-slice_fusion.1), channel_id=1, source_target_pairs={{0,1},{1,0},{2,3},{3,2},{4,5},{5,4},{6,7},{7,6},{8,9},{9,8},{10,11... | collective-permute-start | bytes 786440 | tf_op jit(solution)/shard_map/ppermute | solution.py:356
  12.0 1.2 copy-done.3
  13.2 1.2 copy-done.4
  14.4 2.6 %shard_map.73 = (bf16[512,512]{1,0:T(8,128)(2,1)S(1)}, bf16[16,72,512]{2,1,0:T(8,128)(2,1)}) custom-call(s32[1,512]{1,0:T(1,128)S(1)} %constant_dynamic-slice_fusion.2.rows_ref, bf16[1024,512]{1,0:T(8,128)(2,1)S(1)} %copy-done.3, bf16[1,512]{1,0:T(2,128)(2,1)S(1)} %reshape.431.gain_ref, bf16[1,512]{1,0:T(2,128)(2,1)S(1)} %reshape.432.router_ref, ...), custom_call_target="tpu_custom_call" | custom-call | flops 1073741824 | bytes 5242880 | tf_op jit(solution)/shard_map/pallas_call | solution.py:203
  17.9 10.4 %all-to-all-start = ((bf16[16,72,512]{2,1,0:T(8,128)(2,1)}), bf16[16,72,512]{2,1,0:T(8,128)(2,1)}, u32[]{:S(2)}, u32[]{:S(2)}) async-start(bf16[16,72,512]{2,1,0:T(8,128)(2,1)} %get-tuple-element.48), calls=%async_computation | async-start | bytes 2359296 | tf_op jit(solution)/shard_map/all_to_all | solution.py:364
  28.3 3.5 %collective-permute-start.1 = (bf16[512,512]{1,0:T(8,128)(2,1)S(1)}, bf16[512,512]{1,0:T(8,128)(2,1)S(1)}, u32[]{:S(2)}, u32[]{:S(2)}) collective-permute-start(bf16[512,512]{1,0:T(8,128)(2,1)S(1)} %get-tuple-element.49.x_ref), channel_id=1, source_target_pairs={{0,1},{1,0},{2,3},{3,2},{4,5},{5,4},{6,7},{7,6},{8,9},{9,8},{10,11... | collective-permute-start | bytes 1572872 | tf_op jit(solution)/shard_map/ppermute | solution.py:360
  32.0 2.4 %copy-done = bf16[512,4096]{1,0:T(8,128)(2,1)S(1)} copy-done((bf16[512,4096]{1,0:T(8,128)(2,1)S(1)}, bf16[512,4096]{1,0:T(8,128)(2,1)}, u32[]{:S(2)}) %copy-start) | copy-done | bytes 4194328
  34.4 2.8 %shard_map.74.own_ref = bf16[8,512,256]{2,1,0:T(8,128)(2,1)S(1)} custom-call(s32[1]{0:T(128)} %bitcast.35.y_ref, bf16[512,512]{1,0:T(8,128)(2,1)S(1)} %get-tuple-element.49.x_ref, bf16[512,4096]{1,0:T(8,128)(2,1)S(1)} %copy-done), custom_call_target="tpu_custom_call" | custom-call | flops 1073741824 | bytes 4194304 | tf_op jit(solution)/shard_map/pallas_call | solution.py:254
  37.7 1.0 constant_dynamic-slice_fusion
  38.7 21.3 %all-to-all-done = bf16[16,72,512]{2,1,0:T(8,128)(2,1)} async-done(((bf16[16,72,512]{2,1,0:T(8,128)(2,1)}), bf16[16,72,512]{2,1,0:T(8,128)(2,1)}, u32[]{:S(2)}, u32[]{:S(2)}) %all-to-all-start) | async-done | bytes 1179680 | tf_op jit(solution)/shard_map/all_to_all | solution.py:364
  60.0 1.4 convert_reduce_fusion
  61.5 1.6 copy-done.2
  63.1 4.3 %shard_map.75 = bf16[8,512,256]{2,1,0:T(8,128)(2,1)} custom-call(bf16[512,512]{1,0:T(8,128)(2,1)S(1)} %collective-permute-done.1.x_ref, bf16[8,512,256]{2,1,0:T(8,128)(2,1)S(1)} %bitcast.71, bf16[8,512,256]{2,1,0:T(8,128)(2,1)S(1)} %shard_map.74.own_ref), custom_call_target="tpu_custom_call" | custom-call | flops 1073741824 | bytes 6291456 | tf_op jit(solution)/shard_map/pallas_call | solution.py:276
  68.3 1.7 collective-permute-start.4
  70.0 1.2 collective-permute-start.2
  71.2 1.4 collective-permute-done.4.refs_3_
  72.6 4.1 %collective-permute-done.3.refs_2_ = bf16[64,512]{1,0:T(8,128)(2,1)S(1)} collective-permute-done((bf16[64,512]{1,0:T(8,128)(2,1)S(1)}, bf16[64,512]{1,0:T(8,128)(2,1)S(1)}, u32[]{:S(2)}, u32[]{:S(2)}) %collective-permute-start.3) | collective-permute-done | bytes 65568 | tf_op jit(solution)/shard_map/ppermute | solution.py:386
  77.3 1.8 shard_map.76
  79.2 1.4 collective-permute-start.8
  81.4 2.4 %collective-permute-start.6 = (bf16[512,256]{1,0:T(8,128)(2,1)}, bf16[512,256]{1,0:T(8,128)(2,1)S(1)}, u32[]{:S(2)}, u32[]{:S(2)}) collective-permute-start(bf16[512,256]{1,0:T(8,128)(2,1)} %shard_map.76), channel_id=1, source_target_pairs={{0,32},{16,48},{32,64},{48,80},{64,96},{80,112},{96,0},{112,16},{1... | collective-permute-start | bytes 786440 | tf_op jit(solution)/shard_map/ppermute | solution.py:396
  83.8 1.9 %collective-permute-done.8 = bf16[512,256]{1,0:T(8,128)(2,1)S(1)} collective-permute-done((bf16[512,256]{1,0:T(8,128)(2,1)}, bf16[512,256]{1,0:T(8,128)(2,1)S(1)}, u32[]{:S(2)}, u32[]{:S(2)}) %collective-permute-start.8) | collective-permute-done | bytes 262176 | tf_op jit(solution)/shard_map/ppermute | solution.py:399
  85.7 2.6 %collective-permute-done.7 = bf16[512,256]{1,0:T(8,128)(2,1)S(1)} collective-permute-done((bf16[512,256]{1,0:T(8,128)(2,1)}, bf16[512,256]{1,0:T(8,128)(2,1)S(1)}, u32[]{:S(2)}, u32[]{:S(2)}) %collective-permute-start.7) | collective-permute-done | bytes 262176 | tf_op jit(solution)/shard_map/ppermute | solution.py:396
  88.6 3.2 %collective-permute-start.9 = (bf16[512,256]{1,0:T(8,128)(2,1)S(1)}, bf16[512,256]{1,0:T(8,128)(2,1)S(1)}, u32[]{:S(2)}, u32[]{:S(2)}) collective-permute-start(bf16[512,256]{1,0:T(8,128)(2,1)S(1)} %collective-permute-done.8), channel_id=1, source_target_pairs={{0,32},{16,48},{32,64},{48,80},{64,96},{80,112},{96,0},{112,16},{1... | collective-permute-start | bytes 786440 | tf_op jit(solution)/shard_map/ppermute | solution.py:396
  91.9 3.2 %collective-permute-start.11 = (bf16[256,256]{1,0:T(8,128)(2,1)S(1)}, bf16[256,256]{1,0:T(8,128)(2,1)S(1)}, u32[]{:S(2)}, u32[]{:S(2)}) collective-permute-start(bf16[256,256]{1,0:T(8,128)(2,1)S(1)} %slice.38), channel_id=1, source_target_pairs={{0,32},{16,48},{32,64},{48,80},{64,96},{80,112},{96,0},{112,16},{1... | collective-permute-start | bytes 393224 | tf_op jit(solution)/shard_map/ppermute | solution.py:396
  95.2 3.2 %collective-permute-done.12 = bf16[256,256]{1,0:T(8,128)(2,1)S(1)} collective-permute-done((bf16[256,256]{1,0:T(8,128)(2,1)S(1)}, bf16[256,256]{1,0:T(8,128)(2,1)S(1)}, u32[]{:S(2)}, u32[]{:S(2)}) %collective-permute-start.12) | collective-permute-done | bytes 131104 | tf_op jit(solution)/shard_map/ppermute | solution.py:396
  99.0 3.1 %collective-permute-start.13 = (bf16[256,256]{1,0:T(8,128)(2,1)S(1)}, bf16[256,256]{1,0:T(8,128)(2,1)S(1)}, u32[]{:S(2)}, u32[]{:S(2)}) collective-permute-start(bf16[256,256]{1,0:T(8,128)(2,1)S(1)} %slice.40), channel_id=1, source_target_pairs={{0,32},{16,48},{32,64},{48,80},{64,96},{80,112},{96,0},{112,16},{1... | collective-permute-start | bytes 393224 | tf_op jit(solution)/shard_map/ppermute | solution.py:396
  102.1 1.1 pad_maximum_fusion.refs_0_
  103.4 1.6 collective-permute-done.14
  105.6 1.1 fusion.11.q_ref
  106.7 1.4 collective-permute-done.16.refs_3_
  108.0 11.4 %shard_map.77.refs_0_ = bf16[512,256]{1,0:T(8,128)(2,1)S(1)} custom-call(s32[16,3]{1,0:T(8,128)S(1)} %copy.11.info_ref, bf16[512,256]{1,0:T(8,128)(2,1)S(1)} %fusion.11.q_ref, bf16[4,512,256]{2,1,0:T(8,128)(2,1)S(1)} %pad_maximum_fusion.refs_0_, bf16[4,512,256]{2,1,0:T(8,128)(2,1)S(1)} %pad_maximum_fusion.1.refs_1_, ...), custom_call_target="tpu_custom_call" | custom-call | flops 4294967296 | bytes 4194304 | tf_op jit(solution)/shard_map/pallas_call | solution.py:151
  120.2 1.4 collective-permute-start.17
  121.6 5.7 %collective-permute-done.18.refs_2_ = bf16[512,256]{1,0:T(8,128)(2,1)S(1)} collective-permute-done((bf16[512,256]{1,0:T(8,128)(2,1)S(1)}, bf16[512,256]{1,0:T(8,128)(2,1)S(1)}, u32[]{:S(2)}, u32[]{:S(2)}) %collective-permute-start.18) | collective-permute-done | bytes 262176 | tf_op jit(solution)/shard_map/ppermute | solution.py:417
  127.3 2.2 %collective-permute-done.17.refs_1_ = bf16[512,256]{1,0:T(8,128)(2,1)S(1)} collective-permute-done((bf16[512,256]{1,0:T(8,128)(2,1)S(1)}, bf16[512,256]{1,0:T(8,128)(2,1)S(1)}, u32[]{:S(2)}, u32[]{:S(2)}) %collective-permute-start.17) | collective-permute-done | bytes 262176 | tf_op jit(solution)/shard_map/ppermute | solution.py:414
  129.6 3.0 %collective-permute-start.20 = (bf16[512,256]{1,0:T(8,128)(2,1)S(1)}, bf16[512,256]{1,0:T(8,128)(2,1)S(1)}, u32[]{:S(2)}, u32[]{:S(2)}) collective-permute-start(bf16[512,256]{1,0:T(8,128)(2,1)S(1)} %collective-permute-done.18.refs_2_), channel_id=1, source_target_pairs={{0,14},{1,15},{2,0},{3,1},{4,2},{5,3},{6,4},{7,5},{8,6},{9,7},{10,... | collective-permute-start | bytes 786440 | tf_op jit(solution)/shard_map/ppermute | solution.py:417
  133.1 1.4 fusion.24
  134.5 1.2 fusion.22
  135.7 3.8 %collective-permute-done.19.refs_3_ = bf16[512,256]{1,0:T(8,128)(2,1)S(1)} collective-permute-done((bf16[512,256]{1,0:T(8,128)(2,1)S(1)}, bf16[512,256]{1,0:T(8,128)(2,1)S(1)}, u32[]{:S(2)}, u32[]{:S(2)}) %collective-permute-start.19) | collective-permute-done | bytes 262176 | tf_op jit(solution)/shard_map/ppermute | solution.py:414
  139.5 1.0 collective-permute-start.21
  140.5 2.4 %collective-permute-start.22 = (bf16[512,256]{1,0:T(8,128)(2,1)S(1)}, bf16[512,256]{1,0:T(8,128)(2,1)S(1)}, u32[]{:S(2)}, u32[]{:S(2)}) collective-permute-start(bf16[512,256]{1,0:T(8,128)(2,1)S(1)} %collective-permute-done.20.refs_4_), channel_id=1, source_target_pairs={{0,14},{1,15},{2,0},{3,1},{4,2},{5,3},{6,4},{7,5},{8,6},{9,7},{10,... | collective-permute-start | bytes 786440 | tf_op jit(solution)/shard_map/ppermute | solution.py:417
  143.5 6.0 %collective-permute-done.21.refs_5_ = bf16[512,256]{1,0:T(8,128)(2,1)S(1)} collective-permute-done((bf16[512,256]{1,0:T(8,128)(2,1)S(1)}, bf16[512,256]{1,0:T(8,128)(2,1)S(1)}, u32[]{:S(2)}, u32[]{:S(2)}) %collective-permute-start.21) | collective-permute-done | bytes 262176 | tf_op jit(solution)/shard_map/ppermute | solution.py:414
  149.6 3.0 %collective-permute-start.24 = (bf16[512,128]{1,0:T(8,128)(2,1)S(1)}, bf16[512,128]{1,0:T(8,128)(2,1)S(1)}, u32[]{:S(2)}, u32[]{:S(2)}) collective-permute-start(bf16[512,128]{1,0:T(8,128)(2,1)S(1)} %slice.43), channel_id=1, source_target_pairs={{0,14},{1,15},{2,0},{3,1},{4,2},{5,3},{6,4},{7,5},{8,6},{9,7},{10,... | collective-permute-start | bytes 393224 | tf_op jit(solution)/shard_map/ppermute | solution.py:417
  153.2 5.6 %collective-permute-done.23.refs_7_ = bf16[512,128]{1,0:T(8,128)(2,1)S(1)} collective-permute-done((bf16[512,128]{1,0:T(8,128)(2,1)S(1)}, bf16[512,128]{1,0:T(8,128)(2,1)S(1)}, u32[]{:S(2)}, u32[]{:S(2)}) %collective-permute-start.23) | collective-permute-done | bytes 131104 | tf_op jit(solution)/shard_map/ppermute | solution.py:414
  159.9 2.2 %collective-permute-start.25 = (bf16[512,512]{1,0:T(8,128)(2,1)S(1)}, bf16[512,512]{1,0:T(8,128)(2,1)S(1)}, u32[]{:S(2)}, u32[]{:S(2)}) collective-permute-start(bf16[512,512]{1,0:T(8,128)(2,1)S(1)} %fusion.9), channel_id=1, source_target_pairs={{0,1},{1,0},{2,3},{3,2},{4,5},{5,4},{6,7},{7,6},{8,9},{9,8},{10,11... | collective-permute-start | bytes 1572872 | tf_op jit(solution)/shard_map/ppermute | solution.py:442
  162.2 2.2 %copy-done.1 = bf16[4096,512]{1,0:T(8,128)(2,1)S(1)} copy-done((bf16[4096,512]{1,0:T(8,128)(2,1)S(1)}, bf16[4096,512]{1,0:T(8,128)(2,1)}, u32[]{:S(2)}) %copy-start.1) | copy-done | bytes 4194328
  164.4 2.7 %shard_map.78 = f32[512,512]{1,0:T(8,128)S(1)} custom-call(s32[9]{0:T(128)S(1)} %broadcast_add_fusion.starts_ref, bf16[4096,512]{1,0:T(8,128)(2,1)S(1)} %copy-done.1, bf16[512,256]{1,0:T(8,128)(2,1)S(1)} %shard_map.77.refs_0_, bf16[512,256]{1,0:T(8,128)(2,1)S(1)} %collective-permute-done.17.refs_1_, bf16[512,256]{1,0:T(8,128)(2,1)S(1)} %collective-permute-done.18.refs_2_, ...), custom_call_target="tpu_custom_call" | custom-call | flops 1073741824 | bytes 5242880 | tf_op jit(solution)/shard_map/pallas_call | solution.py:319
  167.1 6.1 %collective-permute-done.25 = bf16[512,512]{1,0:T(8,128)(2,1)S(1)} collective-permute-done((bf16[512,512]{1,0:T(8,128)(2,1)S(1)}, bf16[512,512]{1,0:T(8,128)(2,1)S(1)}, u32[]{:S(2)}, u32[]{:S(2)}) %collective-permute-start.25) | collective-permute-done | bytes 524320 | tf_op jit(solution)/shard_map/ppermute | solution.py:442
  173.2 2.0 %fusion.1 = bf16[1024,512]{1,0:T(8,128)(2,1)} fusion(s32[512]{0:T(512)S(1)} %bitcast.72, f32[512,512]{1,0:T(8,128)S(1)} %shard_map.78, bf16[512,512]{1,0:T(8,128)(2,1)S(1)} %collective-permute-done.25, f32[512]{0:T(512)S(1)} %bitcast.82), kind=kOutput, calls=%fused_computation.3 | convolution fusion | flops 538968064 | bytes 2625536 | tf_op jit(solution)/shard_map/dot_general | solution.py:449
  (88 shorter events, 12.3 us)
Async XLA Ops:
  6.5 53.5 %all-gather.5.cloned.1.call-start = ((), (), s32[]{:S(2)}) async-start(), calls=%async_computation.3 | async-start | bytes 2359296 | tf_op jit(solution)/shard_map/all_gather | solution.py:353
  7.5 9.6 %collective-permute-start = (bf16[512,256]{1,0:T(8,128)(2,1)S(1)}, bf16[512,256]{1,0:T(8,128)(2,1)S(1)}, u32[]{:S(2)}, u32[]{:S(2)}) collective-permute-start(bf16[512,256]{1,0:T(8,128)(2,1)S(1)} %constant_dynamic-slice_fusion.1), channel_id=1, source_target_pairs={{0,1},{1,0},{2,3},{3,2},{4,5},{5,4},{6,7},{7,6},{8,9},{9,8},{10,11... | collective-permute-start | bytes 786440 | tf_op jit(solution)/shard_map/ppermute | solution.py:356
  12.0 1.2 copy-start.3
  13.2 1.2 copy-start.4
  17.1 0.7 copy-start.8
  17.9 42.1 %all-to-all-start = ((bf16[16,72,512]{2,1,0:T(8,128)(2,1)}), bf16[16,72,512]{2,1,0:T(8,128)(2,1)}, u32[]{:S(2)}, u32[]{:S(2)}) async-start(bf16[16,72,512]{2,1,0:T(8,128)(2,1)} %get-tuple-element.48), calls=%async_computation | async-start | bytes 2359296 | tf_op jit(solution)/shard_map/all_to_all | solution.py:364
  28.2 77.3 %reduce-scatter.2.cloned.1.call-start = ((), (), s32[]{:S(2)}) async-start(), calls=%async_computation.2 | async-start | bytes 2359296 | tf_op jit(solution)/shard_map/reduce_scatter | solution.py:383
  28.3 33.2 %collective-permute-start.1 = (bf16[512,512]{1,0:T(8,128)(2,1)S(1)}, bf16[512,512]{1,0:T(8,128)(2,1)S(1)}, u32[]{:S(2)}, u32[]{:S(2)}) collective-permute-start(bf16[512,512]{1,0:T(8,128)(2,1)S(1)} %get-tuple-element.49.x_ref), channel_id=1, source_target_pairs={{0,1},{1,0},{2,3},{3,2},{4,5},{5,4},{6,7},{7,6},{8,9},{9,8},{10,11... | collective-permute-start | bytes 1572872 | tf_op jit(solution)/shard_map/ppermute | solution.py:360
  32.0 2.5 %copy-start = (bf16[512,4096]{1,0:T(8,128)(2,1)S(1)}, bf16[512,4096]{1,0:T(8,128)(2,1)}, u32[]{:S(2)}) copy-start(bf16[512,4096]{1,0:T(8,128)(2,1)} %w_ref.1) | copy-start | bytes 12582916
  34.4 2.8 %copy-start.12 = (s32[16,512]{1,0:T(8,128)S(1)}, s32[16,512]{1,0:T(8,128)}, u32[]{:S(2)}) copy-start(s32[16,512]{1,0:T(8,128)} %param.13) | copy-start | bytes 98308
  61.5 8.5 %copy-start.6 = (bf16[64,512]{1,0:T(8,128)(2,1)}, bf16[64,512]{1,0:T(8,128)(2,1)S(1)}, u32[]{:S(2)}) copy-start(bf16[64,512]{1,0:T(8,128)(2,1)S(1)} %fusion.26.refs_0_) | copy-start | bytes 196612
  61.5 1.6 copy-start.2
  67.5 65.6 %all-gather.7.cloned.1.call-start = ((), (), s32[]{:S(2)}) async-start(), calls=%async_computation.4 | async-start | bytes 2359296 | tf_op jit(solution)/shard_map/all_gather | solution.py:353
  67.5 9.2 %collective-permute-start.5 = (bf16[256,512]{1,0:T(8,128)(2,1)S(1)}, bf16[256,512]{1,0:T(8,128)(2,1)S(1)}, u32[]{:S(2)}, u32[]{:S(2)}) collective-permute-start(bf16[256,512]{1,0:T(8,128)(2,1)S(1)} %constant_dynamic-slice_fusion), channel_id=1, source_target_pairs={{0,1},{1,0},{2,3},{3,2},{4,5},{5,4},{6,7},{7,6},{8,9},{9,8},{10,11... | collective-permute-start | bytes 786440 | tf_op jit(solution)/shard_map/ppermute | solution.py:387
  68.3 4.3 %collective-permute-start.4 = (bf16[64,512]{1,0:T(8,128)(2,1)S(1)}, bf16[64,512]{1,0:T(8,128)(2,1)S(1)}, u32[]{:S(2)}, u32[]{:S(2)}) collective-permute-start(bf16[64,512]{1,0:T(8,128)(2,1)S(1)} %fusion.26.refs_0_), channel_id=1, source_target_pairs={{0,6},{1,7},{2,0},{3,1},{4,2},{5,3},{6,4},{7,5},{8,14},{9,15},{10,... | collective-permute-start | bytes 196616 | tf_op jit(solution)/shard_map/ppermute | solution.py:386
  70.0 6.7 %collective-permute-start.3 = (bf16[64,512]{1,0:T(8,128)(2,1)S(1)}, bf16[64,512]{1,0:T(8,128)(2,1)S(1)}, u32[]{:S(2)}, u32[]{:S(2)}) collective-permute-start(bf16[64,512]{1,0:T(8,128)(2,1)S(1)} %fusion.26.refs_0_), channel_id=1, source_target_pairs={{0,4},{1,5},{2,6},{3,7},{4,0},{5,1},{6,2},{7,3},{8,12},{9,13},{10,... | collective-permute-start | bytes 196616 | tf_op jit(solution)/shard_map/ppermute | solution.py:386
  70.0 6.7 %collective-permute-start.2 = (bf16[64,512]{1,0:T(8,128)(2,1)S(1)}, bf16[64,512]{1,0:T(8,128)(2,1)S(1)}, u32[]{:S(2)}, u32[]{:S(2)}) collective-permute-start(bf16[64,512]{1,0:T(8,128)(2,1)S(1)} %fusion.26.refs_0_), channel_id=1, source_target_pairs={{0,2},{1,3},{2,4},{3,5},{4,6},{5,7},{6,0},{7,1},{8,10},{9,11},{10,... | collective-permute-start | bytes 196616 | tf_op jit(solution)/shard_map/ppermute | solution.py:386
  72.6 4.1 %copy-start.9 = (bf16[64,512]{1,0:T(8,128)(2,1)}, bf16[64,512]{1,0:T(8,128)(2,1)S(1)}, u32[]{:S(2)}) copy-start(bf16[64,512]{1,0:T(8,128)(2,1)S(1)} %collective-permute-done.4.refs_3_) | copy-start | bytes 196612
  76.7 0.6 copy-start.10
  76.7 0.7 copy-start.11
  76.7 11.7 %copy-start.7 = (bf16[256,512]{1,0:T(8,128)(2,1)}, bf16[256,512]{1,0:T(8,128)(2,1)S(1)}, u32[]{:S(2)}) copy-start(bf16[256,512]{1,0:T(8,128)(2,1)S(1)} %collective-permute-done.5) | copy-start | bytes 786436
  79.2 6.6 %collective-permute-start.8 = (bf16[512,256]{1,0:T(8,128)(2,1)}, bf16[512,256]{1,0:T(8,128)(2,1)S(1)}, u32[]{:S(2)}, u32[]{:S(2)}) collective-permute-start(bf16[512,256]{1,0:T(8,128)(2,1)} %shard_map.76), channel_id=1, source_target_pairs={{0,128},{16,144},{32,160},{48,176},{64,192},{80,208},{96,224},{112... | collective-permute-start | bytes 786440 | tf_op jit(solution)/shard_map/ppermute | solution.py:399
  80.6 7.8 %collective-permute-start.7 = (bf16[512,256]{1,0:T(8,128)(2,1)}, bf16[512,256]{1,0:T(8,128)(2,1)S(1)}, u32[]{:S(2)}, u32[]{:S(2)}) collective-permute-start(bf16[512,256]{1,0:T(8,128)(2,1)} %shard_map.76), channel_id=1, source_target_pairs={{0,96},{16,112},{32,0},{48,16},{64,32},{80,48},{96,64},{112,80},{1... | collective-permute-start | bytes 786440 | tf_op jit(solution)/shard_map/ppermute | solution.py:396
  81.4 7.0 %collective-permute-start.6 = (bf16[512,256]{1,0:T(8,128)(2,1)}, bf16[512,256]{1,0:T(8,128)(2,1)S(1)}, u32[]{:S(2)}, u32[]{:S(2)}) collective-permute-start(bf16[512,256]{1,0:T(8,128)(2,1)} %shard_map.76), channel_id=1, source_target_pairs={{0,32},{16,48},{32,64},{48,80},{64,96},{80,112},{96,0},{112,16},{1... | collective-permute-start | bytes 786440 | tf_op jit(solution)/shard_map/ppermute | solution.py:396
  88.4 10.0 %collective-permute-start.10 = (bf16[512,256]{1,0:T(8,128)(2,1)S(1)}, bf16[512,256]{1,0:T(8,128)(2,1)S(1)}, u32[]{:S(2)}, u32[]{:S(2)}) collective-permute-start(bf16[512,256]{1,0:T(8,128)(2,1)S(1)} %collective-permute-done.8), channel_id=1, source_target_pairs={{0,96},{16,112},{32,0},{48,16},{64,32},{80,48},{96,64},{112,80},{1... | collective-permute-start | bytes 786440 | tf_op jit(solution)/shard_map/ppermute | solution.py:396
  88.6 9.7 %collective-permute-start.9 = (bf16[512,256]{1,0:T(8,128)(2,1)S(1)}, bf16[512,256]{1,0:T(8,128)(2,1)S(1)}, u32[]{:S(2)}, u32[]{:S(2)}) collective-permute-start(bf16[512,256]{1,0:T(8,128)(2,1)S(1)} %collective-permute-done.8), channel_id=1, source_target_pairs={{0,32},{16,48},{32,64},{48,80},{64,96},{80,112},{96,0},{112,16},{1... | collective-permute-start | bytes 786440 | tf_op jit(solution)/shard_map/ppermute | solution.py:396
  91.9 6.5 %collective-permute-start.12 = (bf16[256,256]{1,0:T(8,128)(2,1)S(1)}, bf16[256,256]{1,0:T(8,128)(2,1)S(1)}, u32[]{:S(2)}, u32[]{:S(2)}) collective-permute-start(bf16[256,256]{1,0:T(8,128)(2,1)S(1)} %slice.39), channel_id=1, source_target_pairs={{0,96},{16,112},{32,0},{48,16},{64,32},{80,48},{96,64},{112,80},{1... | collective-permute-start | bytes 393224 | tf_op jit(solution)/shard_map/ppermute | solution.py:396
  91.9 6.4 %collective-permute-start.11 = (bf16[256,256]{1,0:T(8,128)(2,1)S(1)}, bf16[256,256]{1,0:T(8,128)(2,1)S(1)}, u32[]{:S(2)}, u32[]{:S(2)}) collective-permute-start(bf16[256,256]{1,0:T(8,128)(2,1)S(1)} %slice.38), channel_id=1, source_target_pairs={{0,32},{16,48},{32,64},{48,80},{64,96},{80,112},{96,0},{112,16},{1... | collective-permute-start | bytes 393224 | tf_op jit(solution)/shard_map/ppermute | solution.py:396
  98.4 6.6 %collective-permute-start.14 = (bf16[256,256]{1,0:T(8,128)(2,1)S(1)}, bf16[256,256]{1,0:T(8,128)(2,1)S(1)}, u32[]{:S(2)}, u32[]{:S(2)}) collective-permute-start(bf16[256,256]{1,0:T(8,128)(2,1)S(1)} %slice.41), channel_id=1, source_target_pairs={{0,96},{16,112},{32,0},{48,16},{64,32},{80,48},{96,64},{112,80},{1... | collective-permute-start | bytes 393224 | tf_op jit(solution)/shard_map/ppermute | solution.py:396
  99.0 6.0 %collective-permute-start.13 = (bf16[256,256]{1,0:T(8,128)(2,1)S(1)}, bf16[256,256]{1,0:T(8,128)(2,1)S(1)}, u32[]{:S(2)}, u32[]{:S(2)}) collective-permute-start(bf16[256,256]{1,0:T(8,128)(2,1)S(1)} %slice.40), channel_id=1, source_target_pairs={{0,32},{16,48},{32,64},{48,80},{64,96},{80,112},{96,0},{112,16},{1... | collective-permute-start | bytes 393224 | tf_op jit(solution)/shard_map/ppermute | solution.py:396
  103.2 3.4 %collective-permute-start.15 = (bf16[4,512,256]{2,1,0:T(8,128)(2,1)S(1)}, bf16[4,512,256]{2,1,0:T(8,128)(2,1)}, u32[]{:S(2)}, u32[]{:S(2)}) collective-permute-start(bf16[4,512,256]{2,1,0:T(8,128)(2,1)S(1)} %pad_maximum_fusion.refs_0_), channel_id=1, source_target_pairs={{0,16},{16,0},{32,48},{48,32},{64,80},{80,64},{96,112},{112,96},{1... | collective-permute-start | bytes 3145736 | tf_op jit(solution)/shard_map/ppermute | solution.py:410
  105.2 2.9 %collective-permute-start.16 = (bf16[4,512,256]{2,1,0:T(8,128)(2,1)S(1)}, bf16[4,512,256]{2,1,0:T(8,128)(2,1)}, u32[]{:S(2)}, u32[]{:S(2)}) collective-permute-start(bf16[4,512,256]{2,1,0:T(8,128)(2,1)S(1)} %pad_maximum_fusion.1.refs_1_), channel_id=1, source_target_pairs={{0,16},{16,0},{32,48},{48,32},{64,80},{80,64},{96,112},{112,96},{1... | collective-permute-start | bytes 3145736 | tf_op jit(solution)/shard_map/ppermute | solution.py:410
  119.5 7.8 %collective-permute-start.18 = (bf16[512,256]{1,0:T(8,128)(2,1)S(1)}, bf16[512,256]{1,0:T(8,128)(2,1)S(1)}, u32[]{:S(2)}, u32[]{:S(2)}) collective-permute-start(bf16[512,256]{1,0:T(8,128)(2,1)S(1)} %shard_map.77.refs_0_), channel_id=1, source_target_pairs={{0,14},{1,15},{2,0},{3,1},{4,2},{5,3},{6,4},{7,5},{8,6},{9,7},{10,... | collective-permute-start | bytes 786440 | tf_op jit(solution)/shard_map/ppermute | solution.py:417
  120.2 9.3 %collective-permute-start.17 = (bf16[512,256]{1,0:T(8,128)(2,1)S(1)}, bf16[512,256]{1,0:T(8,128)(2,1)S(1)}, u32[]{:S(2)}, u32[]{:S(2)}) collective-permute-start(bf16[512,256]{1,0:T(8,128)(2,1)S(1)} %shard_map.77.refs_0_), channel_id=1, source_target_pairs={{0,2},{1,3},{2,4},{3,5},{4,6},{5,7},{6,8},{7,9},{8,10},{9,11},{10,... | collective-permute-start | bytes 786440 | tf_op jit(solution)/shard_map/ppermute | solution.py:414
  129.4 10.1 %collective-permute-start.19 = (bf16[512,256]{1,0:T(8,128)(2,1)S(1)}, bf16[512,256]{1,0:T(8,128)(2,1)S(1)}, u32[]{:S(2)}, u32[]{:S(2)}) collective-permute-start(bf16[512,256]{1,0:T(8,128)(2,1)S(1)} %collective-permute-done.17.refs_1_), channel_id=1, source_target_pairs={{0,2},{1,3},{2,4},{3,5},{4,6},{5,7},{6,8},{7,9},{8,10},{9,11},{10,... | collective-permute-start | bytes 786440 | tf_op jit(solution)/shard_map/ppermute | solution.py:414
  129.6 9.9 %collective-permute-start.20 = (bf16[512,256]{1,0:T(8,128)(2,1)S(1)}, bf16[512,256]{1,0:T(8,128)(2,1)S(1)}, u32[]{:S(2)}, u32[]{:S(2)}) collective-permute-start(bf16[512,256]{1,0:T(8,128)(2,1)S(1)} %collective-permute-done.18.refs_2_), channel_id=1, source_target_pairs={{0,14},{1,15},{2,0},{3,1},{4,2},{5,3},{6,4},{7,5},{8,6},{9,7},{10,... | collective-permute-start | bytes 786440 | tf_op jit(solution)/shard_map/ppermute | solution.py:417
  133.1 9.9 %copy-start.5 = (bf16[2048,512]{1,0:T(8,128)(2,1)S(1)}, bf16[2048,512]{1,0:T(8,128)(2,1)}, u32[]{:S(2)}) copy-start(bf16[2048,512]{1,0:T(8,128)(2,1)} %all-gather.7.cloned.1.call-done) | copy-start | bytes 6291460
  139.5 10.0 %collective-permute-start.21 = (bf16[512,256]{1,0:T(8,128)(2,1)S(1)}, bf16[512,256]{1,0:T(8,128)(2,1)S(1)}, u32[]{:S(2)}, u32[]{:S(2)}) collective-permute-start(bf16[512,256]{1,0:T(8,128)(2,1)S(1)} %collective-permute-done.19.refs_3_), channel_id=1, source_target_pairs={{0,2},{1,3},{2,4},{3,5},{4,6},{5,7},{6,8},{7,9},{8,10},{9,11},{10,... | collective-permute-start | bytes 786440 | tf_op jit(solution)/shard_map/ppermute | solution.py:414
  140.5 9.0 %collective-permute-start.22 = (bf16[512,256]{1,0:T(8,128)(2,1)S(1)}, bf16[512,256]{1,0:T(8,128)(2,1)S(1)}, u32[]{:S(2)}, u32[]{:S(2)}) collective-permute-start(bf16[512,256]{1,0:T(8,128)(2,1)S(1)} %collective-permute-done.20.refs_4_), channel_id=1, source_target_pairs={{0,14},{1,15},{2,0},{3,1},{4,2},{5,3},{6,4},{7,5},{8,6},{9,7},{10,... | collective-permute-start | bytes 786440 | tf_op jit(solution)/shard_map/ppermute | solution.py:417
  149.6 9.5 %collective-permute-start.24 = (bf16[512,128]{1,0:T(8,128)(2,1)S(1)}, bf16[512,128]{1,0:T(8,128)(2,1)S(1)}, u32[]{:S(2)}, u32[]{:S(2)}) collective-permute-start(bf16[512,128]{1,0:T(8,128)(2,1)S(1)} %slice.43), channel_id=1, source_target_pairs={{0,14},{1,15},{2,0},{3,1},{4,2},{5,3},{6,4},{7,5},{8,6},{9,7},{10,... | collective-permute-start | bytes 393224 | tf_op jit(solution)/shard_map/ppermute | solution.py:417
  152.6 6.2 %collective-permute-start.23 = (bf16[512,128]{1,0:T(8,128)(2,1)S(1)}, bf16[512,128]{1,0:T(8,128)(2,1)S(1)}, u32[]{:S(2)}, u32[]{:S(2)}) collective-permute-start(bf16[512,128]{1,0:T(8,128)(2,1)S(1)} %slice.42), channel_id=1, source_target_pairs={{0,2},{1,3},{2,4},{3,5},{4,6},{5,7},{6,8},{7,9},{8,10},{9,11},{10,... | collective-permute-start | bytes 393224 | tf_op jit(solution)/shard_map/ppermute | solution.py:414
  159.9 13.3 %collective-permute-start.25 = (bf16[512,512]{1,0:T(8,128)(2,1)S(1)}, bf16[512,512]{1,0:T(8,128)(2,1)S(1)}, u32[]{:S(2)}, u32[]{:S(2)}) collective-permute-start(bf16[512,512]{1,0:T(8,128)(2,1)S(1)} %fusion.9), channel_id=1, source_target_pairs={{0,1},{1,0},{2,3},{3,2},{4,5},{5,4},{6,7},{7,6},{8,9},{9,8},{10,11... | collective-permute-start | bytes 1572872 | tf_op jit(solution)/shard_map/ppermute | solution.py:442
  162.2 2.2 %copy-start.1 = (bf16[4096,512]{1,0:T(8,128)(2,1)S(1)}, bf16[4096,512]{1,0:T(8,128)(2,1)}, u32[]{:S(2)}) copy-start(bf16[4096,512]{1,0:T(8,128)(2,1)} %w_hbm.1) | copy-start | bytes 12582916
Sparse Core Ops, SparseCore 0:
  18.0 29.2 all-gather.4
  67.6 37.9 reduce-scatter.1
  107.4 25.6 all-gather.6

commit v12 on v11

--- a/solution.py
+++ b/solution.py
@@ -428,6 +428,8 @@
     from_left, from_right = mixed, mixed
     for step in (1, 2, 3):
         from_left, from_right = both(from_left, from_right)
+        if step == 2:
+            from_left, from_right, wo_in = lax.optimization_barrier((from_left, from_right, wo_in))
         pieces += [from_left, from_right]
         starts += [-step, step]
     pieces += [right(from_left[:, :cut]), left(from_right[:, cut:])]

time: 182 us -> 184 us (1.011)
    ppermute x8, waiting for transfers between devices: 7.5 us -> 15.3 us  [x_hop(): return lax.ppermute(block, 'ctx', along(step))]
    ppermute x4, waiting for transfers between devices: 5.7 us -> 0.59 us  [left(): return lax.ppermute(a.astype(bf16), 'tp', z_shift(-1))]
    ppermute x8, starting transfers between devices: 13.7 us -> 10.7 us  [x_hop(): return lax.ppermute(block, 'ctx', along(step))]
    ppermute x4, waiting for transfers between devices: 17.5 us -> 20.3 us  [right(): return lax.ppermute(a.astype(bf16), 'tp', z_shift(1))]
    ppermute x4, starting transfers between devices: 2.62 us -> 4.95 us  [right(): return lax.ppermute(a.astype(bf16), 'tp', z_shift(1))]
    ppermute x3, waiting for transfers between devices: 5.51 us -> 3.38 us  [shards(): pieces = [lax.ppermute(piece, 'tp', quad_shift(k)) for k in (1, 2, 3)]]
    ppermute x1, waiting for transfers between devices: 1.91 us -> 0.06 us  [shards(): lax.ppermute(kv_own, 'ctx', [(c, (c + shard_n // 2) % shard_n) for c in r...]
  transfers between devices with their start and end apart: 30 -> 30, of which waited for: 17 -> 19; matrix products, arithmetic and copies ran while one was open for 7% -> 5% of each run, Pallas kernels for 12% -> 12%
where the time goes in v12:
time: 184 us; the launch traced here: 183 us
  waiting for transfers between devices  68.2 us (37%)
  starting transfers between devices  50.1 us (27%)
  Pallas kernels  25.6 us (14%)
  local copies, waits for them, and re-layouts  14.5 us (8%)
  between operations  13.4 us (7%)
  matrix products  6.76 us (4%)
  other arithmetic  4.28 us (2%)
    all_to_all x1, waiting for transfers between devices, shards(): exchanged = lax.all_to_all(sent, 'tp', 0, 0, tiled=True)  21.3 us
    ppermute x4, waiting for transfers between devices, right(): return lax.ppermute(a.astype(bf16), 'tp', z_shift(1))  20.3 us
    ppermute x8, waiting for transfers between devices, x_hop(): return lax.ppermute(block, 'ctx', along(step))  15.3 us
    pallas_call x1, Pallas kernels, attention(): pl.pallas_call(attention_kernel, out_shape=jax.ShapeDtypeStruct(queries.s...  11.4 us
    ppermute x8, starting transfers between devices, x_hop(): return lax.ppermute(block, 'ctx', along(step))  10.7 us
    all_to_all x1, starting transfers between devices, shards(): exchanged = lax.all_to_all(sent, 'tp', 0, 0, tiled=True)  10.4 us
    unnamed x26, local copies, waits for them, and re-layouts  10 us
    ppermute x4, starting transfers between devices, left(): return lax.ppermute(a.astype(bf16), 'tp', z_shift(-1))  9.01 us
  transfers between devices with their start and end apart: 30, of which 19 were waited for; matrix products, arithmetic and copies ran while one was open for 5% of the time, Pallas kernels for 12%

profile of v12, /device:TPU:14, one launch (start us, length us, event | category | flops | bytes accessed | tf_op | source)
XLA Modules:
  0.0 183.0 jit_solution(5472708673354655411)
XLA Ops:
  7.5 2.4 %collective-permute-start = (bf16[512,256]{1,0:T(8,128)(2,1)S(1)}, bf16[512,256]{1,0:T(8,128)(2,1)S(1)}, u32[]{:S(2)}, u32[]{:S(2)}) collective-permute-start(bf16[512,256]{1,0:T(8,128)(2,1)S(1)} %constant_dynamic-slice_fusion.1), channel_id=1, source_target_pairs={{0,1},{1,0},{2,3},{3,2},{4,5},{5,4},{6,7},{7,6},{8,9},{9,8},{10,11... | collective-permute-start | bytes 786440 | tf_op jit(solution)/shard_map/ppermute | solution.py:356
  12.0 1.2 copy-done.3
  13.2 1.2 copy-done.4
  14.4 2.6 %shard_map.73 = (bf16[512,512]{1,0:T(8,128)(2,1)S(1)}, bf16[16,72,512]{2,1,0:T(8,128)(2,1)}) custom-call(s32[1,512]{1,0:T(1,128)S(1)} %constant_dynamic-slice_fusion.2.rows_ref, bf16[1024,512]{1,0:T(8,128)(2,1)S(1)} %copy-done.3, bf16[1,512]{1,0:T(2,128)(2,1)S(1)} %reshape.431.gain_ref, bf16[1,512]{1,0:T(2,128)(2,1)S(1)} %reshape.432.router_ref, ...), custom_call_target="tpu_custom_call" | custom-call | flops 1073741824 | bytes 5242880 | tf_op jit(solution)/shard_map/pallas_call | solution.py:203
  17.9 10.4 %all-to-all-start = ((bf16[16,72,512]{2,1,0:T(8,128)(2,1)}), bf16[16,72,512]{2,1,0:T(8,128)(2,1)}, u32[]{:S(2)}, u32[]{:S(2)}) async-start(bf16[16,72,512]{2,1,0:T(8,128)(2,1)} %get-tuple-element.51), calls=%async_computation | async-start | bytes 2359296 | tf_op jit(solution)/shard_map/all_to_all | solution.py:364
  28.3 3.5 %collective-permute-start.1 = (bf16[512,512]{1,0:T(8,128)(2,1)S(1)}, bf16[512,512]{1,0:T(8,128)(2,1)S(1)}, u32[]{:S(2)}, u32[]{:S(2)}) collective-permute-start(bf16[512,512]{1,0:T(8,128)(2,1)S(1)} %get-tuple-element.52.x_ref), channel_id=1, source_target_pairs={{0,1},{1,0},{2,3},{3,2},{4,5},{5,4},{6,7},{7,6},{8,9},{9,8},{10,11... | collective-permute-start | bytes 1572872 | tf_op jit(solution)/shard_map/ppermute | solution.py:360
  32.0 2.4 %copy-done = bf16[512,4096]{1,0:T(8,128)(2,1)S(1)} copy-done((bf16[512,4096]{1,0:T(8,128)(2,1)S(1)}, bf16[512,4096]{1,0:T(8,128)(2,1)}, u32[]{:S(2)}) %copy-start) | copy-done | bytes 4194328
  34.4 2.8 %shard_map.74.own_ref = bf16[8,512,256]{2,1,0:T(8,128)(2,1)S(1)} custom-call(s32[1]{0:T(128)} %bitcast.35.y_ref, bf16[512,512]{1,0:T(8,128)(2,1)S(1)} %get-tuple-element.52.x_ref, bf16[512,4096]{1,0:T(8,128)(2,1)S(1)} %copy-done), custom_call_target="tpu_custom_call" | custom-call | flops 1073741824 | bytes 4194304 | tf_op jit(solution)/shard_map/pallas_call | solution.py:254
  37.7 1.0 constant_dynamic-slice_fusion
  38.7 21.3 %all-to-all-done = bf16[16,72,512]{2,1,0:T(8,128)(2,1)} async-done(((bf16[16,72,512]{2,1,0:T(8,128)(2,1)}), bf16[16,72,512]{2,1,0:T(8,128)(2,1)}, u32[]{:S(2)}, u32[]{:S(2)}) %all-to-all-start) | async-done | bytes 1179680 | tf_op jit(solution)/shard_map/all_to_all | solution.py:364
  60.0 1.4 convert_reduce_fusion
  61.5 1.6 copy-done.2
  63.1 4.3 %shard_map.75 = bf16[8,512,256]{2,1,0:T(8,128)(2,1)} custom-call(bf16[512,512]{1,0:T(8,128)(2,1)S(1)} %collective-permute-done.1.x_ref, bf16[8,512,256]{2,1,0:T(8,128)(2,1)S(1)} %bitcast.71, bf16[8,512,256]{2,1,0:T(8,128)(2,1)S(1)} %shard_map.74.own_ref), custom_call_target="tpu_custom_call" | custom-call | flops 1073741824 | bytes 6291456 | tf_op jit(solution)/shard_map/pallas_call | solution.py:276
  68.3 2.3 %collective-permute-start.3 = (bf16[64,512]{1,0:T(8,128)(2,1)S(1)}, bf16[64,512]{1,0:T(8,128)(2,1)S(1)}, u32[]{:S(2)}, u32[]{:S(2)}) collective-permute-start(bf16[64,512]{1,0:T(8,128)(2,1)S(1)} %fusion.22.refs_0_), channel_id=1, source_target_pairs={{0,4},{1,5},{2,6},{3,7},{4,0},{5,1},{6,2},{7,3},{8,12},{9,13},{10,... | collective-permute-start | bytes 196616 | tf_op jit(solution)/shard_map/ppermute | solution.py:386
  70.6 1.6 collective-permute-start.4
  72.1 2.4 %collective-permute-done.2.refs_1_ = bf16[64,512]{1,0:T(8,128)(2,1)S(1)} collective-permute-done((bf16[64,512]{1,0:T(8,128)(2,1)S(1)}, bf16[64,512]{1,0:T(8,128)(2,1)S(1)}, u32[]{:S(2)}, u32[]{:S(2)}) %collective-permute-start.2) | collective-permute-done | bytes 65568 | tf_op jit(solution)/shard_map/ppermute | solution.py:386
  74.5 1.0 collective-permute-done.3.refs_2_
  76.2 1.8 shard_map.76
  78.5 1.5 collective-permute-start.7
  80.0 1.3 collective-permute-start.8
  81.4 4.2 %collective-permute-done.6 = bf16[512,256]{1,0:T(8,128)(2,1)S(1)} collective-permute-done((bf16[512,256]{1,0:T(8,128)(2,1)}, bf16[512,256]{1,0:T(8,128)(2,1)S(1)}, u32[]{:S(2)}, u32[]{:S(2)}) %collective-permute-start.6) | collective-permute-done | bytes 262176 | tf_op jit(solution)/shard_map/ppermute | solution.py:396
  85.6 1.4 collective-permute-done.7
  88.0 2.4 %collective-permute-start.9 = (bf16[512,256]{1,0:T(8,128)(2,1)S(1)}, bf16[512,256]{1,0:T(8,128)(2,1)S(1)}, u32[]{:S(2)}, u32[]{:S(2)}) collective-permute-start(bf16[512,256]{1,0:T(8,128)(2,1)S(1)} %collective-permute-done.8), channel_id=1, source_target_pairs={{0,32},{16,48},{32,64},{48,80},{64,96},{80,112},{96,0},{112,16},{1... | collective-permute-start | bytes 786440 | tf_op jit(solution)/shard_map/ppermute | solution.py:396
  90.9 1.8 collective-permute-start.12
  92.8 3.9 %collective-permute-done.11 = bf16[256,256]{1,0:T(8,128)(2,1)S(1)} collective-permute-done((bf16[256,256]{1,0:T(8,128)(2,1)S(1)}, bf16[256,256]{1,0:T(8,128)(2,1)S(1)}, u32[]{:S(2)}, u32[]{:S(2)}) %collective-permute-start.11) | collective-permute-done | bytes 131104 | tf_op jit(solution)/shard_map/ppermute | solution.py:396
  97.5 2.9 %collective-permute-start.13 = (bf16[256,256]{1,0:T(8,128)(2,1)S(1)}, bf16[256,256]{1,0:T(8,128)(2,1)S(1)}, u32[]{:S(2)}, u32[]{:S(2)}) collective-permute-start(bf16[256,256]{1,0:T(8,128)(2,1)S(1)} %slice.40), channel_id=1, source_target_pairs={{0,32},{16,48},{32,64},{48,80},{64,96},{80,112},{96,0},{112,16},{1... | collective-permute-start | bytes 393224 | tf_op jit(solution)/shard_map/ppermute | solution.py:396
  100.5 1.1 pad_maximum_fusion.refs_0_
  101.7 1.2 collective-permute-done.13
  102.9 3.7 %collective-permute-done.14 = bf16[256,256]{1,0:T(8,128)(2,1)S(1)} collective-permute-done((bf16[256,256]{1,0:T(8,128)(2,1)S(1)}, bf16[256,256]{1,0:T(8,128)(2,1)S(1)}, u32[]{:S(2)}, u32[]{:S(2)}) %collective-permute-start.14) | collective-permute-done | bytes 131104 | tf_op jit(solution)/shard_map/ppermute | solution.py:396
  107.0 1.1 fusion.9.q_ref
  108.2 1.6 collective-permute-done.16.refs_3_
  109.7 11.4 %shard_map.77.refs_0_ = bf16[512,256]{1,0:T(8,128)(2,1)S(1)} custom-call(s32[16,3]{1,0:T(8,128)S(1)} %copy.11.info_ref, bf16[512,256]{1,0:T(8,128)(2,1)S(1)} %fusion.9.q_ref, bf16[4,512,256]{2,1,0:T(8,128)(2,1)S(1)} %pad_maximum_fusion.refs_0_, bf16[4,512,256]{2,1,0:T(8,128)(2,1)S(1)} %pad_maximum_fusion.1.refs_1_, ...), custom_call_target="tpu_custom_call" | custom-call | flops 4294967296 | bytes 4194304 | tf_op jit(solution)/shard_map/pallas_call | solution.py:151
  122.0 2.5 %collective-permute-start.18 = (bf16[512,256]{1,0:T(8,128)(2,1)S(1)}, bf16[512,256]{1,0:T(8,128)(2,1)S(1)}, u32[]{:S(2)}, u32[]{:S(2)}) collective-permute-start(bf16[512,256]{1,0:T(8,128)(2,1)S(1)} %shard_map.77.refs_0_), channel_id=1, source_target_pairs={{0,14},{1,15},{2,0},{3,1},{4,2},{5,3},{6,4},{7,5},{8,6},{9,7},{10,... | collective-permute-start | bytes 786440 | tf_op jit(solution)/shard_map/ppermute | solution.py:417
  124.5 5.7 %collective-permute-done.17.refs_1_ = bf16[512,256]{1,0:T(8,128)(2,1)S(1)} collective-permute-done((bf16[512,256]{1,0:T(8,128)(2,1)S(1)}, bf16[512,256]{1,0:T(8,128)(2,1)S(1)}, u32[]{:S(2)}, u32[]{:S(2)}) %collective-permute-start.17) | collective-permute-done | bytes 262176 | tf_op jit(solution)/shard_map/ppermute | solution.py:414
  131.1 2.6 %collective-permute-start.20 = (bf16[512,256]{1,0:T(8,128)(2,1)S(1)}, bf16[512,256]{1,0:T(8,128)(2,1)S(1)}, u32[]{:S(2)}, u32[]{:S(2)}) collective-permute-start(bf16[512,256]{1,0:T(8,128)(2,1)S(1)} %collective-permute-done.18.refs_2_), channel_id=1, source_target_pairs={{0,14},{1,15},{2,0},{3,1},{4,2},{5,3},{6,4},{7,5},{8,6},{9,7},{10,... | collective-permute-start | bytes 786440 | tf_op jit(solution)/shard_map/ppermute | solution.py:417
  133.7 6.5 %collective-permute-done.19.refs_3_ = bf16[512,256]{1,0:T(8,128)(2,1)S(1)} collective-permute-done((bf16[512,256]{1,0:T(8,128)(2,1)S(1)}, bf16[512,256]{1,0:T(8,128)(2,1)S(1)}, u32[]{:S(2)}, u32[]{:S(2)}) %collective-permute-start.19) | collective-permute-done | bytes 262176 | tf_op jit(solution)/shard_map/ppermute | solution.py:414
  140.3 1.4 fusion.19
  141.7 1.2 fusion.17
  143.0 2.3 %collective-permute-start.21 = (bf16[512,256]{1,0:T(8,128)(2,1)S(1)}, bf16[512,256]{1,0:T(8,128)(2,1)S(1)}, u32[]{:S(2)}, u32[]{:S(2)}) collective-permute-start(bf16[512,256]{1,0:T(8,128)(2,1)S(1)} %collective-permute-done.19.refs_3_), channel_id=1, source_target_pairs={{0,2},{1,3},{2,4},{3,5},{4,6},{5,7},{6,8},{7,9},{8,10},{9,11},{10,... | collective-permute-start | bytes 786440 | tf_op jit(solution)/shard_map/ppermute | solution.py:414
  145.6 1.4 collective-permute-start.22
  147.6 5.5 %collective-permute-done.21.refs_5_ = bf16[512,256]{1,0:T(8,128)(2,1)S(1)} collective-permute-done((bf16[512,256]{1,0:T(8,128)(2,1)S(1)}, bf16[512,256]{1,0:T(8,128)(2,1)S(1)}, u32[]{:S(2)}, u32[]{:S(2)}) %collective-permute-start.21) | collective-permute-done | bytes 262176 | tf_op jit(solution)/shard_map/ppermute | solution.py:414
  154.6 2.5 %collective-permute-start.24 = (bf16[512,128]{1,0:T(8,128)(2,1)S(1)}, bf16[512,128]{1,0:T(8,128)(2,1)S(1)}, u32[]{:S(2)}, u32[]{:S(2)}) collective-permute-start(bf16[512,128]{1,0:T(8,128)(2,1)S(1)} %slice.43), channel_id=1, source_target_pairs={{0,14},{1,15},{2,0},{3,1},{4,2},{5,3},{6,4},{7,5},{8,6},{9,7},{10,... | collective-permute-start | bytes 393224 | tf_op jit(solution)/shard_map/ppermute | solution.py:417
  157.4 2.6 %collective-permute-done.23.refs_7_ = bf16[512,128]{1,0:T(8,128)(2,1)S(1)} collective-permute-done((bf16[512,128]{1,0:T(8,128)(2,1)S(1)}, bf16[512,128]{1,0:T(8,128)(2,1)S(1)}, u32[]{:S(2)}, u32[]{:S(2)}) %collective-permute-start.23) | collective-permute-done | bytes 131104 | tf_op jit(solution)/shard_map/ppermute | solution.py:414
  160.9 3.1 %collective-permute-start.25 = (bf16[512,512]{1,0:T(8,128)(2,1)S(1)}, bf16[512,512]{1,0:T(8,128)(2,1)S(1)}, u32[]{:S(2)}, u32[]{:S(2)}) collective-permute-start(bf16[512,512]{1,0:T(8,128)(2,1)S(1)} %fusion.7), channel_id=1, source_target_pairs={{0,1},{1,0},{2,3},{3,2},{4,5},{5,4},{6,7},{7,6},{8,9},{9,8},{10,11... | collective-permute-start | bytes 1572872 | tf_op jit(solution)/shard_map/ppermute | solution.py:444
  164.1 2.2 %copy-done.1 = bf16[4096,512]{1,0:T(8,128)(2,1)S(1)} copy-done((bf16[4096,512]{1,0:T(8,128)(2,1)S(1)}, bf16[4096,512]{1,0:T(8,128)(2,1)}, u32[]{:S(2)}) %copy-start.1) | copy-done | bytes 4194328
  166.3 2.7 %shard_map.78 = f32[512,512]{1,0:T(8,128)S(1)} custom-call(s32[9]{0:T(128)S(1)} %broadcast_add_fusion.starts_ref, bf16[4096,512]{1,0:T(8,128)(2,1)S(1)} %copy-done.1, bf16[512,256]{1,0:T(8,128)(2,1)S(1)} %shard_map.77.refs_0_, bf16[512,256]{1,0:T(8,128)(2,1)S(1)} %collective-permute-done.17.refs_1_, bf16[512,256]{1,0:T(8,128)(2,1)S(1)} %collective-permute-done.18.refs_2_, ...), custom_call_target="tpu_custom_call" | custom-call | flops 1073741824 | bytes 5242880 | tf_op jit(solution)/shard_map/pallas_call | solution.py:319
  168.9 5.5 %collective-permute-done.25 = bf16[512,512]{1,0:T(8,128)(2,1)S(1)} collective-permute-done((bf16[512,512]{1,0:T(8,128)(2,1)S(1)}, bf16[512,512]{1,0:T(8,128)(2,1)S(1)}, u32[]{:S(2)}, u32[]{:S(2)}) %collective-permute-start.25) | collective-permute-done | bytes 524320 | tf_op jit(solution)/shard_map/ppermute | solution.py:444
  174.4 2.0 %fusion.1 = bf16[1024,512]{1,0:T(8,128)(2,1)} fusion(s32[512]{0:T(512)S(1)} %bitcast.72, f32[512,512]{1,0:T(8,128)S(1)} %shard_map.78, bf16[512,512]{1,0:T(8,128)(2,1)S(1)} %collective-permute-done.25, f32[512]{0:T(512)S(1)} %bitcast.82), kind=kOutput, calls=%fused_computation.3 | convolution fusion | flops 538968064 | bytes 2625536 | tf_op jit(solution)/shard_map/dot_general | solution.py:451
  (88 shorter events, 15.1 us)
Async XLA Ops:
  6.5 53.5 %all-gather.5.cloned.1.call-start = ((), (), s32[]{:S(2)}) async-start(), calls=%async_computation.3 | async-start | bytes 2359296 | tf_op jit(solution)/shard_map/all_gather | solution.py:353
  7.5 9.6 %collective-permute-start = (bf16[512,256]{1,0:T(8,128)(2,1)S(1)}, bf16[512,256]{1,0:T(8,128)(2,1)S(1)}, u32[]{:S(2)}, u32[]{:S(2)}) collective-permute-start(bf16[512,256]{1,0:T(8,128)(2,1)S(1)} %constant_dynamic-slice_fusion.1), channel_id=1, source_target_pairs={{0,1},{1,0},{2,3},{3,2},{4,5},{5,4},{6,7},{7,6},{8,9},{9,8},{10,11... | collective-permute-start | bytes 786440 | tf_op jit(solution)/shard_map/ppermute | solution.py:356
  12.0 1.2 copy-start.3
  13.2 1.2 copy-start.4
  17.1 0.7 copy-start.8
  17.9 42.1 %all-to-all-start = ((bf16[16,72,512]{2,1,0:T(8,128)(2,1)}), bf16[16,72,512]{2,1,0:T(8,128)(2,1)}, u32[]{:S(2)}, u32[]{:S(2)}) async-start(bf16[16,72,512]{2,1,0:T(8,128)(2,1)} %get-tuple-element.51), calls=%async_computation | async-start | bytes 2359296 | tf_op jit(solution)/shard_map/all_to_all | solution.py:364
  28.2 78.8 %reduce-scatter.2.cloned.1.call-start = ((), (), s32[]{:S(2)}) async-start(), calls=%async_computation.2 | async-start | bytes 2359296 | tf_op jit(solution)/shard_map/reduce_scatter | solution.py:383
  28.3 33.2 %collective-permute-start.1 = (bf16[512,512]{1,0:T(8,128)(2,1)S(1)}, bf16[512,512]{1,0:T(8,128)(2,1)S(1)}, u32[]{:S(2)}, u32[]{:S(2)}) collective-permute-start(bf16[512,512]{1,0:T(8,128)(2,1)S(1)} %get-tuple-element.52.x_ref), channel_id=1, source_target_pairs={{0,1},{1,0},{2,3},{3,2},{4,5},{5,4},{6,7},{7,6},{8,9},{9,8},{10,11... | collective-permute-start | bytes 1572872 | tf_op jit(solution)/shard_map/ppermute | solution.py:360
  32.0 2.5 %copy-start = (bf16[512,4096]{1,0:T(8,128)(2,1)S(1)}, bf16[512,4096]{1,0:T(8,128)(2,1)}, u32[]{:S(2)}) copy-start(bf16[512,4096]{1,0:T(8,128)(2,1)} %w_ref.1) | copy-start | bytes 12582916
  34.4 2.8 %copy-start.12 = (s32[16,512]{1,0:T(8,128)S(1)}, s32[16,512]{1,0:T(8,128)}, u32[]{:S(2)}) copy-start(s32[16,512]{1,0:T(8,128)} %param.13) | copy-start | bytes 98308
  61.5 9.1 %copy-start.6 = (bf16[64,512]{1,0:T(8,128)(2,1)}, bf16[64,512]{1,0:T(8,128)(2,1)S(1)}, u32[]{:S(2)}) copy-start(bf16[64,512]{1,0:T(8,128)(2,1)S(1)} %fusion.22.refs_0_) | copy-start | bytes 196612
  61.5 1.6 copy-start.2
  67.5 72.9 %all-gather.7.cloned.1.call-start = ((), (), s32[]{:S(2)}) async-start(), calls=%async_computation.4 | async-start | bytes 2359296 | tf_op jit(solution)/shard_map/all_gather | solution.py:353
  67.5 8.0 %collective-permute-start.5 = (bf16[256,512]{1,0:T(8,128)(2,1)S(1)}, bf16[256,512]{1,0:T(8,128)(2,1)S(1)}, u32[]{:S(2)}, u32[]{:S(2)}) collective-permute-start(bf16[256,512]{1,0:T(8,128)(2,1)S(1)} %constant_dynamic-slice_fusion), channel_id=1, source_target_pairs={{0,1},{1,0},{2,3},{3,2},{4,5},{5,4},{6,7},{7,6},{8,9},{9,8},{10,11... | collective-permute-start | bytes 786440 | tf_op jit(solution)/shard_map/ppermute | solution.py:387
  68.3 6.2 %collective-permute-start.2 = (bf16[64,512]{1,0:T(8,128)(2,1)S(1)}, bf16[64,512]{1,0:T(8,128)(2,1)S(1)}, u32[]{:S(2)}, u32[]{:S(2)}) collective-permute-start(bf16[64,512]{1,0:T(8,128)(2,1)S(1)} %fusion.22.refs_0_), channel_id=1, source_target_pairs={{0,2},{1,3},{2,4},{3,5},{4,6},{5,7},{6,0},{7,1},{8,10},{9,11},{10,... | collective-permute-start | bytes 196616 | tf_op jit(solution)/shard_map/ppermute | solution.py:386
  68.3 7.2 %collective-permute-start.3 = (bf16[64,512]{1,0:T(8,128)(2,1)S(1)}, bf16[64,512]{1,0:T(8,128)(2,1)S(1)}, u32[]{:S(2)}, u32[]{:S(2)}) collective-permute-start(bf16[64,512]{1,0:T(8,128)(2,1)S(1)} %fusion.22.refs_0_), channel_id=1, source_target_pairs={{0,4},{1,5},{2,6},{3,7},{4,0},{5,1},{6,2},{7,3},{8,12},{9,13},{10,... | collective-permute-start | bytes 196616 | tf_op jit(solution)/shard_map/ppermute | solution.py:386
  70.6 4.9 %collective-permute-start.4 = (bf16[64,512]{1,0:T(8,128)(2,1)S(1)}, bf16[64,512]{1,0:T(8,128)(2,1)S(1)}, u32[]{:S(2)}, u32[]{:S(2)}) collective-permute-start(bf16[64,512]{1,0:T(8,128)(2,1)S(1)} %fusion.22.refs_0_), channel_id=1, source_target_pairs={{0,6},{1,7},{2,0},{3,1},{4,2},{5,3},{6,4},{7,5},{8,14},{9,15},{10,... | collective-permute-start | bytes 196616 | tf_op jit(solution)/shard_map/ppermute | solution.py:386
  74.5 1.0 copy-start.9
  75.5 0.6 copy-start.10
  75.5 0.6 copy-start.11
  75.5 11.5 %copy-start.7 = (bf16[256,512]{1,0:T(8,128)(2,1)}, bf16[256,512]{1,0:T(8,128)(2,1)S(1)}, u32[]{:S(2)}) copy-start(bf16[256,512]{1,0:T(8,128)(2,1)S(1)} %collective-permute-done.5) | copy-start | bytes 786436
  78.0 7.6 %collective-permute-start.6 = (bf16[512,256]{1,0:T(8,128)(2,1)}, bf16[512,256]{1,0:T(8,128)(2,1)S(1)}, u32[]{:S(2)}, u32[]{:S(2)}) collective-permute-start(bf16[512,256]{1,0:T(8,128)(2,1)} %shard_map.76), channel_id=1, source_target_pairs={{0,32},{16,48},{32,64},{48,80},{64,96},{80,112},{96,0},{112,16},{1... | collective-permute-start | bytes 786440 | tf_op jit(solution)/shard_map/ppermute | solution.py:396
  78.5 8.5 %collective-permute-start.7 = (bf16[512,256]{1,0:T(8,128)(2,1)}, bf16[512,256]{1,0:T(8,128)(2,1)S(1)}, u32[]{:S(2)}, u32[]{:S(2)}) collective-permute-start(bf16[512,256]{1,0:T(8,128)(2,1)} %shard_map.76), channel_id=1, source_target_pairs={{0,96},{16,112},{32,0},{48,16},{64,32},{80,48},{96,64},{112,80},{1... | collective-permute-start | bytes 786440 | tf_op jit(solution)/shard_map/ppermute | solution.py:396
  80.0 7.0 %collective-permute-start.8 = (bf16[512,256]{1,0:T(8,128)(2,1)}, bf16[512,256]{1,0:T(8,128)(2,1)S(1)}, u32[]{:S(2)}, u32[]{:S(2)}) collective-permute-start(bf16[512,256]{1,0:T(8,128)(2,1)} %shard_map.76), channel_id=1, source_target_pairs={{0,128},{16,144},{32,160},{48,176},{64,192},{80,208},{96,224},{112... | collective-permute-start | bytes 786440 | tf_op jit(solution)/shard_map/ppermute | solution.py:399
  87.1 10.5 %collective-permute-start.10 = (bf16[512,256]{1,0:T(8,128)(2,1)S(1)}, bf16[512,256]{1,0:T(8,128)(2,1)S(1)}, u32[]{:S(2)}, u32[]{:S(2)}) collective-permute-start(bf16[512,256]{1,0:T(8,128)(2,1)S(1)} %collective-permute-done.8), channel_id=1, source_target_pairs={{0,96},{16,112},{32,0},{48,16},{64,32},{80,48},{96,64},{112,80},{1... | collective-permute-start | bytes 786440 | tf_op jit(solution)/shard_map/ppermute | solution.py:396
  88.0 9.6 %collective-permute-start.9 = (bf16[512,256]{1,0:T(8,128)(2,1)S(1)}, bf16[512,256]{1,0:T(8,128)(2,1)S(1)}, u32[]{:S(2)}, u32[]{:S(2)}) collective-permute-start(bf16[512,256]{1,0:T(8,128)(2,1)S(1)} %collective-permute-done.8), channel_id=1, source_target_pairs={{0,32},{16,48},{32,64},{48,80},{64,96},{80,112},{96,0},{112,16},{1... | collective-permute-start | bytes 786440 | tf_op jit(solution)/shard_map/ppermute | solution.py:396
  90.4 6.2 %collective-permute-start.11 = (bf16[256,256]{1,0:T(8,128)(2,1)S(1)}, bf16[256,256]{1,0:T(8,128)(2,1)S(1)}, u32[]{:S(2)}, u32[]{:S(2)}) collective-permute-start(bf16[256,256]{1,0:T(8,128)(2,1)S(1)} %slice.38), channel_id=1, source_target_pairs={{0,32},{16,48},{32,64},{48,80},{64,96},{80,112},{96,0},{112,16},{1... | collective-permute-start | bytes 393224 | tf_op jit(solution)/shard_map/ppermute | solution.py:396
  90.9 6.6 %collective-permute-start.12 = (bf16[256,256]{1,0:T(8,128)(2,1)S(1)}, bf16[256,256]{1,0:T(8,128)(2,1)S(1)}, u32[]{:S(2)}, u32[]{:S(2)}) collective-permute-start(bf16[256,256]{1,0:T(8,128)(2,1)S(1)} %slice.39), channel_id=1, source_target_pairs={{0,96},{16,112},{32,0},{48,16},{64,32},{80,48},{96,64},{112,80},{1... | collective-permute-start | bytes 393224 | tf_op jit(solution)/shard_map/ppermute | solution.py:396
  97.5 5.4 %collective-permute-start.13 = (bf16[256,256]{1,0:T(8,128)(2,1)S(1)}, bf16[256,256]{1,0:T(8,128)(2,1)S(1)}, u32[]{:S(2)}, u32[]{:S(2)}) collective-permute-start(bf16[256,256]{1,0:T(8,128)(2,1)S(1)} %slice.40), channel_id=1, source_target_pairs={{0,32},{16,48},{32,64},{48,80},{64,96},{80,112},{96,0},{112,16},{1... | collective-permute-start | bytes 393224 | tf_op jit(solution)/shard_map/ppermute | solution.py:396
  100.4 6.3 %collective-permute-start.14 = (bf16[256,256]{1,0:T(8,128)(2,1)S(1)}, bf16[256,256]{1,0:T(8,128)(2,1)S(1)}, u32[]{:S(2)}, u32[]{:S(2)}) collective-permute-start(bf16[256,256]{1,0:T(8,128)(2,1)S(1)} %slice.41), channel_id=1, source_target_pairs={{0,96},{16,112},{32,0},{48,16},{64,32},{80,48},{96,64},{112,80},{1... | collective-permute-start | bytes 393224 | tf_op jit(solution)/shard_map/ppermute | solution.py:396
  101.6 6.5 %collective-permute-start.15 = (bf16[4,512,256]{2,1,0:T(8,128)(2,1)S(1)}, bf16[4,512,256]{2,1,0:T(8,128)(2,1)}, u32[]{:S(2)}, u32[]{:S(2)}) collective-permute-start(bf16[4,512,256]{2,1,0:T(8,128)(2,1)S(1)} %pad_maximum_fusion.refs_0_), channel_id=1, source_target_pairs={{0,16},{16,0},{32,48},{48,32},{64,80},{80,64},{96,112},{112,96},{1... | collective-permute-start | bytes 3145736 | tf_op jit(solution)/shard_map/ppermute | solution.py:410
  106.9 2.9 %collective-permute-start.16 = (bf16[4,512,256]{2,1,0:T(8,128)(2,1)S(1)}, bf16[4,512,256]{2,1,0:T(8,128)(2,1)}, u32[]{:S(2)}, u32[]{:S(2)}) collective-permute-start(bf16[4,512,256]{2,1,0:T(8,128)(2,1)S(1)} %pad_maximum_fusion.1.refs_1_), channel_id=1, source_target_pairs={{0,16},{16,0},{32,48},{48,32},{64,80},{80,64},{96,112},{112,96},{1... | collective-permute-start | bytes 3145736 | tf_op jit(solution)/shard_map/ppermute | solution.py:410
  121.2 9.0 %collective-permute-start.17 = (bf16[512,256]{1,0:T(8,128)(2,1)S(1)}, bf16[512,256]{1,0:T(8,128)(2,1)S(1)}, u32[]{:S(2)}, u32[]{:S(2)}) collective-permute-start(bf16[512,256]{1,0:T(8,128)(2,1)S(1)} %shard_map.77.refs_0_), channel_id=1, source_target_pairs={{0,2},{1,3},{2,4},{3,5},{4,6},{5,7},{6,8},{7,9},{8,10},{9,11},{10,... | collective-permute-start | bytes 786440 | tf_op jit(solution)/shard_map/ppermute | solution.py:414
  122.0 8.2 %collective-permute-start.18 = (bf16[512,256]{1,0:T(8,128)(2,1)S(1)}, bf16[512,256]{1,0:T(8,128)(2,1)S(1)}, u32[]{:S(2)}, u32[]{:S(2)}) collective-permute-start(bf16[512,256]{1,0:T(8,128)(2,1)S(1)} %shard_map.77.refs_0_), channel_id=1, source_target_pairs={{0,14},{1,15},{2,0},{3,1},{4,2},{5,3},{6,4},{7,5},{8,6},{9,7},{10,... | collective-permute-start | bytes 786440 | tf_op jit(solution)/shard_map/ppermute | solution.py:417
  130.2 10.1 %collective-permute-start.19 = (bf16[512,256]{1,0:T(8,128)(2,1)S(1)}, bf16[512,256]{1,0:T(8,128)(2,1)S(1)}, u32[]{:S(2)}, u32[]{:S(2)}) collective-permute-start(bf16[512,256]{1,0:T(8,128)(2,1)S(1)} %collective-permute-done.17.refs_1_), channel_id=1, source_target_pairs={{0,2},{1,3},{2,4},{3,5},{4,6},{5,7},{6,8},{7,9},{8,10},{9,11},{10,... | collective-permute-start | bytes 786440 | tf_op jit(solution)/shard_map/ppermute | solution.py:414
  131.1 9.2 %collective-permute-start.20 = (bf16[512,256]{1,0:T(8,128)(2,1)S(1)}, bf16[512,256]{1,0:T(8,128)(2,1)S(1)}, u32[]{:S(2)}, u32[]{:S(2)}) collective-permute-start(bf16[512,256]{1,0:T(8,128)(2,1)S(1)} %collective-permute-done.18.refs_2_), channel_id=1, source_target_pairs={{0,14},{1,15},{2,0},{3,1},{4,2},{5,3},{6,4},{7,5},{8,6},{9,7},{10,... | collective-permute-start | bytes 786440 | tf_op jit(solution)/shard_map/ppermute | solution.py:417
  140.3 4.9 %copy-start.5 = (bf16[2048,512]{1,0:T(8,128)(2,1)S(1)}, bf16[2048,512]{1,0:T(8,128)(2,1)}, u32[]{:S(2)}) copy-start(bf16[2048,512]{1,0:T(8,128)(2,1)} %all-gather.7.cloned.1.call-done) | copy-start | bytes 6291460
  143.0 10.2 %collective-permute-start.21 = (bf16[512,256]{1,0:T(8,128)(2,1)S(1)}, bf16[512,256]{1,0:T(8,128)(2,1)S(1)}, u32[]{:S(2)}, u32[]{:S(2)}) collective-permute-start(bf16[512,256]{1,0:T(8,128)(2,1)S(1)} %collective-permute-done.19.refs_3_), channel_id=1, source_target_pairs={{0,2},{1,3},{2,4},{3,5},{4,6},{5,7},{6,8},{7,9},{8,10},{9,11},{10,... | collective-permute-start | bytes 786440 | tf_op jit(solution)/shard_map/ppermute | solution.py:414
  145.6 8.1 %collective-permute-start.22 = (bf16[512,256]{1,0:T(8,128)(2,1)S(1)}, bf16[512,256]{1,0:T(8,128)(2,1)S(1)}, u32[]{:S(2)}, u32[]{:S(2)}) collective-permute-start(bf16[512,256]{1,0:T(8,128)(2,1)S(1)} %collective-permute-done.20.refs_4_), channel_id=1, source_target_pairs={{0,14},{1,15},{2,0},{3,1},{4,2},{5,3},{6,4},{7,5},{8,6},{9,7},{10,... | collective-permute-start | bytes 786440 | tf_op jit(solution)/shard_map/ppermute | solution.py:417
  153.7 6.3 %collective-permute-start.23 = (bf16[512,128]{1,0:T(8,128)(2,1)S(1)}, bf16[512,128]{1,0:T(8,128)(2,1)S(1)}, u32[]{:S(2)}, u32[]{:S(2)}) collective-permute-start(bf16[512,128]{1,0:T(8,128)(2,1)S(1)} %slice.42), channel_id=1, source_target_pairs={{0,2},{1,3},{2,4},{3,5},{4,6},{5,7},{6,8},{7,9},{8,10},{9,11},{10,... | collective-permute-start | bytes 393224 | tf_op jit(solution)/shard_map/ppermute | solution.py:414
  154.6 5.6 %collective-permute-start.24 = (bf16[512,128]{1,0:T(8,128)(2,1)S(1)}, bf16[512,128]{1,0:T(8,128)(2,1)S(1)}, u32[]{:S(2)}, u32[]{:S(2)}) collective-permute-start(bf16[512,128]{1,0:T(8,128)(2,1)S(1)} %slice.43), channel_id=1, source_target_pairs={{0,14},{1,15},{2,0},{3,1},{4,2},{5,3},{6,4},{7,5},{8,6},{9,7},{10,... | collective-permute-start | bytes 393224 | tf_op jit(solution)/shard_map/ppermute | solution.py:417
  160.9 13.6 %collective-permute-start.25 = (bf16[512,512]{1,0:T(8,128)(2,1)S(1)}, bf16[512,512]{1,0:T(8,128)(2,1)S(1)}, u32[]{:S(2)}, u32[]{:S(2)}) collective-permute-start(bf16[512,512]{1,0:T(8,128)(2,1)S(1)} %fusion.7), channel_id=1, source_target_pairs={{0,1},{1,0},{2,3},{3,2},{4,5},{5,4},{6,7},{7,6},{8,9},{9,8},{10,11... | collective-permute-start | bytes 1572872 | tf_op jit(solution)/shard_map/ppermute | solution.py:444
  164.1 2.2 %copy-start.1 = (bf16[4096,512]{1,0:T(8,128)(2,1)S(1)}, bf16[4096,512]{1,0:T(8,128)(2,1)}, u32[]{:S(2)}) copy-start(bf16[4096,512]{1,0:T(8,128)(2,1)} %w_hbm.1) | copy-start | bytes 12582916
Sparse Core Ops, SparseCore 0:
  18.0 29.2 all-gather.4
  67.6 37.9 reduce-scatter.1
  107.4 25.5 all-gather.6
